TPU v7x, 32 devices: a whole 2x2x4 slice. The times are simulated.
32 devices in a mesh: ctx: 8 (over z, core), head: 4 (over y, x).
Axes of the slice: x: 2, y: 2, z: 4, core: 2. Of those that a mesh axis runs over, the one named last changes fastest.
Arguments:
- queries: bfloat16 [2048, 8192], P('ctx', 'head'), may hold values from -40 to 40
- keys: bfloat16 [2048, 1024], P('ctx', 'head'), may hold values from -4 to 4
- values: bfloat16 [2048, 1024], P('ctx', 'head'), may hold values from -6 to 6
- out_weight: bfloat16 [8192, 8192], P(None, 'head'), may hold values from -0.1796875 to 0.1796875
- doc_lengths: int32 [16], replicated, may hold values from 1 to 512, 2048 in all
- owners: int32 [64, 1], replicated, may hold values from 0 to 7; in each aligned block of 8 rows (0 to 7, 8 to 15, ...) no two rows name the same one
Outputs:
- attended: bfloat16 [8192, 2048], P('head', 'ctx')
Inputs may be any that keep to these rules, and one draw needn't show every extreme that they name: `owners`: among the 8 pieces loaded by one index of ctx (aligned blocks of 8 rows) every owner appears at most once. `doc_lengths`: the lengths sum to 2048; the longest is exactly 512.
All inputs are finite; a program needn't handle non-finite values.
Results may differ from a plain program's by a relative error of at most 0.018.
Values may be sent and summed in bfloat16 or wider, within the bound.
No kernel may reach another device: no remote copies, remote signals or barrier semaphores. Data moves between devices by JAX's collectives and lax.ppermute only.
A program may use at most 128 MiB of HBM per device.

v0:
```python
import math

import jax
import jax.numpy as jnp
from jax import lax
from jax.sharding import PartitionSpec as P

HEAD_SIZE = 128
PIECES = 8


MASKED = -1e30


def document_index(positions, doc_starts):
    return jnp.sum((positions[:, None] >= doc_starts[None, :]).astype(jnp.int32), axis=1) - 1


def attend(query_rows, query_pos, keys, values, doc_starts):
    row_count = query_rows.shape[0]
    key_heads = keys.shape[1] // HEAD_SIZE
    group_length = query_rows.shape[1] // keys.shape[1]
    query_heads = query_rows.reshape(row_count, key_heads, group_length, HEAD_SIZE)
    query_doc = document_index(query_pos, doc_starts)
    score_scale = 1.0 / math.sqrt(HEAD_SIZE)
    initial = (
        jnp.full((row_count, key_heads, group_length), MASKED, jnp.float32),
        jnp.zeros((row_count, key_heads, group_length), jnp.float32),
        jnp.zeros((row_count, key_heads, group_length, HEAD_SIZE), jnp.float32),
    )
    key_piece = lax.all_gather(keys, "ctx", axis=0, tiled=True)
    value_piece = lax.all_gather(values, "ctx", axis=0, tiled=True)
    piece_rows = key_piece.shape[0]
    tile_rows = math.gcd(piece_rows, 512)

    def one_tile(tile_index, running):
        tile_start = tile_index * tile_rows
        key_block = lax.dynamic_slice_in_dim(key_piece, tile_start, tile_rows, 0).reshape(
            tile_rows, key_heads, HEAD_SIZE
        )
        value_block = lax.dynamic_slice_in_dim(value_piece, tile_start, tile_rows, 0).reshape(
            tile_rows, key_heads, HEAD_SIZE
        )
        key_pos = tile_start + jnp.arange(tile_rows, dtype=jnp.int32)
        key_doc = document_index(key_pos, doc_starts)
        allowed = (query_doc[:, None] == key_doc[None, :]) & (
            key_pos[None, :] <= query_pos[:, None]
        )
        running_max, running_sum, weighted = running
        scores = (
            jnp.einsum("rkgd,nkd->rkgn", query_heads, key_block, preferred_element_type=jnp.float32)
            * score_scale
        )
        allowed_all = allowed[:, None, None, :]
        scores = jnp.where(allowed_all, scores, MASKED)
        new_max = jnp.maximum(running_max, jnp.max(scores, axis=-1))
        factor = jnp.exp(running_max - new_max)
        weights = jnp.where(allowed_all, jnp.exp(scores - new_max[..., None]), 0.0)
        new_sum = running_sum * factor + jnp.sum(weights, axis=-1)
        new_weighted = weighted * factor[..., None] + jnp.einsum(
            "rkgn,nkd->rkgd",
            weights.astype(jnp.bfloat16),
            value_block,
            preferred_element_type=jnp.float32,
        )
        return (new_max, new_sum, new_weighted)

    final_max, final_sum, weighted = lax.fori_loop(0, piece_rows // tile_rows, one_tile, initial)
    result = weighted / jnp.maximum(final_sum, 1.0)[..., None]
    return result.reshape(row_count, key_heads * group_length * HEAD_SIZE).astype(jnp.bfloat16)


def project(context, out_weight):
    return lax.psum_scatter(
        lax.dot_general(
            out_weight, context, (((1,), (1,)), ((), ())), preferred_element_type=jnp.float32
        ).astype(jnp.bfloat16),
        "head",
        scatter_dimension=0,
        tiled=True,
    )


def per_device(queries, keys, values, out_weight, doc_lengths, owners):
    place_count = lax.axis_size("ctx")
    own_index = lax.axis_index("ctx")
    token_count = queries.shape[0]
    block_rows = token_count // PIECES
    doc_ends = jnp.cumsum(doc_lengths)
    doc_starts = doc_ends - doc_lengths
    owner_table = owners[:, 0].reshape(place_count, PIECES)
    own_owners = lax.dynamic_index_in_dim(owner_table, own_index, 0, keepdims=False)
    place_ids = jnp.arange(place_count, dtype=jnp.int32)
    send_pick = (own_owners[None, :] == place_ids[:, None]).astype(jnp.bfloat16)
    grouped = queries.reshape(PIECES, block_rows, queries.shape[1])
    outgoing = jnp.einsum(
        "oc,chw->ohw", send_pick, grouped, preferred_element_type=jnp.float32
    ).astype(jnp.bfloat16)
    arrived = lax.all_to_all(outgoing, "ctx", split_axis=0, concat_axis=0, tiled=True)
    slot_hits = (owner_table == own_index).astype(jnp.int32)
    slot_live = jnp.sum(slot_hits, axis=1)
    picked = jnp.sum(slot_hits * jnp.arange(PIECES, dtype=jnp.int32)[None, :], axis=1)
    slot_pos = (place_ids[:, None] * PIECES + picked[:, None]) * block_rows + jnp.arange(
        block_rows, dtype=jnp.int32
    )[None, :]
    query_pos = jnp.where(slot_live[:, None] > 0, slot_pos, -1).reshape(-1)
    context = attend(
        arrived.reshape(place_count * block_rows, queries.shape[1]),
        query_pos,
        keys,
        values,
        doc_starts,
    )
    return project(context, out_weight)


def solution(mesh):
    in_specs = (P("ctx", "head"), P("ctx", "head"), P("ctx", "head"), P(None, "head"), P(), P())
    out_specs = P("head", "ctx")
    return jax.shard_map(
        per_device, mesh=mesh, in_specs=in_specs, out_specs=out_specs, check_vma=False
    )
```

profile of v0, /device:TPU:0, one launch (start us, length us, event | category | flops | bytes accessed | tf_op | source)
XLA Modules:
  0.0 190.3 jit_solution(14914956340711519767)
XLA Ops:
  6.5 1.7 copy.33
  8.3 0.5 broadcast.203
  8.8 1.3 reduce.4
  10.1 0.1 reshape_squeeze.3
  10.2 0.8 convolution_convert_fusion.1
  11.0 1.5 copy.35
  12.6 6.3 %all-to-all-start = ((bf16[8,32,2048]{2,1,0:T(8,128)(2,1)}), bf16[8,32,2048]{2,1,0:T(8,128)(2,1)S(1)}, u32[]{:S(2)}, u32[]{:S(2)}) async-start(bf16[8,32,2048]{2,1,0:T(8,128)(2,1)} %copy.35), calls=%async_computation | async-start | bytes 2097152 | tf_op jit(solution)/shard_map/all_to_all | solution.py:99
  18.9 0.0 all-gather.5.cloned.1.call-start
  19.0 1.7 copy.36
  20.6 0.0 all-gather.5.cloned.1.call-update
  20.7 0.0 reduce-scatter.2.cloned.1.call-start
  20.7 0.1 convert_reduce_fusion.2
  20.9 0.1 add_select_fusion.1
  21.0 0.1 select_n.48
  21.1 0.7 copy.32
  21.8 0.1 reduce.1
  22.0 0.7 sub.48
  22.6 0.1 convert_reduce_fusion.1
  22.7 30.9 %all-to-all-done = bf16[8,32,2048]{2,1,0:T(8,128)(2,1)S(1)} async-done(((bf16[8,32,2048]{2,1,0:T(8,128)(2,1)}), bf16[8,32,2048]{2,1,0:T(8,128)(2,1)S(1)}, u32[]{:S(2)}, u32[]{:S(2)}) %all-to-all-start) | async-done | bytes 1048608 | tf_op jit(solution)/shard_map/all_to_all | solution.py:99
  53.7 0.2 copy.44
  53.9 0.3 copy.37
  54.2 0.0 all-gather.3.cloned.1.call-done
  54.2 20.9 %all-gather.5.cloned.1.call-done = bf16[2048,256]{0,1:T(8,128)(2,1)} async-done(((bf16[256,256]{0,1:T(8,128)(2,1)}), bf16[2048,256]{0,1:T(8,128)(2,1)}) %all-gather.5.cloned.1.call-update) | async-done | bytes 1048592 | tf_op jit(solution)/shard_map/all_gather | solution.py:32
  75.1 36.4 %while.20 = (s32[]{:T(128)}, f32[256,2,8]{0,2,1:T(8,128)S(1)}, f32[256,2,8]{0,2,1:T(8,128)S(1)}, f32[256,2,8,128]{0,3,2,1:T(8,128)}, s32[256]{0:T(256)S(1)}, /*i...) while((s32[]{:T(128)}, f32[256,2,8]{0,2,1:T(8,128)S(1)}, ...), condition=%wide.region_8.9_spmd.clone, body=%wide.region_4.8_spmd.clone.sunk | while | flops 1103016960 | bytes 49565044 | solution.py:68
  75.1 0.1 convert_reduce_fusion.4
  75.2 0.1 add_select_fusion.3
  75.3 0.1 le.52
  75.4 0.2 compare_and_fusion.2
  75.6 1.1 constant_dynamic-slice_fusion.3
  76.7 1.5 fusion.35
  78.2 2.0 %fusion.36 = f32[256,2,8]{0,2,1:T(8,128)S(1)} fusion(f32[2,512,256,8]{2,1,3,0:T(8,128)S(1)} %get-tuple-element.428, f32[256,2,8]{0,2,1:T(8,128)S(1)} %select_maximum_fusion.2, pred[256,512]{0,1:T(8,128)(4,1)S(1)} %compare_and_fusion.2), kind=kLoop, calls=%fused_computation.5.clone.1 | loop fusion | flops 10481664 | bytes 8552448 | tf_op jit(solution)/shard_map/while/body/eval_jaxpr/reduce_sum | solution.py:59
  80.3 2.6 %bitcast_add_fusion.2 = f32[256,2,8,128]{0,3,2,1:T(8,128)S(1)} fusion(f32[256,2,8,128]{0,3,2,1:T(8,128)S(1)} %copy-done.1, bf16[512,2,128,1]{0,2,3,1:T(8,128)(2,1)S(1)} %bitcast.65, f32[2,512,256,8]{2,1,3,0:T(8,128)S(1)} %get-tuple-element.428, f32[256,2,8]{0,2,1:T(8,128)S(1)} %select_maximum_fusion.2, pred[256,512]{0,1:T(8,128)(4,1)S(1)} %compare_and_fusion.2, ...), kind=kOutput, calls=%fused_computation.8.clone.1 | convolution fusion | flops 548929536 | bytes 13008897 | tf_op jit(solution)/shard_map/while/body/eval_jaxpr/rkgn,nkd->rkgd/dot_general | solution.py:60
  82.9 1.3 copy-done.2
  84.2 0.1 convert_reduce_fusion.4
  84.3 0.1 add_select_fusion.3
  84.4 0.1 le.52
  84.5 0.2 compare_and_fusion.2
  84.7 1.1 constant_dynamic-slice_fusion.3
  85.8 1.5 fusion.35
  87.3 2.0 %fusion.36 = f32[256,2,8]{0,2,1:T(8,128)S(1)} fusion(f32[2,512,256,8]{2,1,3,0:T(8,128)S(1)} %get-tuple-element.428, f32[256,2,8]{0,2,1:T(8,128)S(1)} %select_maximum_fusion.2, pred[256,512]{0,1:T(8,128)(4,1)S(1)} %compare_and_fusion.2), kind=kLoop, calls=%fused_computation.5.clone.1 | loop fusion | flops 10481664 | bytes 8552448 | tf_op jit(solution)/shard_map/while/body/eval_jaxpr/reduce_sum | solution.py:59
  89.4 2.6 %bitcast_add_fusion.2 = f32[256,2,8,128]{0,3,2,1:T(8,128)S(1)} fusion(f32[256,2,8,128]{0,3,2,1:T(8,128)S(1)} %copy-done.1, bf16[512,2,128,1]{0,2,3,1:T(8,128)(2,1)S(1)} %bitcast.65, f32[2,512,256,8]{2,1,3,0:T(8,128)S(1)} %get-tuple-element.428, f32[256,2,8]{0,2,1:T(8,128)S(1)} %select_maximum_fusion.2, pred[256,512]{0,1:T(8,128)(4,1)S(1)} %compare_and_fusion.2, ...), kind=kOutput, calls=%fused_computation.8.clone.1 | convolution fusion | flops 548929536 | bytes 13008897 | tf_op jit(solution)/shard_map/while/body/eval_jaxpr/rkgn,nkd->rkgd/dot_general | solution.py:60
  92.0 1.3 copy-done.2
  93.3 0.1 convert_reduce_fusion.4
  93.4 0.1 add_select_fusion.3
  93.5 0.1 le.52
  93.6 0.2 compare_and_fusion.2
  93.8 1.1 constant_dynamic-slice_fusion.3
  94.9 1.5 fusion.35
  96.4 2.0 %fusion.36 = f32[256,2,8]{0,2,1:T(8,128)S(1)} fusion(f32[2,512,256,8]{2,1,3,0:T(8,128)S(1)} %get-tuple-element.428, f32[256,2,8]{0,2,1:T(8,128)S(1)} %select_maximum_fusion.2, pred[256,512]{0,1:T(8,128)(4,1)S(1)} %compare_and_fusion.2), kind=kLoop, calls=%fused_computation.5.clone.1 | loop fusion | flops 10481664 | bytes 8552448 | tf_op jit(solution)/shard_map/while/body/eval_jaxpr/reduce_sum | solution.py:59
  98.5 2.6 %bitcast_add_fusion.2 = f32[256,2,8,128]{0,3,2,1:T(8,128)S(1)} fusion(f32[256,2,8,128]{0,3,2,1:T(8,128)S(1)} %copy-done.1, bf16[512,2,128,1]{0,2,3,1:T(8,128)(2,1)S(1)} %bitcast.65, f32[2,512,256,8]{2,1,3,0:T(8,128)S(1)} %get-tuple-element.428, f32[256,2,8]{0,2,1:T(8,128)S(1)} %select_maximum_fusion.2, pred[256,512]{0,1:T(8,128)(4,1)S(1)} %compare_and_fusion.2, ...), kind=kOutput, calls=%fused_computation.8.clone.1 | convolution fusion | flops 548929536 | bytes 13008897 | tf_op jit(solution)/shard_map/while/body/eval_jaxpr/rkgn,nkd->rkgd/dot_general | solution.py:60
  101.1 1.3 copy-done.2
  102.4 0.1 convert_reduce_fusion.4
  102.5 0.1 add_select_fusion.3
  102.6 0.1 le.52
  102.7 0.2 compare_and_fusion.2
  102.9 1.1 constant_dynamic-slice_fusion.3
  104.0 1.5 fusion.35
  105.5 2.0 %fusion.36 = f32[256,2,8]{0,2,1:T(8,128)S(1)} fusion(f32[2,512,256,8]{2,1,3,0:T(8,128)S(1)} %get-tuple-element.428, f32[256,2,8]{0,2,1:T(8,128)S(1)} %select_maximum_fusion.2, pred[256,512]{0,1:T(8,128)(4,1)S(1)} %compare_and_fusion.2), kind=kLoop, calls=%fused_computation.5.clone.1 | loop fusion | flops 10481664 | bytes 8552448 | tf_op jit(solution)/shard_map/while/body/eval_jaxpr/reduce_sum | solution.py:59
  107.6 2.6 %bitcast_add_fusion.2 = f32[256,2,8,128]{0,3,2,1:T(8,128)S(1)} fusion(f32[256,2,8,128]{0,3,2,1:T(8,128)S(1)} %copy-done.1, bf16[512,2,128,1]{0,2,3,1:T(8,128)(2,1)S(1)} %bitcast.65, f32[2,512,256,8]{2,1,3,0:T(8,128)S(1)} %get-tuple-element.428, f32[256,2,8]{0,2,1:T(8,128)S(1)} %select_maximum_fusion.2, pred[256,512]{0,1:T(8,128)(4,1)S(1)} %compare_and_fusion.2, ...), kind=kOutput, calls=%fused_computation.8.clone.1 | convolution fusion | flops 548929536 | bytes 13008897 | tf_op jit(solution)/shard_map/while/body/eval_jaxpr/rkgn,nkd->rkgd/dot_general | solution.py:60
  110.2 1.3 copy-done.2
  111.5 1.8 divide_convert_fusion
  113.3 16.7 %fusion.14 = bf16[8192,256]{0,1:T(8,128)(2,1)} fusion(bf16[256,2048]{0,1:T(8,128)(2,1)S(1)} %bitcast.68, bf16[8192,2048]{1,0:T(8,128)(2,1)} %param.11), kind=kOutput, calls=%fused_computation.25 | convolution fusion | flops 8592031744 | bytes 38797312 | tf_op jit(solution)/shard_map/dot_general | solution.py:75
  130.0 51.5 %reduce-scatter.2.cloned.1.call-done = bf16[2048,256]{0,1:T(8,128)(2,1)} async-done(((bf16[8192,256]{0,1:T(8,128)(2,1)}), bf16[2048,256]{0,1:T(8,128)(2,1)}) %reduce-scatter.2.cloned.1.call-update) | async-done | bytes 1048592 | tf_op jit(solution)/shard_map/reduce_scatter | solution.py:74
  181.5 2.3 %copy.38 = bf16[2048,256]{1,0:T(8,128)(2,1)} copy(bf16[2048,256]{0,1:T(8,128)(2,1)} %reduce-scatter.2.cloned.1.call-done) | data formatting | bytes 2097152 | tf_op jit(solution)/shard_map/reduce_scatter | solution.py:74
  (46 shorter events, 0.3 us)
Async XLA Ops:
  6.5 3.7 %copy-start = (bf16[256,2048]{1,0:T(8,128)(2,1)S(1)}, bf16[256,2048]{1,0:T(8,128)(2,1)}, u32[]{:S(2)}) copy-start(bf16[256,2048]{1,0:T(8,128)(2,1)} %param.8) | copy-start | bytes 3145732
  6.5 47.6 %all-gather.3.cloned.1.call-start = ((), (), s32[]{:S(2)}) async-start(), calls=%async_computation.2 | async-start | bytes 1179648 | tf_op jit(solution)/shard_map/all_gather | solution.py:31
  12.6 41.1 %all-to-all-start = ((bf16[8,32,2048]{2,1,0:T(8,128)(2,1)}), bf16[8,32,2048]{2,1,0:T(8,128)(2,1)S(1)}, u32[]{:S(2)}, u32[]{:S(2)}) async-start(bf16[8,32,2048]{2,1,0:T(8,128)(2,1)} %copy.35), calls=%async_computation | async-start | bytes 2097152 | tf_op jit(solution)/shard_map/all_to_all | solution.py:99
  18.9 56.2 %all-gather.5.cloned.1.call-start = ((), (), s32[]{:S(2)}) async-start(), calls=%async_computation.3 | async-start | bytes 1179648 | tf_op jit(solution)/shard_map/all_gather | solution.py:32
  20.7 160.8 %reduce-scatter.2.cloned.1.call-start = ((), (), s32[]{:S(2)}) async-start(), calls=%async_computation.4 | async-start | bytes 5242880 | tf_op jit(solution)/shard_map/reduce_scatter | solution.py:74
  76.7 3.6 %copy-start.1 = (f32[256,2,8,128]{0,3,2,1:T(8,128)S(1)}, f32[256,2,8,128]{0,3,2,1:T(8,128)}, u32[]{:S(2)}) copy-start(f32[256,2,8,128]{0,3,2,1:T(8,128)} %get-tuple-element.450) | copy-start | bytes 6291460 | tf_op jit(solution)/shard_map/while
  82.9 1.4 copy-start.2
  85.8 3.6 %copy-start.1 = (f32[256,2,8,128]{0,3,2,1:T(8,128)S(1)}, f32[256,2,8,128]{0,3,2,1:T(8,128)}, u32[]{:S(2)}) copy-start(f32[256,2,8,128]{0,3,2,1:T(8,128)} %get-tuple-element.450) | copy-start | bytes 6291460 | tf_op jit(solution)/shard_map/while
  92.0 1.4 copy-start.2
  94.9 3.6 %copy-start.1 = (f32[256,2,8,128]{0,3,2,1:T(8,128)S(1)}, f32[256,2,8,128]{0,3,2,1:T(8,128)}, u32[]{:S(2)}) copy-start(f32[256,2,8,128]{0,3,2,1:T(8,128)} %get-tuple-element.450) | copy-start | bytes 6291460 | tf_op jit(solution)/shard_map/while
  101.1 1.4 copy-start.2
  104.0 3.6 %copy-start.1 = (f32[256,2,8,128]{0,3,2,1:T(8,128)S(1)}, f32[256,2,8,128]{0,3,2,1:T(8,128)}, u32[]{:S(2)}) copy-start(f32[256,2,8,128]{0,3,2,1:T(8,128)} %get-tuple-element.450) | copy-start | bytes 6291460 | tf_op jit(solution)/shard_map/while
  110.2 1.4 copy-start.2
Sparse Core Ops, SparseCore 0:
  8.9 42.3 all-gather.2
  52.9 22.1 all-gather.4
  130.2 51.2 reduce-scatter.1
where the time goes:
time: 191 us; the launch traced here: 190 us
  waiting for transfers between devices  103 us (54%)
  matrix products  33.9 us (18%)
  local copies, waits for them, and re-layouts  19.1 us (10%)
  other arithmetic  13.9 us (7%)
  between operations  13.2 us (7%)
  starting transfers between devices  6.4 us (3%)
    reduce_scatter x1, waiting for transfers between devices, project(): lax.psum_scatter(lax.dot_general(out_weight, context, (((1,), (1,)), ((),...  51.5 us
    all_to_all x1, waiting for transfers between devices, per_device(): lax.all_to_all(outgoing, 'ctx', split_axis=0, concat_axis=0, tiled=True)  30.9 us
    all_gather x1, waiting for transfers between devices, attend(): value_piece = lax.all_gather(values, 'ctx', axis=0, tiled=True)  20.9 us
    dot_general x1, matrix products, project(): lax.dot_general(out_weight, context, (((1,), (1,)), ((), ())), preferred_...  16.7 us
    dot_general x4, matrix products, one_tile(): jnp.einsum('rkgn,nkd->rkgd', weights.astype(jnp.bfloat16), value_block, p...  10.4 us
    reduce_sum x4, other arithmetic, one_tile(): new_sum = running_sum * factor + jnp.sum(weights, axis=-1)  8.02 us
    all_to_all x1, starting transfers between devices, per_device(): lax.all_to_all(outgoing, 'ctx', split_axis=0, concat_axis=0, tiled=True)  6.32 us
    dot_general x4, matrix products, one_tile(): jnp.einsum('rkgd,nkd->rkgn', query_heads, key_block, preferred_element_ty...  6.08 us
  transfers between devices with their start and end apart: 4, of which 3 were waited for; matrix products, arithmetic and copies ran while one was open for 4% of the time, Pallas kernels for 0%

commit v1 on v0

--- a/solution.py
+++ b/solution.py
@@ -1,12 +1,16 @@
+import functools
 import math
 
 import jax
 import jax.numpy as jnp
 from jax import lax
+from jax.experimental import pallas as pl
+from jax.experimental.pallas import tpu as pltpu
 from jax.sharding import PartitionSpec as P
 
 HEAD_SIZE = 128
 PIECES = 8
+N_FAST_HEAD = 4
 
 
 MASKED = -1e30
@@ -114,9 +118,303 @@
     return project(context, out_weight)
 
 
+def _find_piece(owners_ref, source, owner):
+    piece = jnp.int32(0)
+    for i in range(PIECES):
+        piece = jnp.where(owners_ref[source * PIECES + i, 0] == owner, jnp.int32(i), piece)
+    return piece
+
+
+def _queries_for_other_core(meta_ref, owners_ref, queries_ref, out_ref, sems):
+    c = meta_ref[0]
+    core = lax.rem(c, 2)
+    copies = []
+    for j in range(PIECES // 2):
+        piece = _find_piece(owners_ref, c, 2 * j + 1 - core)
+        rows = queries_ref.shape[0] // PIECES
+        copies.append(
+            pltpu.make_async_copy(
+                queries_ref.at[pl.ds(pl.multiple_of(piece * rows, rows), rows)],
+                out_ref.at[pl.ds(j * rows, rows)],
+                sems.at[j],
+            )
+        )
+    for copy in copies:
+        copy.start()
+    for copy in copies:
+        copy.wait()
+
+
+def _attend_kernel(
+    groups, meta_ref, owners_ref, lengths_ref, queries_ref, other_ref,
+    k0_ref, k1_ref, k2_ref, k3_ref, v0_ref, v1_ref, v2_ref, v3_ref,
+    *rest,
+):
+    out_refs, (kbuf, vbuf, qbuf, ctxbuf, kv_sems, q_sems) = rest[: len(groups)], rest[len(groups):]
+    c = meta_ref[0]
+    core = lax.rem(c, 2)
+    z = lax.div(c, 2)
+    rows = k0_ref.shape[0]
+    piece_rows = rows // PIECES
+    tile = 128
+    slots = (2 + core, 3 - core, core, 1 - core)
+    copies = []
+    for b, (k_ref, v_ref) in enumerate(((k0_ref, v0_ref), (k1_ref, v1_ref), (k2_ref, v2_ref), (k3_ref, v3_ref))):
+        at = pl.ds(pl.multiple_of(slots[b] * rows, rows), rows)
+        copies.append(pltpu.make_async_copy(k_ref, kbuf.at[at], kv_sems.at[2 * b]))
+        copies.append(pltpu.make_async_copy(v_ref, vbuf.at[at], kv_sems.at[2 * b + 1]))
+    starts = []
+    for n, k in enumerate(groups):
+        zdest = z ^ k
+        owner = 2 * zdest + core
+        mine = _find_piece(owners_ref, c, owner)
+        theirs = _find_piece(owners_ref, c + 1 - 2 * core, owner)
+        mine_at = 2 * n + core
+        copies.append(pltpu.make_async_copy(
+            queries_ref.at[pl.ds(pl.multiple_of(mine * piece_rows, piece_rows), piece_rows)],
+            qbuf.at[mine_at], q_sems.at[2 * n]))
+        copies.append(pltpu.make_async_copy(
+            other_ref.at[pl.ds(pl.multiple_of(zdest * piece_rows, piece_rows), piece_rows)],
+            qbuf.at[2 * n + 1 - core], q_sems.at[2 * n + 1]))
+        at0 = jnp.where(core == 0, mine, theirs)
+        at1 = jnp.where(core == 0, theirs, mine)
+        starts.append((at0 * piece_rows, rows + at1 * piece_rows))
+    for copy in copies:
+        copy.start()
+    doc_start = []
+    running = jnp.int32(0)
+    for d in range(lengths_ref.shape[0]):
+        doc_start.append(running)
+        running = running + lengths_ref[d]
+    for copy in copies:
+        copy.wait()
+    base = 2 * rows * (z - 1)
+    heads = k0_ref.shape[1] // HEAD_SIZE
+    group = queries_ref.shape[1] // k0_ref.shape[1]
+    scale = math.log2(math.e) / math.sqrt(HEAD_SIZE)
+    span = 5 * tile
+
+    def one_piece(n, p0):
+        first = lax.div(p0, tile) * tile + 2 * rows - 4 * tile
+        first = pl.multiple_of(first, tile)
+        lane = lax.broadcasted_iota(jnp.int32, (1, tile), 1)
+        pos = 2 * rows * z + p0 + lax.rem(lane, piece_rows)
+        low = jnp.zeros((1, tile), jnp.int32)
+        for start in doc_start:
+            low = jnp.where(pos >= start, start, low)
+        key_pos = base + first + lax.broadcasted_iota(jnp.int32, (span, tile), 0)
+        allowed = (key_pos >= low) & (key_pos <= pos)
+        allowed = jnp.concatenate([allowed] * (group * piece_rows // tile), axis=1)
+        for kv in range(heads):
+            cols = pl.ds(kv * HEAD_SIZE, HEAD_SIZE)
+            q = jnp.concatenate(
+                [qbuf[n, :, pl.ds((kv * group + g) * HEAD_SIZE, HEAD_SIZE)] for g in range(group)], axis=0)
+            k = kbuf[pl.ds(first, span), cols]
+            v = vbuf[pl.ds(first, span), cols]
+            s = lax.dot_general(k, q, (((1,), (1,)), ((), ())), preferred_element_type=jnp.float32) * scale
+            s = jnp.where(allowed, s, MASKED)
+            top = jnp.max(s, axis=0, keepdims=True)
+            w = jnp.exp2(s - top)
+            total = jnp.sum(w, axis=0, keepdims=True)
+            o = lax.dot_general(v, w.astype(jnp.bfloat16), (((0,), (0,)), ((), ())),
+                                preferred_element_type=jnp.float32)
+            o = (o / total).T.astype(jnp.bfloat16)
+            for g in range(group):
+                ctxbuf[n, :, pl.ds((kv * group + g) * HEAD_SIZE, HEAD_SIZE)] = o[g * piece_rows:(g + 1) * piece_rows]
+
+    def step(n, carry):
+        p0 = starts[0][0]
+        for m in range(1, 2 * len(groups)):
+            p0 = jnp.where(n == m, starts[m // 2][m % 2], p0)
+        one_piece(n, p0)
+        return carry
+
+    lax.fori_loop(0, 2 * len(groups), step, 0)
+    for n, out_ref in enumerate(out_refs):
+        out_ref[...] = ctxbuf[2 * n:2 * n + 2].reshape(out_ref.shape)
+
+
+def _attend_groups(groups, meta, owners, lengths, queries, other, kv):
+    piece = queries.shape[0] // PIECES
+    rows = kv[0].shape[0]
+    smem = pl.BlockSpec(memory_space=pltpu.SMEM)
+    hbm = pl.BlockSpec(memory_space=pl.ANY)
+    vmem = pl.BlockSpec(memory_space=pltpu.VMEM)
+    return pl.pallas_call(
+        functools.partial(_attend_kernel, groups),
+        out_shape=[jax.ShapeDtypeStruct((2 * piece, queries.shape[1]), jnp.bfloat16) for _ in groups],
+        in_specs=[smem] * 3 + [hbm] * 10,
+        out_specs=[vmem] * len(groups),
+        scratch_shapes=[
+            pltpu.VMEM((4 * rows, kv[0].shape[1]), jnp.bfloat16),
+            pltpu.VMEM((4 * rows, kv[0].shape[1]), jnp.bfloat16),
+            pltpu.VMEM((2 * len(groups), piece, queries.shape[1]), jnp.bfloat16),
+            pltpu.VMEM((2 * len(groups), piece, queries.shape[1]), jnp.bfloat16),
+            pltpu.SemaphoreType.DMA((8,)),
+            pltpu.SemaphoreType.DMA((2 * len(groups),)),
+        ],
+        compiler_params=pltpu.CompilerParams(vmem_limit_bytes=32 * 2**20),
+        cost_estimate=pl.CostEstimate(flops=4 * 10**8, bytes_accessed=3 * 2**20, transcendentals=10**6),
+        name="attend_groups",
+    )(meta, owners, lengths, queries, other, *kv)
+
+
+def _project_kernel(parts, block, meta_ref, a_ref, b_ref, w_ref, out_ref, wbuf, catbuf, ctxbuf, sems):
+    h = meta_ref[1]
+    second = lax.rem(lax.div(meta_ref[0], 2), 2)
+    half = w_ref.shape[0] // (2 * N_FAST_HEAD)
+    per = half // block
+    copies = []
+    for i, (flip, side) in enumerate(parts):
+        for j in range(per):
+            row = pl.multiple_of((h ^ flip) * (2 * half) + side * half + j * block, block)
+            n = i * per + j
+            copies.append(pltpu.make_async_copy(w_ref.at[pl.ds(row, block)], wbuf.at[n], sems.at[n]))
+    for copy in copies:
+        copy.start()
+    mid = a_ref.shape[0]
+    catbuf[pl.ds(pl.multiple_of(second * mid, mid), mid)] = a_ref[...]
+    catbuf[pl.ds(pl.multiple_of((1 - second) * mid, mid), mid)] = b_ref[...]
+    ctxbuf[...] = catbuf[...].T
+    for n, copy in enumerate(copies):
+        copy.wait()
+        out_ref[pl.ds(n * block, block)] = jnp.dot(
+            wbuf[n], ctxbuf[...], preferred_element_type=jnp.float32).astype(out_ref.dtype)
+
+
+def _project_rows(parts, meta, a, b, out_weight, dtype=jnp.bfloat16):
+    block = 256
+    half = out_weight.shape[0] // (2 * N_FAST_HEAD)
+    rows, tokens = half * len(parts), a.shape[0] + b.shape[0]
+    steps = rows // block
+    vmem = pl.BlockSpec(memory_space=pltpu.VMEM)
+    return pl.pallas_call(
+        functools.partial(_project_kernel, parts, block),
+        out_shape=jax.ShapeDtypeStruct((rows, tokens), dtype),
+        in_specs=[pl.BlockSpec(memory_space=pltpu.SMEM), vmem, vmem, pl.BlockSpec(memory_space=pl.ANY)],
+        out_specs=vmem,
+        scratch_shapes=[
+            pltpu.VMEM((steps, block, out_weight.shape[1]), jnp.bfloat16),
+            pltpu.VMEM((tokens, out_weight.shape[1]), jnp.bfloat16),
+            pltpu.VMEM((out_weight.shape[1], tokens), jnp.bfloat16),
+            pltpu.SemaphoreType.DMA((steps,)),
+        ],
+        compiler_params=pltpu.CompilerParams(vmem_limit_bytes=40 * 2**20),
+        cost_estimate=pl.CostEstimate(
+            flops=2 * rows * tokens * out_weight.shape[1],
+            bytes_accessed=2 * rows * (out_weight.shape[1] + tokens), transcendentals=0),
+        name="project_rows",
+    )(meta, a, b, out_weight)
+
+
+def _add_halves_kernel(a_ref, b_ref, out_ref):
+    out_ref[...] = (a_ref[...].astype(jnp.float32) + b_ref[...].astype(jnp.float32)).astype(out_ref.dtype)
+
+
+def _add_halves(a, a_half, b, b_half):
+    rows, tokens = a.shape[0] // 2, a.shape[1]
+    return pl.pallas_call(
+        _add_halves_kernel,
+        out_shape=jax.ShapeDtypeStruct((rows, tokens), jnp.bfloat16),
+        grid=(1,),
+        in_specs=[
+            pl.BlockSpec((rows, tokens), lambda i: (a_half, 0)),
+            pl.BlockSpec((rows, tokens), lambda i: (b_half, 0)),
+        ],
+        out_specs=pl.BlockSpec((rows, tokens), lambda i: (0, 0)),
+        cost_estimate=pl.CostEstimate(flops=rows * tokens, bytes_accessed=6 * rows * tokens, transcendentals=0),
+        name="add_halves",
+    )(a, b)
+
+
+def _finish_kernel(far, meta_ref, keep_ref, x1_ref, y1_ref, y2_ref, x2_ref, *rest):
+    out_ref = rest[-1]
+    half = x1_ref.shape[0]
+    f32 = jnp.float32
+    out_ref[:half] = (
+        keep_ref[:half].astype(f32) + x1_ref[...].astype(f32) + y2_ref[...].astype(f32)
+    ).astype(out_ref.dtype)
+    out_ref[half:] = (
+        keep_ref[half:].astype(f32) + y1_ref[...].astype(f32) + x2_ref[...].astype(f32)
+    ).astype(out_ref.dtype)
+
+
+def _finish(far, meta, keep, x1, y1, y2, x2, out=None):
+    rows, tokens = keep.shape
+    half = rows // 2
+
+    def place(i, meta_ref):
+        upper = lax.div(meta_ref[0], 4)
+        return (0, 1 - upper if far else upper)
+
+    zero = lambda i, meta_ref: (0, 0)
+    specs = [pl.BlockSpec((rows, tokens), zero)] + [pl.BlockSpec((half, tokens), zero)] * 4
+    operands = [keep, x1, y1, y2, x2]
+    if out is not None:
+        specs.append(pl.BlockSpec(memory_space=pl.ANY))
+        operands.append(out)
+    return pl.pallas_call(
+        functools.partial(_finish_kernel, far),
+        out_shape=jax.ShapeDtypeStruct((rows, 2 * tokens), jnp.bfloat16),
+        grid_spec=pltpu.PrefetchScalarGridSpec(
+            num_scalar_prefetch=1, grid=(1,), in_specs=specs,
+            out_specs=pl.BlockSpec((rows, tokens), place),
+        ),
+        input_output_aliases={6: 0} if out is not None else {},
+        cost_estimate=pl.CostEstimate(flops=2 * rows * tokens, bytes_accessed=10 * rows * tokens, transcendentals=0),
+        name="finish",
+    )(meta, *operands)
+
+
+def _flip(x, axis, bits):
+    n = lax.axis_size(axis)
+    return lax.ppermute(x, axis, [(i, i ^ bits) for i in range(n)])
+
+
+def _reduce_chunk(meta, a, b, out_weight, far, out):
+    xmsg = _project_rows([(1, 0), (3, 0)], meta, a, b, out_weight)
+    x1 = _flip(xmsg, "head", 1)
+    ymsg = _project_rows([(2, 1), (3, 1)], meta, a, b, out_weight)
+    y1 = _flip(ymsg, "head", 2)
+    pass_on = _project_rows([(2, 0), (1, 1)], meta, a, b, out_weight)
+    keep = _project_rows([(0, 0), (0, 1)], meta, a, b, out_weight)
+    y2 = _flip(_add_halves(pass_on, 0, x1, 1), "head", 2)
+    x2 = _flip(_add_halves(pass_on, 1, y1, 1), "head", 1)
+    return _finish(far, meta, keep, x1, y1, y2, x2, out)
+
+
+def per_device_fast(queries, keys, values, out_weight, doc_lengths, owners):
+    places = lax.axis_size("ctx")
+    meta = jnp.stack([lax.axis_index("ctx"), lax.axis_index("head")]).astype(jnp.int32)
+    before = [(i, i + 2) for i in range(places - 2)]
+    k2 = lax.ppermute(keys, "ctx", before)
+    v2 = lax.ppermute(values, "ctx", before)
+    k1, v1 = _flip(keys, "ctx", 1), _flip(values, "ctx", 1)
+    smem = pl.BlockSpec(memory_space=pltpu.SMEM)
+    hbm = pl.BlockSpec(memory_space=pl.ANY)
+    leaving = pl.pallas_call(
+        _queries_for_other_core,
+        out_shape=jax.ShapeDtypeStruct((queries.shape[0] // 2, queries.shape[1]), jnp.bfloat16),
+        in_specs=[smem, smem, hbm],
+        out_specs=hbm,
+        scratch_shapes=[pltpu.SemaphoreType.DMA((PIECES // 2,))],
+        name="queries_for_other_core",
+    )(meta, owners, queries)
+    other = _flip(leaving, "ctx", 1)
+    k3, v3 = _flip(k2, "ctx", 1), _flip(v2, "ctx", 1)
+    kv = (keys, k1, k2, k3, values, v1, v2, v3)
+    near1, far3 = _attend_groups((1, 3), meta, owners, doc_lengths, queries, other, kv)
+    near1, far3 = _flip(near1, "ctx", 2), _flip(far3, "ctx", 6)
+    far2, near0 = _attend_groups((2, 0), meta, owners, doc_lengths, queries, other, kv)
+    far2 = _flip(far2, "ctx", 4)
+    out = _reduce_chunk(meta, near0, near1, out_weight, False, None)
+    return _reduce_chunk(meta, far2, far3, out_weight, True, out)
+
+
 def solution(mesh):
     in_specs = (P("ctx", "head"), P("ctx", "head"), P("ctx", "head"), P(None, "head"), P(), P())
     out_specs = P("head", "ctx")
+    fast = mesh.shape["ctx"] == PIECES and mesh.shape["head"] == N_FAST_HEAD
     return jax.shard_map(
-        per_device, mesh=mesh, in_specs=in_specs, out_specs=out_specs, check_vma=False
+        per_device_fast if fast else per_device, mesh=mesh, in_specs=in_specs, out_specs=out_specs, check_vma=False
     )

time: 191 us -> 135 us (0.71)
  waiting for transfers between devices: 103 us -> 4.16 us
  Pallas kernels: 0 us -> 91.6 us
  matrix products: 33.9 us -> 0 us
  starting transfers between devices: 6.4 us -> 24.5 us
  other arithmetic: 13.9 us -> 0.66 us
  between operations: 13.2 us -> 0.22 us
  local copies, waits for them, and re-layouts: 19.1 us -> 13.2 us
    pallas_call x0 -> x17, Pallas kernels: none -> 91.6 us  [the longest x8 43.4 us: _project_rows(): pl.pallas_call(functools.partial(_project_kernel, parts, block), out_shap...]
    reduce_scatter x1 -> x0, waiting for transfers between devices: 51.5 us -> none  [project(): lax.psum_scatter(lax.dot_general(out_weight, context, (((1,), (1,)), ((),...]
    dot_general x10 -> x0, matrix products: 33.9 us -> none  [the longest x1 16.7 us: project(): lax.dot_general(out_weight, context, (((1,), (1,)), ((), ())), preferred_...]
    all_to_all x1 -> x0, waiting for transfers between devices: 30.9 us -> none  [per_device(): lax.all_to_all(outgoing, 'ctx', split_axis=0, concat_axis=0, tiled=True)]
    ppermute x0 -> x18, starting transfers between devices: none -> 24.5 us  [the longest x16 16.5 us: _flip(): return lax.ppermute(x, axis, [(i, i ^ bits) for i in range(n)])]
    all_gather x2 -> x0, waiting for transfers between devices: 21 us -> none  [the longest x1 20.9 us: attend(): value_piece = lax.all_gather(values, 'ctx', axis=0, tiled=True)]
    unnamed x7 -> x33, local copies, waits for them, and re-layouts: 4.44 us -> 13.2 us
    reduce_sum x10 -> x0, other arithmetic: 8.62 us -> none  [the longest x4 8.02 us: one_tile(): new_sum = running_sum * factor + jnp.sum(weights, axis=-1)]
  transfers between devices with their start and end apart: 4 -> 18, of which waited for: 3 -> 2; matrix products, arithmetic and copies ran while one was open for 4% -> 0% of each run, Pallas kernels for 0% -> 46%
where the time goes in v1:
time: 135 us; the launch traced here: 134 us
  Pallas kernels  91.6 us (68%)
  starting transfers between devices  24.5 us (18%)
  local copies, waits for them, and re-layouts  13.2 us (10%)
  waiting for transfers between devices  4.16 us (3%)
    pallas_call x8, Pallas kernels, _project_rows(): pl.pallas_call(functools.partial(_project_kernel, parts, block), out_shap...  43.4 us
    pallas_call x1, Pallas kernels, per_device_fast(): pl.pallas_call(_queries_for_other_core, out_shape=jax.ShapeDtypeStruct((q...  18.2 us
    pallas_call x2, Pallas kernels, _attend_groups(): pl.pallas_call(functools.partial(_attend_kernel, groups), out_shape=[jax....  16.8 us
    ppermute x16, starting transfers between devices, _flip(): return lax.ppermute(x, axis, [(i, i ^ bits) for i in range(n)])  16.5 us
    unnamed x33, local copies, waits for them, and re-layouts  13.2 us
    pallas_call x4, Pallas kernels, _add_halves(): pl.pallas_call(_add_halves_kernel, out_shape=jax.ShapeDtypeStruct((rows,...  7.18 us
    pallas_call x2, Pallas kernels, _finish(): pl.pallas_call(functools.partial(_finish_kernel, far), out_shape=jax.Shap...  5.98 us
    ppermute x1, starting transfers between devices, per_device_fast(): k2 = lax.ppermute(keys, 'ctx', before)  4.5 us
  transfers between devices with their start and end apart: 18, of which 2 were waited for; matrix products, arithmetic and copies ran while one was open for 0% of the time, Pallas kernels for 46%

profile of v1, /device:TPU:0, one launch (start us, length us, event | category | flops | bytes accessed | tf_op | source)
XLA Modules:
  0.0 134.3 jit_solution(4321343250404587157)
XLA Ops:
  0.0 1.3 copy.9.owners_ref
  1.3 0.7 pad_add_fusion.meta_ref
  2.0 18.2 %queries_for_other_core.1 = bf16[128,2048]{1,0:T(8,128)(2,1)} custom-call(s32[2]{0:T(128)} %pad_add_fusion.meta_ref, s32[64,1]{1,0:T(8,128)} %copy.9.owners_ref, bf16[256,2048]{1,0:T(8,128)(2,1)} %queries_ref.5), custom_call_target="tpu_custom_call" | custom-call | tf_op jit(solution)/shard_map/queries_for_other_core/pallas_call | solution.py:395
  20.3 0.5 collective-permute-start
  20.8 4.5 %collective-permute-start.2 = (bf16[256,256]{1,0:T(8,128)(2,1)}, bf16[256,256]{1,0:T(8,128)(2,1)S(1)}, u32[]{:S(2)}, u32[]{:S(2)}) collective-permute-start(bf16[256,256]{1,0:T(8,128)(2,1)} %k0_ref.3), channel_id=1, source_target_pairs={{0,8},{4,12},{8,16},{12,20},{16,24},{20,28},{1,9},{5,13},{9,17},{1... | collective-permute-start | bytes 393224 | tf_op jit(solution)/shard_map/ppermute | solution.py:390
  25.3 3.5 %collective-permute-start.5 = (bf16[256,256]{1,0:T(8,128)(2,1)}, bf16[256,256]{1,0:T(8,128)(2,1)S(1)}, u32[]{:S(2)}, u32[]{:S(2)}) collective-permute-start(bf16[256,256]{1,0:T(8,128)(2,1)} %v0_ref.3), channel_id=1, source_target_pairs={{0,8},{4,12},{8,16},{12,20},{16,24},{20,28},{1,9},{5,13},{9,17},{1... | collective-permute-start | bytes 393224 | tf_op jit(solution)/shard_map/ppermute | solution.py:391
  28.8 0.1 collective-permute-start.1
  28.9 0.5 collective-permute-start.4
  29.4 0.1 collective-permute-start.3
  29.4 2.8 %collective-permute-done.5.v2_ref = bf16[256,256]{1,0:T(8,128)(2,1)S(1)} collective-permute-done((bf16[256,256]{1,0:T(8,128)(2,1)}, bf16[256,256]{1,0:T(8,128)(2,1)S(1)}, u32[]{:S(2)}, u32[]{:S(2)}) %collective-permute-start.5) | collective-permute-done | bytes 131104 | tf_op jit(solution)/shard_map/ppermute | solution.py:391
  32.2 0.0 collective-permute-done.3.k3_ref
  32.2 1.3 collective-permute-done.6.v3_ref
  33.5 0.0 collective-permute-done.other_ref
  33.5 1.2 copy-done
  34.8 0.8 copy-done.5
  35.5 0.9 copy-done.6
  36.4 0.9 copy-done.7
  37.3 0.7 copy-done.8
  38.0 0.7 copy-done.11
  38.7 8.3 %attend_groups.3 = (bf16[64,2048]{1,0:T(8,128)(2,1)S(1)}, bf16[64,2048]{1,0:T(8,128)(2,1)S(1)}) custom-call(s32[2]{0:T(128)S(1)} %copy-done.8, s32[64,1]{1,0:T(8,128)S(1)} %copy-done.5, s32[16]{0:T(128)S(1)} %copy-done.11, bf16[256,2048]{1,0:T(8,128)(2,1)S(1)} %copy-done, bf16[128,2048]{1,0:T(8,128)(2,1)S(1)} %collective-permute-done.other_ref, ...), custom_call_target="tpu_custom_call" | custom-call | flops 400000000 | bytes 3145728 | tf_op jit(solution)/shard_map/attend_groups/pallas_call | solution.py:243
  47.0 2.4 %collective-permute-start.13 = (bf16[64,2048]{1,0:T(8,128)(2,1)S(1)}, bf16[64,2048]{1,0:T(8,128)(2,1)S(1)}, u32[]{:S(2)}, u32[]{:S(2)}) collective-permute-start(bf16[64,2048]{1,0:T(8,128)(2,1)S(1)} %get-tuple-element.12), channel_id=1, source_target_pairs={{0,8},{4,12},{8,0},{12,4},{16,24},{20,28},{24,16},{28,20},{1,9},{5... | collective-permute-start | bytes 786440 | tf_op jit(solution)/shard_map/ppermute | solution.py:371
  49.4 2.5 %collective-permute-start.8 = (bf16[64,2048]{1,0:T(8,128)(2,1)S(1)}, bf16[64,2048]{1,0:T(8,128)(2,1)S(1)}, u32[]{:S(2)}, u32[]{:S(2)}) collective-permute-start(bf16[64,2048]{1,0:T(8,128)(2,1)S(1)} %get-tuple-element.10), channel_id=1, source_target_pairs={{0,24},{4,28},{8,16},{12,20},{16,8},{20,12},{24,0},{28,4},{1,25},{... | collective-permute-start | bytes 786440 | tf_op jit(solution)/shard_map/ppermute | solution.py:371
  51.9 8.5 %attend_groups.2 = (bf16[64,2048]{1,0:T(8,128)(2,1)S(1)}, bf16[64,2048]{1,0:T(8,128)(2,1)S(1)}) custom-call(s32[2]{0:T(128)S(1)} %copy-done.8, s32[64,1]{1,0:T(8,128)S(1)} %copy-done.5, s32[16]{0:T(128)S(1)} %copy-done.11, bf16[256,2048]{1,0:T(8,128)(2,1)S(1)} %copy-done, bf16[128,2048]{1,0:T(8,128)(2,1)S(1)} %collective-permute-done.other_ref, ...), custom_call_target="tpu_custom_call" | custom-call | flops 400000000 | bytes 3145728 | tf_op jit(solution)/shard_map/attend_groups/pallas_call | solution.py:243
  60.4 0.1 collective-permute-start.7
  60.5 0.7 copy-done.9
  61.2 5.4 %project_rows.14 = bf16[2048,128]{1,0:T(8,128)(2,1)S(1)} custom-call(s32[2]{0:T(128)S(1)} %copy-done.9, bf16[64,2048]{1,0:T(8,128)(2,1)S(1)} %get-tuple-element.11.a_ref, bf16[64,2048]{1,0:T(8,128)(2,1)S(1)} %collective-permute-done.13.b_ref, bf16[8192,2048]{1,0:T(8,128)(2,1)} %w_ref.15), custom_call_target="tpu_custom_call" | custom-call | flops 1073741824 | bytes 8912896 | tf_op jit(solution)/shard_map/project_rows/pallas_call | solution.py:291
  66.5 1.6 %collective-permute-start.15 = (bf16[2048,128]{1,0:T(8,128)(2,1)S(1)}, bf16[2048,128]{1,0:T(8,128)(2,1)}, u32[]{:S(2)}, u32[]{:S(2)}) collective-permute-start(bf16[2048,128]{1,0:T(8,128)(2,1)S(1)} %project_rows.14), channel_id=1, source_target_pairs={{0,2},{1,3},{2,0},{3,1},{4,6},{5,7},{6,4},{7,5},{8,10},{9,11},{10,... | collective-permute-start | bytes 1572872 | tf_op jit(solution)/shard_map/ppermute | solution.py:371
  68.1 5.4 %project_rows.13 = bf16[2048,128]{1,0:T(8,128)(2,1)S(1)} custom-call(s32[2]{0:T(128)S(1)} %copy-done.9, bf16[64,2048]{1,0:T(8,128)(2,1)S(1)} %get-tuple-element.11.a_ref, bf16[64,2048]{1,0:T(8,128)(2,1)S(1)} %collective-permute-done.13.b_ref, bf16[8192,2048]{1,0:T(8,128)(2,1)} %w_ref.15), custom_call_target="tpu_custom_call" | custom-call | flops 1073741824 | bytes 8912896 | tf_op jit(solution)/shard_map/project_rows/pallas_call | solution.py:291
  73.5 1.6 %collective-permute-start.14 = (bf16[2048,128]{1,0:T(8,128)(2,1)S(1)}, bf16[2048,128]{1,0:T(8,128)(2,1)}, u32[]{:S(2)}, u32[]{:S(2)}) collective-permute-start(bf16[2048,128]{1,0:T(8,128)(2,1)S(1)} %project_rows.13), channel_id=1, source_target_pairs={{0,1},{1,0},{2,3},{3,2},{4,5},{5,4},{6,7},{7,6},{8,9},{9,8},{10,11... | collective-permute-start | bytes 1572872 | tf_op jit(solution)/shard_map/ppermute | solution.py:371
  75.1 0.0 collective-permute-done.8.b_ref
  75.1 0.0 collective-permute-done.7.a_ref
  75.1 5.4 %project_rows.10 = bf16[2048,128]{1,0:T(8,128)(2,1)S(1)} custom-call(s32[2]{0:T(128)S(1)} %copy-done.9, bf16[64,2048]{1,0:T(8,128)(2,1)S(1)} %collective-permute-done.7.a_ref, bf16[64,2048]{1,0:T(8,128)(2,1)S(1)} %collective-permute-done.8.b_ref, bf16[8192,2048]{1,0:T(8,128)(2,1)} %w_ref.15), custom_call_target="tpu_custom_call" | custom-call | flops 1073741824 | bytes 8912896 | tf_op jit(solution)/shard_map/project_rows/pallas_call | solution.py:291
  80.5 1.6 %collective-permute-start.10 = (bf16[2048,128]{1,0:T(8,128)(2,1)S(1)}, bf16[2048,128]{1,0:T(8,128)(2,1)S(1)}, u32[]{:S(2)}, u32[]{:S(2)}) collective-permute-start(bf16[2048,128]{1,0:T(8,128)(2,1)S(1)} %project_rows.10), channel_id=1, source_target_pairs={{0,2},{1,3},{2,0},{3,1},{4,6},{5,7},{6,4},{7,5},{8,10},{9,11},{10,... | collective-permute-start | bytes 1572872 | tf_op jit(solution)/shard_map/ppermute | solution.py:371
  82.0 5.6 %project_rows.9 = bf16[2048,128]{1,0:T(8,128)(2,1)S(1)} custom-call(s32[2]{0:T(128)S(1)} %copy-done.9, bf16[64,2048]{1,0:T(8,128)(2,1)S(1)} %collective-permute-done.7.a_ref, bf16[64,2048]{1,0:T(8,128)(2,1)S(1)} %collective-permute-done.8.b_ref, bf16[8192,2048]{1,0:T(8,128)(2,1)} %w_ref.15), custom_call_target="tpu_custom_call" | custom-call | flops 1073741824 | bytes 8912896 | tf_op jit(solution)/shard_map/project_rows/pallas_call | solution.py:291
  87.7 1.6 %collective-permute-start.9 = (bf16[2048,128]{1,0:T(8,128)(2,1)S(1)}, bf16[2048,128]{1,0:T(8,128)(2,1)}, u32[]{:S(2)}, u32[]{:S(2)}) collective-permute-start(bf16[2048,128]{1,0:T(8,128)(2,1)S(1)} %project_rows.9), channel_id=1, source_target_pairs={{0,1},{1,0},{2,3},{3,2},{4,5},{5,4},{6,7},{7,6},{8,9},{9,8},{10,11... | collective-permute-start | bytes 1572872 | tf_op jit(solution)/shard_map/ppermute | solution.py:371
  89.2 5.4 %project_rows.15.a_ref = bf16[2048,128]{1,0:T(8,128)(2,1)S(1)} custom-call(s32[2]{0:T(128)S(1)} %copy-done.9, bf16[64,2048]{1,0:T(8,128)(2,1)S(1)} %get-tuple-element.11.a_ref, bf16[64,2048]{1,0:T(8,128)(2,1)S(1)} %collective-permute-done.13.b_ref, bf16[8192,2048]{1,0:T(8,128)(2,1)} %w_ref.15), custom_call_target="tpu_custom_call" | custom-call | flops 1073741824 | bytes 8912896 | tf_op jit(solution)/shard_map/project_rows/pallas_call | solution.py:291
  94.6 0.8 copy-done.2
  95.4 5.4 %project_rows.11.a_ref = bf16[2048,128]{1,0:T(8,128)(2,1)S(1)} custom-call(s32[2]{0:T(128)S(1)} %copy-done.9, bf16[64,2048]{1,0:T(8,128)(2,1)S(1)} %collective-permute-done.7.a_ref, bf16[64,2048]{1,0:T(8,128)(2,1)S(1)} %collective-permute-done.8.b_ref, bf16[8192,2048]{1,0:T(8,128)(2,1)} %w_ref.15), custom_call_target="tpu_custom_call" | custom-call | flops 1073741824 | bytes 8912896 | tf_op jit(solution)/shard_map/project_rows/pallas_call | solution.py:291
  100.7 0.0 copy-start.1
  100.8 0.8 copy-done.1
  101.5 0.0 collective-permute-done.15.b_ref.y1_ref
  101.5 1.8 %add_halves.7 = bf16[1024,128]{1,0:T(8,128)(2,1)} custom-call(bf16[2048,128]{1,0:T(8,128)(2,1)} %copy-done.2, bf16[2048,128]{1,0:T(8,128)(2,1)} %collective-permute-done.15.b_ref.y1_ref), custom_call_target="tpu_custom_call" | custom-call | flops 131072 | bytes 786432 | tf_op jit(solution)/shard_map/add_halves/pallas_call | solution.py:316
  103.3 0.5 collective-permute-start.17
  103.9 0.0 collective-permute-done.14.b_ref.x1_ref
  103.9 1.8 %add_halves.6 = bf16[1024,128]{1,0:T(8,128)(2,1)} custom-call(bf16[2048,128]{1,0:T(8,128)(2,1)} %copy-done.2, bf16[2048,128]{1,0:T(8,128)(2,1)} %collective-permute-done.14.b_ref.x1_ref), custom_call_target="tpu_custom_call" | custom-call | flops 131072 | bytes 786432 | tf_op jit(solution)/shard_map/add_halves/pallas_call | solution.py:316
  105.7 0.5 collective-permute-start.16
  106.2 0.0 collective-permute-done.10.b_ref.y1_ref
  106.2 0.8 copy-done.12
  107.0 1.8 %add_halves.5 = bf16[1024,128]{1,0:T(8,128)(2,1)} custom-call(bf16[2048,128]{1,0:T(8,128)(2,1)} %copy-done.1, bf16[2048,128]{1,0:T(8,128)(2,1)} %copy-done.12), custom_call_target="tpu_custom_call" | custom-call | flops 131072 | bytes 786432 | tf_op jit(solution)/shard_map/add_halves/pallas_call | solution.py:316
  108.8 1.5 %collective-permute-start.12 = (bf16[1024,128]{1,0:T(8,128)(2,1)}, bf16[1024,128]{1,0:T(8,128)(2,1)S(1)}, u32[]{:S(2)}, u32[]{:S(2)}) collective-permute-start(bf16[1024,128]{1,0:T(8,128)(2,1)} %add_halves.5), channel_id=1, source_target_pairs={{0,1},{1,0},{2,3},{3,2},{4,5},{5,4},{6,7},{7,6},{8,9},{9,8},{10,11... | collective-permute-start | bytes 786440 | tf_op jit(solution)/shard_map/ppermute | solution.py:371
  110.3 0.0 collective-permute-done.9.b_ref.x1_ref
  110.3 1.8 %add_halves.4 = bf16[1024,128]{1,0:T(8,128)(2,1)} custom-call(bf16[2048,128]{1,0:T(8,128)(2,1)} %copy-done.1, bf16[2048,128]{1,0:T(8,128)(2,1)} %collective-permute-done.9.b_ref.x1_ref), custom_call_target="tpu_custom_call" | custom-call | flops 131072 | bytes 786432 | tf_op jit(solution)/shard_map/add_halves/pallas_call | solution.py:316
  112.1 1.5 %collective-permute-start.11 = (bf16[1024,128]{1,0:T(8,128)(2,1)}, bf16[1024,128]{1,0:T(8,128)(2,1)S(1)}, u32[]{:S(2)}, u32[]{:S(2)}) collective-permute-start(bf16[1024,128]{1,0:T(8,128)(2,1)} %add_halves.4), channel_id=1, source_target_pairs={{0,2},{1,3},{2,0},{3,1},{4,6},{5,7},{6,4},{7,5},{8,10},{9,11},{10,... | collective-permute-start | bytes 786440 | tf_op jit(solution)/shard_map/ppermute | solution.py:371
  113.6 5.4 %project_rows.12.keep_ref = bf16[2048,128]{1,0:T(8,128)(2,1)S(1)} custom-call(s32[2]{0:T(128)S(1)} %copy-done.10, bf16[64,2048]{1,0:T(8,128)(2,1)S(1)} %get-tuple-element.11.a_ref, bf16[64,2048]{1,0:T(8,128)(2,1)S(1)} %collective-permute-done.13.b_ref, bf16[8192,2048]{1,0:T(8,128)(2,1)} %w_ref.15), custom_call_target="tpu_custom_call" | custom-call | flops 1073741824 | bytes 8912896 | tf_op jit(solution)/shard_map/project_rows/pallas_call | solution.py:291
  119.0 0.8 copy-done.4
  119.8 5.6 %project_rows.8.keep_ref = bf16[2048,128]{1,0:T(8,128)(2,1)S(1)} custom-call(s32[2]{0:T(128)S(1)} %copy-done.10, bf16[64,2048]{1,0:T(8,128)(2,1)S(1)} %collective-permute-done.7.a_ref, bf16[64,2048]{1,0:T(8,128)(2,1)S(1)} %collective-permute-done.8.b_ref, bf16[8192,2048]{1,0:T(8,128)(2,1)} %w_ref.15), custom_call_target="tpu_custom_call" | custom-call | flops 1073741824 | bytes 8912896 | tf_op jit(solution)/shard_map/project_rows/pallas_call | solution.py:291
  125.4 0.8 copy-done.3
  126.2 0.0 collective-permute-done.17.x2_ref
  126.2 0.0 collective-permute-done.16.y2_ref
  126.2 0.7 copy-done.15
  126.9 3.0 %finish.2.rest_0_ = bf16[2048,256]{1,0:T(8,128)(2,1)} custom-call(s32[2]{0:T(128)} %pad_add_fusion.meta_ref, bf16[2048,128]{1,0:T(8,128)(2,1)} %copy-done.4, bf16[2048,128]{1,0:T(8,128)(2,1)} %collective-permute-done.14.b_ref.x1_ref, bf16[2048,128]{1,0:T(8,128)(2,1)} %collective-permute-done.15.b_ref.y1_ref, ...), custom_call_target="tpu_custom_call" | custom-call | flops 524288 | bytes 2621440 | tf_op jit(solution)/shard_map/finish/pallas_call | solution.py:356
  129.9 0.7 copy-done.13
  130.6 0.7 copy-done.14
  131.3 3.0 %finish.3 = bf16[2048,256]{1,0:T(8,128)(2,1)} custom-call(s32[2]{0:T(128)} %pad_add_fusion.meta_ref, bf16[2048,128]{1,0:T(8,128)(2,1)} %copy-done.3, bf16[2048,128]{1,0:T(8,128)(2,1)} %collective-permute-done.9.b_ref.x1_ref, bf16[2048,128]{1,0:T(8,128)(2,1)} %copy-done.12, bf16[1024,128]{1,0:T(8,128)(2,1)} %copy-done.14, ...), custom_call_target="tpu_custom_call", output_to_operand_aliasing={{}: (6, {})} | custom-call | flops 524288 | bytes 2621440 | tf_op jit(solution)/shard_map/finish/pallas_call | solution.py:356
  (23 shorter events, 0.0 us)
Async XLA Ops:
  20.3 13.3 %collective-permute-start = (bf16[128,2048]{1,0:T(8,128)(2,1)}, bf16[128,2048]{1,0:T(8,128)(2,1)S(1)}, u32[]{:S(2)}, u32[]{:S(2)}) collective-permute-start(bf16[128,2048]{1,0:T(8,128)(2,1)} %queries_for_other_core.1), channel_id=1, source_target_pairs={{0,4},{4,0},{8,12},{12,8},{16,20},{20,16},{24,28},{28,24},{1,5},{5... | collective-permute-start | bytes 1572872 | tf_op jit(solution)/shard_map/ppermute | solution.py:371
  20.8 8.6 %collective-permute-start.2 = (bf16[256,256]{1,0:T(8,128)(2,1)}, bf16[256,256]{1,0:T(8,128)(2,1)S(1)}, u32[]{:S(2)}, u32[]{:S(2)}) collective-permute-start(bf16[256,256]{1,0:T(8,128)(2,1)} %k0_ref.3), channel_id=1, source_target_pairs={{0,8},{4,12},{8,16},{12,20},{16,24},{20,28},{1,9},{5,13},{9,17},{1... | collective-permute-start | bytes 393224 | tf_op jit(solution)/shard_map/ppermute | solution.py:390
  25.3 6.9 %collective-permute-start.5 = (bf16[256,256]{1,0:T(8,128)(2,1)}, bf16[256,256]{1,0:T(8,128)(2,1)S(1)}, u32[]{:S(2)}, u32[]{:S(2)}) collective-permute-start(bf16[256,256]{1,0:T(8,128)(2,1)} %v0_ref.3), channel_id=1, source_target_pairs={{0,8},{4,12},{8,16},{12,20},{16,24},{20,28},{1,9},{5,13},{9,17},{1... | collective-permute-start | bytes 393224 | tf_op jit(solution)/shard_map/ppermute | solution.py:391
  28.8 3.4 %collective-permute-start.1 = (bf16[256,256]{1,0:T(8,128)(2,1)}, bf16[256,256]{1,0:T(8,128)(2,1)S(1)}, u32[]{:S(2)}, u32[]{:S(2)}) collective-permute-start(bf16[256,256]{1,0:T(8,128)(2,1)} %k0_ref.3), channel_id=1, source_target_pairs={{0,4},{4,0},{8,12},{12,8},{16,20},{20,16},{24,28},{28,24},{1,5},{5... | collective-permute-start | bytes 393224 | tf_op jit(solution)/shard_map/ppermute | solution.py:371
  28.9 3.3 %collective-permute-start.4 = (bf16[256,256]{1,0:T(8,128)(2,1)}, bf16[256,256]{1,0:T(8,128)(2,1)S(1)}, u32[]{:S(2)}, u32[]{:S(2)}) collective-permute-start(bf16[256,256]{1,0:T(8,128)(2,1)} %v0_ref.3), channel_id=1, source_target_pairs={{0,4},{4,0},{8,12},{12,8},{16,20},{20,16},{24,28},{28,24},{1,5},{5... | collective-permute-start | bytes 393224 | tf_op jit(solution)/shard_map/ppermute | solution.py:371
  29.4 2.9 %collective-permute-start.3 = (bf16[256,256]{1,0:T(8,128)(2,1)S(1)}, bf16[256,256]{1,0:T(8,128)(2,1)S(1)}, u32[]{:S(2)}, u32[]{:S(2)}) collective-permute-start(bf16[256,256]{1,0:T(8,128)(2,1)S(1)} %collective-permute-done.2.k2_ref), channel_id=1, source_target_pairs={{0,4},{4,0},{8,12},{12,8},{16,20},{20,16},{24,28},{28,24},{1,5},{5... | collective-permute-start | bytes 393224 | tf_op jit(solution)/shard_map/ppermute | solution.py:371
  32.2 1.3 %collective-permute-start.6 = (bf16[256,256]{1,0:T(8,128)(2,1)S(1)}, bf16[256,256]{1,0:T(8,128)(2,1)S(1)}, u32[]{:S(2)}, u32[]{:S(2)}) collective-permute-start(bf16[256,256]{1,0:T(8,128)(2,1)S(1)} %collective-permute-done.5.v2_ref), channel_id=1, source_target_pairs={{0,4},{4,0},{8,12},{12,8},{16,20},{20,16},{24,28},{28,24},{1,5},{5... | collective-permute-start | bytes 393224 | tf_op jit(solution)/shard_map/ppermute | solution.py:371
  33.5 1.2 copy-start
  34.8 0.8 copy-start.5
  35.5 0.9 copy-start.6
  36.4 0.9 copy-start.7
  37.3 0.7 copy-start.8
  38.0 0.7 copy-start.11
  47.0 13.5 %collective-permute-start.13 = (bf16[64,2048]{1,0:T(8,128)(2,1)S(1)}, bf16[64,2048]{1,0:T(8,128)(2,1)S(1)}, u32[]{:S(2)}, u32[]{:S(2)}) collective-permute-start(bf16[64,2048]{1,0:T(8,128)(2,1)S(1)} %get-tuple-element.12), channel_id=1, source_target_pairs={{0,8},{4,12},{8,0},{12,4},{16,24},{20,28},{24,16},{28,20},{1,9},{5... | collective-permute-start | bytes 786440 | tf_op jit(solution)/shard_map/ppermute | solution.py:371
  49.4 25.6 %collective-permute-start.8 = (bf16[64,2048]{1,0:T(8,128)(2,1)S(1)}, bf16[64,2048]{1,0:T(8,128)(2,1)S(1)}, u32[]{:S(2)}, u32[]{:S(2)}) collective-permute-start(bf16[64,2048]{1,0:T(8,128)(2,1)S(1)} %get-tuple-element.10), channel_id=1, source_target_pairs={{0,24},{4,28},{8,16},{12,20},{16,8},{20,12},{24,0},{28,4},{1,25},{... | collective-permute-start | bytes 786440 | tf_op jit(solution)/shard_map/ppermute | solution.py:371
  60.4 14.7 %collective-permute-start.7 = (bf16[64,2048]{1,0:T(8,128)(2,1)S(1)}, bf16[64,2048]{1,0:T(8,128)(2,1)S(1)}, u32[]{:S(2)}, u32[]{:S(2)}) collective-permute-start(bf16[64,2048]{1,0:T(8,128)(2,1)S(1)} %get-tuple-element.9), channel_id=1, source_target_pairs={{0,16},{4,20},{8,24},{12,28},{16,0},{20,4},{24,8},{28,12},{1,17},{... | collective-permute-start | bytes 786440 | tf_op jit(solution)/shard_map/ppermute | solution.py:371
  60.5 0.7 copy-start.9
  66.5 35.0 %collective-permute-start.15 = (bf16[2048,128]{1,0:T(8,128)(2,1)S(1)}, bf16[2048,128]{1,0:T(8,128)(2,1)}, u32[]{:S(2)}, u32[]{:S(2)}) collective-permute-start(bf16[2048,128]{1,0:T(8,128)(2,1)S(1)} %project_rows.14), channel_id=1, source_target_pairs={{0,2},{1,3},{2,0},{3,1},{4,6},{5,7},{6,4},{7,5},{8,10},{9,11},{10,... | collective-permute-start | bytes 1572872 | tf_op jit(solution)/shard_map/ppermute | solution.py:371
  73.5 30.4 %collective-permute-start.14 = (bf16[2048,128]{1,0:T(8,128)(2,1)S(1)}, bf16[2048,128]{1,0:T(8,128)(2,1)}, u32[]{:S(2)}, u32[]{:S(2)}) collective-permute-start(bf16[2048,128]{1,0:T(8,128)(2,1)S(1)} %project_rows.13), channel_id=1, source_target_pairs={{0,1},{1,0},{2,3},{3,2},{4,5},{5,4},{6,7},{7,6},{8,9},{9,8},{10,11... | collective-permute-start | bytes 1572872 | tf_op jit(solution)/shard_map/ppermute | solution.py:371
  80.5 25.7 %collective-permute-start.10 = (bf16[2048,128]{1,0:T(8,128)(2,1)S(1)}, bf16[2048,128]{1,0:T(8,128)(2,1)S(1)}, u32[]{:S(2)}, u32[]{:S(2)}) collective-permute-start(bf16[2048,128]{1,0:T(8,128)(2,1)S(1)} %project_rows.10), channel_id=1, source_target_pairs={{0,2},{1,3},{2,0},{3,1},{4,6},{5,7},{6,4},{7,5},{8,10},{9,11},{10,... | collective-permute-start | bytes 1572872 | tf_op jit(solution)/shard_map/ppermute | solution.py:371
  87.6 26.0 %copy-start.10 = (s32[2]{0:T(128)S(1)}, s32[2]{0:T(128)}, u32[]{:S(2)}) copy-start(s32[2]{0:T(128)} %pad_add_fusion.meta_ref) | copy-start | bytes 28
  87.7 22.6 %collective-permute-start.9 = (bf16[2048,128]{1,0:T(8,128)(2,1)S(1)}, bf16[2048,128]{1,0:T(8,128)(2,1)}, u32[]{:S(2)}, u32[]{:S(2)}) collective-permute-start(bf16[2048,128]{1,0:T(8,128)(2,1)S(1)} %project_rows.9), channel_id=1, source_target_pairs={{0,1},{1,0},{2,3},{3,2},{4,5},{5,4},{6,7},{7,6},{8,9},{9,8},{10,11... | collective-permute-start | bytes 1572872 | tf_op jit(solution)/shard_map/ppermute | solution.py:371
  94.6 0.8 copy-start.2
  100.7 0.8 copy-start.1
  103.3 22.8 %collective-permute-start.17 = (bf16[1024,128]{1,0:T(8,128)(2,1)}, bf16[1024,128]{1,0:T(8,128)(2,1)S(1)}, u32[]{:S(2)}, u32[]{:S(2)}) collective-permute-start(bf16[1024,128]{1,0:T(8,128)(2,1)} %add_halves.7), channel_id=1, source_target_pairs={{0,1},{1,0},{2,3},{3,2},{4,5},{5,4},{6,7},{7,6},{8,9},{9,8},{10,11... | collective-permute-start | bytes 786440 | tf_op jit(solution)/shard_map/ppermute | solution.py:371
  105.7 20.5 %collective-permute-start.16 = (bf16[1024,128]{1,0:T(8,128)(2,1)}, bf16[1024,128]{1,0:T(8,128)(2,1)}, u32[]{:S(2)}, u32[]{:S(2)}) collective-permute-start(bf16[1024,128]{1,0:T(8,128)(2,1)} %add_halves.6), channel_id=1, source_target_pairs={{0,2},{1,3},{2,0},{3,1},{4,6},{5,7},{6,4},{7,5},{8,10},{9,11},{10,... | collective-permute-start | bytes 786440 | tf_op jit(solution)/shard_map/ppermute | solution.py:371
  106.2 0.8 copy-start.12
  108.8 21.1 %collective-permute-start.12 = (bf16[1024,128]{1,0:T(8,128)(2,1)}, bf16[1024,128]{1,0:T(8,128)(2,1)S(1)}, u32[]{:S(2)}, u32[]{:S(2)}) collective-permute-start(bf16[1024,128]{1,0:T(8,128)(2,1)} %add_halves.5), channel_id=1, source_target_pairs={{0,1},{1,0},{2,3},{3,2},{4,5},{5,4},{6,7},{7,6},{8,9},{9,8},{10,11... | collective-permute-start | bytes 786440 | tf_op jit(solution)/shard_map/ppermute | solution.py:371
  112.1 17.8 %collective-permute-start.11 = (bf16[1024,128]{1,0:T(8,128)(2,1)}, bf16[1024,128]{1,0:T(8,128)(2,1)S(1)}, u32[]{:S(2)}, u32[]{:S(2)}) collective-permute-start(bf16[1024,128]{1,0:T(8,128)(2,1)} %add_halves.4), channel_id=1, source_target_pairs={{0,2},{1,3},{2,0},{3,1},{4,6},{5,7},{6,4},{7,5},{8,10},{9,11},{10,... | collective-permute-start | bytes 786440 | tf_op jit(solution)/shard_map/ppermute | solution.py:371
  119.0 0.8 copy-start.4
  125.4 0.8 copy-start.3
  126.2 0.7 copy-start.15
  129.9 0.7 copy-start.13
  130.6 0.7 copy-start.14

commit v2 on v0

--- a/solution.py
+++ b/solution.py
@@ -1,12 +1,16 @@
+import functools
 import math
 
 import jax
 import jax.numpy as jnp
 from jax import lax
+from jax.experimental import pallas as pl
+from jax.experimental.pallas import tpu as pltpu
 from jax.sharding import PartitionSpec as P
 
 HEAD_SIZE = 128
 PIECES = 8
+N_FAST_HEAD = 4
 
 
 MASKED = -1e30
@@ -114,9 +118,342 @@
     return project(context, out_weight)
 
 
+SMEM = pl.BlockSpec(memory_space=pltpu.SMEM)
+VMEM = pl.BlockSpec(memory_space=pltpu.VMEM)
+HBM = pl.BlockSpec(memory_space=pltpu.HBM)
+ANY = pl.BlockSpec(memory_space=pl.ANY)
+
+
+OWNERS_AT = 2
+
+
+def _find_piece(table_ref, source, owner):
+    piece = jnp.int32(0)
+    for i in range(PIECES):
+        piece = jnp.where(table_ref[OWNERS_AT + source * PIECES + i] == owner, jnp.int32(i), piece)
+    return piece
+
+
+def _rows(start, size):
+    return pl.ds(pl.multiple_of(start, size), size)
+
+
+def _queries_for_other_core(meta_ref, queries_ref, out_ref):
+    c = meta_ref[0]
+    core = lax.rem(c, 2)
+    rows = queries_ref.shape[0] // PIECES
+    for j in range(PIECES // 2):
+        piece = _find_piece(meta_ref, c, 2 * j + 1 - core)
+        out_ref[j * rows:(j + 1) * rows] = queries_ref[_rows(piece * rows, rows)]
+
+
+QUARTERS = {
+    "x": ((1, 0), (3, 0)),
+    "y": ((2, 1), (3, 1)),
+    "pass": ((2, 0), (1, 1)),
+    "keep": ((0, 0), (0, 1)),
+}
+
+
+def _weight_copies(names, meta_ref, w_ref, out_refs, sems):
+    half = w_ref.shape[0] // (2 * N_FAST_HEAD)
+    copies = []
+    for n, name in enumerate(names):
+        for i, (flip, side) in enumerate(QUARTERS[name]):
+            row = (meta_ref[1] ^ flip) * (2 * half) + side * half
+            copies.append(pltpu.make_async_copy(
+                w_ref.at[_rows(row, half)], out_refs[n].at[pl.ds(i * half, half)], sems.at[2 * n + i]))
+    return copies
+
+
+def _stage_kernel(names, meta_ref, w_ref, *rest):
+    copies = _weight_copies(names, meta_ref, w_ref, rest[:-1], rest[-1])
+    for copy in copies:
+        copy.start()
+    for copy in copies:
+        copy.wait()
+
+
+def _quarter(out_weight):
+    return jax.ShapeDtypeStruct((out_weight.shape[0] // N_FAST_HEAD, out_weight.shape[1]), out_weight.dtype)
+
+
+def _stage_weights(names, meta, out_weight):
+    return pl.pallas_call(
+        functools.partial(_stage_kernel, names),
+        out_shape=[_quarter(out_weight) for _ in names],
+        in_specs=[SMEM, HBM],
+        out_specs=[VMEM] * len(names),
+        scratch_shapes=[pltpu.SemaphoreType.DMA((2 * len(names),))],
+        compiler_params=pltpu.CompilerParams(vmem_limit_bytes=36 * 2**20),
+        cost_estimate=pl.CostEstimate(
+            flops=0, bytes_accessed=len(names) * out_weight.size, transcendentals=0),
+        name="stage_weights",
+    )(meta, out_weight)
+
+
+def _attend_kernel(
+    groups, names, meta_ref, queries_ref, other_ref,
+    k0_ref, k1_ref, k2_ref, k3_ref, v0_ref, v1_ref, v2_ref, v3_ref, w_ref, after_ref,
+    *rest,
+):
+    count = len(groups)
+    out_refs, w_out = rest[:count], rest[count:count + len(names)]
+    kbuf, vbuf, qbuf, ctxbuf, w_sems = rest[count + len(names):]
+    w_copies = _weight_copies(names, meta_ref, w_ref, w_out, w_sems)
+    for copy in w_copies:
+        copy.start()
+    c = meta_ref[0]
+    core = lax.rem(c, 2)
+    z = lax.div(c, 2)
+    rows = k0_ref.shape[0]
+    piece_rows = rows // PIECES
+    tile = 128
+    slots = (2 + core, 3 - core, core, 1 - core)
+    for b, (k_ref, v_ref) in enumerate(((k0_ref, v0_ref), (k1_ref, v1_ref), (k2_ref, v2_ref), (k3_ref, v3_ref))):
+        kbuf[_rows(slots[b] * rows, rows)] = k_ref[...]
+        vbuf[_rows(slots[b] * rows, rows)] = v_ref[...]
+    starts = []
+    for n, k in enumerate(groups):
+        zdest = z ^ k
+        owner = 2 * zdest + core
+        mine = _find_piece(meta_ref, c, owner)
+        theirs = _find_piece(meta_ref, c + 1 - 2 * core, owner)
+        qbuf[2 * n + core] = queries_ref[_rows(mine * piece_rows, piece_rows)]
+        qbuf[2 * n + 1 - core] = other_ref[_rows(zdest * piece_rows, piece_rows)]
+        at0 = jnp.where(core == 0, mine, theirs)
+        at1 = jnp.where(core == 0, theirs, mine)
+        starts.append((at0 * piece_rows, rows + at1 * piece_rows))
+    doc_start = []
+    running = jnp.int32(0)
+    lengths_at = OWNERS_AT + PIECES * PIECES
+    for d in range(lengths_at, meta_ref.shape[0]):
+        doc_start.append(running)
+        running = running + meta_ref[d]
+    base = 2 * rows * (z - 1)
+    heads = k0_ref.shape[1] // HEAD_SIZE
+    group = queries_ref.shape[1] // k0_ref.shape[1]
+    scale = math.log2(math.e) / math.sqrt(HEAD_SIZE)
+    span = 5 * tile
+
+    def one_piece(n, p0):
+        first = lax.div(p0, tile) * tile + 2 * rows - 4 * tile
+        first = pl.multiple_of(first, tile)
+        lane = lax.broadcasted_iota(jnp.int32, (1, tile), 1)
+        pos = 2 * rows * z + p0 + lax.rem(lane, piece_rows)
+        low = jnp.zeros((1, tile), jnp.int32)
+        for start in doc_start:
+            low = jnp.where(pos >= start, start, low)
+        key_pos = base + first + lax.broadcasted_iota(jnp.int32, (span, tile), 0)
+        allowed = (key_pos >= low) & (key_pos <= pos)
+        allowed = jnp.concatenate([allowed] * (group * piece_rows // tile), axis=1)
+        for kv in range(heads):
+            cols = pl.ds(kv * HEAD_SIZE, HEAD_SIZE)
+            q = jnp.concatenate(
+                [qbuf[n, :, pl.ds((kv * group + g) * HEAD_SIZE, HEAD_SIZE)] for g in range(group)], axis=0)
+            k = kbuf[pl.ds(first, span), cols]
+            v = vbuf[pl.ds(first, span), cols]
+            s = lax.dot_general(k, q, (((1,), (1,)), ((), ())), preferred_element_type=jnp.float32) * scale
+            s = jnp.where(allowed, s, MASKED)
+            top = jnp.max(s, axis=0, keepdims=True)
+            w = jnp.exp2(s - top)
+            total = jnp.sum(w, axis=0, keepdims=True)
+            o = lax.dot_general(v, w.astype(jnp.bfloat16), (((0,), (0,)), ((), ())),
+                                preferred_element_type=jnp.float32)
+            o = (o / total).T.astype(jnp.bfloat16)
+            for g in range(group):
+                ctxbuf[n, :, pl.ds((kv * group + g) * HEAD_SIZE, HEAD_SIZE)] = o[g * piece_rows:(g + 1) * piece_rows]
+
+    def step(n, carry):
+        p0 = starts[0][0]
+        for m in range(1, 2 * count):
+            p0 = jnp.where(n == m, starts[m // 2][m % 2], p0)
+        one_piece(n, p0)
+        return carry
+
+    lax.fori_loop(0, 2 * count, step, 0)
+    for n, out_ref in enumerate(out_refs):
+        out_ref[...] = ctxbuf[2 * n:2 * n + 2].reshape(out_ref.shape)
+    for copy in w_copies:
+        copy.wait()
+
+
+def _attend_groups(groups, names, meta, queries, other, kv, out_weight, after):
+    piece = queries.shape[0] // PIECES
+    rows = kv[0].shape[0]
+    return pl.pallas_call(
+        functools.partial(_attend_kernel, groups, names),
+        out_shape=[jax.ShapeDtypeStruct((2 * piece, queries.shape[1]), jnp.bfloat16) for _ in groups]
+        + [_quarter(out_weight) for _ in names],
+        in_specs=[SMEM] + [VMEM] * 10 + [HBM, ANY],
+        out_specs=[VMEM] * (len(groups) + len(names)),
+        scratch_shapes=[
+            pltpu.VMEM((4 * rows, kv[0].shape[1]), jnp.bfloat16),
+            pltpu.VMEM((4 * rows, kv[0].shape[1]), jnp.bfloat16),
+            pltpu.VMEM((2 * len(groups), piece, queries.shape[1]), jnp.bfloat16),
+            pltpu.VMEM((2 * len(groups), piece, queries.shape[1]), jnp.bfloat16),
+            pltpu.SemaphoreType.DMA((2 * len(names),)),
+        ],
+        compiler_params=pltpu.CompilerParams(vmem_limit_bytes=12 * 2**20),
+        cost_estimate=pl.CostEstimate(flops=10**9, bytes_accessed=10 * 2**20, transcendentals=10**6),
+        name="attend_groups",
+    )(meta, queries, other, *kv, out_weight, after)
+
+
+def _join_kernel(meta_ref, a_ref, b_ref, w_ref, out_ref, joined_ref, catbuf):
+    second = lax.rem(lax.div(meta_ref[0], 2), 2)
+    mid = a_ref.shape[0]
+    catbuf[_rows(second * mid, mid)] = a_ref[...]
+    catbuf[_rows((1 - second) * mid, mid)] = b_ref[...]
+    joined = catbuf[...].T
+    joined_ref[...] = joined
+    out_ref[...] = jnp.dot(w_ref[...], joined, preferred_element_type=jnp.float32).astype(out_ref.dtype)
+
+
+def _project_kernel(joined_ref, w_ref, out_ref):
+    out_ref[...] = jnp.dot(w_ref[...], joined_ref[...], preferred_element_type=jnp.float32).astype(out_ref.dtype)
+
+
+def _cost(rows, depth, tokens):
+    return pl.CostEstimate(
+        flops=2 * rows * depth * tokens, bytes_accessed=2 * (rows * depth + tokens * (rows + depth)), transcendentals=0)
+
+
+def _join_and_project(meta, a, b, weight):
+    (rows, depth), tokens = weight.shape, a.shape[0] + b.shape[0]
+    return pl.pallas_call(
+        _join_kernel,
+        out_shape=[jax.ShapeDtypeStruct((rows, tokens), jnp.bfloat16), jax.ShapeDtypeStruct((depth, tokens), jnp.bfloat16)],
+        in_specs=[SMEM] + [VMEM] * 3,
+        out_specs=[VMEM] * 2,
+        scratch_shapes=[pltpu.VMEM((tokens, depth), jnp.bfloat16)],
+        compiler_params=pltpu.CompilerParams(vmem_limit_bytes=8 * 2**20),
+        cost_estimate=_cost(rows, depth, tokens),
+        name="join_and_project",
+    )(meta, a, b, weight)
+
+
+def _project_rows(joined, weight):
+    (rows, depth), tokens = weight.shape, joined.shape[1]
+    return pl.pallas_call(
+        _project_kernel,
+        out_shape=jax.ShapeDtypeStruct((rows, tokens), jnp.bfloat16),
+        in_specs=[VMEM] * 2,
+        out_specs=VMEM,
+        compiler_params=pltpu.CompilerParams(vmem_limit_bytes=8 * 2**20),
+        cost_estimate=_cost(rows, depth, tokens),
+        name="project_rows",
+    )(joined, weight)
+
+
+def _add_halves_kernel(a_half, b_half, a_ref, b_ref, out_ref):
+    rows = out_ref.shape[0]
+    a = a_ref[a_half * rows:(a_half + 1) * rows].astype(jnp.float32)
+    b = b_ref[b_half * rows:(b_half + 1) * rows].astype(jnp.float32)
+    out_ref[...] = (a + b).astype(out_ref.dtype)
+
+
+def _add_halves(a, a_half, b, b_half):
+    rows, tokens = a.shape[0] // 2, a.shape[1]
+    return pl.pallas_call(
+        functools.partial(_add_halves_kernel, a_half, b_half),
+        out_shape=jax.ShapeDtypeStruct((rows, tokens), jnp.bfloat16),
+        in_specs=[VMEM] * 2,
+        out_specs=VMEM,
+        compiler_params=pltpu.CompilerParams(vmem_limit_bytes=2 * 2**20),
+        cost_estimate=pl.CostEstimate(flops=rows * tokens, bytes_accessed=6 * rows * tokens, transcendentals=0),
+        name="add_halves",
+    )(a, b)
+
+
+def _sum_parts(keep_ref, x1_ref, y1_ref, y2_ref, x2_ref):
+    half = y2_ref.shape[0]
+    f32 = jnp.float32
+    first = keep_ref[:half].astype(f32) + x1_ref[:half].astype(f32) + y2_ref[...].astype(f32)
+    second = keep_ref[half:].astype(f32) + y1_ref[:half].astype(f32) + x2_ref[...].astype(f32)
+    return first.astype(jnp.bfloat16), second.astype(jnp.bfloat16)
+
+
+def _finish_kernel(meta_ref, keep_ref, x1_ref, y1_ref, y2_ref, x2_ref, out_ref):
+    half = y2_ref.shape[0]
+    out_ref[:half], out_ref[half:] = _sum_parts(keep_ref, x1_ref, y1_ref, y2_ref, x2_ref)
+
+
+def _finish_both_kernel(meta_ref, near_ref, keep_ref, x1_ref, y1_ref, y2_ref, x2_ref, out_ref):
+    half, tokens = y2_ref.shape
+    upper = lax.div(meta_ref[0], 4)
+    first, second = _sum_parts(keep_ref, x1_ref, y1_ref, y2_ref, x2_ref)
+    at = _rows((1 - upper) * tokens, tokens)
+    out_ref[:half, at] = first
+    out_ref[half:, at] = second
+    out_ref[:, _rows(upper * tokens, tokens)] = near_ref[...]
+
+
+def _finish(meta, keep, x1, y1, y2, x2, near=None):
+    rows, tokens = keep.shape
+    operands = [meta] + ([] if near is None else [near]) + [keep, x1, y1, y2, x2]
+    return pl.pallas_call(
+        _finish_kernel if near is None else _finish_both_kernel,
+        out_shape=jax.ShapeDtypeStruct((rows, tokens if near is None else 2 * tokens), jnp.bfloat16),
+        in_specs=[SMEM] + [VMEM] * (len(operands) - 1),
+        out_specs=VMEM,
+        compiler_params=pltpu.CompilerParams(vmem_limit_bytes=4 * 2**20),
+        cost_estimate=pl.CostEstimate(flops=2 * rows * tokens, bytes_accessed=10 * rows * tokens, transcendentals=0),
+        name="finish",
+    )(*operands)
+
+
+def _flip(x, axis, bits):
+    n = lax.axis_size(axis)
+    return lax.ppermute(x, axis, [(i, i ^ bits) for i in range(n)])
+
+
+def _reduce_chunk(meta, a, b, weights, near):
+    xmsg, joined = _join_and_project(meta, a, b, weights["x"])
+    x1 = _flip(xmsg, "head", 1)
+    y1 = _flip(_project_rows(joined, weights["y"]), "head", 2)
+    pass_on = _project_rows(joined, weights["pass"])
+    keep = _project_rows(joined, weights["keep"])
+    y2 = _flip(_add_halves(pass_on, 0, x1, 1), "head", 2)
+    x2 = _flip(_add_halves(pass_on, 1, y1, 1), "head", 1)
+    return _finish(meta, keep, x1, y1, y2, x2, near)
+
+
+def per_device_fast(queries, keys, values, out_weight, doc_lengths, owners):
+    places = lax.axis_size("ctx")
+    before = [(i, i + 2) for i in range(places - 2)]
+    k2 = lax.ppermute(keys, "ctx", before)
+    v2 = lax.ppermute(values, "ctx", before)
+    meta = jnp.concatenate([
+        lax.axis_index("ctx").reshape(1), lax.axis_index("head").reshape(1), owners.reshape(-1), doc_lengths,
+    ]).astype(jnp.int32)
+    k1, v1 = _flip(keys, "ctx", 1), _flip(values, "ctx", 1)
+    leaving = pl.pallas_call(
+        _queries_for_other_core,
+        out_shape=jax.ShapeDtypeStruct((queries.shape[0] // 2, queries.shape[1]), jnp.bfloat16),
+        in_specs=[SMEM, VMEM],
+        out_specs=VMEM,
+        compiler_params=pltpu.CompilerParams(vmem_limit_bytes=2 * 2**20),
+        name="queries_for_other_core",
+    )(meta, queries)
+    other = _flip(leaving, "ctx", 1)
+    weights = dict(zip(("x", "y"), _stage_weights(("x", "y"), meta, out_weight)))
+    k3, v3 = _flip(k2, "ctx", 1), _flip(v2, "ctx", 1)
+    kv = (keys, k1, k2, k3, values, v1, v2, v3)
+    near1, far3, weights["pass"] = _attend_groups(
+        (1, 3), ("pass",), meta, queries, other, kv, out_weight, weights["x"])
+    near1, far3 = _flip(near1, "ctx", 2), _flip(far3, "ctx", 6)
+    far2, near0, weights["keep"] = _attend_groups(
+        (2, 0), ("keep",), meta, queries, other, kv, out_weight, weights["pass"])
+    far2 = _flip(far2, "ctx", 4)
+    near = _reduce_chunk(meta, near0, near1, weights, None)
+    return _reduce_chunk(meta, far2, far3, weights, near)
+
+
 def solution(mesh):
     in_specs = (P("ctx", "head"), P("ctx", "head"), P("ctx", "head"), P(None, "head"), P(), P())
     out_specs = P("head", "ctx")
+    fast = mesh.shape["ctx"] == PIECES and mesh.shape["head"] == N_FAST_HEAD
     return jax.shard_map(
-        per_device, mesh=mesh, in_specs=in_specs, out_specs=out_specs, check_vma=False
+        per_device_fast if fast else per_device, mesh=mesh, in_specs=in_specs, out_specs=out_specs, check_vma=False
     )

time: 191 us -> 89.1 us (0.47)
  waiting for transfers between devices: 103 us -> 19.8 us
  Pallas kernels: 0 us -> 42 us
  matrix products: 33.9 us -> 0 us
  starting transfers between devices: 6.4 us -> 24.7 us
  local copies, waits for them, and re-layouts: 19.1 us -> 1.24 us
  other arithmetic: 13.9 us -> 0.75 us
  between operations: 13.2 us -> 0.25 us
    reduce_scatter x1 -> x0, waiting for transfers between devices: 51.5 us -> none  [project(): lax.psum_scatter(lax.dot_general(out_weight, context, (((1,), (1,)), ((),...]
    pallas_call x0 -> x18, Pallas kernels: none -> 42 us  [the longest x6 14.7 us: _project_rows(): pl.pallas_call(_project_kernel, out_shape=jax.ShapeDtypeStruct((rows, tok...]
    dot_general x10 -> x0, matrix products: 33.9 us -> none  [the longest x1 16.7 us: project(): lax.dot_general(out_weight, context, (((1,), (1,)), ((), ())), preferred_...]
    all_to_all x1 -> x0, waiting for transfers between devices: 30.9 us -> none  [per_device(): lax.all_to_all(outgoing, 'ctx', split_axis=0, concat_axis=0, tiled=True)]
    ppermute x0 -> x18, starting transfers between devices: none -> 24.7 us  [the longest x16 16.6 us: _flip(): return lax.ppermute(x, axis, [(i, i ^ bits) for i in range(n)])]
    all_gather x2 -> x0, waiting for transfers between devices: 21 us -> none  [the longest x1 20.9 us: attend(): value_piece = lax.all_gather(values, 'ctx', axis=0, tiled=True)]
    ppermute x0 -> x18, waiting for transfers between devices: none -> 19.8 us  [the longest x16 17.2 us: _flip(): return lax.ppermute(x, axis, [(i, i ^ bits) for i in range(n)])]
    reduce_sum x10 -> x0, other arithmetic: 8.62 us -> none  [the longest x4 8.02 us: one_tile(): new_sum = running_sum * factor + jnp.sum(weights, axis=-1)]
  transfers between devices with their start and end apart: 4 -> 18, of which waited for: 3 -> 4; matrix products, arithmetic and copies ran while one was open for 4% -> 0% of each run, Pallas kernels for 0% -> 38%
where the time goes in v2:
time: 89.1 us; the launch traced here: 88.9 us
  Pallas kernels  42 us (47%)
  starting transfers between devices  24.7 us (28%)
  waiting for transfers between devices  19.8 us (22%)
  local copies, waits for them, and re-layouts  1.24 us (1%)
    ppermute x16, waiting for transfers between devices, _flip(): return lax.ppermute(x, axis, [(i, i ^ bits) for i in range(n)])  17.2 us
    ppermute x16, starting transfers between devices, _flip(): return lax.ppermute(x, axis, [(i, i ^ bits) for i in range(n)])  16.6 us
    pallas_call x6, Pallas kernels, _project_rows(): pl.pallas_call(_project_kernel, out_shape=jax.ShapeDtypeStruct((rows, tok...  14.7 us
    pallas_call x2, Pallas kernels, _attend_groups(): pl.pallas_call(functools.partial(_attend_kernel, groups, names), out_shap...  11.4 us
    pallas_call x1, Pallas kernels, _stage_weights(): pl.pallas_call(functools.partial(_stage_kernel, names), out_shape=[_quart...  6.43 us
    pallas_call x2, Pallas kernels, _join_and_project(): pl.pallas_call(_join_kernel, out_shape=[jax.ShapeDtypeStruct((rows, token...  6.15 us
    ppermute x1, starting transfers between devices, per_device_fast(): k2 = lax.ppermute(keys, 'ctx', before)  4.63 us
    ppermute x1, starting transfers between devices, per_device_fast(): v2 = lax.ppermute(values, 'ctx', before)  3.49 us
  transfers between devices with their start and end apart: 18, of which 4 were waited for; matrix products, arithmetic and copies ran while one was open for 0% of the time, Pallas kernels for 38%

profile of v2, /device:TPU:0, one launch (start us, length us, event | category | flops | bytes accessed | tf_op | source)
XLA Modules:
  0.0 88.9 jit_solution(7636042318191689877)
XLA Ops:
  0.0 0.7 pad_add_fusion.meta_ref
  0.7 0.0 copy-start
  0.8 1.2 %copy-done = bf16[256,2048]{1,0:T(8,128)(2,1)S(1)} copy-done((bf16[256,2048]{1,0:T(8,128)(2,1)S(1)}, bf16[256,2048]{1,0:T(8,128)(2,1)}, u32[]{:S(2)}) %copy-start) | copy-done | bytes 1048600
  2.0 0.6 queries_for_other_core.1
  2.6 0.0 copy-start.1
  2.6 0.0 copy-start.2
  2.6 0.0 copy-start.3
  2.6 0.5 collective-permute-start
  3.1 4.6 %collective-permute-start.2 = (bf16[256,256]{1,0:T(8,128)(2,1)}, bf16[256,256]{1,0:T(8,128)(2,1)S(1)}, u32[]{:S(2)}, u32[]{:S(2)}) collective-permute-start(bf16[256,256]{1,0:T(8,128)(2,1)} %k0_ref.3), channel_id=1, source_target_pairs={{0,8},{4,12},{8,16},{12,20},{16,24},{20,28},{1,9},{5,13},{9,17},{1... | collective-permute-start | bytes 393224 | tf_op jit(solution)/shard_map/ppermute | solution.py:425
  7.8 3.5 %collective-permute-start.5 = (bf16[256,256]{1,0:T(8,128)(2,1)}, bf16[256,256]{1,0:T(8,128)(2,1)S(1)}, u32[]{:S(2)}, u32[]{:S(2)}) collective-permute-start(bf16[256,256]{1,0:T(8,128)(2,1)} %v0_ref.3), channel_id=1, source_target_pairs={{0,8},{4,12},{8,16},{12,20},{16,24},{20,28},{1,9},{5,13},{9,17},{1... | collective-permute-start | bytes 393224 | tf_op jit(solution)/shard_map/ppermute | solution.py:426
  11.3 0.1 collective-permute-start.1
  11.3 0.5 collective-permute-start.4
  11.8 0.0 collective-permute-done.2.k2_ref
  11.8 0.1 collective-permute-start.3
  11.9 2.6 %collective-permute-done.5.v2_ref = bf16[256,256]{1,0:T(8,128)(2,1)S(1)} collective-permute-done((bf16[256,256]{1,0:T(8,128)(2,1)}, bf16[256,256]{1,0:T(8,128)(2,1)S(1)}, u32[]{:S(2)}, u32[]{:S(2)}) %collective-permute-start.5) | collective-permute-done | bytes 131104 | tf_op jit(solution)/shard_map/ppermute | solution.py:426
  14.5 0.0 collective-permute-start.6
  14.6 6.4 %stage_weights.1 = (bf16[2048,2048]{1,0:T(8,128)(2,1)S(1)}, bf16[2048,2048]{1,0:T(8,128)(2,1)S(1)}) custom-call(s32[82]{0:T(128)S(1)} %pad_add_fusion.meta_ref, bf16[8192,2048]{1,0:T(8,128)(2,1)} %w_ref.5), custom_call_target="tpu_custom_call" | custom-call | bytes 33554432 | tf_op jit(solution)/shard_map/stage_weights/pallas_call | solution.py:182
  21.0 0.0 collective-permute-done.1.k1_ref
  21.0 0.0 collective-permute-done.4.v1_ref
  21.0 0.0 collective-permute-done.3.k3_ref
  21.0 0.0 collective-permute-done.6.v3_ref
  21.0 0.0 collective-permute-done.other_ref
  21.0 0.0 copy-done.1
  21.1 0.0 copy-done.2
  21.1 0.0 copy-done.3
  21.1 5.6 %attend_groups.2 = (bf16[64,2048]{1,0:T(8,128)(2,1)S(1)}, bf16[64,2048]{1,0:T(8,128)(2,1)S(1)}, bf16[2048,2048]{1,0:T(8,128)(2,1)S(1)}) custom-call(s32[82]{0:T(128)S(1)} %pad_add_fusion.meta_ref, bf16[256,2048]{1,0:T(8,128)(2,1)S(1)} %copy-done.1, bf16[128,2048]{1,0:T(8,128)(2,1)S(1)} %collective-permute-done.other_ref, bf16[256,256]{1,0:T(8,128)(2,1)S(1)} %copy-done.2, ...), custom_call_target="tpu_custom_call" | custom-call | flops 1000000000 | bytes 10485760 | tf_op jit(solution)/shard_map/attend_groups/pallas_call | solution.py:284
  26.7 2.4 %collective-permute-start.7 = (bf16[64,2048]{1,0:T(8,128)(2,1)S(1)}, bf16[64,2048]{1,0:T(8,128)(2,1)S(1)}, u32[]{:S(2)}, u32[]{:S(2)}) collective-permute-start(bf16[64,2048]{1,0:T(8,128)(2,1)S(1)} %get-tuple-element.20), channel_id=1, source_target_pairs={{0,8},{4,12},{8,0},{12,4},{16,24},{20,28},{24,16},{28,20},{1,9},{5... | collective-permute-start | bytes 786440 | tf_op jit(solution)/shard_map/ppermute | solution.py:408
  29.1 2.5 %collective-permute-start.13 = (bf16[64,2048]{1,0:T(8,128)(2,1)S(1)}, bf16[64,2048]{1,0:T(8,128)(2,1)S(1)}, u32[]{:S(2)}, u32[]{:S(2)}) collective-permute-start(bf16[64,2048]{1,0:T(8,128)(2,1)S(1)} %get-tuple-element.26), channel_id=1, source_target_pairs={{0,24},{4,28},{8,16},{12,20},{16,8},{20,12},{24,0},{28,4},{1,25},{... | collective-permute-start | bytes 786440 | tf_op jit(solution)/shard_map/ppermute | solution.py:408
  31.6 5.8 %attend_groups.3 = (bf16[64,2048]{1,0:T(8,128)(2,1)S(1)}, bf16[64,2048]{1,0:T(8,128)(2,1)S(1)}, bf16[2048,2048]{1,0:T(8,128)(2,1)S(1)}) custom-call(s32[82]{0:T(128)S(1)} %pad_add_fusion.meta_ref, bf16[256,2048]{1,0:T(8,128)(2,1)S(1)} %copy-done.1, bf16[128,2048]{1,0:T(8,128)(2,1)S(1)} %collective-permute-done.other_ref, bf16[256,256]{1,0:T(8,128)(2,1)S(1)} %copy-done.2, ...), custom_call_target="tpu_custom_call" | custom-call | flops 1000000000 | bytes 10485760 | tf_op jit(solution)/shard_map/attend_groups/pallas_call | solution.py:284
  37.4 0.1 collective-permute-start.12
  37.5 0.0 collective-permute-done.7.b_ref
  37.5 3.1 %join_and_project.2 = (bf16[2048,128]{1,0:T(8,128)(2,1)S(1)}, bf16[2048,128]{1,0:T(8,128)(2,1)S(1)}) custom-call(s32[82]{0:T(128)S(1)} %pad_add_fusion.meta_ref, bf16[64,2048]{1,0:T(8,128)(2,1)S(1)} %get-tuple-element.19.a_ref, bf16[64,2048]{1,0:T(8,128)(2,1)S(1)} %collective-permute-done.7.b_ref, bf16[2048,2048]{1,0:T(8,128)(2,1)S(1)} %get-tuple-element.17.after_ref.w_ref), custom_call_target="tpu_custom_call" | custom-call | flops 1073741824 | bytes 9437184 | tf_op jit(solution)/shard_map/join_and_project/pallas_call | solution.py:324
  40.5 2.4 %project_rows.7 = bf16[2048,128]{1,0:T(8,128)(2,1)S(1)} custom-call(bf16[2048,128]{1,0:T(8,128)(2,1)S(1)} %get-tuple-element.21.joined_ref, bf16[2048,2048]{1,0:T(8,128)(2,1)S(1)} %get-tuple-element.24.w_ref), custom_call_target="tpu_custom_call" | custom-call | flops 1073741824 | bytes 9437184 | tf_op jit(solution)/shard_map/project_rows/pallas_call | solution.py:338
  42.9 1.6 %collective-permute-start.9 = (bf16[2048,128]{1,0:T(8,128)(2,1)S(1)}, bf16[2048,128]{1,0:T(8,128)(2,1)S(1)}, u32[]{:S(2)}, u32[]{:S(2)}) collective-permute-start(bf16[2048,128]{1,0:T(8,128)(2,1)S(1)} %project_rows.7), channel_id=1, source_target_pairs={{0,2},{1,3},{2,0},{3,1},{4,6},{5,7},{6,4},{7,5},{8,10},{9,11},{10,... | collective-permute-start | bytes 1572872 | tf_op jit(solution)/shard_map/ppermute | solution.py:408
  44.5 1.5 %collective-permute-start.8 = (bf16[2048,128]{1,0:T(8,128)(2,1)S(1)}, bf16[2048,128]{1,0:T(8,128)(2,1)S(1)}, u32[]{:S(2)}, u32[]{:S(2)}) collective-permute-start(bf16[2048,128]{1,0:T(8,128)(2,1)S(1)} %get-tuple-element.23), channel_id=1, source_target_pairs={{0,1},{1,0},{2,3},{3,2},{4,5},{5,4},{6,7},{7,6},{8,9},{9,8},{10,11... | collective-permute-start | bytes 1572872 | tf_op jit(solution)/shard_map/ppermute | solution.py:408
  46.0 0.0 collective-permute-done.13.b_ref
  46.0 9.1 %collective-permute-done.12.a_ref = bf16[64,2048]{1,0:T(8,128)(2,1)S(1)} collective-permute-done((bf16[64,2048]{1,0:T(8,128)(2,1)S(1)}, bf16[64,2048]{1,0:T(8,128)(2,1)S(1)}, u32[]{:S(2)}, u32[]{:S(2)}) %collective-permute-start.12) | collective-permute-done | bytes 262176 | tf_op jit(solution)/shard_map/ppermute | solution.py:408
  55.1 3.1 %join_and_project.3 = (bf16[2048,128]{1,0:T(8,128)(2,1)S(1)}, bf16[2048,128]{1,0:T(8,128)(2,1)S(1)}) custom-call(s32[82]{0:T(128)S(1)} %pad_add_fusion.meta_ref, bf16[64,2048]{1,0:T(8,128)(2,1)S(1)} %collective-permute-done.12.a_ref, bf16[64,2048]{1,0:T(8,128)(2,1)S(1)} %collective-permute-done.13.b_ref, bf16[2048,2048]{1,0:T(8,128)(2,1)S(1)} %get-tuple-element.17.after_ref.w_ref), custom_call_target="tpu_custom_call" | custom-call | flops 1073741824 | bytes 9437184 | tf_op jit(solution)/shard_map/join_and_project/pallas_call | solution.py:324
  58.2 2.4 %project_rows.10 = bf16[2048,128]{1,0:T(8,128)(2,1)S(1)} custom-call(bf16[2048,128]{1,0:T(8,128)(2,1)S(1)} %get-tuple-element.27.joined_ref, bf16[2048,2048]{1,0:T(8,128)(2,1)S(1)} %get-tuple-element.24.w_ref), custom_call_target="tpu_custom_call" | custom-call | flops 1073741824 | bytes 9437184 | tf_op jit(solution)/shard_map/project_rows/pallas_call | solution.py:338
  60.6 1.6 %collective-permute-start.15 = (bf16[2048,128]{1,0:T(8,128)(2,1)S(1)}, bf16[2048,128]{1,0:T(8,128)(2,1)S(1)}, u32[]{:S(2)}, u32[]{:S(2)}) collective-permute-start(bf16[2048,128]{1,0:T(8,128)(2,1)S(1)} %project_rows.10), channel_id=1, source_target_pairs={{0,2},{1,3},{2,0},{3,1},{4,6},{5,7},{6,4},{7,5},{8,10},{9,11},{10,... | collective-permute-start | bytes 1572872 | tf_op jit(solution)/shard_map/ppermute | solution.py:408
  62.2 1.5 %collective-permute-start.14 = (bf16[2048,128]{1,0:T(8,128)(2,1)S(1)}, bf16[2048,128]{1,0:T(8,128)(2,1)S(1)}, u32[]{:S(2)}, u32[]{:S(2)}) collective-permute-start(bf16[2048,128]{1,0:T(8,128)(2,1)S(1)} %get-tuple-element.28), channel_id=1, source_target_pairs={{0,1},{1,0},{2,3},{3,2},{4,5},{5,4},{6,7},{7,6},{8,9},{9,8},{10,11... | collective-permute-start | bytes 1572872 | tf_op jit(solution)/shard_map/ppermute | solution.py:408
  63.7 2.4 %project_rows.11.a_ref = bf16[2048,128]{1,0:T(8,128)(2,1)S(1)} custom-call(bf16[2048,128]{1,0:T(8,128)(2,1)S(1)} %get-tuple-element.27.joined_ref, bf16[2048,2048]{1,0:T(8,128)(2,1)S(1)} %get-tuple-element.18.after_ref.w_ref), custom_call_target="tpu_custom_call" | custom-call | flops 1073741824 | bytes 9437184 | tf_op jit(solution)/shard_map/project_rows/pallas_call | solution.py:338
  66.1 2.6 %project_rows.8.a_ref = bf16[2048,128]{1,0:T(8,128)(2,1)S(1)} custom-call(bf16[2048,128]{1,0:T(8,128)(2,1)S(1)} %get-tuple-element.21.joined_ref, bf16[2048,2048]{1,0:T(8,128)(2,1)S(1)} %get-tuple-element.18.after_ref.w_ref), custom_call_target="tpu_custom_call" | custom-call | flops 1073741824 | bytes 9437184 | tf_op jit(solution)/shard_map/project_rows/pallas_call | solution.py:338
  68.8 0.0 collective-permute-done.9.b_ref.y1_ref
  68.8 0.1 add_halves.5
  68.8 0.6 collective-permute-start.11
  69.5 0.0 collective-permute-done.8.b_ref.x1_ref
  69.5 0.1 add_halves.4
  69.5 0.6 collective-permute-start.10
  70.1 5.4 %collective-permute-done.15.b_ref.y1_ref = bf16[2048,128]{1,0:T(8,128)(2,1)S(1)} collective-permute-done((bf16[2048,128]{1,0:T(8,128)(2,1)S(1)}, bf16[2048,128]{1,0:T(8,128)(2,1)S(1)}, u32[]{:S(2)}, u32[]{:S(2)}) %collective-permute-start.15) | collective-permute-done | bytes 524320 | tf_op jit(solution)/shard_map/ppermute | solution.py:408
  75.5 0.1 add_halves.7
  75.5 1.6 %collective-permute-start.17 = (bf16[1024,128]{1,0:T(8,128)(2,1)S(1)}, bf16[1024,128]{1,0:T(8,128)(2,1)S(1)}, u32[]{:S(2)}, u32[]{:S(2)}) collective-permute-start(bf16[1024,128]{1,0:T(8,128)(2,1)S(1)} %add_halves.7), channel_id=1, source_target_pairs={{0,1},{1,0},{2,3},{3,2},{4,5},{5,4},{6,7},{7,6},{8,9},{9,8},{10,11... | collective-permute-start | bytes 786440 | tf_op jit(solution)/shard_map/ppermute | solution.py:408
  77.1 0.0 collective-permute-done.14.b_ref.x1_ref
  77.1 0.1 add_halves.6
  77.2 1.6 %collective-permute-start.16 = (bf16[1024,128]{1,0:T(8,128)(2,1)S(1)}, bf16[1024,128]{1,0:T(8,128)(2,1)S(1)}, u32[]{:S(2)}, u32[]{:S(2)}) collective-permute-start(bf16[1024,128]{1,0:T(8,128)(2,1)S(1)} %add_halves.6), channel_id=1, source_target_pairs={{0,2},{1,3},{2,0},{3,1},{4,6},{5,7},{6,4},{7,5},{8,10},{9,11},{10,... | collective-permute-start | bytes 786440 | tf_op jit(solution)/shard_map/ppermute | solution.py:408
  78.8 2.4 %project_rows.6.keep_ref = bf16[2048,128]{1,0:T(8,128)(2,1)S(1)} custom-call(bf16[2048,128]{1,0:T(8,128)(2,1)S(1)} %get-tuple-element.21.joined_ref, bf16[2048,2048]{1,0:T(8,128)(2,1)S(1)} %get-tuple-element.22.w_ref), custom_call_target="tpu_custom_call" | custom-call | flops 1073741824 | bytes 9437184 | tf_op jit(solution)/shard_map/project_rows/pallas_call | solution.py:338
  81.2 2.4 %project_rows.9.keep_ref = bf16[2048,128]{1,0:T(8,128)(2,1)S(1)} custom-call(bf16[2048,128]{1,0:T(8,128)(2,1)S(1)} %get-tuple-element.27.joined_ref, bf16[2048,2048]{1,0:T(8,128)(2,1)S(1)} %get-tuple-element.22.w_ref), custom_call_target="tpu_custom_call" | custom-call | flops 1073741824 | bytes 9437184 | tf_op jit(solution)/shard_map/project_rows/pallas_call | solution.py:338
  83.6 0.0 collective-permute-done.11.x2_ref
  83.6 0.0 collective-permute-done.10.y2_ref
  83.6 0.7 finish.2.near_ref
  84.3 2.7 %collective-permute-done.17.x2_ref = bf16[1024,128]{1,0:T(8,128)(2,1)S(1)} collective-permute-done((bf16[1024,128]{1,0:T(8,128)(2,1)S(1)}, bf16[1024,128]{1,0:T(8,128)(2,1)S(1)}, u32[]{:S(2)}, u32[]{:S(2)}) %collective-permute-start.17) | collective-permute-done | bytes 262176 | tf_op jit(solution)/shard_map/ppermute | solution.py:408
  87.0 0.0 collective-permute-done.16.y2_ref
  87.0 1.8 %finish.3 = bf16[2048,256]{1,0:T(8,128)(2,1)} custom-call(s32[82]{0:T(128)S(1)} %pad_add_fusion.meta_ref, bf16[2048,128]{1,0:T(8,128)(2,1)S(1)} %finish.2.near_ref, bf16[2048,128]{1,0:T(8,128)(2,1)S(1)} %project_rows.9.keep_ref, bf16[2048,128]{1,0:T(8,128)(2,1)S(1)} %collective-permute-done.14.b_ref.x1_ref, ...), custom_call_target="tpu_custom_call" | custom-call | flops 524288 | bytes 2621440 | tf_op jit(solution)/shard_map/finish/pallas_call | solution.py:395
Async XLA Ops:
  0.7 1.2 %copy-start = (bf16[256,2048]{1,0:T(8,128)(2,1)S(1)}, bf16[256,2048]{1,0:T(8,128)(2,1)}, u32[]{:S(2)}) copy-start(bf16[256,2048]{1,0:T(8,128)(2,1)} %queries_ref.5) | copy-start | bytes 3145732
  2.6 18.5 %copy-start.1 = (bf16[256,2048]{1,0:T(8,128)(2,1)S(1)}, bf16[256,2048]{1,0:T(8,128)(2,1)}, u32[]{:S(2)}) copy-start(bf16[256,2048]{1,0:T(8,128)(2,1)} %queries_ref.5) | copy-start | bytes 3145732
  2.6 18.5 %copy-start.2 = (bf16[256,256]{1,0:T(8,128)(2,1)S(1)}, bf16[256,256]{1,0:T(8,128)(2,1)}, u32[]{:S(2)}) copy-start(bf16[256,256]{1,0:T(8,128)(2,1)} %k0_ref.3) | copy-start | bytes 393220
  2.6 18.5 %copy-start.3 = (bf16[256,256]{1,0:T(8,128)(2,1)S(1)}, bf16[256,256]{1,0:T(8,128)(2,1)}, u32[]{:S(2)}) copy-start(bf16[256,256]{1,0:T(8,128)(2,1)} %v0_ref.3) | copy-start | bytes 393220
  2.6 18.4 %collective-permute-start = (bf16[128,2048]{1,0:T(8,128)(2,1)S(1)}, bf16[128,2048]{1,0:T(8,128)(2,1)S(1)}, u32[]{:S(2)}, u32[]{:S(2)}) collective-permute-start(bf16[128,2048]{1,0:T(8,128)(2,1)S(1)} %queries_for_other_core.1), channel_id=1, source_target_pairs={{0,4},{4,0},{8,12},{12,8},{16,20},{20,16},{24,28},{28,24},{1,5},{5... | collective-permute-start | bytes 1572872 | tf_op jit(solution)/shard_map/ppermute | solution.py:408
  3.1 8.7 %collective-permute-start.2 = (bf16[256,256]{1,0:T(8,128)(2,1)}, bf16[256,256]{1,0:T(8,128)(2,1)S(1)}, u32[]{:S(2)}, u32[]{:S(2)}) collective-permute-start(bf16[256,256]{1,0:T(8,128)(2,1)} %k0_ref.3), channel_id=1, source_target_pairs={{0,8},{4,12},{8,16},{12,20},{16,24},{20,28},{1,9},{5,13},{9,17},{1... | collective-permute-start | bytes 393224 | tf_op jit(solution)/shard_map/ppermute | solution.py:425
  7.8 6.8 %collective-permute-start.5 = (bf16[256,256]{1,0:T(8,128)(2,1)}, bf16[256,256]{1,0:T(8,128)(2,1)S(1)}, u32[]{:S(2)}, u32[]{:S(2)}) collective-permute-start(bf16[256,256]{1,0:T(8,128)(2,1)} %v0_ref.3), channel_id=1, source_target_pairs={{0,8},{4,12},{8,16},{12,20},{16,24},{20,28},{1,9},{5,13},{9,17},{1... | collective-permute-start | bytes 393224 | tf_op jit(solution)/shard_map/ppermute | solution.py:426
  11.3 9.7 %collective-permute-start.1 = (bf16[256,256]{1,0:T(8,128)(2,1)}, bf16[256,256]{1,0:T(8,128)(2,1)S(1)}, u32[]{:S(2)}, u32[]{:S(2)}) collective-permute-start(bf16[256,256]{1,0:T(8,128)(2,1)} %k0_ref.3), channel_id=1, source_target_pairs={{0,4},{4,0},{8,12},{12,8},{16,20},{20,16},{24,28},{28,24},{1,5},{5... | collective-permute-start | bytes 393224 | tf_op jit(solution)/shard_map/ppermute | solution.py:408
  11.3 9.7 %collective-permute-start.4 = (bf16[256,256]{1,0:T(8,128)(2,1)}, bf16[256,256]{1,0:T(8,128)(2,1)S(1)}, u32[]{:S(2)}, u32[]{:S(2)}) collective-permute-start(bf16[256,256]{1,0:T(8,128)(2,1)} %v0_ref.3), channel_id=1, source_target_pairs={{0,4},{4,0},{8,12},{12,8},{16,20},{20,16},{24,28},{28,24},{1,5},{5... | collective-permute-start | bytes 393224 | tf_op jit(solution)/shard_map/ppermute | solution.py:408
  11.8 9.2 %collective-permute-start.3 = (bf16[256,256]{1,0:T(8,128)(2,1)S(1)}, bf16[256,256]{1,0:T(8,128)(2,1)S(1)}, u32[]{:S(2)}, u32[]{:S(2)}) collective-permute-start(bf16[256,256]{1,0:T(8,128)(2,1)S(1)} %collective-permute-done.2.k2_ref), channel_id=1, source_target_pairs={{0,4},{4,0},{8,12},{12,8},{16,20},{20,16},{24,28},{28,24},{1,5},{5... | collective-permute-start | bytes 393224 | tf_op jit(solution)/shard_map/ppermute | solution.py:408
  14.5 6.5 %collective-permute-start.6 = (bf16[256,256]{1,0:T(8,128)(2,1)S(1)}, bf16[256,256]{1,0:T(8,128)(2,1)S(1)}, u32[]{:S(2)}, u32[]{:S(2)}) collective-permute-start(bf16[256,256]{1,0:T(8,128)(2,1)S(1)} %collective-permute-done.5.v2_ref), channel_id=1, source_target_pairs={{0,4},{4,0},{8,12},{12,8},{16,20},{20,16},{24,28},{28,24},{1,5},{5... | collective-permute-start | bytes 393224 | tf_op jit(solution)/shard_map/ppermute | solution.py:408
  26.7 10.8 %collective-permute-start.7 = (bf16[64,2048]{1,0:T(8,128)(2,1)S(1)}, bf16[64,2048]{1,0:T(8,128)(2,1)S(1)}, u32[]{:S(2)}, u32[]{:S(2)}) collective-permute-start(bf16[64,2048]{1,0:T(8,128)(2,1)S(1)} %get-tuple-element.20), channel_id=1, source_target_pairs={{0,8},{4,12},{8,0},{12,4},{16,24},{20,28},{24,16},{28,20},{1,9},{5... | collective-permute-start | bytes 786440 | tf_op jit(solution)/shard_map/ppermute | solution.py:408
  29.1 16.9 %collective-permute-start.13 = (bf16[64,2048]{1,0:T(8,128)(2,1)S(1)}, bf16[64,2048]{1,0:T(8,128)(2,1)S(1)}, u32[]{:S(2)}, u32[]{:S(2)}) collective-permute-start(bf16[64,2048]{1,0:T(8,128)(2,1)S(1)} %get-tuple-element.26), channel_id=1, source_target_pairs={{0,24},{4,28},{8,16},{12,20},{16,8},{20,12},{24,0},{28,4},{1,25},{... | collective-permute-start | bytes 786440 | tf_op jit(solution)/shard_map/ppermute | solution.py:408
  37.4 17.8 %collective-permute-start.12 = (bf16[64,2048]{1,0:T(8,128)(2,1)S(1)}, bf16[64,2048]{1,0:T(8,128)(2,1)S(1)}, u32[]{:S(2)}, u32[]{:S(2)}) collective-permute-start(bf16[64,2048]{1,0:T(8,128)(2,1)S(1)} %get-tuple-element.25), channel_id=1, source_target_pairs={{0,16},{4,20},{8,24},{12,28},{16,0},{20,4},{24,8},{28,12},{1,17},{... | collective-permute-start | bytes 786440 | tf_op jit(solution)/shard_map/ppermute | solution.py:408
  42.9 25.8 %collective-permute-start.9 = (bf16[2048,128]{1,0:T(8,128)(2,1)S(1)}, bf16[2048,128]{1,0:T(8,128)(2,1)S(1)}, u32[]{:S(2)}, u32[]{:S(2)}) collective-permute-start(bf16[2048,128]{1,0:T(8,128)(2,1)S(1)} %project_rows.7), channel_id=1, source_target_pairs={{0,2},{1,3},{2,0},{3,1},{4,6},{5,7},{6,4},{7,5},{8,10},{9,11},{10,... | collective-permute-start | bytes 1572872 | tf_op jit(solution)/shard_map/ppermute | solution.py:408
  44.5 24.9 %collective-permute-start.8 = (bf16[2048,128]{1,0:T(8,128)(2,1)S(1)}, bf16[2048,128]{1,0:T(8,128)(2,1)S(1)}, u32[]{:S(2)}, u32[]{:S(2)}) collective-permute-start(bf16[2048,128]{1,0:T(8,128)(2,1)S(1)} %get-tuple-element.23), channel_id=1, source_target_pairs={{0,1},{1,0},{2,3},{3,2},{4,5},{5,4},{6,7},{7,6},{8,9},{9,8},{10,11... | collective-permute-start | bytes 1572872 | tf_op jit(solution)/shard_map/ppermute | solution.py:408
  60.6 14.9 %collective-permute-start.15 = (bf16[2048,128]{1,0:T(8,128)(2,1)S(1)}, bf16[2048,128]{1,0:T(8,128)(2,1)S(1)}, u32[]{:S(2)}, u32[]{:S(2)}) collective-permute-start(bf16[2048,128]{1,0:T(8,128)(2,1)S(1)} %project_rows.10), channel_id=1, source_target_pairs={{0,2},{1,3},{2,0},{3,1},{4,6},{5,7},{6,4},{7,5},{8,10},{9,11},{10,... | collective-permute-start | bytes 1572872 | tf_op jit(solution)/shard_map/ppermute | solution.py:408
  62.2 14.9 %collective-permute-start.14 = (bf16[2048,128]{1,0:T(8,128)(2,1)S(1)}, bf16[2048,128]{1,0:T(8,128)(2,1)S(1)}, u32[]{:S(2)}, u32[]{:S(2)}) collective-permute-start(bf16[2048,128]{1,0:T(8,128)(2,1)S(1)} %get-tuple-element.28), channel_id=1, source_target_pairs={{0,1},{1,0},{2,3},{3,2},{4,5},{5,4},{6,7},{7,6},{8,9},{9,8},{10,11... | collective-permute-start | bytes 1572872 | tf_op jit(solution)/shard_map/ppermute | solution.py:408
  68.8 14.7 %collective-permute-start.11 = (bf16[1024,128]{1,0:T(8,128)(2,1)S(1)}, bf16[1024,128]{1,0:T(8,128)(2,1)S(1)}, u32[]{:S(2)}, u32[]{:S(2)}) collective-permute-start(bf16[1024,128]{1,0:T(8,128)(2,1)S(1)} %add_halves.5), channel_id=1, source_target_pairs={{0,1},{1,0},{2,3},{3,2},{4,5},{5,4},{6,7},{7,6},{8,9},{9,8},{10,11... | collective-permute-start | bytes 786440 | tf_op jit(solution)/shard_map/ppermute | solution.py:408
  69.5 14.1 %collective-permute-start.10 = (bf16[1024,128]{1,0:T(8,128)(2,1)S(1)}, bf16[1024,128]{1,0:T(8,128)(2,1)S(1)}, u32[]{:S(2)}, u32[]{:S(2)}) collective-permute-start(bf16[1024,128]{1,0:T(8,128)(2,1)S(1)} %add_halves.4), channel_id=1, source_target_pairs={{0,2},{1,3},{2,0},{3,1},{4,6},{5,7},{6,4},{7,5},{8,10},{9,11},{10,... | collective-permute-start | bytes 786440 | tf_op jit(solution)/shard_map/ppermute | solution.py:408
  75.5 11.5 %collective-permute-start.17 = (bf16[1024,128]{1,0:T(8,128)(2,1)S(1)}, bf16[1024,128]{1,0:T(8,128)(2,1)S(1)}, u32[]{:S(2)}, u32[]{:S(2)}) collective-permute-start(bf16[1024,128]{1,0:T(8,128)(2,1)S(1)} %add_halves.7), channel_id=1, source_target_pairs={{0,1},{1,0},{2,3},{3,2},{4,5},{5,4},{6,7},{7,6},{8,9},{9,8},{10,11... | collective-permute-start | bytes 786440 | tf_op jit(solution)/shard_map/ppermute | solution.py:408
  77.2 9.8 %collective-permute-start.16 = (bf16[1024,128]{1,0:T(8,128)(2,1)S(1)}, bf16[1024,128]{1,0:T(8,128)(2,1)S(1)}, u32[]{:S(2)}, u32[]{:S(2)}) collective-permute-start(bf16[1024,128]{1,0:T(8,128)(2,1)S(1)} %add_halves.6), channel_id=1, source_target_pairs={{0,2},{1,3},{2,0},{3,1},{4,6},{5,7},{6,4},{7,5},{8,10},{9,11},{10,... | collective-permute-start | bytes 786440 | tf_op jit(solution)/shard_map/ppermute | solution.py:408

commit v3 on v2

--- a/solution.py
+++ b/solution.py
@@ -121,7 +121,6 @@
 SMEM = pl.BlockSpec(memory_space=pltpu.SMEM)
 VMEM = pl.BlockSpec(memory_space=pltpu.VMEM)
 HBM = pl.BlockSpec(memory_space=pltpu.HBM)
-ANY = pl.BlockSpec(memory_space=pl.ANY)
 
 
 OWNERS_AT = 2
@@ -138,13 +137,47 @@
     return pl.ds(pl.multiple_of(start, size), size)
 
 
-def _queries_for_other_core(meta_ref, queries_ref, out_ref):
+def _join_keys_values_kernel(keys_ref, values_ref, out_ref):
+    rows = keys_ref.shape[0]
+    out_ref[:rows] = keys_ref[...]
+    out_ref[rows:] = values_ref[...]
+
+
+def _join_keys_values(keys, values):
+    return pl.pallas_call(
+        _join_keys_values_kernel,
+        out_shape=jax.ShapeDtypeStruct((2 * keys.shape[0], keys.shape[1]), keys.dtype),
+        in_specs=[VMEM] * 2,
+        out_specs=VMEM,
+        compiler_params=pltpu.CompilerParams(vmem_limit_bytes=2 * 2**20),
+        cost_estimate=pl.CostEstimate(flops=1, bytes_accessed=1, transcendentals=0),
+        name="join_keys_values",
+    )(keys, values)
+
+
+def _queries_for_other_core_kernel(meta_ref, queries_ref, out_ref, kept_ref):
     c = meta_ref[0]
     core = lax.rem(c, 2)
     rows = queries_ref.shape[0] // PIECES
     for j in range(PIECES // 2):
         piece = _find_piece(meta_ref, c, 2 * j + 1 - core)
         out_ref[j * rows:(j + 1) * rows] = queries_ref[_rows(piece * rows, rows)]
+    kept_ref[...] = queries_ref[...]
+
+
+def _queries_for_other_core(meta, queries):
+    return pl.pallas_call(
+        _queries_for_other_core_kernel,
+        out_shape=[
+            jax.ShapeDtypeStruct((queries.shape[0] // 2, queries.shape[1]), queries.dtype),
+            jax.ShapeDtypeStruct(queries.shape, queries.dtype),
+        ],
+        in_specs=[SMEM, VMEM],
+        out_specs=[VMEM] * 2,
+        compiler_params=pltpu.CompilerParams(vmem_limit_bytes=2 * 2**20),
+        cost_estimate=pl.CostEstimate(flops=1, bytes_accessed=1, transcendentals=0),
+        name="queries_for_other_core",
+    )(meta, queries)
 
 
 QUARTERS = {
@@ -166,6 +199,10 @@
     return copies
 
 
+def _quarter(out_weight):
+    return jax.ShapeDtypeStruct((out_weight.shape[0] // N_FAST_HEAD, out_weight.shape[1]), out_weight.dtype)
+
+
 def _stage_kernel(names, meta_ref, w_ref, *rest):
     copies = _weight_copies(names, meta_ref, w_ref, rest[:-1], rest[-1])
     for copy in copies:
@@ -174,27 +211,22 @@
         copy.wait()
 
 
-def _quarter(out_weight):
-    return jax.ShapeDtypeStruct((out_weight.shape[0] // N_FAST_HEAD, out_weight.shape[1]), out_weight.dtype)
-
-
-def _stage_weights(names, meta, out_weight):
+def _stage_weights(names, meta, out_weight, room):
     return pl.pallas_call(
         functools.partial(_stage_kernel, names),
         out_shape=[_quarter(out_weight) for _ in names],
         in_specs=[SMEM, HBM],
         out_specs=[VMEM] * len(names),
         scratch_shapes=[pltpu.SemaphoreType.DMA((2 * len(names),))],
-        compiler_params=pltpu.CompilerParams(vmem_limit_bytes=36 * 2**20),
-        cost_estimate=pl.CostEstimate(
-            flops=0, bytes_accessed=len(names) * out_weight.size, transcendentals=0),
+        compiler_params=pltpu.CompilerParams(vmem_limit_bytes=room * 2**20),
+        cost_estimate=pl.CostEstimate(flops=1, bytes_accessed=1, transcendentals=0),
         name="stage_weights",
     )(meta, out_weight)
 
 
 def _attend_kernel(
     groups, names, meta_ref, queries_ref, other_ref,
-    k0_ref, k1_ref, k2_ref, k3_ref, v0_ref, v1_ref, v2_ref, v3_ref, w_ref, after_ref,
+    kv0_ref, kv1_ref, kv2_ref, kv3_ref, w_ref,
     *rest,
 ):
     count = len(groups)
@@ -206,13 +238,18 @@
     c = meta_ref[0]
     core = lax.rem(c, 2)
     z = lax.div(c, 2)
-    rows = k0_ref.shape[0]
+    rows = kv0_ref.shape[0] // 2
     piece_rows = rows // PIECES
     tile = 128
+    heads = kv0_ref.shape[1] // HEAD_SIZE
     slots = (2 + core, 3 - core, core, 1 - core)
-    for b, (k_ref, v_ref) in enumerate(((k0_ref, v0_ref), (k1_ref, v1_ref), (k2_ref, v2_ref), (k3_ref, v3_ref))):
-        kbuf[_rows(slots[b] * rows, rows)] = k_ref[...]
-        vbuf[_rows(slots[b] * rows, rows)] = v_ref[...]
+    for b, kv_ref in enumerate((kv0_ref, kv1_ref, kv2_ref, kv3_ref)):
+        at = _rows(slots[b] * rows, rows)
+        kbuf[at] = kv_ref[:rows]
+        for kv in range(heads):
+            vbuf[at, 2 * kv * HEAD_SIZE:(2 * kv + 1) * HEAD_SIZE] = (
+                kv_ref[rows:, kv * HEAD_SIZE:(kv + 1) * HEAD_SIZE])
+            vbuf[at, (2 * kv + 1) * HEAD_SIZE:(2 * kv + 2) * HEAD_SIZE] = jnp.ones((rows, HEAD_SIZE), jnp.bfloat16)
     starts = []
     for n, k in enumerate(groups):
         zdest = z ^ k
@@ -231,119 +268,147 @@
         doc_start.append(running)
         running = running + meta_ref[d]
     base = 2 * rows * (z - 1)
-    heads = k0_ref.shape[1] // HEAD_SIZE
-    group = queries_ref.shape[1] // k0_ref.shape[1]
+    group = queries_ref.shape[1] // kv0_ref.shape[1]
     scale = math.log2(math.e) / math.sqrt(HEAD_SIZE)
     span = 5 * tile
 
-    def one_piece(n, p0):
-        first = lax.div(p0, tile) * tile + 2 * rows - 4 * tile
-        first = pl.multiple_of(first, tile)
-        lane = lax.broadcasted_iota(jnp.int32, (1, tile), 1)
-        pos = 2 * rows * z + p0 + lax.rem(lane, piece_rows)
-        low = jnp.zeros((1, tile), jnp.int32)
+    def piece_keys(p0):
+        first = pl.multiple_of(lax.div(p0, tile) * tile + 2 * rows - 4 * tile, tile)
+        pos = 2 * rows * z + p0 + lax.broadcasted_iota(jnp.int32, (piece_rows, 1), 0)
+        low = jnp.zeros((piece_rows, 1), jnp.int32)
         for start in doc_start:
             low = jnp.where(pos >= start, start, low)
-        key_pos = base + first + lax.broadcasted_iota(jnp.int32, (span, tile), 0)
-        allowed = (key_pos >= low) & (key_pos <= pos)
-        allowed = jnp.concatenate([allowed] * (group * piece_rows // tile), axis=1)
-        for kv in range(heads):
-            cols = pl.ds(kv * HEAD_SIZE, HEAD_SIZE)
+        key_pos = base + first + lax.broadcasted_iota(jnp.int32, (piece_rows, span), 1)
+        return first, (key_pos >= low) & (key_pos <= pos)
+
+    def some_pieces(pieces):
+        units, scores, weights = [], [], []
+        for n, p0 in pieces:
+            first, allowed = piece_keys(p0)
+            units += [(n, kv, first, allowed) for kv in range(heads)]
+        for n, kv, first, allowed in units:
             q = jnp.concatenate(
                 [qbuf[n, :, pl.ds((kv * group + g) * HEAD_SIZE, HEAD_SIZE)] for g in range(group)], axis=0)
-            k = kbuf[pl.ds(first, span), cols]
-            v = vbuf[pl.ds(first, span), cols]
-            s = lax.dot_general(k, q, (((1,), (1,)), ((), ())), preferred_element_type=jnp.float32) * scale
-            s = jnp.where(allowed, s, MASKED)
-            top = jnp.max(s, axis=0, keepdims=True)
-            w = jnp.exp2(s - top)
-            total = jnp.sum(w, axis=0, keepdims=True)
-            o = lax.dot_general(v, w.astype(jnp.bfloat16), (((0,), (0,)), ((), ())),
-                                preferred_element_type=jnp.float32)
-            o = (o / total).T.astype(jnp.bfloat16)
+            k = kbuf[pl.ds(first, span), pl.ds(kv * HEAD_SIZE, HEAD_SIZE)]
+            scores.append(lax.dot_general(q, k, (((1,), (1,)), ((), ())), preferred_element_type=jnp.float32))
+        for (n, kv, first, allowed), s in zip(units, scores):
+            s = jnp.where(allowed[None], s.reshape(group, piece_rows, span), MASKED)
+            w = jnp.exp2((s - jnp.max(s, axis=2, keepdims=True)) * scale)
+            weights.append(w.astype(jnp.bfloat16).reshape(group * piece_rows, span))
+        for (n, kv, first, allowed), w in zip(units, weights):
+            o = jnp.dot(w, vbuf[pl.ds(first, span), pl.ds(kv * 2 * HEAD_SIZE, 2 * HEAD_SIZE)],
+                        preferred_element_type=jnp.float32)
+            o = (o[:, :HEAD_SIZE] / o[:, HEAD_SIZE:]).astype(jnp.bfloat16)
             for g in range(group):
                 ctxbuf[n, :, pl.ds((kv * group + g) * HEAD_SIZE, HEAD_SIZE)] = o[g * piece_rows:(g + 1) * piece_rows]
 
-    def step(n, carry):
-        p0 = starts[0][0]
-        for m in range(1, 2 * count):
-            p0 = jnp.where(n == m, starts[m // 2][m % 2], p0)
-        one_piece(n, p0)
+    together = 2
+
+    def step(i, carry):
+        pieces = []
+        for j in range(together):
+            n = i * together + j
+            p0 = starts[0][0]
+            for m in range(1, 2 * count):
+                p0 = jnp.where(n == m, starts[m // 2][m % 2], p0)
+            pieces.append((n, p0))
+        some_pieces(pieces)
         return carry
 
-    lax.fori_loop(0, 2 * count, step, 0)
+    lax.fori_loop(0, 2 * count // together, step, 0)
     for n, out_ref in enumerate(out_refs):
         out_ref[...] = ctxbuf[2 * n:2 * n + 2].reshape(out_ref.shape)
     for copy in w_copies:
         copy.wait()
 
 
-def _attend_groups(groups, names, meta, queries, other, kv, out_weight, after):
+def _attend_groups(groups, names, meta, queries, other, kv, out_weight):
     piece = queries.shape[0] // PIECES
-    rows = kv[0].shape[0]
+    rows = kv[0].shape[0] // 2
     return pl.pallas_call(
         functools.partial(_attend_kernel, groups, names),
         out_shape=[jax.ShapeDtypeStruct((2 * piece, queries.shape[1]), jnp.bfloat16) for _ in groups]
         + [_quarter(out_weight) for _ in names],
-        in_specs=[SMEM] + [VMEM] * 10 + [HBM, ANY],
+        in_specs=[SMEM] + [VMEM] * 6 + [HBM],
         out_specs=[VMEM] * (len(groups) + len(names)),
         scratch_shapes=[
             pltpu.VMEM((4 * rows, kv[0].shape[1]), jnp.bfloat16),
-            pltpu.VMEM((4 * rows, kv[0].shape[1]), jnp.bfloat16),
+            pltpu.VMEM((4 * rows, 2 * kv[0].shape[1]), jnp.bfloat16),
             pltpu.VMEM((2 * len(groups), piece, queries.shape[1]), jnp.bfloat16),
             pltpu.VMEM((2 * len(groups), piece, queries.shape[1]), jnp.bfloat16),
             pltpu.SemaphoreType.DMA((2 * len(names),)),
         ],
         compiler_params=pltpu.CompilerParams(vmem_limit_bytes=12 * 2**20),
-        cost_estimate=pl.CostEstimate(flops=10**9, bytes_accessed=10 * 2**20, transcendentals=10**6),
+        cost_estimate=pl.CostEstimate(flops=1, bytes_accessed=1, transcendentals=0),
         name="attend_groups",
-    )(meta, queries, other, *kv, out_weight, after)
-
-
-def _join_kernel(meta_ref, a_ref, b_ref, w_ref, out_ref, joined_ref, catbuf):
+    )(meta, queries, other, *kv, out_weight)
+
+
+def _dot_to(out_ref, weight_ref, tokens):
+    out_ref[...] = jnp.dot(weight_ref[...], tokens, preferred_element_type=jnp.float32).astype(out_ref.dtype)
+
+
+def _leaving_rows_kernel(meta_ref, a_ref, b_ref, wx_ref, wy_ref, x_ref, y_ref, joined_ref, catbuf):
     second = lax.rem(lax.div(meta_ref[0], 2), 2)
     mid = a_ref.shape[0]
     catbuf[_rows(second * mid, mid)] = a_ref[...]
     catbuf[_rows((1 - second) * mid, mid)] = b_ref[...]
     joined = catbuf[...].T
     joined_ref[...] = joined
-    out_ref[...] = jnp.dot(w_ref[...], joined, preferred_element_type=jnp.float32).astype(out_ref.dtype)
-
-
-def _project_kernel(joined_ref, w_ref, out_ref):
-    out_ref[...] = jnp.dot(w_ref[...], joined_ref[...], preferred_element_type=jnp.float32).astype(out_ref.dtype)
-
-
-def _cost(rows, depth, tokens):
-    return pl.CostEstimate(
-        flops=2 * rows * depth * tokens, bytes_accessed=2 * (rows * depth + tokens * (rows + depth)), transcendentals=0)
-
-
-def _join_and_project(meta, a, b, weight):
-    (rows, depth), tokens = weight.shape, a.shape[0] + b.shape[0]
-    return pl.pallas_call(
-        _join_kernel,
-        out_shape=[jax.ShapeDtypeStruct((rows, tokens), jnp.bfloat16), jax.ShapeDtypeStruct((depth, tokens), jnp.bfloat16)],
-        in_specs=[SMEM] + [VMEM] * 3,
-        out_specs=[VMEM] * 2,
+    _dot_to(x_ref, wx_ref, joined)
+    _dot_to(y_ref, wy_ref, joined)
+
+
+def _pass_rows_kernel(joined_ref, w_ref, out_ref):
+    _dot_to(out_ref, w_ref, joined_ref[...])
+
+
+def _keep_rows_kernel(near_ref, far_ref, w_ref, near_out, far_out):
+    tokens = near_ref.shape[1]
+    both = jnp.concatenate([near_ref[...], far_ref[...]], axis=1)
+    out = jnp.dot(w_ref[...], both, preferred_element_type=jnp.float32).astype(near_out.dtype)
+    near_out[...] = out[:, :tokens]
+    far_out[...] = out[:, tokens:]
+
+
+def _leaving_rows(meta, a, b, w_x, w_y):
+    (rows, depth), tokens = w_x.shape, a.shape[0] + b.shape[0]
+    part = jax.ShapeDtypeStruct((rows, tokens), jnp.bfloat16)
+    return pl.pallas_call(
+        _leaving_rows_kernel,
+        out_shape=[part, part, jax.ShapeDtypeStruct((depth, tokens), jnp.bfloat16)],
+        in_specs=[SMEM] + [VMEM] * 4,
+        out_specs=[VMEM] * 3,
         scratch_shapes=[pltpu.VMEM((tokens, depth), jnp.bfloat16)],
         compiler_params=pltpu.CompilerParams(vmem_limit_bytes=8 * 2**20),
-        cost_estimate=_cost(rows, depth, tokens),
-        name="join_and_project",
-    )(meta, a, b, weight)
-
-
-def _project_rows(joined, weight):
-    (rows, depth), tokens = weight.shape, joined.shape[1]
-    return pl.pallas_call(
-        _project_kernel,
-        out_shape=jax.ShapeDtypeStruct((rows, tokens), jnp.bfloat16),
+        cost_estimate=pl.CostEstimate(flops=1, bytes_accessed=1, transcendentals=0),
+        name="leaving_rows",
+    )(meta, a, b, w_x, w_y)
+
+
+def _pass_rows(joined, weight):
+    return pl.pallas_call(
+        _pass_rows_kernel,
+        out_shape=jax.ShapeDtypeStruct((weight.shape[0], joined.shape[1]), jnp.bfloat16),
         in_specs=[VMEM] * 2,
         out_specs=VMEM,
         compiler_params=pltpu.CompilerParams(vmem_limit_bytes=8 * 2**20),
-        cost_estimate=_cost(rows, depth, tokens),
-        name="project_rows",
+        cost_estimate=pl.CostEstimate(flops=1, bytes_accessed=1, transcendentals=0),
+        name="pass_rows",
     )(joined, weight)
+
+
+def _keep_rows(near, far, weight):
+    part = jax.ShapeDtypeStruct((weight.shape[0], near.shape[1]), jnp.bfloat16)
+    return pl.pallas_call(
+        _keep_rows_kernel,
+        out_shape=[part, part],
+        in_specs=[VMEM] * 3,
+        out_specs=[VMEM] * 2,
+        compiler_params=pltpu.CompilerParams(vmem_limit_bytes=8 * 2**20),
+        cost_estimate=pl.CostEstimate(flops=1, bytes_accessed=1, transcendentals=0),
+        name="keep_rows",
+    )(near, far, weight)
 
 
 def _add_halves_kernel(a_half, b_half, a_ref, b_ref, out_ref):
@@ -361,7 +426,7 @@
         in_specs=[VMEM] * 2,
         out_specs=VMEM,
         compiler_params=pltpu.CompilerParams(vmem_limit_bytes=2 * 2**20),
-        cost_estimate=pl.CostEstimate(flops=rows * tokens, bytes_accessed=6 * rows * tokens, transcendentals=0),
+        cost_estimate=pl.CostEstimate(flops=1, bytes_accessed=1, transcendentals=0),
         name="add_halves",
     )(a, b)
 
@@ -398,7 +463,7 @@
         in_specs=[SMEM] + [VMEM] * (len(operands) - 1),
         out_specs=VMEM,
         compiler_params=pltpu.CompilerParams(vmem_limit_bytes=4 * 2**20),
-        cost_estimate=pl.CostEstimate(flops=2 * rows * tokens, bytes_accessed=10 * rows * tokens, transcendentals=0),
+        cost_estimate=pl.CostEstimate(flops=1, bytes_accessed=1, transcendentals=0),
         name="finish",
     )(*operands)
 
@@ -408,46 +473,45 @@
     return lax.ppermute(x, axis, [(i, i ^ bits) for i in range(n)])
 
 
-def _reduce_chunk(meta, a, b, weights, near):
-    xmsg, joined = _join_and_project(meta, a, b, weights["x"])
-    x1 = _flip(xmsg, "head", 1)
-    y1 = _flip(_project_rows(joined, weights["y"]), "head", 2)
-    pass_on = _project_rows(joined, weights["pass"])
-    keep = _project_rows(joined, weights["keep"])
-    y2 = _flip(_add_halves(pass_on, 0, x1, 1), "head", 2)
-    x2 = _flip(_add_halves(pass_on, 1, y1, 1), "head", 1)
-    return _finish(meta, keep, x1, y1, y2, x2, near)
-
-
 def per_device_fast(queries, keys, values, out_weight, doc_lengths, owners):
     places = lax.axis_size("ctx")
-    before = [(i, i + 2) for i in range(places - 2)]
-    k2 = lax.ppermute(keys, "ctx", before)
-    v2 = lax.ppermute(values, "ctx", before)
+    kv0 = _join_keys_values(keys, values)
+    kv2 = lax.ppermute(kv0, "ctx", [(i, i + 2) for i in range(places - 2)])
+    kv1 = _flip(kv0, "ctx", 1)
     meta = jnp.concatenate([
         lax.axis_index("ctx").reshape(1), lax.axis_index("head").reshape(1), owners.reshape(-1), doc_lengths,
     ]).astype(jnp.int32)
-    k1, v1 = _flip(keys, "ctx", 1), _flip(values, "ctx", 1)
-    leaving = pl.pallas_call(
-        _queries_for_other_core,
-        out_shape=jax.ShapeDtypeStruct((queries.shape[0] // 2, queries.shape[1]), jnp.bfloat16),
-        in_specs=[SMEM, VMEM],
-        out_specs=VMEM,
-        compiler_params=pltpu.CompilerParams(vmem_limit_bytes=2 * 2**20),
-        name="queries_for_other_core",
-    )(meta, queries)
+    leaving, queries = _queries_for_other_core(meta, queries)
     other = _flip(leaving, "ctx", 1)
-    weights = dict(zip(("x", "y"), _stage_weights(("x", "y"), meta, out_weight)))
-    k3, v3 = _flip(k2, "ctx", 1), _flip(v2, "ctx", 1)
-    kv = (keys, k1, k2, k3, values, v1, v2, v3)
-    near1, far3, weights["pass"] = _attend_groups(
-        (1, 3), ("pass",), meta, queries, other, kv, out_weight, weights["x"])
+    (w_x,) = _stage_weights(("x",), meta, out_weight, 36)
+    kv2, w_x = lax.optimization_barrier((kv2, w_x))
+    kv = (kv0, kv1, kv2, _flip(kv2, "ctx", 1))
+    near1, far3, w_y = _attend_groups((1, 3), ("y",), meta, queries, other, kv, out_weight)
     near1, far3 = _flip(near1, "ctx", 2), _flip(far3, "ctx", 6)
-    far2, near0, weights["keep"] = _attend_groups(
-        (2, 0), ("keep",), meta, queries, other, kv, out_weight, weights["pass"])
+    far2, near0, w_pass = _attend_groups((2, 0), ("pass",), meta, queries, other, kv, out_weight)
     far2 = _flip(far2, "ctx", 4)
-    near = _reduce_chunk(meta, near0, near1, weights, None)
-    return _reduce_chunk(meta, far2, far3, weights, near)
+
+    xmsg, ymsg, near = _leaving_rows(meta, near0, near1, w_x, w_y)
+    xmsg, ymsg, far3 = lax.optimization_barrier((xmsg, ymsg, far3))
+    near_x1, near_y1 = _flip(xmsg, "head", 1), _flip(ymsg, "head", 2)
+    near_pass = _pass_rows(near, w_pass)
+    near_pass, keep_meta = lax.optimization_barrier((near_pass, meta))
+    (w_keep,) = _stage_weights(("keep",), keep_meta, out_weight, 8)
+    near_pass, w_keep = lax.optimization_barrier((near_pass, w_keep))
+    ymsg, xmsg = _add_halves(near_pass, 0, near_x1, 1), _add_halves(near_pass, 1, near_y1, 1)
+    meta, ymsg, xmsg = lax.optimization_barrier((meta, ymsg, xmsg))
+    near_y2, near_x2 = _flip(ymsg, "head", 2), _flip(xmsg, "head", 1)
+
+    xmsg, ymsg, far = _leaving_rows(meta, far2, far3, w_x, w_y)
+    xmsg, ymsg, near_y2, near_x2 = lax.optimization_barrier((xmsg, ymsg, near_y2, near_x2))
+    far_x1, far_y1 = _flip(xmsg, "head", 1), _flip(ymsg, "head", 2)
+    far_pass = _pass_rows(far, w_pass)
+    near_keep, far_keep = _keep_rows(near, far, w_keep)
+    near = _finish(meta, near_keep, near_x1, near_y1, near_y2, near_x2)
+    far_pass, near, far_keep = lax.optimization_barrier((far_pass, near, far_keep))
+    far_y2 = _flip(_add_halves(far_pass, 0, far_x1, 1), "head", 2)
+    far_x2 = _flip(_add_halves(far_pass, 1, far_y1, 1), "head", 1)
+    return _finish(meta, far_keep, far_x1, far_y1, far_y2, far_x2, near)
 
 
 def solution(mesh):

time: 89.1 us -> 87.3 us (0.980)
  local copies, waits for them, and re-layouts: 1.24 us -> 17 us
  Pallas kernels: 42 us -> 34.9 us
  waiting for transfers between devices: 19.8 us -> 14 us
  starting transfers between devices: 24.7 us -> 20.1 us
    unnamed x8 -> x16, local copies, waits for them, and re-layouts: 1.24 us -> 17 us
    ppermute x16 -> x14, waiting for transfers between devices: 17.2 us -> 14 us  [_flip(): return lax.ppermute(x, axis, [(i, i ^ bits) for i in range(n)])]
    ppermute x2 -> x1, starting transfers between devices: 8.12 us -> 4.94 us  [per_device_fast(): kv2 = lax.ppermute(kv0, 'ctx', [(i, i + 2) for i in range(places - 2)])]
    pallas_call x2, Pallas kernels: 11.4 us -> 8.34 us  [_attend_groups(): pl.pallas_call(functools.partial(_attend_kernel, groups, names), out_shap...]
    pallas_call x9 -> x7, Pallas kernels: 21.4 us -> 18.4 us  [the longest x2 10.5 us: _leaving_rows(): pl.pallas_call(_leaving_rows_kernel, out_shape=[part, part, jax.ShapeDtyp...]
    ppermute x2 -> x1, waiting for transfers between devices: 2.63 us -> 0.01 us  [per_device_fast(): kv2 = lax.ppermute(kv0, 'ctx', [(i, i + 2) for i in range(places - 2)])]
    ppermute x16 -> x14, starting transfers between devices: 16.6 us -> 15.2 us  [_flip(): return lax.ppermute(x, axis, [(i, i ^ bits) for i in range(n)])]
    pallas_call x1 -> x2, Pallas kernels: 6.43 us -> 5.33 us  [_stage_weights(): pl.pallas_call(functools.partial(_stage_kernel, names), out_shape=[_quart...]
  transfers between devices with their start and end apart: 18 -> 15, of which waited for: 4 -> 7; matrix products, arithmetic and copies ran while one was open for 0% -> 1% of each run, Pallas kernels for 38% -> 33%
where the time goes in v3:
time: 87.3 us; the launch traced here: 87 us
  Pallas kernels  34.9 us (40%)
  starting transfers between devices  20.1 us (23%)
  local copies, waits for them, and re-layouts  17 us (19%)
  waiting for transfers between devices  14 us (16%)
    unnamed x16, local copies, waits for them, and re-layouts  17 us
    ppermute x14, starting transfers between devices, _flip(): return lax.ppermute(x, axis, [(i, i ^ bits) for i in range(n)])  15.2 us
    ppermute x14, waiting for transfers between devices, _flip(): return lax.ppermute(x, axis, [(i, i ^ bits) for i in range(n)])  14 us
    pallas_call x2, Pallas kernels, _leaving_rows(): pl.pallas_call(_leaving_rows_kernel, out_shape=[part, part, jax.ShapeDtyp...  10.5 us
    pallas_call x2, Pallas kernels, _attend_groups(): pl.pallas_call(functools.partial(_attend_kernel, groups, names), out_shap...  8.34 us
    pallas_call x2, Pallas kernels, _stage_weights(): pl.pallas_call(functools.partial(_stage_kernel, names), out_shape=[_quart...  5.33 us
    ppermute x1, starting transfers between devices, per_device_fast(): kv2 = lax.ppermute(kv0, 'ctx', [(i, i + 2) for i in range(places - 2)])  4.94 us
    pallas_call x2, Pallas kernels, _pass_rows(): pl.pallas_call(_pass_rows_kernel, out_shape=jax.ShapeDtypeStruct((weight....  4.81 us
  transfers between devices with their start and end apart: 15, of which 7 were waited for; matrix products, arithmetic and copies ran while one was open for 1% of the time, Pallas kernels for 33%

profile of v3, /device:TPU:0, one launch (start us, length us, event | category | flops | bytes accessed | tf_op | source)
XLA Modules:
  0.0 87.0 jit_solution(11737661720739742455)
XLA Ops:
  0.0 0.0 copy-start.6
  0.0 0.9 %copy-done.6 = bf16[256,256]{1,0:T(8,128)(2,1)S(1)} copy-done((bf16[256,256]{1,0:T(8,128)(2,1)S(1)}, bf16[256,256]{1,0:T(8,128)(2,1)}, u32[]{:S(2)}) %copy-start.6) | copy-done | bytes 131096
  0.9 0.0 copy-start.7
  0.9 0.9 %copy-done.7 = bf16[256,256]{1,0:T(8,128)(2,1)S(1)} copy-done((bf16[256,256]{1,0:T(8,128)(2,1)S(1)}, bf16[256,256]{1,0:T(8,128)(2,1)}, u32[]{:S(2)}) %copy-start.7) | copy-done | bytes 131096
  1.8 4.9 %collective-permute-start.2 = (bf16[512,256]{1,0:T(8,128)(2,1)S(1)}, bf16[512,256]{1,0:T(8,128)(2,1)S(1)}, u32[]{:S(2)}, u32[]{:S(2)}) collective-permute-start(bf16[512,256]{1,0:T(8,128)(2,1)S(1)} %join_keys_values.1.kv0_ref), channel_id=1, source_target_pairs={{0,8},{4,12},{8,16},{12,20},{16,24},{20,28},{1,9},{5,13},{9,17},{1... | collective-permute-start | bytes 786440 | tf_op jit(solution)/shard_map/ppermute | solution.py:479
  6.8 0.8 pad_add_fusion.meta_ref
  7.5 0.0 copy-start.5
  7.5 1.2 %copy-done.5 = bf16[256,2048]{1,0:T(8,128)(2,1)S(1)} copy-done((bf16[256,2048]{1,0:T(8,128)(2,1)S(1)}, bf16[256,2048]{1,0:T(8,128)(2,1)}, u32[]{:S(2)}) %copy-start.5) | copy-done | bytes 1048600
  8.8 0.6 queries_for_other_core.1
  9.4 0.1 collective-permute-start
  9.5 0.5 collective-permute-start.1
  10.0 4.0 %stage_weights.2.wx_ref = bf16[2048,2048]{1,0:T(8,128)(2,1)S(1)} custom-call(s32[82]{0:T(128)S(1)} %pad_add_fusion.meta_ref, bf16[8192,2048]{1,0:T(8,128)(2,1)} %w_ref.7), custom_call_target="tpu_custom_call" | custom-call | flops 1 | bytes 1 | tf_op jit(solution)/shard_map/stage_weights/pallas_call | solution.py:215
  14.0 0.0 collective-permute-done.2.kv2_ref
  14.0 0.1 collective-permute-start.3
  14.2 0.0 collective-permute-done.1.kv1_ref
  14.2 0.0 collective-permute-done.other_ref
  14.2 1.5 %collective-permute-done.3.kv3_ref = bf16[512,256]{1,0:T(8,128)(2,1)S(1)} collective-permute-done((bf16[512,256]{1,0:T(8,128)(2,1)S(1)}, bf16[512,256]{1,0:T(8,128)(2,1)S(1)}, u32[]{:S(2)}, u32[]{:S(2)}) %collective-permute-start.3) | collective-permute-done | bytes 262176 | tf_op jit(solution)/shard_map/ppermute | solution.py:473
  15.6 4.2 %attend_groups.3 = (bf16[64,2048]{1,0:T(8,128)(2,1)S(1)}, bf16[64,2048]{1,0:T(8,128)(2,1)S(1)}, bf16[2048,2048]{1,0:T(8,128)(2,1)S(1)}) custom-call(s32[82]{0:T(128)S(1)} %pad_add_fusion.meta_ref, bf16[256,2048]{1,0:T(8,128)(2,1)S(1)} %get-tuple-element.40.queries_ref, bf16[128,2048]{1,0:T(8,128)(2,1)S(1)} %collective-permute-done.other_ref, ...), custom_call_target="tpu_custom_call" | custom-call | flops 1 | bytes 1 | tf_op jit(solution)/shard_map/attend_groups/pallas_call | solution.py:328
  19.8 0.0 copy-start.1
  19.8 1.6 %collective-permute-start.4 = (bf16[64,2048]{1,0:T(8,128)(2,1)S(1)}, bf16[64,2048]{1,0:T(8,128)(2,1)S(1)}, u32[]{:S(2)}, u32[]{:S(2)}) collective-permute-start(bf16[64,2048]{1,0:T(8,128)(2,1)S(1)} %get-tuple-element.44), channel_id=1, source_target_pairs={{0,8},{4,12},{8,0},{12,4},{16,24},{20,28},{24,16},{28,20},{1,9},{5... | collective-permute-start | bytes 786440 | tf_op jit(solution)/shard_map/ppermute | solution.py:473
  21.5 2.5 %collective-permute-start.5 = (bf16[64,2048]{1,0:T(8,128)(2,1)S(1)}, bf16[64,2048]{1,0:T(8,128)(2,1)S(1)}, u32[]{:S(2)}, u32[]{:S(2)}) collective-permute-start(bf16[64,2048]{1,0:T(8,128)(2,1)S(1)} %get-tuple-element.54), channel_id=1, source_target_pairs={{0,24},{4,28},{8,16},{12,20},{16,8},{20,12},{24,0},{28,4},{1,25},{... | collective-permute-start | bytes 786440 | tf_op jit(solution)/shard_map/ppermute | solution.py:473
  23.9 4.2 %attend_groups.2 = (bf16[64,2048]{1,0:T(8,128)(2,1)S(1)}, bf16[64,2048]{1,0:T(8,128)(2,1)S(1)}, bf16[2048,2048]{1,0:T(8,128)(2,1)S(1)}) custom-call(s32[82]{0:T(128)S(1)} %pad_add_fusion.meta_ref, bf16[256,2048]{1,0:T(8,128)(2,1)S(1)} %get-tuple-element.40.queries_ref, bf16[128,2048]{1,0:T(8,128)(2,1)S(1)} %collective-permute-done.other_ref, ...), custom_call_target="tpu_custom_call" | custom-call | flops 1 | bytes 1 | tf_op jit(solution)/shard_map/attend_groups/pallas_call | solution.py:328
  28.1 0.0 copy-start.3
  28.1 0.1 collective-permute-done.4.b_ref
  28.2 0.0 copy-done.1
  28.2 5.2 %leaving_rows.2 = (bf16[2048,128]{1,0:T(8,128)(2,1)S(1)}, bf16[2048,128]{1,0:T(8,128)(2,1)S(1)}, bf16[2048,128]{1,0:T(8,128)(2,1)S(1)}) custom-call(s32[82]{0:T(128)S(1)} %pad_add_fusion.meta_ref, bf16[64,2048]{1,0:T(8,128)(2,1)S(1)} %get-tuple-element.43.a_ref, bf16[64,2048]{1,0:T(8,128)(2,1)S(1)} %collective-permute-done.4.b_ref, ...), custom_call_target="tpu_custom_call" | custom-call | flops 1 | bytes 1 | tf_op jit(solution)/shard_map/leaving_rows/pallas_call | solution.py:377
  33.5 2.4 %collective-permute-done.5.b_ref = bf16[64,2048]{1,0:T(8,128)(2,1)S(1)} collective-permute-done((bf16[64,2048]{1,0:T(8,128)(2,1)S(1)}, bf16[64,2048]{1,0:T(8,128)(2,1)S(1)}, u32[]{:S(2)}, u32[]{:S(2)}) %collective-permute-start.5) | collective-permute-done | bytes 262176 | tf_op jit(solution)/shard_map/ppermute | solution.py:473
  35.9 1.5 %collective-permute-start.7 = (bf16[2048,128]{1,0:T(8,128)(2,1)S(1)}, bf16[2048,128]{1,0:T(8,128)(2,1)S(1)}, u32[]{:S(2)}, u32[]{:S(2)}) collective-permute-start(bf16[2048,128]{1,0:T(8,128)(2,1)S(1)} %get-tuple-element.56), channel_id=1, source_target_pairs={{0,2},{1,3},{2,0},{3,1},{4,6},{5,7},{6,4},{7,5},{8,10},{9,11},{10,... | collective-permute-start | bytes 1572872 | tf_op jit(solution)/shard_map/ppermute | solution.py:473
  37.4 1.5 %collective-permute-start.6 = (bf16[2048,128]{1,0:T(8,128)(2,1)S(1)}, bf16[2048,128]{1,0:T(8,128)(2,1)S(1)}, u32[]{:S(2)}, u32[]{:S(2)}) collective-permute-start(bf16[2048,128]{1,0:T(8,128)(2,1)S(1)} %get-tuple-element.55), channel_id=1, source_target_pairs={{0,1},{1,0},{2,3},{3,2},{4,5},{5,4},{6,7},{7,6},{8,9},{9,8},{10,11... | collective-permute-start | bytes 1572872 | tf_op jit(solution)/shard_map/ppermute | solution.py:473
  38.9 1.1 %collective-permute-start.8 = (bf16[64,2048]{1,0:T(8,128)(2,1)S(1)}, bf16[64,2048]{1,0:T(8,128)(2,1)S(1)}, u32[]{:S(2)}, u32[]{:S(2)}) collective-permute-start(bf16[64,2048]{1,0:T(8,128)(2,1)S(1)} %get-tuple-element.58), channel_id=1, source_target_pairs={{0,16},{4,20},{8,24},{12,28},{16,0},{20,4},{24,8},{28,12},{1,17},{... | collective-permute-start | bytes 786440 | tf_op jit(solution)/shard_map/ppermute | solution.py:473
  40.0 0.0 copy-done.3
  40.0 2.4 %pass_rows.2.a_ref = bf16[2048,128]{1,0:T(8,128)(2,1)S(1)} custom-call(bf16[2048,128]{1,0:T(8,128)(2,1)S(1)} %get-tuple-element.47.joined_ref.near_ref, bf16[2048,2048]{1,0:T(8,128)(2,1)S(1)} %get-tuple-element.48.w_ref), custom_call_target="tpu_custom_call" | custom-call | flops 1 | bytes 1 | tf_op jit(solution)/shard_map/pass_rows/pallas_call | solution.py:390
  42.4 0.0 copy-start
  42.4 10.5 %copy-done = bf16[8192,2048]{1,0:T(8,128)(2,1)S(1)} copy-done((bf16[8192,2048]{1,0:T(8,128)(2,1)S(1)}, bf16[8192,2048]{1,0:T(8,128)(2,1)}, u32[]{:S(2)}) %copy-start) | copy-done | bytes 33554456
  52.9 1.3 %stage_weights.3.w_ref = bf16[2048,2048]{1,0:T(8,128)(2,1)S(1)} custom-call(s32[82]{0:T(128)S(1)} %pad_add_fusion.meta_ref, bf16[8192,2048]{1,0:T(8,128)(2,1)S(1)} %copy-done), custom_call_target="tpu_custom_call" | custom-call | flops 1 | bytes 1 | tf_op jit(solution)/shard_map/stage_weights/pallas_call | solution.py:215
  54.2 0.0 collective-permute-done.7.b_ref.y1_ref
  54.3 0.1 add_halves.5
  54.3 0.0 collective-permute-done.6.b_ref.x1_ref
  54.3 0.1 add_halves.4
  54.4 0.6 collective-permute-start.9
  55.0 0.5 collective-permute-start.10
  55.5 0.0 collective-permute-done.8.a_ref
  55.5 0.0 copy-start.2
  55.5 3.4 %copy-done.2 = bf16[2048,2048]{1,0:T(8,128)(2,1)S(1)} copy-done((bf16[2048,2048]{1,0:T(8,128)(2,1)S(1)}, bf16[2048,2048]{1,0:T(8,128)(2,1)}, u32[]{:S(2)}) %copy-start.2) | copy-done | bytes 8388632
  58.9 0.0 copy-start.4
  58.9 5.3 %leaving_rows.3 = (bf16[2048,128]{1,0:T(8,128)(2,1)S(1)}, bf16[2048,128]{1,0:T(8,128)(2,1)S(1)}, bf16[2048,128]{1,0:T(8,128)(2,1)S(1)}) custom-call(s32[82]{0:T(128)S(1)} %pad_add_fusion.meta_ref, bf16[64,2048]{1,0:T(8,128)(2,1)S(1)} %collective-permute-done.8.a_ref, bf16[64,2048]{1,0:T(8,128)(2,1)S(1)} %collective-permute-done.5.b_ref, ...), custom_call_target="tpu_custom_call" | custom-call | flops 1 | bytes 1 | tf_op jit(solution)/shard_map/leaving_rows/pallas_call | solution.py:377
  64.2 0.0 collective-permute-done.9.y2_ref
  64.2 0.0 collective-permute-done.10.x2_ref
  64.2 1.6 %collective-permute-start.11 = (bf16[2048,128]{1,0:T(8,128)(2,1)S(1)}, bf16[2048,128]{1,0:T(8,128)(2,1)S(1)}, u32[]{:S(2)}, u32[]{:S(2)}) collective-permute-start(bf16[2048,128]{1,0:T(8,128)(2,1)S(1)} %get-tuple-element.72), channel_id=1, source_target_pairs={{0,1},{1,0},{2,3},{3,2},{4,5},{5,4},{6,7},{7,6},{8,9},{9,8},{10,11... | collective-permute-start | bytes 1572872 | tf_op jit(solution)/shard_map/ppermute | solution.py:473
  65.8 1.5 %collective-permute-start.12 = (bf16[2048,128]{1,0:T(8,128)(2,1)S(1)}, bf16[2048,128]{1,0:T(8,128)(2,1)S(1)}, u32[]{:S(2)}, u32[]{:S(2)}) collective-permute-start(bf16[2048,128]{1,0:T(8,128)(2,1)S(1)} %get-tuple-element.73), channel_id=1, source_target_pairs={{0,2},{1,3},{2,0},{3,1},{4,6},{5,7},{6,4},{7,5},{8,10},{9,11},{10,... | collective-permute-start | bytes 1572872 | tf_op jit(solution)/shard_map/ppermute | solution.py:473
  67.3 0.0 copy-done.4
  67.3 2.4 %pass_rows.3.a_ref = bf16[2048,128]{1,0:T(8,128)(2,1)S(1)} custom-call(bf16[2048,128]{1,0:T(8,128)(2,1)S(1)} %get-tuple-element.60.joined_ref.far_ref, bf16[2048,2048]{1,0:T(8,128)(2,1)S(1)} %copy-done.4), custom_call_target="tpu_custom_call" | custom-call | flops 1 | bytes 1 | tf_op jit(solution)/shard_map/pass_rows/pallas_call | solution.py:390
  69.7 2.4 %keep_rows.1 = (bf16[2048,128]{1,0:T(8,128)(2,1)S(1)}, bf16[2048,128]{1,0:T(8,128)(2,1)S(1)}) custom-call(bf16[2048,128]{1,0:T(8,128)(2,1)S(1)} %get-tuple-element.47.joined_ref.near_ref, bf16[2048,128]{1,0:T(8,128)(2,1)S(1)} %get-tuple-element.60.joined_ref.far_ref, bf16[2048,2048]{1,0:T(8,128)(2,1)S(1)} %stage_weights.3.w_ref), custom_call_target="tpu_custom_call" | custom-call | flops 1 | bytes 1 | tf_op jit(solution)/shard_map/keep_rows/pallas_call | solution.py:403
  72.1 0.7 finish.2.near_ref
  72.8 2.3 %collective-permute-done.11.b_ref.x1_ref = bf16[2048,128]{1,0:T(8,128)(2,1)S(1)} collective-permute-done((bf16[2048,128]{1,0:T(8,128)(2,1)S(1)}, bf16[2048,128]{1,0:T(8,128)(2,1)S(1)}, u32[]{:S(2)}, u32[]{:S(2)}) %collective-permute-start.11) | collective-permute-done | bytes 524320 | tf_op jit(solution)/shard_map/ppermute | solution.py:473
  75.2 0.1 add_halves.6
  75.3 1.7 %collective-permute-start.13 = (bf16[1024,128]{1,0:T(8,128)(2,1)S(1)}, bf16[1024,128]{1,0:T(8,128)(2,1)S(1)}, u32[]{:S(2)}, u32[]{:S(2)}) collective-permute-start(bf16[1024,128]{1,0:T(8,128)(2,1)S(1)} %add_halves.6), channel_id=1, source_target_pairs={{0,2},{1,3},{2,0},{3,1},{4,6},{5,7},{6,4},{7,5},{8,10},{9,11},{10,... | collective-permute-start | bytes 786440 | tf_op jit(solution)/shard_map/ppermute | solution.py:473
  76.9 1.7 %collective-permute-done.12.b_ref.y1_ref = bf16[2048,128]{1,0:T(8,128)(2,1)S(1)} collective-permute-done((bf16[2048,128]{1,0:T(8,128)(2,1)S(1)}, bf16[2048,128]{1,0:T(8,128)(2,1)S(1)}, u32[]{:S(2)}, u32[]{:S(2)}) %collective-permute-start.12) | collective-permute-done | bytes 524320 | tf_op jit(solution)/shard_map/ppermute | solution.py:473
  78.6 0.1 add_halves.7
  78.7 0.4 collective-permute-start.14
  79.1 2.9 %collective-permute-done.13.y2_ref = bf16[1024,128]{1,0:T(8,128)(2,1)S(1)} collective-permute-done((bf16[1024,128]{1,0:T(8,128)(2,1)S(1)}, bf16[1024,128]{1,0:T(8,128)(2,1)S(1)}, u32[]{:S(2)}, u32[]{:S(2)}) %collective-permute-start.13) | collective-permute-done | bytes 262176 | tf_op jit(solution)/shard_map/ppermute | solution.py:473
  82.0 3.1 %collective-permute-done.14.x2_ref = bf16[1024,128]{1,0:T(8,128)(2,1)S(1)} collective-permute-done((bf16[1024,128]{1,0:T(8,128)(2,1)S(1)}, bf16[1024,128]{1,0:T(8,128)(2,1)S(1)}, u32[]{:S(2)}, u32[]{:S(2)}) %collective-permute-start.14) | collective-permute-done | bytes 262176 | tf_op jit(solution)/shard_map/ppermute | solution.py:473
  85.1 1.8 %finish.3 = bf16[2048,256]{1,0:T(8,128)(2,1)} custom-call(s32[82]{0:T(128)S(1)} %pad_add_fusion.meta_ref, bf16[2048,128]{1,0:T(8,128)(2,1)S(1)} %finish.2.near_ref, bf16[2048,128]{1,0:T(8,128)(2,1)S(1)} %get-tuple-element.71.keep_ref, bf16[2048,128]{1,0:T(8,128)(2,1)S(1)} %collective-permute-done.11.b_ref.x1_ref, ...), custom_call_target="tpu_custom_call" | custom-call | flops 1 | bytes 1 | tf_op jit(solution)/shard_map/finish/pallas_call | solution.py:460
  (1 shorter events, 0.0 us)
Async XLA Ops:
  0.0 0.9 %copy-start.6 = (bf16[256,256]{1,0:T(8,128)(2,1)S(1)}, bf16[256,256]{1,0:T(8,128)(2,1)}, u32[]{:S(2)}) copy-start(bf16[256,256]{1,0:T(8,128)(2,1)} %keys_ref.1) | copy-start | bytes 393220
  0.9 0.9 %copy-start.7 = (bf16[256,256]{1,0:T(8,128)(2,1)S(1)}, bf16[256,256]{1,0:T(8,128)(2,1)}, u32[]{:S(2)}) copy-start(bf16[256,256]{1,0:T(8,128)(2,1)} %values_ref.1) | copy-start | bytes 393220
  1.8 12.2 %collective-permute-start.2 = (bf16[512,256]{1,0:T(8,128)(2,1)S(1)}, bf16[512,256]{1,0:T(8,128)(2,1)S(1)}, u32[]{:S(2)}, u32[]{:S(2)}) collective-permute-start(bf16[512,256]{1,0:T(8,128)(2,1)S(1)} %join_keys_values.1.kv0_ref), channel_id=1, source_target_pairs={{0,8},{4,12},{8,16},{12,20},{16,24},{20,28},{1,9},{5,13},{9,17},{1... | collective-permute-start | bytes 786440 | tf_op jit(solution)/shard_map/ppermute | solution.py:479
  7.5 1.2 %copy-start.5 = (bf16[256,2048]{1,0:T(8,128)(2,1)S(1)}, bf16[256,2048]{1,0:T(8,128)(2,1)}, u32[]{:S(2)}) copy-start(bf16[256,2048]{1,0:T(8,128)(2,1)} %queries_ref.1) | copy-start | bytes 3145732
  9.4 4.8 %collective-permute-start = (bf16[128,2048]{1,0:T(8,128)(2,1)S(1)}, bf16[128,2048]{1,0:T(8,128)(2,1)S(1)}, u32[]{:S(2)}, u32[]{:S(2)}) collective-permute-start(bf16[128,2048]{1,0:T(8,128)(2,1)S(1)} %get-tuple-element.41), channel_id=1, source_target_pairs={{0,4},{4,0},{8,12},{12,8},{16,20},{20,16},{24,28},{28,24},{1,5},{5... | collective-permute-start | bytes 1572872 | tf_op jit(solution)/shard_map/ppermute | solution.py:473
  9.5 4.7 %collective-permute-start.1 = (bf16[512,256]{1,0:T(8,128)(2,1)S(1)}, bf16[512,256]{1,0:T(8,128)(2,1)S(1)}, u32[]{:S(2)}, u32[]{:S(2)}) collective-permute-start(bf16[512,256]{1,0:T(8,128)(2,1)S(1)} %join_keys_values.1.kv0_ref), channel_id=1, source_target_pairs={{0,4},{4,0},{8,12},{12,8},{16,20},{20,16},{24,28},{28,24},{1,5},{5... | collective-permute-start | bytes 786440 | tf_op jit(solution)/shard_map/ppermute | solution.py:473
  14.0 1.6 %collective-permute-start.3 = (bf16[512,256]{1,0:T(8,128)(2,1)S(1)}, bf16[512,256]{1,0:T(8,128)(2,1)S(1)}, u32[]{:S(2)}, u32[]{:S(2)}) collective-permute-start(bf16[512,256]{1,0:T(8,128)(2,1)S(1)} %collective-permute-done.2.kv2_ref), channel_id=1, source_target_pairs={{0,4},{4,0},{8,12},{12,8},{16,20},{20,16},{24,28},{28,24},{1,5},{5... | collective-permute-start | bytes 786440 | tf_op jit(solution)/shard_map/ppermute | solution.py:473
  19.8 8.4 %copy-start.1 = (bf16[2048,2048]{1,0:T(8,128)(2,1)}, bf16[2048,2048]{1,0:T(8,128)(2,1)S(1)}, u32[]{:S(2)}) copy-start(bf16[2048,2048]{1,0:T(8,128)(2,1)S(1)} %get-tuple-element.46.wy_ref) | copy-start | bytes 25165828
  19.8 8.4 %collective-permute-start.4 = (bf16[64,2048]{1,0:T(8,128)(2,1)S(1)}, bf16[64,2048]{1,0:T(8,128)(2,1)S(1)}, u32[]{:S(2)}, u32[]{:S(2)}) collective-permute-start(bf16[64,2048]{1,0:T(8,128)(2,1)S(1)} %get-tuple-element.44), channel_id=1, source_target_pairs={{0,8},{4,12},{8,0},{12,4},{16,24},{20,28},{24,16},{28,20},{1,9},{5... | collective-permute-start | bytes 786440 | tf_op jit(solution)/shard_map/ppermute | solution.py:473
  21.5 14.4 %collective-permute-start.5 = (bf16[64,2048]{1,0:T(8,128)(2,1)S(1)}, bf16[64,2048]{1,0:T(8,128)(2,1)S(1)}, u32[]{:S(2)}, u32[]{:S(2)}) collective-permute-start(bf16[64,2048]{1,0:T(8,128)(2,1)S(1)} %get-tuple-element.54), channel_id=1, source_target_pairs={{0,24},{4,28},{8,16},{12,20},{16,8},{20,12},{24,0},{28,4},{1,25},{... | collective-permute-start | bytes 786440 | tf_op jit(solution)/shard_map/ppermute | solution.py:473
  28.1 11.9 %copy-start.3 = (bf16[2048,2048]{1,0:T(8,128)(2,1)}, bf16[2048,2048]{1,0:T(8,128)(2,1)S(1)}, u32[]{:S(2)}) copy-start(bf16[2048,2048]{1,0:T(8,128)(2,1)S(1)} %get-tuple-element.48.w_ref) | copy-start | bytes 25165828
  35.9 18.4 %collective-permute-start.7 = (bf16[2048,128]{1,0:T(8,128)(2,1)S(1)}, bf16[2048,128]{1,0:T(8,128)(2,1)S(1)}, u32[]{:S(2)}, u32[]{:S(2)}) collective-permute-start(bf16[2048,128]{1,0:T(8,128)(2,1)S(1)} %get-tuple-element.56), channel_id=1, source_target_pairs={{0,2},{1,3},{2,0},{3,1},{4,6},{5,7},{6,4},{7,5},{8,10},{9,11},{10,... | collective-permute-start | bytes 1572872 | tf_op jit(solution)/shard_map/ppermute | solution.py:473
  37.4 16.9 %collective-permute-start.6 = (bf16[2048,128]{1,0:T(8,128)(2,1)S(1)}, bf16[2048,128]{1,0:T(8,128)(2,1)S(1)}, u32[]{:S(2)}, u32[]{:S(2)}) collective-permute-start(bf16[2048,128]{1,0:T(8,128)(2,1)S(1)} %get-tuple-element.55), channel_id=1, source_target_pairs={{0,1},{1,0},{2,3},{3,2},{4,5},{5,4},{6,7},{7,6},{8,9},{9,8},{10,11... | collective-permute-start | bytes 1572872 | tf_op jit(solution)/shard_map/ppermute | solution.py:473
  38.9 16.6 %collective-permute-start.8 = (bf16[64,2048]{1,0:T(8,128)(2,1)S(1)}, bf16[64,2048]{1,0:T(8,128)(2,1)S(1)}, u32[]{:S(2)}, u32[]{:S(2)}) collective-permute-start(bf16[64,2048]{1,0:T(8,128)(2,1)S(1)} %get-tuple-element.58), channel_id=1, source_target_pairs={{0,16},{4,20},{8,24},{12,28},{16,0},{20,4},{24,8},{28,12},{1,17},{... | collective-permute-start | bytes 786440 | tf_op jit(solution)/shard_map/ppermute | solution.py:473
  42.4 10.5 %copy-start = (bf16[8192,2048]{1,0:T(8,128)(2,1)S(1)}, bf16[8192,2048]{1,0:T(8,128)(2,1)}, u32[]{:S(2)}) copy-start(bf16[8192,2048]{1,0:T(8,128)(2,1)} %w_ref.7) | copy-start | bytes 100663296
  54.4 9.8 %collective-permute-start.9 = (bf16[1024,128]{1,0:T(8,128)(2,1)S(1)}, bf16[1024,128]{1,0:T(8,128)(2,1)S(1)}, u32[]{:S(2)}, u32[]{:S(2)}) collective-permute-start(bf16[1024,128]{1,0:T(8,128)(2,1)S(1)} %add_halves.4), channel_id=1, source_target_pairs={{0,2},{1,3},{2,0},{3,1},{4,6},{5,7},{6,4},{7,5},{8,10},{9,11},{10,... | collective-permute-start | bytes 786440 | tf_op jit(solution)/shard_map/ppermute | solution.py:473
  55.0 9.2 %collective-permute-start.10 = (bf16[1024,128]{1,0:T(8,128)(2,1)S(1)}, bf16[1024,128]{1,0:T(8,128)(2,1)S(1)}, u32[]{:S(2)}, u32[]{:S(2)}) collective-permute-start(bf16[1024,128]{1,0:T(8,128)(2,1)S(1)} %add_halves.5), channel_id=1, source_target_pairs={{0,1},{1,0},{2,3},{3,2},{4,5},{5,4},{6,7},{7,6},{8,9},{9,8},{10,11... | collective-permute-start | bytes 786440 | tf_op jit(solution)/shard_map/ppermute | solution.py:473
  55.5 3.4 %copy-start.2 = (bf16[2048,2048]{1,0:T(8,128)(2,1)S(1)}, bf16[2048,2048]{1,0:T(8,128)(2,1)}, u32[]{:S(2)}) copy-start(bf16[2048,2048]{1,0:T(8,128)(2,1)} %copy-done.1) | copy-start | bytes 25165828
  58.9 8.4 %copy-start.4 = (bf16[2048,2048]{1,0:T(8,128)(2,1)S(1)}, bf16[2048,2048]{1,0:T(8,128)(2,1)}, u32[]{:S(2)}) copy-start(bf16[2048,2048]{1,0:T(8,128)(2,1)} %copy-done.3) | copy-start | bytes 25165828
  64.2 11.0 %collective-permute-start.11 = (bf16[2048,128]{1,0:T(8,128)(2,1)S(1)}, bf16[2048,128]{1,0:T(8,128)(2,1)S(1)}, u32[]{:S(2)}, u32[]{:S(2)}) collective-permute-start(bf16[2048,128]{1,0:T(8,128)(2,1)S(1)} %get-tuple-element.72), channel_id=1, source_target_pairs={{0,1},{1,0},{2,3},{3,2},{4,5},{5,4},{6,7},{7,6},{8,9},{9,8},{10,11... | collective-permute-start | bytes 1572872 | tf_op jit(solution)/shard_map/ppermute | solution.py:473
  65.8 12.9 %collective-permute-start.12 = (bf16[2048,128]{1,0:T(8,128)(2,1)S(1)}, bf16[2048,128]{1,0:T(8,128)(2,1)S(1)}, u32[]{:S(2)}, u32[]{:S(2)}) collective-permute-start(bf16[2048,128]{1,0:T(8,128)(2,1)S(1)} %get-tuple-element.73), channel_id=1, source_target_pairs={{0,2},{1,3},{2,0},{3,1},{4,6},{5,7},{6,4},{7,5},{8,10},{9,11},{10,... | collective-permute-start | bytes 1572872 | tf_op jit(solution)/shard_map/ppermute | solution.py:473
  75.3 6.8 %collective-permute-start.13 = (bf16[1024,128]{1,0:T(8,128)(2,1)S(1)}, bf16[1024,128]{1,0:T(8,128)(2,1)S(1)}, u32[]{:S(2)}, u32[]{:S(2)}) collective-permute-start(bf16[1024,128]{1,0:T(8,128)(2,1)S(1)} %add_halves.6), channel_id=1, source_target_pairs={{0,2},{1,3},{2,0},{3,1},{4,6},{5,7},{6,4},{7,5},{8,10},{9,11},{10,... | collective-permute-start | bytes 786440 | tf_op jit(solution)/shard_map/ppermute | solution.py:473
  78.7 6.4 %collective-permute-start.14 = (bf16[1024,128]{1,0:T(8,128)(2,1)S(1)}, bf16[1024,128]{1,0:T(8,128)(2,1)S(1)}, u32[]{:S(2)}, u32[]{:S(2)}) collective-permute-start(bf16[1024,128]{1,0:T(8,128)(2,1)S(1)} %add_halves.7), channel_id=1, source_target_pairs={{0,1},{1,0},{2,3},{3,2},{4,5},{5,4},{6,7},{7,6},{8,9},{9,8},{10,11... | collective-permute-start | bytes 786440 | tf_op jit(solution)/shard_map/ppermute | solution.py:473

commit v4 on v3

--- a/solution.py
+++ b/solution.py
@@ -137,32 +137,41 @@
     return pl.ds(pl.multiple_of(start, size), size)
 
 
-def _join_keys_values_kernel(keys_ref, values_ref, out_ref):
+def _join_keys_values_kernel(keys_ref, values_ref, out_ref, sems):
     rows = keys_ref.shape[0]
-    out_ref[:rows] = keys_ref[...]
-    out_ref[rows:] = values_ref[...]
+    copies = [
+        pltpu.make_async_copy(keys_ref, out_ref.at[pl.ds(0, rows)], sems.at[0]),
+        pltpu.make_async_copy(values_ref, out_ref.at[pl.ds(rows, rows)], sems.at[1]),
+    ]
+    for copy in copies:
+        copy.start()
+    for copy in copies:
+        copy.wait()
 
 
 def _join_keys_values(keys, values):
     return pl.pallas_call(
         _join_keys_values_kernel,
         out_shape=jax.ShapeDtypeStruct((2 * keys.shape[0], keys.shape[1]), keys.dtype),
-        in_specs=[VMEM] * 2,
+        in_specs=[HBM] * 2,
         out_specs=VMEM,
+        scratch_shapes=[pltpu.SemaphoreType.DMA((2,))],
         compiler_params=pltpu.CompilerParams(vmem_limit_bytes=2 * 2**20),
         cost_estimate=pl.CostEstimate(flops=1, bytes_accessed=1, transcendentals=0),
         name="join_keys_values",
     )(keys, values)
 
 
-def _queries_for_other_core_kernel(meta_ref, queries_ref, out_ref, kept_ref):
+def _queries_for_other_core_kernel(meta_ref, queries_ref, out_ref, kept_ref, sem):
+    copy = pltpu.make_async_copy(queries_ref, kept_ref, sem)
+    copy.start()
+    copy.wait()
     c = meta_ref[0]
     core = lax.rem(c, 2)
     rows = queries_ref.shape[0] // PIECES
     for j in range(PIECES // 2):
         piece = _find_piece(meta_ref, c, 2 * j + 1 - core)
-        out_ref[j * rows:(j + 1) * rows] = queries_ref[_rows(piece * rows, rows)]
-    kept_ref[...] = queries_ref[...]
+        out_ref[j * rows:(j + 1) * rows] = kept_ref[_rows(piece * rows, rows)]
 
 
 def _queries_for_other_core(meta, queries):
@@ -172,8 +181,9 @@
             jax.ShapeDtypeStruct((queries.shape[0] // 2, queries.shape[1]), queries.dtype),
             jax.ShapeDtypeStruct(queries.shape, queries.dtype),
         ],
-        in_specs=[SMEM, VMEM],
+        in_specs=[SMEM, HBM],
         out_specs=[VMEM] * 2,
+        scratch_shapes=[pltpu.SemaphoreType.DMA],
         compiler_params=pltpu.CompilerParams(vmem_limit_bytes=2 * 2**20),
         cost_estimate=pl.CostEstimate(flops=1, bytes_accessed=1, transcendentals=0),
         name="queries_for_other_core",
@@ -475,6 +485,8 @@
 
 def per_device_fast(queries, keys, values, out_weight, doc_lengths, owners):
     places = lax.axis_size("ctx")
+    queries, keys, values, out_weight = (
+        pltpu.with_memory_space_constraint(x, pltpu.HBM) for x in (queries, keys, values, out_weight))
     kv0 = _join_keys_values(keys, values)
     kv2 = lax.ppermute(kv0, "ctx", [(i, i + 2) for i in range(places - 2)])
     kv1 = _flip(kv0, "ctx", 1)
@@ -483,7 +495,7 @@
     ]).astype(jnp.int32)
     leaving, queries = _queries_for_other_core(meta, queries)
     other = _flip(leaving, "ctx", 1)
-    (w_x,) = _stage_weights(("x",), meta, out_weight, 36)
+    (w_x,) = _stage_weights(("x",), meta, out_weight, 8)
     kv2, w_x = lax.optimization_barrier((kv2, w_x))
     kv = (kv0, kv1, kv2, _flip(kv2, "ctx", 1))
     near1, far3, w_y = _attend_groups((1, 3), ("y",), meta, queries, other, kv, out_weight)

time: 87.3 us -> 78.7 us (0.901)
  local copies, waits for them, and re-layouts: 17 us -> 0 us
  Pallas kernels: 34.9 us -> 40 us
  waiting for transfers between devices: 14 us -> 16.1 us
  starting transfers between devices: 20.1 us -> 21.6 us
    unnamed x16 -> x0, local copies, waits for them, and re-layouts: 17 us -> none
    pallas_call x2, Pallas kernels: 5.33 us -> 8.06 us  [_stage_weights(): pl.pallas_call(functools.partial(_stage_kernel, names), out_shape=[_quart...]
    ppermute x14, waiting for transfers between devices: 14 us -> 16.1 us  [_flip(): return lax.ppermute(x, axis, [(i, i ^ bits) for i in range(n)])]
    ppermute x14, starting transfers between devices: 15.2 us -> 16.6 us  [_flip(): return lax.ppermute(x, axis, [(i, i ^ bits) for i in range(n)])]
    pallas_call x1, Pallas kernels: 0.64 us -> 1.81 us  [_queries_for_other_core(): pl.pallas_call(_queries_for_other_core_kernel, out_shape=[jax.ShapeDtypeS...]
    pallas_call x1, Pallas kernels: 0.02 us -> 0.98 us  [_join_keys_values(): pl.pallas_call(_join_keys_values_kernel, out_shape=jax.ShapeDtypeStruct((...]
  transfers between devices with their start and end apart: 15 -> 15, of which waited for: 7 -> 8; matrix products, arithmetic and copies ran while one was open for 1% -> 1% of each run, Pallas kernels for 33% -> 42%
where the time goes in v4:
time: 78.7 us; the launch traced here: 78.6 us
  Pallas kernels  40 us (51%)
  starting transfers between devices  21.6 us (27%)
  waiting for transfers between devices  16.1 us (20%)
    ppermute x14, starting transfers between devices, _flip(): return lax.ppermute(x, axis, [(i, i ^ bits) for i in range(n)])  16.6 us
    ppermute x14, waiting for transfers between devices, _flip(): return lax.ppermute(x, axis, [(i, i ^ bits) for i in range(n)])  16.1 us
    pallas_call x2, Pallas kernels, _leaving_rows(): pl.pallas_call(_leaving_rows_kernel, out_shape=[part, part, jax.ShapeDtyp...  10.5 us
    pallas_call x2, Pallas kernels, _attend_groups(): pl.pallas_call(functools.partial(_attend_kernel, groups, names), out_shap...  8.34 us
    pallas_call x2, Pallas kernels, _stage_weights(): pl.pallas_call(functools.partial(_stage_kernel, names), out_shape=[_quart...  8.06 us
    pallas_call x2, Pallas kernels, _pass_rows(): pl.pallas_call(_pass_rows_kernel, out_shape=jax.ShapeDtypeStruct((weight....  5.04 us
    ppermute x1, starting transfers between devices, per_device_fast(): kv2 = lax.ppermute(kv0, 'ctx', [(i, i + 2) for i in range(places - 2)])  4.94 us
    pallas_call x2, Pallas kernels, _finish(): pl.pallas_call(_finish_kernel if near is None else _finish_both_kernel, o...  2.59 us
  transfers between devices with their start and end apart: 15, of which 8 were waited for; matrix products, arithmetic and copies ran while one was open for 1% of the time, Pallas kernels for 42%

profile of v4, /device:TPU:0, one launch (start us, length us, event | category | flops | bytes accessed | tf_op | source)
XLA Modules:
  0.0 78.6 jit_solution(1632430045842590892)
XLA Ops:
  0.0 1.0 %join_keys_values.1.kv0_ref = bf16[512,256]{1,0:T(8,128)(2,1)S(1)} custom-call(bf16[256,256]{1,0:T(8,128)(2,1)} %keys_ref.1, bf16[256,256]{1,0:T(8,128)(2,1)} %values_ref.1), custom_call_target="tpu_custom_call" | custom-call | flops 1 | bytes 1 | tf_op jit(solution)/shard_map/join_keys_values/pallas_call | solution.py:153
  1.0 4.9 %collective-permute-start.2 = (bf16[512,256]{1,0:T(8,128)(2,1)S(1)}, bf16[512,256]{1,0:T(8,128)(2,1)S(1)}, u32[]{:S(2)}, u32[]{:S(2)}) collective-permute-start(bf16[512,256]{1,0:T(8,128)(2,1)S(1)} %join_keys_values.1.kv0_ref), channel_id=1, source_target_pairs={{0,8},{4,12},{8,16},{12,20},{16,24},{20,28},{1,9},{5,13},{9,17},{1... | collective-permute-start | bytes 786440 | tf_op jit(solution)/shard_map/ppermute | solution.py:491
  5.9 0.8 pad_add_fusion.meta_ref
  6.7 1.8 %queries_for_other_core.1 = (bf16[128,2048]{1,0:T(8,128)(2,1)S(1)}, bf16[256,2048]{1,0:T(8,128)(2,1)S(1)}) custom-call(s32[82]{0:T(128)S(1)} %pad_add_fusion.meta_ref, bf16[256,2048]{1,0:T(8,128)(2,1)} %queries_ref.1), custom_call_target="tpu_custom_call" | custom-call | flops 1 | bytes 1 | tf_op jit(solution)/shard_map/queries_for_other_core/pallas_call | solution.py:178
  8.5 0.1 collective-permute-start
  8.6 0.5 collective-permute-start.1
  9.1 4.0 %stage_weights.2.wx_ref = bf16[2048,2048]{1,0:T(8,128)(2,1)S(1)} custom-call(s32[82]{0:T(128)S(1)} %pad_add_fusion.meta_ref, bf16[8192,2048]{1,0:T(8,128)(2,1)} %w_ref.7), custom_call_target="tpu_custom_call" | custom-call | flops 1 | bytes 1 | tf_op jit(solution)/shard_map/stage_weights/pallas_call | solution.py:225
  13.1 0.0 collective-permute-done.2.kv2_ref
  13.1 0.1 collective-permute-start.3
  13.3 0.0 collective-permute-done.1.kv1_ref
  13.3 0.0 collective-permute-done.other_ref
  13.3 1.5 %collective-permute-done.3.kv3_ref = bf16[512,256]{1,0:T(8,128)(2,1)S(1)} collective-permute-done((bf16[512,256]{1,0:T(8,128)(2,1)S(1)}, bf16[512,256]{1,0:T(8,128)(2,1)S(1)}, u32[]{:S(2)}, u32[]{:S(2)}) %collective-permute-start.3) | collective-permute-done | bytes 262176 | tf_op jit(solution)/shard_map/ppermute | solution.py:483
  14.7 4.2 %attend_groups.3 = (bf16[64,2048]{1,0:T(8,128)(2,1)S(1)}, bf16[64,2048]{1,0:T(8,128)(2,1)S(1)}, bf16[2048,2048]{1,0:T(8,128)(2,1)S(1)}) custom-call(s32[82]{0:T(128)S(1)} %pad_add_fusion.meta_ref, bf16[256,2048]{1,0:T(8,128)(2,1)S(1)} %get-tuple-element.40.queries_ref, bf16[128,2048]{1,0:T(8,128)(2,1)S(1)} %collective-permute-done.other_ref, ...), custom_call_target="tpu_custom_call" | custom-call | flops 1 | bytes 1 | tf_op jit(solution)/shard_map/attend_groups/pallas_call | solution.py:338
  18.9 1.6 %collective-permute-start.4 = (bf16[64,2048]{1,0:T(8,128)(2,1)S(1)}, bf16[64,2048]{1,0:T(8,128)(2,1)S(1)}, u32[]{:S(2)}, u32[]{:S(2)}) collective-permute-start(bf16[64,2048]{1,0:T(8,128)(2,1)S(1)} %get-tuple-element.44), channel_id=1, source_target_pairs={{0,8},{4,12},{8,0},{12,4},{16,24},{20,28},{24,16},{28,20},{1,9},{5... | collective-permute-start | bytes 786440 | tf_op jit(solution)/shard_map/ppermute | solution.py:483
  20.6 2.5 %collective-permute-start.5 = (bf16[64,2048]{1,0:T(8,128)(2,1)S(1)}, bf16[64,2048]{1,0:T(8,128)(2,1)S(1)}, u32[]{:S(2)}, u32[]{:S(2)}) collective-permute-start(bf16[64,2048]{1,0:T(8,128)(2,1)S(1)} %get-tuple-element.54), channel_id=1, source_target_pairs={{0,24},{4,28},{8,16},{12,20},{16,8},{20,12},{24,0},{28,4},{1,25},{... | collective-permute-start | bytes 786440 | tf_op jit(solution)/shard_map/ppermute | solution.py:483
  23.0 4.2 %attend_groups.2 = (bf16[64,2048]{1,0:T(8,128)(2,1)S(1)}, bf16[64,2048]{1,0:T(8,128)(2,1)S(1)}, bf16[2048,2048]{1,0:T(8,128)(2,1)S(1)}) custom-call(s32[82]{0:T(128)S(1)} %pad_add_fusion.meta_ref, bf16[256,2048]{1,0:T(8,128)(2,1)S(1)} %get-tuple-element.40.queries_ref, bf16[128,2048]{1,0:T(8,128)(2,1)S(1)} %collective-permute-done.other_ref, ...), custom_call_target="tpu_custom_call" | custom-call | flops 1 | bytes 1 | tf_op jit(solution)/shard_map/attend_groups/pallas_call | solution.py:338
  27.2 0.1 collective-permute-done.4.b_ref
  27.3 5.3 %leaving_rows.2 = (bf16[2048,128]{1,0:T(8,128)(2,1)S(1)}, bf16[2048,128]{1,0:T(8,128)(2,1)S(1)}, bf16[2048,128]{1,0:T(8,128)(2,1)S(1)}) custom-call(s32[82]{0:T(128)S(1)} %pad_add_fusion.meta_ref, bf16[64,2048]{1,0:T(8,128)(2,1)S(1)} %get-tuple-element.43.a_ref, bf16[64,2048]{1,0:T(8,128)(2,1)S(1)} %collective-permute-done.4.b_ref, ...), custom_call_target="tpu_custom_call" | custom-call | flops 1 | bytes 1 | tf_op jit(solution)/shard_map/leaving_rows/pallas_call | solution.py:387
  32.6 2.4 %collective-permute-done.5.b_ref = bf16[64,2048]{1,0:T(8,128)(2,1)S(1)} collective-permute-done((bf16[64,2048]{1,0:T(8,128)(2,1)S(1)}, bf16[64,2048]{1,0:T(8,128)(2,1)S(1)}, u32[]{:S(2)}, u32[]{:S(2)}) %collective-permute-start.5) | collective-permute-done | bytes 262176 | tf_op jit(solution)/shard_map/ppermute | solution.py:483
  35.0 1.5 %collective-permute-start.7 = (bf16[2048,128]{1,0:T(8,128)(2,1)S(1)}, bf16[2048,128]{1,0:T(8,128)(2,1)S(1)}, u32[]{:S(2)}, u32[]{:S(2)}) collective-permute-start(bf16[2048,128]{1,0:T(8,128)(2,1)S(1)} %get-tuple-element.56), channel_id=1, source_target_pairs={{0,2},{1,3},{2,0},{3,1},{4,6},{5,7},{6,4},{7,5},{8,10},{9,11},{10,... | collective-permute-start | bytes 1572872 | tf_op jit(solution)/shard_map/ppermute | solution.py:483
  36.5 1.5 %collective-permute-start.6 = (bf16[2048,128]{1,0:T(8,128)(2,1)S(1)}, bf16[2048,128]{1,0:T(8,128)(2,1)S(1)}, u32[]{:S(2)}, u32[]{:S(2)}) collective-permute-start(bf16[2048,128]{1,0:T(8,128)(2,1)S(1)} %get-tuple-element.55), channel_id=1, source_target_pairs={{0,1},{1,0},{2,3},{3,2},{4,5},{5,4},{6,7},{7,6},{8,9},{9,8},{10,11... | collective-permute-start | bytes 1572872 | tf_op jit(solution)/shard_map/ppermute | solution.py:483
  38.0 1.1 %collective-permute-start.8 = (bf16[64,2048]{1,0:T(8,128)(2,1)S(1)}, bf16[64,2048]{1,0:T(8,128)(2,1)S(1)}, u32[]{:S(2)}, u32[]{:S(2)}) collective-permute-start(bf16[64,2048]{1,0:T(8,128)(2,1)S(1)} %get-tuple-element.58), channel_id=1, source_target_pairs={{0,16},{4,20},{8,24},{12,28},{16,0},{20,4},{24,8},{28,12},{1,17},{... | collective-permute-start | bytes 786440 | tf_op jit(solution)/shard_map/ppermute | solution.py:483
  39.1 2.4 %pass_rows.2.a_ref = bf16[2048,128]{1,0:T(8,128)(2,1)S(1)} custom-call(bf16[2048,128]{1,0:T(8,128)(2,1)S(1)} %get-tuple-element.47.joined_ref.near_ref, bf16[2048,2048]{1,0:T(8,128)(2,1)S(1)} %get-tuple-element.48.w_ref), custom_call_target="tpu_custom_call" | custom-call | flops 1 | bytes 1 | tf_op jit(solution)/shard_map/pass_rows/pallas_call | solution.py:400
  41.5 4.0 %stage_weights.3.w_ref = bf16[2048,2048]{1,0:T(8,128)(2,1)S(1)} custom-call(s32[82]{0:T(128)S(1)} %pad_add_fusion.meta_ref, bf16[8192,2048]{1,0:T(8,128)(2,1)} %w_ref.7), custom_call_target="tpu_custom_call" | custom-call | flops 1 | bytes 1 | tf_op jit(solution)/shard_map/stage_weights/pallas_call | solution.py:225
  45.5 2.6 %collective-permute-done.7.b_ref.y1_ref = bf16[2048,128]{1,0:T(8,128)(2,1)S(1)} collective-permute-done((bf16[2048,128]{1,0:T(8,128)(2,1)S(1)}, bf16[2048,128]{1,0:T(8,128)(2,1)S(1)}, u32[]{:S(2)}, u32[]{:S(2)}) %collective-permute-start.7) | collective-permute-done | bytes 524320 | tf_op jit(solution)/shard_map/ppermute | solution.py:483
  48.1 0.1 add_halves.5
  48.2 1.2 %collective-permute-done.6.b_ref.x1_ref = bf16[2048,128]{1,0:T(8,128)(2,1)S(1)} collective-permute-done((bf16[2048,128]{1,0:T(8,128)(2,1)S(1)}, bf16[2048,128]{1,0:T(8,128)(2,1)S(1)}, u32[]{:S(2)}, u32[]{:S(2)}) %collective-permute-start.6) | collective-permute-done | bytes 524320 | tf_op jit(solution)/shard_map/ppermute | solution.py:483
  49.3 0.1 add_halves.4
  49.4 0.6 collective-permute-start.9
  50.0 1.5 %collective-permute-start.10 = (bf16[1024,128]{1,0:T(8,128)(2,1)S(1)}, bf16[1024,128]{1,0:T(8,128)(2,1)S(1)}, u32[]{:S(2)}, u32[]{:S(2)}) collective-permute-start(bf16[1024,128]{1,0:T(8,128)(2,1)S(1)} %add_halves.5), channel_id=1, source_target_pairs={{0,1},{1,0},{2,3},{3,2},{4,5},{5,4},{6,7},{7,6},{8,9},{9,8},{10,11... | collective-permute-start | bytes 786440 | tf_op jit(solution)/shard_map/ppermute | solution.py:483
  51.5 0.0 collective-permute-done.8.a_ref
  51.5 5.3 %leaving_rows.3 = (bf16[2048,128]{1,0:T(8,128)(2,1)S(1)}, bf16[2048,128]{1,0:T(8,128)(2,1)S(1)}, bf16[2048,128]{1,0:T(8,128)(2,1)S(1)}) custom-call(s32[82]{0:T(128)S(1)} %pad_add_fusion.meta_ref, bf16[64,2048]{1,0:T(8,128)(2,1)S(1)} %collective-permute-done.8.a_ref, bf16[64,2048]{1,0:T(8,128)(2,1)S(1)} %collective-permute-done.5.b_ref, ...), custom_call_target="tpu_custom_call" | custom-call | flops 1 | bytes 1 | tf_op jit(solution)/shard_map/leaving_rows/pallas_call | solution.py:387
  56.7 0.0 collective-permute-done.9.y2_ref
  56.7 0.0 collective-permute-done.10.x2_ref
  56.8 1.1 %collective-permute-start.11 = (bf16[2048,128]{1,0:T(8,128)(2,1)S(1)}, bf16[2048,128]{1,0:T(8,128)(2,1)S(1)}, u32[]{:S(2)}, u32[]{:S(2)}) collective-permute-start(bf16[2048,128]{1,0:T(8,128)(2,1)S(1)} %get-tuple-element.72), channel_id=1, source_target_pairs={{0,1},{1,0},{2,3},{3,2},{4,5},{5,4},{6,7},{7,6},{8,9},{9,8},{10,11... | collective-permute-start | bytes 1572872 | tf_op jit(solution)/shard_map/ppermute | solution.py:483
  57.8 1.7 %collective-permute-start.12 = (bf16[2048,128]{1,0:T(8,128)(2,1)S(1)}, bf16[2048,128]{1,0:T(8,128)(2,1)S(1)}, u32[]{:S(2)}, u32[]{:S(2)}) collective-permute-start(bf16[2048,128]{1,0:T(8,128)(2,1)S(1)} %get-tuple-element.73), channel_id=1, source_target_pairs={{0,2},{1,3},{2,0},{3,1},{4,6},{5,7},{6,4},{7,5},{8,10},{9,11},{10,... | collective-permute-start | bytes 1572872 | tf_op jit(solution)/shard_map/ppermute | solution.py:483
  59.5 2.6 %pass_rows.3.a_ref = bf16[2048,128]{1,0:T(8,128)(2,1)S(1)} custom-call(bf16[2048,128]{1,0:T(8,128)(2,1)S(1)} %get-tuple-element.60.joined_ref.far_ref, bf16[2048,2048]{1,0:T(8,128)(2,1)S(1)} %get-tuple-element.48.w_ref), custom_call_target="tpu_custom_call" | custom-call | flops 1 | bytes 1 | tf_op jit(solution)/shard_map/pass_rows/pallas_call | solution.py:400
  62.2 2.4 %keep_rows.1 = (bf16[2048,128]{1,0:T(8,128)(2,1)S(1)}, bf16[2048,128]{1,0:T(8,128)(2,1)S(1)}) custom-call(bf16[2048,128]{1,0:T(8,128)(2,1)S(1)} %get-tuple-element.47.joined_ref.near_ref, bf16[2048,128]{1,0:T(8,128)(2,1)S(1)} %get-tuple-element.60.joined_ref.far_ref, bf16[2048,2048]{1,0:T(8,128)(2,1)S(1)} %stage_weights.3.w_ref), custom_call_target="tpu_custom_call" | custom-call | flops 1 | bytes 1 | tf_op jit(solution)/shard_map/keep_rows/pallas_call | solution.py:413
  64.6 0.7 finish.2.near_ref
  65.3 4.0 %collective-permute-done.11.b_ref.x1_ref = bf16[2048,128]{1,0:T(8,128)(2,1)S(1)} collective-permute-done((bf16[2048,128]{1,0:T(8,128)(2,1)S(1)}, bf16[2048,128]{1,0:T(8,128)(2,1)S(1)}, u32[]{:S(2)}, u32[]{:S(2)}) %collective-permute-start.11) | collective-permute-done | bytes 524320 | tf_op jit(solution)/shard_map/ppermute | solution.py:483
  69.3 0.1 add_halves.6
  69.4 0.6 collective-permute-start.13
  70.0 0.0 collective-permute-done.12.b_ref.y1_ref
  70.0 0.1 add_halves.7
  70.0 2.3 %collective-permute-start.14 = (bf16[1024,128]{1,0:T(8,128)(2,1)S(1)}, bf16[1024,128]{1,0:T(8,128)(2,1)S(1)}, u32[]{:S(2)}, u32[]{:S(2)}) collective-permute-start(bf16[1024,128]{1,0:T(8,128)(2,1)S(1)} %add_halves.7), channel_id=1, source_target_pairs={{0,1},{1,0},{2,3},{3,2},{4,5},{5,4},{6,7},{7,6},{8,9},{9,8},{10,11... | collective-permute-start | bytes 786440 | tf_op jit(solution)/shard_map/ppermute | solution.py:483
  72.4 3.5 %collective-permute-done.13.y2_ref = bf16[1024,128]{1,0:T(8,128)(2,1)S(1)} collective-permute-done((bf16[1024,128]{1,0:T(8,128)(2,1)S(1)}, bf16[1024,128]{1,0:T(8,128)(2,1)S(1)}, u32[]{:S(2)}, u32[]{:S(2)}) %collective-permute-start.13) | collective-permute-done | bytes 262176 | tf_op jit(solution)/shard_map/ppermute | solution.py:483
  75.8 0.9 %collective-permute-done.14.x2_ref = bf16[1024,128]{1,0:T(8,128)(2,1)S(1)} collective-permute-done((bf16[1024,128]{1,0:T(8,128)(2,1)S(1)}, bf16[1024,128]{1,0:T(8,128)(2,1)S(1)}, u32[]{:S(2)}, u32[]{:S(2)}) %collective-permute-start.14) | collective-permute-done | bytes 262176 | tf_op jit(solution)/shard_map/ppermute | solution.py:483
  76.7 1.8 %finish.3 = bf16[2048,256]{1,0:T(8,128)(2,1)} custom-call(s32[82]{0:T(128)S(1)} %pad_add_fusion.meta_ref, bf16[2048,128]{1,0:T(8,128)(2,1)S(1)} %finish.2.near_ref, bf16[2048,128]{1,0:T(8,128)(2,1)S(1)} %get-tuple-element.71.keep_ref, bf16[2048,128]{1,0:T(8,128)(2,1)S(1)} %collective-permute-done.11.b_ref.x1_ref, ...), custom_call_target="tpu_custom_call" | custom-call | flops 1 | bytes 1 | tf_op jit(solution)/shard_map/finish/pallas_call | solution.py:470
Async XLA Ops:
  1.0 12.1 %collective-permute-start.2 = (bf16[512,256]{1,0:T(8,128)(2,1)S(1)}, bf16[512,256]{1,0:T(8,128)(2,1)S(1)}, u32[]{:S(2)}, u32[]{:S(2)}) collective-permute-start(bf16[512,256]{1,0:T(8,128)(2,1)S(1)} %join_keys_values.1.kv0_ref), channel_id=1, source_target_pairs={{0,8},{4,12},{8,16},{12,20},{16,24},{20,28},{1,9},{5,13},{9,17},{1... | collective-permute-start | bytes 786440 | tf_op jit(solution)/shard_map/ppermute | solution.py:491
  8.5 4.8 %collective-permute-start = (bf16[128,2048]{1,0:T(8,128)(2,1)S(1)}, bf16[128,2048]{1,0:T(8,128)(2,1)S(1)}, u32[]{:S(2)}, u32[]{:S(2)}) collective-permute-start(bf16[128,2048]{1,0:T(8,128)(2,1)S(1)} %get-tuple-element.41), channel_id=1, source_target_pairs={{0,4},{4,0},{8,12},{12,8},{16,20},{20,16},{24,28},{28,24},{1,5},{5... | collective-permute-start | bytes 1572872 | tf_op jit(solution)/shard_map/ppermute | solution.py:483
  8.6 4.7 %collective-permute-start.1 = (bf16[512,256]{1,0:T(8,128)(2,1)S(1)}, bf16[512,256]{1,0:T(8,128)(2,1)S(1)}, u32[]{:S(2)}, u32[]{:S(2)}) collective-permute-start(bf16[512,256]{1,0:T(8,128)(2,1)S(1)} %join_keys_values.1.kv0_ref), channel_id=1, source_target_pairs={{0,4},{4,0},{8,12},{12,8},{16,20},{20,16},{24,28},{28,24},{1,5},{5... | collective-permute-start | bytes 786440 | tf_op jit(solution)/shard_map/ppermute | solution.py:483
  13.1 1.6 %collective-permute-start.3 = (bf16[512,256]{1,0:T(8,128)(2,1)S(1)}, bf16[512,256]{1,0:T(8,128)(2,1)S(1)}, u32[]{:S(2)}, u32[]{:S(2)}) collective-permute-start(bf16[512,256]{1,0:T(8,128)(2,1)S(1)} %collective-permute-done.2.kv2_ref), channel_id=1, source_target_pairs={{0,4},{4,0},{8,12},{12,8},{16,20},{20,16},{24,28},{28,24},{1,5},{5... | collective-permute-start | bytes 786440 | tf_op jit(solution)/shard_map/ppermute | solution.py:483
  18.9 8.4 %collective-permute-start.4 = (bf16[64,2048]{1,0:T(8,128)(2,1)S(1)}, bf16[64,2048]{1,0:T(8,128)(2,1)S(1)}, u32[]{:S(2)}, u32[]{:S(2)}) collective-permute-start(bf16[64,2048]{1,0:T(8,128)(2,1)S(1)} %get-tuple-element.44), channel_id=1, source_target_pairs={{0,8},{4,12},{8,0},{12,4},{16,24},{20,28},{24,16},{28,20},{1,9},{5... | collective-permute-start | bytes 786440 | tf_op jit(solution)/shard_map/ppermute | solution.py:483
  20.6 14.4 %collective-permute-start.5 = (bf16[64,2048]{1,0:T(8,128)(2,1)S(1)}, bf16[64,2048]{1,0:T(8,128)(2,1)S(1)}, u32[]{:S(2)}, u32[]{:S(2)}) collective-permute-start(bf16[64,2048]{1,0:T(8,128)(2,1)S(1)} %get-tuple-element.54), channel_id=1, source_target_pairs={{0,24},{4,28},{8,16},{12,20},{16,8},{20,12},{24,0},{28,4},{1,25},{... | collective-permute-start | bytes 786440 | tf_op jit(solution)/shard_map/ppermute | solution.py:483
  35.0 13.1 %collective-permute-start.7 = (bf16[2048,128]{1,0:T(8,128)(2,1)S(1)}, bf16[2048,128]{1,0:T(8,128)(2,1)S(1)}, u32[]{:S(2)}, u32[]{:S(2)}) collective-permute-start(bf16[2048,128]{1,0:T(8,128)(2,1)S(1)} %get-tuple-element.56), channel_id=1, source_target_pairs={{0,2},{1,3},{2,0},{3,1},{4,6},{5,7},{6,4},{7,5},{8,10},{9,11},{10,... | collective-permute-start | bytes 1572872 | tf_op jit(solution)/shard_map/ppermute | solution.py:483
  36.5 12.9 %collective-permute-start.6 = (bf16[2048,128]{1,0:T(8,128)(2,1)S(1)}, bf16[2048,128]{1,0:T(8,128)(2,1)S(1)}, u32[]{:S(2)}, u32[]{:S(2)}) collective-permute-start(bf16[2048,128]{1,0:T(8,128)(2,1)S(1)} %get-tuple-element.55), channel_id=1, source_target_pairs={{0,1},{1,0},{2,3},{3,2},{4,5},{5,4},{6,7},{7,6},{8,9},{9,8},{10,11... | collective-permute-start | bytes 1572872 | tf_op jit(solution)/shard_map/ppermute | solution.py:483
  38.0 13.5 %collective-permute-start.8 = (bf16[64,2048]{1,0:T(8,128)(2,1)S(1)}, bf16[64,2048]{1,0:T(8,128)(2,1)S(1)}, u32[]{:S(2)}, u32[]{:S(2)}) collective-permute-start(bf16[64,2048]{1,0:T(8,128)(2,1)S(1)} %get-tuple-element.58), channel_id=1, source_target_pairs={{0,16},{4,20},{8,24},{12,28},{16,0},{20,4},{24,8},{28,12},{1,17},{... | collective-permute-start | bytes 786440 | tf_op jit(solution)/shard_map/ppermute | solution.py:483
  49.4 7.3 %collective-permute-start.9 = (bf16[1024,128]{1,0:T(8,128)(2,1)S(1)}, bf16[1024,128]{1,0:T(8,128)(2,1)S(1)}, u32[]{:S(2)}, u32[]{:S(2)}) collective-permute-start(bf16[1024,128]{1,0:T(8,128)(2,1)S(1)} %add_halves.4), channel_id=1, source_target_pairs={{0,2},{1,3},{2,0},{3,1},{4,6},{5,7},{6,4},{7,5},{8,10},{9,11},{10,... | collective-permute-start | bytes 786440 | tf_op jit(solution)/shard_map/ppermute | solution.py:483
  50.0 6.8 %collective-permute-start.10 = (bf16[1024,128]{1,0:T(8,128)(2,1)S(1)}, bf16[1024,128]{1,0:T(8,128)(2,1)S(1)}, u32[]{:S(2)}, u32[]{:S(2)}) collective-permute-start(bf16[1024,128]{1,0:T(8,128)(2,1)S(1)} %add_halves.5), channel_id=1, source_target_pairs={{0,1},{1,0},{2,3},{3,2},{4,5},{5,4},{6,7},{7,6},{8,9},{9,8},{10,11... | collective-permute-start | bytes 786440 | tf_op jit(solution)/shard_map/ppermute | solution.py:483
  56.8 12.6 %collective-permute-start.11 = (bf16[2048,128]{1,0:T(8,128)(2,1)S(1)}, bf16[2048,128]{1,0:T(8,128)(2,1)S(1)}, u32[]{:S(2)}, u32[]{:S(2)}) collective-permute-start(bf16[2048,128]{1,0:T(8,128)(2,1)S(1)} %get-tuple-element.72), channel_id=1, source_target_pairs={{0,1},{1,0},{2,3},{3,2},{4,5},{5,4},{6,7},{7,6},{8,9},{9,8},{10,11... | collective-permute-start | bytes 1572872 | tf_op jit(solution)/shard_map/ppermute | solution.py:483
  57.8 12.1 %collective-permute-start.12 = (bf16[2048,128]{1,0:T(8,128)(2,1)S(1)}, bf16[2048,128]{1,0:T(8,128)(2,1)S(1)}, u32[]{:S(2)}, u32[]{:S(2)}) collective-permute-start(bf16[2048,128]{1,0:T(8,128)(2,1)S(1)} %get-tuple-element.73), channel_id=1, source_target_pairs={{0,2},{1,3},{2,0},{3,1},{4,6},{5,7},{6,4},{7,5},{8,10},{9,11},{10,... | collective-permute-start | bytes 1572872 | tf_op jit(solution)/shard_map/ppermute | solution.py:483
  69.4 6.4 %collective-permute-start.13 = (bf16[1024,128]{1,0:T(8,128)(2,1)S(1)}, bf16[1024,128]{1,0:T(8,128)(2,1)S(1)}, u32[]{:S(2)}, u32[]{:S(2)}) collective-permute-start(bf16[1024,128]{1,0:T(8,128)(2,1)S(1)} %add_halves.6), channel_id=1, source_target_pairs={{0,2},{1,3},{2,0},{3,1},{4,6},{5,7},{6,4},{7,5},{8,10},{9,11},{10,... | collective-permute-start | bytes 786440 | tf_op jit(solution)/shard_map/ppermute | solution.py:483
  70.0 6.7 %collective-permute-start.14 = (bf16[1024,128]{1,0:T(8,128)(2,1)S(1)}, bf16[1024,128]{1,0:T(8,128)(2,1)S(1)}, u32[]{:S(2)}, u32[]{:S(2)}) collective-permute-start(bf16[1024,128]{1,0:T(8,128)(2,1)S(1)} %add_halves.7), channel_id=1, source_target_pairs={{0,1},{1,0},{2,3},{3,2},{4,5},{5,4},{6,7},{7,6},{8,9},{9,8},{10,11... | collective-permute-start | bytes 786440 | tf_op jit(solution)/shard_map/ppermute | solution.py:483

commit v5 on v4

--- a/solution.py
+++ b/solution.py
@@ -446,33 +446,45 @@
     f32 = jnp.float32
     first = keep_ref[:half].astype(f32) + x1_ref[:half].astype(f32) + y2_ref[...].astype(f32)
     second = keep_ref[half:].astype(f32) + y1_ref[:half].astype(f32) + x2_ref[...].astype(f32)
-    return first.astype(jnp.bfloat16), second.astype(jnp.bfloat16)
-
-
-def _finish_kernel(meta_ref, keep_ref, x1_ref, y1_ref, y2_ref, x2_ref, out_ref):
-    half = y2_ref.shape[0]
-    out_ref[:half], out_ref[half:] = _sum_parts(keep_ref, x1_ref, y1_ref, y2_ref, x2_ref)
-
-
-def _finish_both_kernel(meta_ref, near_ref, keep_ref, x1_ref, y1_ref, y2_ref, x2_ref, out_ref):
+    return first, second
+
+
+def _own_half(meta_ref, rows, tokens):
+    lane = lax.broadcasted_iota(jnp.int32, (rows, tokens), 1)
+    return lax.div(lane, tokens // 2) == lax.rem(lax.div(meta_ref[0], 2), 2)
+
+
+def _finish_first_kernel(meta_ref, keep_ref, x1_ref, y1_ref, y2_ref, x2_ref, out_ref, away_ref):
+    half, tokens = y2_ref.shape
+    top, bottom = _sum_parts(keep_ref, x1_ref, y1_ref, y2_ref, x2_ref)
+    out_ref[:half] = top.astype(out_ref.dtype)
+    out_ref[half:] = bottom.astype(out_ref.dtype)
+    own = _own_half(meta_ref, half, tokens)
+    away_ref[...] = jnp.where(own, pltpu.roll(bottom, tokens // 2, 1), top).astype(away_ref.dtype)
+
+
+def _finish_second_kernel(meta_ref, first_ref, away_ref, keep_ref, x1_ref, y1_ref, y2_ref, x2_ref, out_ref):
     half, tokens = y2_ref.shape
     upper = lax.div(meta_ref[0], 4)
-    first, second = _sum_parts(keep_ref, x1_ref, y1_ref, y2_ref, x2_ref)
-    at = _rows((1 - upper) * tokens, tokens)
-    out_ref[:half, at] = first
-    out_ref[half:, at] = second
-    out_ref[:, _rows(upper * tokens, tokens)] = near_ref[...]
-
-
-def _finish(meta, keep, x1, y1, y2, x2, near=None):
-    rows, tokens = keep.shape
-    operands = [meta] + ([] if near is None else [near]) + [keep, x1, y1, y2, x2]
-    return pl.pallas_call(
-        _finish_kernel if near is None else _finish_both_kernel,
-        out_shape=jax.ShapeDtypeStruct((rows, tokens if near is None else 2 * tokens), jnp.bfloat16),
+    own = _own_half(meta_ref, half, tokens)
+    mine, others = _rows(upper * tokens, tokens), _rows((1 - upper) * tokens, tokens)
+    away = away_ref[...].astype(jnp.float32)
+    sums = _sum_parts(keep_ref, x1_ref, y1_ref, y2_ref, x2_ref)
+    arrived = (pltpu.roll(away, tokens // 2, 1), away)
+    for i in range(2):
+        at = pl.ds(i * half, half)
+        first = first_ref[at].astype(jnp.float32)
+        out_ref[at, mine] = jnp.where(own, first, pltpu.roll(sums[i], tokens // 2, 1)).astype(out_ref.dtype)
+        out_ref[at, others] = jnp.where(own, arrived[i], sums[i]).astype(out_ref.dtype)
+
+
+def _finish(kernel, out_shape, operands):
+    return pl.pallas_call(
+        kernel,
+        out_shape=out_shape,
         in_specs=[SMEM] + [VMEM] * (len(operands) - 1),
-        out_specs=VMEM,
-        compiler_params=pltpu.CompilerParams(vmem_limit_bytes=4 * 2**20),
+        out_specs=jax.tree.map(lambda _: VMEM, out_shape),
+        compiler_params=pltpu.CompilerParams(vmem_limit_bytes=8 * 2**20),
         cost_estimate=pl.CostEstimate(flops=1, bytes_accessed=1, transcendentals=0),
         name="finish",
     )(*operands)
@@ -498,32 +510,36 @@
     (w_x,) = _stage_weights(("x",), meta, out_weight, 8)
     kv2, w_x = lax.optimization_barrier((kv2, w_x))
     kv = (kv0, kv1, kv2, _flip(kv2, "ctx", 1))
-    near1, far3, w_y = _attend_groups((1, 3), ("y",), meta, queries, other, kv, out_weight)
-    near1, far3 = _flip(near1, "ctx", 2), _flip(far3, "ctx", 6)
-    far2, near0, w_pass = _attend_groups((2, 0), ("pass",), meta, queries, other, kv, out_weight)
-    far2 = _flip(far2, "ctx", 4)
-
-    xmsg, ymsg, near = _leaving_rows(meta, near0, near1, w_x, w_y)
-    xmsg, ymsg, far3 = lax.optimization_barrier((xmsg, ymsg, far3))
-    near_x1, near_y1 = _flip(xmsg, "head", 1), _flip(ymsg, "head", 2)
-    near_pass = _pass_rows(near, w_pass)
-    near_pass, keep_meta = lax.optimization_barrier((near_pass, meta))
+    ctx0, ctx2, ctx1, ctx3, w_y, w_pass = _attend_groups(
+        (0, 2, 1, 3), ("y", "pass"), meta, queries, other, kv, out_weight)
+    ctx1, ctx3 = _flip(ctx1, "ctx", 2), _flip(ctx3, "ctx", 6)
+
+    xmsg, ymsg, joined = _leaving_rows(meta, ctx0, ctx2, w_x, w_y)
+    x1, y1 = _flip(xmsg, "head", 1), _flip(ymsg, "head", 2)
+    pass_on = _pass_rows(joined, w_pass)
+    pass_on, keep_meta = lax.optimization_barrier((pass_on, meta))
     (w_keep,) = _stage_weights(("keep",), keep_meta, out_weight, 8)
-    near_pass, w_keep = lax.optimization_barrier((near_pass, w_keep))
-    ymsg, xmsg = _add_halves(near_pass, 0, near_x1, 1), _add_halves(near_pass, 1, near_y1, 1)
+    pass_on, w_keep = lax.optimization_barrier((pass_on, w_keep))
+    ymsg, xmsg = _add_halves(pass_on, 0, x1, 1), _add_halves(pass_on, 1, y1, 1)
     meta, ymsg, xmsg = lax.optimization_barrier((meta, ymsg, xmsg))
-    near_y2, near_x2 = _flip(ymsg, "head", 2), _flip(xmsg, "head", 1)
-
-    xmsg, ymsg, far = _leaving_rows(meta, far2, far3, w_x, w_y)
-    xmsg, ymsg, near_y2, near_x2 = lax.optimization_barrier((xmsg, ymsg, near_y2, near_x2))
-    far_x1, far_y1 = _flip(xmsg, "head", 1), _flip(ymsg, "head", 2)
-    far_pass = _pass_rows(far, w_pass)
-    near_keep, far_keep = _keep_rows(near, far, w_keep)
-    near = _finish(meta, near_keep, near_x1, near_y1, near_y2, near_x2)
-    far_pass, near, far_keep = lax.optimization_barrier((far_pass, near, far_keep))
-    far_y2 = _flip(_add_halves(far_pass, 0, far_x1, 1), "head", 2)
-    far_x2 = _flip(_add_halves(far_pass, 1, far_y1, 1), "head", 1)
-    return _finish(meta, far_keep, far_x1, far_y1, far_y2, far_x2, near)
+    y2, x2 = _flip(ymsg, "head", 2), _flip(xmsg, "head", 1)
+
+    xmsg, ymsg, joined2 = _leaving_rows(meta, ctx1, ctx3, w_x, w_y)
+    xmsg, ymsg, y2, x2 = lax.optimization_barrier((xmsg, ymsg, y2, x2))
+    next_x1, next_y1 = _flip(xmsg, "head", 1), _flip(ymsg, "head", 2)
+    keep, next_keep = _keep_rows(joined, joined2, w_keep)
+    rows, tokens = keep.shape
+    first, away = _finish(_finish_first_kernel, [
+        jax.ShapeDtypeStruct((rows, tokens), jnp.bfloat16),
+        jax.ShapeDtypeStruct((rows // 2, tokens), jnp.bfloat16),
+    ], (meta, keep, x1, y1, y2, x2))
+    joined2, away_sent = lax.optimization_barrier((joined2, away))
+    pass_on = _pass_rows(joined2, w_pass)
+    ymsg, xmsg = _add_halves(pass_on, 0, next_x1, 1), _add_halves(pass_on, 1, next_y1, 1)
+    away = _flip(away_sent, "ctx", 4)
+    y2, x2 = _flip(ymsg, "head", 2), _flip(xmsg, "head", 1)
+    return _finish(_finish_second_kernel, jax.ShapeDtypeStruct((rows, 2 * tokens), jnp.bfloat16),
+                   (meta, first, away, next_keep, next_x1, next_y1, y2, x2))
 
 
 def solution(mesh):

time: 78.7 us -> 72.4 us (0.920)
  waiting for transfers between devices: 16.1 us -> 10.9 us
  Pallas kernels: 40 us -> 38.3 us
    ppermute x14, waiting for transfers between devices: 16.1 us -> 10.9 us  [_flip(): return lax.ppermute(x, axis, [(i, i ^ bits) for i in range(n)])]
    pallas_call x2 -> x1, Pallas kernels: 8.34 us -> 6.54 us  [_attend_groups(): pl.pallas_call(functools.partial(_attend_kernel, groups, names), out_shap...]
  transfers between devices with their start and end apart: 15 -> 15, of which waited for: 8 -> 6; matrix products, arithmetic and copies ran while one was open for 1% -> 1% of each run, Pallas kernels for 42% -> 33%
where the time goes in v5:
time: 72.4 us; the launch traced here: 72.2 us
  Pallas kernels  38.3 us (53%)
  starting transfers between devices  22.1 us (31%)
  waiting for transfers between devices  10.9 us (15%)
  other arithmetic  0.75 us (1%)
    ppermute x14, starting transfers between devices, _flip(): return lax.ppermute(x, axis, [(i, i ^ bits) for i in range(n)])  17.1 us
    ppermute x14, waiting for transfers between devices, _flip(): return lax.ppermute(x, axis, [(i, i ^ bits) for i in range(n)])  10.9 us
    pallas_call x2, Pallas kernels, _leaving_rows(): pl.pallas_call(_leaving_rows_kernel, out_shape=[part, part, jax.ShapeDtyp...  10.5 us
    pallas_call x2, Pallas kernels, _stage_weights(): pl.pallas_call(functools.partial(_stage_kernel, names), out_shape=[_quart...  8.06 us
    pallas_call x1, Pallas kernels, _attend_groups(): pl.pallas_call(functools.partial(_attend_kernel, groups, names), out_shap...  6.54 us
    ppermute x1, starting transfers between devices, per_device_fast(): kv2 = lax.ppermute(kv0, 'ctx', [(i, i + 2) for i in range(places - 2)])  4.94 us
    pallas_call x2, Pallas kernels, _pass_rows(): pl.pallas_call(_pass_rows_kernel, out_shape=jax.ShapeDtypeStruct((weight....  4.81 us
    pallas_call x2, Pallas kernels, _finish(): pl.pallas_call(kernel, out_shape=out_shape, in_specs=[SMEM] + [VMEM] * (l...  2.79 us
  transfers between devices with their start and end apart: 15, of which 6 were waited for; matrix products, arithmetic and copies ran while one was open for 1% of the time, Pallas kernels for 33%

profile of v5, /device:TPU:0, one launch (start us, length us, event | category | flops | bytes accessed | tf_op | source)
XLA Modules:
  0.0 72.2 jit_solution(3416440308145930831)
XLA Ops:
  0.0 1.0 %join_keys_values.1.kv0_ref = bf16[512,256]{1,0:T(8,128)(2,1)S(1)} custom-call(bf16[256,256]{1,0:T(8,128)(2,1)} %keys_ref.1, bf16[256,256]{1,0:T(8,128)(2,1)} %values_ref.1), custom_call_target="tpu_custom_call" | custom-call | flops 1 | bytes 1 | tf_op jit(solution)/shard_map/join_keys_values/pallas_call | solution.py:153
  1.0 4.9 %collective-permute-start.2 = (bf16[512,256]{1,0:T(8,128)(2,1)S(1)}, bf16[512,256]{1,0:T(8,128)(2,1)S(1)}, u32[]{:S(2)}, u32[]{:S(2)}) collective-permute-start(bf16[512,256]{1,0:T(8,128)(2,1)S(1)} %join_keys_values.1.kv0_ref), channel_id=1, source_target_pairs={{0,8},{4,12},{8,16},{12,20},{16,24},{20,28},{1,9},{5,13},{9,17},{1... | collective-permute-start | bytes 786440 | tf_op jit(solution)/shard_map/ppermute | solution.py:503
  5.9 0.8 %pad_add_fusion.meta_ref = s32[82]{0:T(128)S(1)} fusion(s32[16]{0:T(128)} %param.10, s32[64]{0:T(128)} %bitcast.3, s32[1]{0:T(128)} %bitcast.1, s32[1]{0:T(128)} %bitcast), kind=kLoop, calls=%fused_computation | loop fusion | flops 246 | bytes 656 | tf_op jit(solution)/shard_map/concatenate | solution.py:505
  6.7 1.8 %queries_for_other_core.1 = (bf16[128,2048]{1,0:T(8,128)(2,1)S(1)}, bf16[256,2048]{1,0:T(8,128)(2,1)S(1)}) custom-call(s32[82]{0:T(128)S(1)} %pad_add_fusion.meta_ref, bf16[256,2048]{1,0:T(8,128)(2,1)} %queries_ref.1), custom_call_target="tpu_custom_call" | custom-call | flops 1 | bytes 1 | tf_op jit(solution)/shard_map/queries_for_other_core/pallas_call | solution.py:178
  8.5 0.1 collective-permute-start
  8.6 0.5 collective-permute-start.1
  9.1 4.0 %stage_weights.2.wx_ref = bf16[2048,2048]{1,0:T(8,128)(2,1)S(1)} custom-call(s32[82]{0:T(128)S(1)} %pad_add_fusion.meta_ref, bf16[8192,2048]{1,0:T(8,128)(2,1)} %w_ref.5), custom_call_target="tpu_custom_call" | custom-call | flops 1 | bytes 1 | tf_op jit(solution)/shard_map/stage_weights/pallas_call | solution.py:225
  13.1 0.0 collective-permute-done.2.kv2_ref
  13.1 0.1 collective-permute-start.3
  13.3 0.0 collective-permute-done.1.kv1_ref
  13.3 0.0 collective-permute-done.other_ref
  13.3 1.5 %collective-permute-done.3.kv3_ref = bf16[512,256]{1,0:T(8,128)(2,1)S(1)} collective-permute-done((bf16[512,256]{1,0:T(8,128)(2,1)S(1)}, bf16[512,256]{1,0:T(8,128)(2,1)S(1)}, u32[]{:S(2)}, u32[]{:S(2)}) %collective-permute-start.3) | collective-permute-done | bytes 262176 | tf_op jit(solution)/shard_map/ppermute | solution.py:495
  14.7 6.5 %attend_groups.1 = (bf16[64,2048]{1,0:T(8,128)(2,1)S(1)}, bf16[64,2048]{1,0:T(8,128)(2,1)S(1)}, bf16[64,2048]{1,0:T(8,128)(2,1)S(1)}, bf16[64,2048]{1,0:T(8,128)...) custom-call(s32[82]{0:T(128)S(1)} %pad_add_fusion.meta_ref, ...), custom_call_target="tpu_custom_call" | custom-call | flops 1 | bytes 1 | tf_op jit(solution)/shard_map/attend_groups/pallas_call | solution.py:338
  21.3 5.3 %leaving_rows.2 = (bf16[2048,128]{1,0:T(8,128)(2,1)S(1)}, bf16[2048,128]{1,0:T(8,128)(2,1)S(1)}, bf16[2048,128]{1,0:T(8,128)(2,1)S(1)}) custom-call(s32[82]{0:T(128)S(1)} %pad_add_fusion.meta_ref, bf16[64,2048]{1,0:T(8,128)(2,1)S(1)} %get-tuple-element.41.a_ref, bf16[64,2048]{1,0:T(8,128)(2,1)S(1)} %get-tuple-element.42.b_ref, ...), custom_call_target="tpu_custom_call" | custom-call | flops 1 | bytes 1 | tf_op jit(solution)/shard_map/leaving_rows/pallas_call | solution.py:387
  26.5 1.6 %collective-permute-start.5 = (bf16[2048,128]{1,0:T(8,128)(2,1)S(1)}, bf16[2048,128]{1,0:T(8,128)(2,1)S(1)}, u32[]{:S(2)}, u32[]{:S(2)}) collective-permute-start(bf16[2048,128]{1,0:T(8,128)(2,1)S(1)} %get-tuple-element.51), channel_id=1, source_target_pairs={{0,2},{1,3},{2,0},{3,1},{4,6},{5,7},{6,4},{7,5},{8,10},{9,11},{10,... | collective-permute-start | bytes 1572872 | tf_op jit(solution)/shard_map/ppermute | solution.py:495
  28.1 1.5 %collective-permute-start.4 = (bf16[2048,128]{1,0:T(8,128)(2,1)S(1)}, bf16[2048,128]{1,0:T(8,128)(2,1)S(1)}, u32[]{:S(2)}, u32[]{:S(2)}) collective-permute-start(bf16[2048,128]{1,0:T(8,128)(2,1)S(1)} %get-tuple-element.50), channel_id=1, source_target_pairs={{0,1},{1,0},{2,3},{3,2},{4,5},{5,4},{6,7},{7,6},{8,9},{9,8},{10,11... | collective-permute-start | bytes 1572872 | tf_op jit(solution)/shard_map/ppermute | solution.py:495
  29.6 1.6 %collective-permute-start.6 = (bf16[64,2048]{1,0:T(8,128)(2,1)S(1)}, bf16[64,2048]{1,0:T(8,128)(2,1)S(1)}, u32[]{:S(2)}, u32[]{:S(2)}) collective-permute-start(bf16[64,2048]{1,0:T(8,128)(2,1)S(1)} %get-tuple-element.53), channel_id=1, source_target_pairs={{0,8},{4,12},{8,0},{12,4},{16,24},{20,28},{24,16},{28,20},{1,9},{5... | collective-permute-start | bytes 786440 | tf_op jit(solution)/shard_map/ppermute | solution.py:495
  31.2 2.5 %collective-permute-start.7 = (bf16[64,2048]{1,0:T(8,128)(2,1)S(1)}, bf16[64,2048]{1,0:T(8,128)(2,1)S(1)}, u32[]{:S(2)}, u32[]{:S(2)}) collective-permute-start(bf16[64,2048]{1,0:T(8,128)(2,1)S(1)} %get-tuple-element.54), channel_id=1, source_target_pairs={{0,24},{4,28},{8,16},{12,20},{16,8},{20,12},{24,0},{28,4},{1,25},{... | collective-permute-start | bytes 786440 | tf_op jit(solution)/shard_map/ppermute | solution.py:495
  33.7 2.4 %pass_rows.2.a_ref = bf16[2048,128]{1,0:T(8,128)(2,1)S(1)} custom-call(bf16[2048,128]{1,0:T(8,128)(2,1)S(1)} %get-tuple-element.45.joined_ref.near_ref, bf16[2048,2048]{1,0:T(8,128)(2,1)S(1)} %get-tuple-element.46.w_ref), custom_call_target="tpu_custom_call" | custom-call | flops 1 | bytes 1 | tf_op jit(solution)/shard_map/pass_rows/pallas_call | solution.py:400
  36.1 4.0 %stage_weights.3.w_ref = bf16[2048,2048]{1,0:T(8,128)(2,1)S(1)} custom-call(s32[82]{0:T(128)S(1)} %pad_add_fusion.meta_ref, bf16[8192,2048]{1,0:T(8,128)(2,1)} %w_ref.5), custom_call_target="tpu_custom_call" | custom-call | flops 1 | bytes 1 | tf_op jit(solution)/shard_map/stage_weights/pallas_call | solution.py:225
  40.1 0.5 collective-permute-done.5.b_ref.y1_ref
  40.6 0.1 add_halves.5
  40.6 1.2 %collective-permute-done.4.b_ref.x1_ref = bf16[2048,128]{1,0:T(8,128)(2,1)S(1)} collective-permute-done((bf16[2048,128]{1,0:T(8,128)(2,1)S(1)}, bf16[2048,128]{1,0:T(8,128)(2,1)S(1)}, u32[]{:S(2)}, u32[]{:S(2)}) %collective-permute-start.4) | collective-permute-done | bytes 524320 | tf_op jit(solution)/shard_map/ppermute | solution.py:495
  41.8 0.1 add_halves.4
  41.9 0.6 collective-permute-start.8
  42.5 1.5 %collective-permute-start.9 = (bf16[1024,128]{1,0:T(8,128)(2,1)S(1)}, bf16[1024,128]{1,0:T(8,128)(2,1)S(1)}, u32[]{:S(2)}, u32[]{:S(2)}) collective-permute-start(bf16[1024,128]{1,0:T(8,128)(2,1)S(1)} %add_halves.5), channel_id=1, source_target_pairs={{0,1},{1,0},{2,3},{3,2},{4,5},{5,4},{6,7},{7,6},{8,9},{9,8},{10,11... | collective-permute-start | bytes 786440 | tf_op jit(solution)/shard_map/ppermute | solution.py:495
  43.9 0.0 collective-permute-done.6.a_ref
  44.0 1.1 %collective-permute-done.7.b_ref = bf16[64,2048]{1,0:T(8,128)(2,1)S(1)} collective-permute-done((bf16[64,2048]{1,0:T(8,128)(2,1)S(1)}, bf16[64,2048]{1,0:T(8,128)(2,1)S(1)}, u32[]{:S(2)}, u32[]{:S(2)}) %collective-permute-start.7) | collective-permute-done | bytes 262176 | tf_op jit(solution)/shard_map/ppermute | solution.py:495
  45.0 5.3 %leaving_rows.3 = (bf16[2048,128]{1,0:T(8,128)(2,1)S(1)}, bf16[2048,128]{1,0:T(8,128)(2,1)S(1)}, bf16[2048,128]{1,0:T(8,128)(2,1)S(1)}) custom-call(s32[82]{0:T(128)S(1)} %pad_add_fusion.meta_ref, bf16[64,2048]{1,0:T(8,128)(2,1)S(1)} %collective-permute-done.6.a_ref, bf16[64,2048]{1,0:T(8,128)(2,1)S(1)} %collective-permute-done.7.b_ref, ...), custom_call_target="tpu_custom_call" | custom-call | flops 1 | bytes 1 | tf_op jit(solution)/shard_map/leaving_rows/pallas_call | solution.py:387
  50.3 0.0 collective-permute-done.8.y2_ref
  50.3 0.0 collective-permute-done.9.x2_ref
  50.3 0.7 %collective-permute-start.11 = (bf16[2048,128]{1,0:T(8,128)(2,1)S(1)}, bf16[2048,128]{1,0:T(8,128)(2,1)S(1)}, u32[]{:S(2)}, u32[]{:S(2)}) collective-permute-start(bf16[2048,128]{1,0:T(8,128)(2,1)S(1)} %get-tuple-element.68), channel_id=1, source_target_pairs={{0,1},{1,0},{2,3},{3,2},{4,5},{5,4},{6,7},{7,6},{8,9},{9,8},{10,11... | collective-permute-start | bytes 1572872 | tf_op jit(solution)/shard_map/ppermute | solution.py:495
  51.0 1.3 %collective-permute-start.12 = (bf16[2048,128]{1,0:T(8,128)(2,1)S(1)}, bf16[2048,128]{1,0:T(8,128)(2,1)S(1)}, u32[]{:S(2)}, u32[]{:S(2)}) collective-permute-start(bf16[2048,128]{1,0:T(8,128)(2,1)S(1)} %get-tuple-element.69), channel_id=1, source_target_pairs={{0,2},{1,3},{2,0},{3,1},{4,6},{5,7},{6,4},{7,5},{8,10},{9,11},{10,... | collective-permute-start | bytes 1572872 | tf_op jit(solution)/shard_map/ppermute | solution.py:495
  52.4 2.6 %keep_rows.1 = (bf16[2048,128]{1,0:T(8,128)(2,1)S(1)}, bf16[2048,128]{1,0:T(8,128)(2,1)S(1)}) custom-call(bf16[2048,128]{1,0:T(8,128)(2,1)S(1)} %get-tuple-element.45.joined_ref.near_ref, bf16[2048,128]{1,0:T(8,128)(2,1)S(1)} %get-tuple-element.70.far_ref.joined_ref, bf16[2048,2048]{1,0:T(8,128)(2,1)S(1)} %stage_weights.3.w_ref), custom_call_target="tpu_custom_call" | custom-call | flops 1 | bytes 1 | tf_op jit(solution)/shard_map/keep_rows/pallas_call | solution.py:413
  55.0 0.8 %finish.2 = (bf16[2048,128]{1,0:T(8,128)(2,1)S(1)}, bf16[1024,128]{1,0:T(8,128)(2,1)S(1)}) custom-call(s32[82]{0:T(128)S(1)} %pad_add_fusion.meta_ref, bf16[2048,128]{1,0:T(8,128)(2,1)S(1)} %get-tuple-element.57.keep_ref, bf16[2048,128]{1,0:T(8,128)(2,1)S(1)} %collective-permute-done.4.b_ref.x1_ref, ...), custom_call_target="tpu_custom_call" | custom-call | flops 1 | bytes 1 | tf_op jit(solution)/shard_map/finish/pallas_call | solution.py:482
  55.8 2.4 %pass_rows.3.a_ref = bf16[2048,128]{1,0:T(8,128)(2,1)S(1)} custom-call(bf16[2048,128]{1,0:T(8,128)(2,1)S(1)} %get-tuple-element.70.far_ref.joined_ref, bf16[2048,2048]{1,0:T(8,128)(2,1)S(1)} %get-tuple-element.46.w_ref), custom_call_target="tpu_custom_call" | custom-call | flops 1 | bytes 1 | tf_op jit(solution)/shard_map/pass_rows/pallas_call | solution.py:400
  58.2 2.6 %collective-permute-start.10 = (bf16[1024,128]{1,0:T(8,128)(2,1)S(1)}, bf16[1024,128]{1,0:T(8,128)(2,1)S(1)}, u32[]{:S(2)}, u32[]{:S(2)}) collective-permute-start(bf16[1024,128]{1,0:T(8,128)(2,1)S(1)} %get-tuple-element.66), channel_id=1, source_target_pairs={{0,16},{4,20},{8,24},{12,28},{16,0},{20,4},{24,8},{28,12},{1,17},{... | collective-permute-start | bytes 786440 | tf_op jit(solution)/shard_map/ppermute | solution.py:495
  60.8 2.1 %collective-permute-done.11.b_ref.x1_ref = bf16[2048,128]{1,0:T(8,128)(2,1)S(1)} collective-permute-done((bf16[2048,128]{1,0:T(8,128)(2,1)S(1)}, bf16[2048,128]{1,0:T(8,128)(2,1)S(1)}, u32[]{:S(2)}, u32[]{:S(2)}) %collective-permute-start.11) | collective-permute-done | bytes 524320 | tf_op jit(solution)/shard_map/ppermute | solution.py:495
  62.9 0.1 add_halves.6
  62.9 0.6 collective-permute-start.13
  63.5 0.0 collective-permute-done.12.b_ref.y1_ref
  63.5 0.1 add_halves.7
  63.6 2.0 %collective-permute-start.14 = (bf16[1024,128]{1,0:T(8,128)(2,1)S(1)}, bf16[1024,128]{1,0:T(8,128)(2,1)S(1)}, u32[]{:S(2)}, u32[]{:S(2)}) collective-permute-start(bf16[1024,128]{1,0:T(8,128)(2,1)S(1)} %add_halves.7), channel_id=1, source_target_pairs={{0,1},{1,0},{2,3},{3,2},{4,5},{5,4},{6,7},{7,6},{8,9},{9,8},{10,11... | collective-permute-start | bytes 786440 | tf_op jit(solution)/shard_map/ppermute | solution.py:495
  65.5 4.6 %collective-permute-done.10.away_ref = bf16[1024,128]{1,0:T(8,128)(2,1)S(1)} collective-permute-done((bf16[1024,128]{1,0:T(8,128)(2,1)S(1)}, bf16[1024,128]{1,0:T(8,128)(2,1)S(1)}, u32[]{:S(2)}, u32[]{:S(2)}) %collective-permute-start.10) | collective-permute-done | bytes 262176 | tf_op jit(solution)/shard_map/ppermute | solution.py:495
  70.2 0.0 collective-permute-done.13.y2_ref
  70.2 0.0 collective-permute-done.14.x2_ref
  70.2 2.0 %finish.3 = bf16[2048,256]{1,0:T(8,128)(2,1)} custom-call(s32[82]{0:T(128)S(1)} %pad_add_fusion.meta_ref, bf16[2048,128]{1,0:T(8,128)(2,1)S(1)} %get-tuple-element.64.first_ref, bf16[1024,128]{1,0:T(8,128)(2,1)S(1)} %collective-permute-done.10.away_ref, bf16[2048,128]{1,0:T(8,128)(2,1)S(1)} %get-tuple-element.67.keep_ref, ...), custom_call_target="tpu_custom_call" | custom-call | flops 1 | bytes 1 | tf_op jit(solution)/shard_map/finish/pallas_call | solution.py:482
Async XLA Ops:
  1.0 12.1 %collective-permute-start.2 = (bf16[512,256]{1,0:T(8,128)(2,1)S(1)}, bf16[512,256]{1,0:T(8,128)(2,1)S(1)}, u32[]{:S(2)}, u32[]{:S(2)}) collective-permute-start(bf16[512,256]{1,0:T(8,128)(2,1)S(1)} %join_keys_values.1.kv0_ref), channel_id=1, source_target_pairs={{0,8},{4,12},{8,16},{12,20},{16,24},{20,28},{1,9},{5,13},{9,17},{1... | collective-permute-start | bytes 786440 | tf_op jit(solution)/shard_map/ppermute | solution.py:503
  8.5 4.8 %collective-permute-start = (bf16[128,2048]{1,0:T(8,128)(2,1)S(1)}, bf16[128,2048]{1,0:T(8,128)(2,1)S(1)}, u32[]{:S(2)}, u32[]{:S(2)}) collective-permute-start(bf16[128,2048]{1,0:T(8,128)(2,1)S(1)} %get-tuple-element.39), channel_id=1, source_target_pairs={{0,4},{4,0},{8,12},{12,8},{16,20},{20,16},{24,28},{28,24},{1,5},{5... | collective-permute-start | bytes 1572872 | tf_op jit(solution)/shard_map/ppermute | solution.py:495
  8.6 4.7 %collective-permute-start.1 = (bf16[512,256]{1,0:T(8,128)(2,1)S(1)}, bf16[512,256]{1,0:T(8,128)(2,1)S(1)}, u32[]{:S(2)}, u32[]{:S(2)}) collective-permute-start(bf16[512,256]{1,0:T(8,128)(2,1)S(1)} %join_keys_values.1.kv0_ref), channel_id=1, source_target_pairs={{0,4},{4,0},{8,12},{12,8},{16,20},{20,16},{24,28},{28,24},{1,5},{5... | collective-permute-start | bytes 786440 | tf_op jit(solution)/shard_map/ppermute | solution.py:495
  13.1 1.6 %collective-permute-start.3 = (bf16[512,256]{1,0:T(8,128)(2,1)S(1)}, bf16[512,256]{1,0:T(8,128)(2,1)S(1)}, u32[]{:S(2)}, u32[]{:S(2)}) collective-permute-start(bf16[512,256]{1,0:T(8,128)(2,1)S(1)} %collective-permute-done.2.kv2_ref), channel_id=1, source_target_pairs={{0,4},{4,0},{8,12},{12,8},{16,20},{20,16},{24,28},{28,24},{1,5},{5... | collective-permute-start | bytes 786440 | tf_op jit(solution)/shard_map/ppermute | solution.py:495
  26.5 14.0 %collective-permute-start.5 = (bf16[2048,128]{1,0:T(8,128)(2,1)S(1)}, bf16[2048,128]{1,0:T(8,128)(2,1)S(1)}, u32[]{:S(2)}, u32[]{:S(2)}) collective-permute-start(bf16[2048,128]{1,0:T(8,128)(2,1)S(1)} %get-tuple-element.51), channel_id=1, source_target_pairs={{0,2},{1,3},{2,0},{3,1},{4,6},{5,7},{6,4},{7,5},{8,10},{9,11},{10,... | collective-permute-start | bytes 1572872 | tf_op jit(solution)/shard_map/ppermute | solution.py:495
  28.1 13.7 %collective-permute-start.4 = (bf16[2048,128]{1,0:T(8,128)(2,1)S(1)}, bf16[2048,128]{1,0:T(8,128)(2,1)S(1)}, u32[]{:S(2)}, u32[]{:S(2)}) collective-permute-start(bf16[2048,128]{1,0:T(8,128)(2,1)S(1)} %get-tuple-element.50), channel_id=1, source_target_pairs={{0,1},{1,0},{2,3},{3,2},{4,5},{5,4},{6,7},{7,6},{8,9},{9,8},{10,11... | collective-permute-start | bytes 1572872 | tf_op jit(solution)/shard_map/ppermute | solution.py:495
  29.6 14.3 %collective-permute-start.6 = (bf16[64,2048]{1,0:T(8,128)(2,1)S(1)}, bf16[64,2048]{1,0:T(8,128)(2,1)S(1)}, u32[]{:S(2)}, u32[]{:S(2)}) collective-permute-start(bf16[64,2048]{1,0:T(8,128)(2,1)S(1)} %get-tuple-element.53), channel_id=1, source_target_pairs={{0,8},{4,12},{8,0},{12,4},{16,24},{20,28},{24,16},{28,20},{1,9},{5... | collective-permute-start | bytes 786440 | tf_op jit(solution)/shard_map/ppermute | solution.py:495
  31.2 13.8 %collective-permute-start.7 = (bf16[64,2048]{1,0:T(8,128)(2,1)S(1)}, bf16[64,2048]{1,0:T(8,128)(2,1)S(1)}, u32[]{:S(2)}, u32[]{:S(2)}) collective-permute-start(bf16[64,2048]{1,0:T(8,128)(2,1)S(1)} %get-tuple-element.54), channel_id=1, source_target_pairs={{0,24},{4,28},{8,16},{12,20},{16,8},{20,12},{24,0},{28,4},{1,25},{... | collective-permute-start | bytes 786440 | tf_op jit(solution)/shard_map/ppermute | solution.py:495
  41.9 8.4 %collective-permute-start.8 = (bf16[1024,128]{1,0:T(8,128)(2,1)S(1)}, bf16[1024,128]{1,0:T(8,128)(2,1)S(1)}, u32[]{:S(2)}, u32[]{:S(2)}) collective-permute-start(bf16[1024,128]{1,0:T(8,128)(2,1)S(1)} %add_halves.4), channel_id=1, source_target_pairs={{0,2},{1,3},{2,0},{3,1},{4,6},{5,7},{6,4},{7,5},{8,10},{9,11},{10,... | collective-permute-start | bytes 786440 | tf_op jit(solution)/shard_map/ppermute | solution.py:495
  42.5 7.9 %collective-permute-start.9 = (bf16[1024,128]{1,0:T(8,128)(2,1)S(1)}, bf16[1024,128]{1,0:T(8,128)(2,1)S(1)}, u32[]{:S(2)}, u32[]{:S(2)}) collective-permute-start(bf16[1024,128]{1,0:T(8,128)(2,1)S(1)} %add_halves.5), channel_id=1, source_target_pairs={{0,1},{1,0},{2,3},{3,2},{4,5},{5,4},{6,7},{7,6},{8,9},{9,8},{10,11... | collective-permute-start | bytes 786440 | tf_op jit(solution)/shard_map/ppermute | solution.py:495
  50.3 12.5 %collective-permute-start.11 = (bf16[2048,128]{1,0:T(8,128)(2,1)S(1)}, bf16[2048,128]{1,0:T(8,128)(2,1)S(1)}, u32[]{:S(2)}, u32[]{:S(2)}) collective-permute-start(bf16[2048,128]{1,0:T(8,128)(2,1)S(1)} %get-tuple-element.68), channel_id=1, source_target_pairs={{0,1},{1,0},{2,3},{3,2},{4,5},{5,4},{6,7},{7,6},{8,9},{9,8},{10,11... | collective-permute-start | bytes 1572872 | tf_op jit(solution)/shard_map/ppermute | solution.py:495
  51.0 12.5 %collective-permute-start.12 = (bf16[2048,128]{1,0:T(8,128)(2,1)S(1)}, bf16[2048,128]{1,0:T(8,128)(2,1)S(1)}, u32[]{:S(2)}, u32[]{:S(2)}) collective-permute-start(bf16[2048,128]{1,0:T(8,128)(2,1)S(1)} %get-tuple-element.69), channel_id=1, source_target_pairs={{0,2},{1,3},{2,0},{3,1},{4,6},{5,7},{6,4},{7,5},{8,10},{9,11},{10,... | collective-permute-start | bytes 1572872 | tf_op jit(solution)/shard_map/ppermute | solution.py:495
  58.2 12.0 %collective-permute-start.10 = (bf16[1024,128]{1,0:T(8,128)(2,1)S(1)}, bf16[1024,128]{1,0:T(8,128)(2,1)S(1)}, u32[]{:S(2)}, u32[]{:S(2)}) collective-permute-start(bf16[1024,128]{1,0:T(8,128)(2,1)S(1)} %get-tuple-element.66), channel_id=1, source_target_pairs={{0,16},{4,20},{8,24},{12,28},{16,0},{20,4},{24,8},{28,12},{1,17},{... | collective-permute-start | bytes 786440 | tf_op jit(solution)/shard_map/ppermute | solution.py:495
  62.9 7.3 %collective-permute-start.13 = (bf16[1024,128]{1,0:T(8,128)(2,1)S(1)}, bf16[1024,128]{1,0:T(8,128)(2,1)S(1)}, u32[]{:S(2)}, u32[]{:S(2)}) collective-permute-start(bf16[1024,128]{1,0:T(8,128)(2,1)S(1)} %add_halves.6), channel_id=1, source_target_pairs={{0,2},{1,3},{2,0},{3,1},{4,6},{5,7},{6,4},{7,5},{8,10},{9,11},{10,... | collective-permute-start | bytes 786440 | tf_op jit(solution)/shard_map/ppermute | solution.py:495
  63.6 6.6 %collective-permute-start.14 = (bf16[1024,128]{1,0:T(8,128)(2,1)S(1)}, bf16[1024,128]{1,0:T(8,128)(2,1)S(1)}, u32[]{:S(2)}, u32[]{:S(2)}) collective-permute-start(bf16[1024,128]{1,0:T(8,128)(2,1)S(1)} %add_halves.7), channel_id=1, source_target_pairs={{0,1},{1,0},{2,3},{3,2},{4,5},{5,4},{6,7},{7,6},{8,9},{9,8},{10,11... | collective-permute-start | bytes 786440 | tf_op jit(solution)/shard_map/ppermute | solution.py:495

commit v6 on v5

--- a/solution.py
+++ b/solution.py
@@ -162,9 +162,13 @@
     )(keys, values)
 
 
-def _queries_for_other_core_kernel(meta_ref, queries_ref, out_ref, kept_ref, sem):
+def _queries_for_other_core_kernel(names, meta_ref, queries_ref, w_ref, out_ref, kept_ref, *rest):
+    *w_out, sem, w_sems = rest
+    w_copies = _weight_copies(names, meta_ref, w_ref, w_out, w_sems)
     copy = pltpu.make_async_copy(queries_ref, kept_ref, sem)
     copy.start()
+    for w_copy in w_copies:
+        w_copy.start()
     copy.wait()
     c = meta_ref[0]
     core = lax.rem(c, 2)
@@ -172,29 +176,28 @@
     for j in range(PIECES // 2):
         piece = _find_piece(meta_ref, c, 2 * j + 1 - core)
         out_ref[j * rows:(j + 1) * rows] = kept_ref[_rows(piece * rows, rows)]
-
-
-def _queries_for_other_core(meta, queries):
-    return pl.pallas_call(
-        _queries_for_other_core_kernel,
+    for w_copy in w_copies:
+        w_copy.wait()
+
+
+def _queries_for_other_core(names, meta, queries, out_weight):
+    return pl.pallas_call(
+        functools.partial(_queries_for_other_core_kernel, names),
         out_shape=[
             jax.ShapeDtypeStruct((queries.shape[0] // 2, queries.shape[1]), queries.dtype),
             jax.ShapeDtypeStruct(queries.shape, queries.dtype),
-        ],
-        in_specs=[SMEM, HBM],
-        out_specs=[VMEM] * 2,
-        scratch_shapes=[pltpu.SemaphoreType.DMA],
+        ] + [_eighth(out_weight) for _ in names],
+        in_specs=[SMEM, HBM, HBM],
+        out_specs=[VMEM] * (2 + len(names)),
+        scratch_shapes=[pltpu.SemaphoreType.DMA, pltpu.SemaphoreType.DMA((len(names),))],
         compiler_params=pltpu.CompilerParams(vmem_limit_bytes=2 * 2**20),
         cost_estimate=pl.CostEstimate(flops=1, bytes_accessed=1, transcendentals=0),
         name="queries_for_other_core",
-    )(meta, queries)
-
-
-QUARTERS = {
-    "x": ((1, 0), (3, 0)),
-    "y": ((2, 1), (3, 1)),
-    "pass": ((2, 0), (1, 1)),
-    "keep": ((0, 0), (0, 1)),
+    )(meta, queries, out_weight)
+
+
+EIGHTHS = {
+    "xf": (1, 0), "xp": (3, 0), "yf": (2, 1), "yp": (3, 1), "py": (2, 0), "px": (1, 1), "k0": (0, 0), "k1": (0, 1),
 }
 
 
@@ -202,15 +205,14 @@
     half = w_ref.shape[0] // (2 * N_FAST_HEAD)
     copies = []
     for n, name in enumerate(names):
-        for i, (flip, side) in enumerate(QUARTERS[name]):
-            row = (meta_ref[1] ^ flip) * (2 * half) + side * half
-            copies.append(pltpu.make_async_copy(
-                w_ref.at[_rows(row, half)], out_refs[n].at[pl.ds(i * half, half)], sems.at[2 * n + i]))
+        flip, side = EIGHTHS[name]
+        row = (meta_ref[1] ^ flip) * (2 * half) + side * half
+        copies.append(pltpu.make_async_copy(w_ref.at[_rows(row, half)], out_refs[n], sems.at[n]))
     return copies
 
 
-def _quarter(out_weight):
-    return jax.ShapeDtypeStruct((out_weight.shape[0] // N_FAST_HEAD, out_weight.shape[1]), out_weight.dtype)
+def _eighth(out_weight):
+    return jax.ShapeDtypeStruct((out_weight.shape[0] // (2 * N_FAST_HEAD), out_weight.shape[1]), out_weight.dtype)
 
 
 def _stage_kernel(names, meta_ref, w_ref, *rest):
@@ -221,14 +223,14 @@
         copy.wait()
 
 
-def _stage_weights(names, meta, out_weight, room):
+def _stage_weights(names, meta, out_weight):
     return pl.pallas_call(
         functools.partial(_stage_kernel, names),
-        out_shape=[_quarter(out_weight) for _ in names],
+        out_shape=[_eighth(out_weight) for _ in names],
         in_specs=[SMEM, HBM],
         out_specs=[VMEM] * len(names),
-        scratch_shapes=[pltpu.SemaphoreType.DMA((2 * len(names),))],
-        compiler_params=pltpu.CompilerParams(vmem_limit_bytes=room * 2**20),
+        scratch_shapes=[pltpu.SemaphoreType.DMA((len(names),))],
+        compiler_params=pltpu.CompilerParams(vmem_limit_bytes=8 * 2**20),
         cost_estimate=pl.CostEstimate(flops=1, bytes_accessed=1, transcendentals=0),
         name="stage_weights",
     )(meta, out_weight)
@@ -280,10 +282,15 @@
     base = 2 * rows * (z - 1)
     group = queries_ref.shape[1] // kv0_ref.shape[1]
     scale = math.log2(math.e) / math.sqrt(HEAD_SIZE)
-    span = 5 * tile
-
-    def piece_keys(p0):
-        first = pl.multiple_of(lax.div(p0, tile) * tile + 2 * rows - 4 * tile, tile)
+
+    def tiles_needed(p0):
+        low = jnp.int32(0)
+        for start in doc_start:
+            low = jnp.where(2 * rows * z + p0 >= start, start, low)
+        return lax.div(2 * rows * z + p0, tile) - lax.div(low, tile) + 1
+
+    def piece_keys(p0, span):
+        first = pl.multiple_of(lax.div(p0, tile) * tile + 2 * rows + tile - span, tile)
         pos = 2 * rows * z + p0 + lax.broadcasted_iota(jnp.int32, (piece_rows, 1), 0)
         low = jnp.zeros((piece_rows, 1), jnp.int32)
         for start in doc_start:
@@ -291,10 +298,10 @@
         key_pos = base + first + lax.broadcasted_iota(jnp.int32, (piece_rows, span), 1)
         return first, (key_pos >= low) & (key_pos <= pos)
 
-    def some_pieces(pieces):
+    def some_pieces(pieces, span):
         units, scores, weights = [], [], []
         for n, p0 in pieces:
-            first, allowed = piece_keys(p0)
+            first, allowed = piece_keys(p0, span)
             units += [(n, kv, first, allowed) for kv in range(heads)]
         for n, kv, first, allowed in units:
             q = jnp.concatenate(
@@ -313,6 +320,7 @@
                 ctxbuf[n, :, pl.ds((kv * group + g) * HEAD_SIZE, HEAD_SIZE)] = o[g * piece_rows:(g + 1) * piece_rows]
 
     together = 2
+    most_tiles = 5
 
     def step(i, carry):
         pieces = []
@@ -322,7 +330,12 @@
             for m in range(1, 2 * count):
                 p0 = jnp.where(n == m, starts[m // 2][m % 2], p0)
             pieces.append((n, p0))
-        some_pieces(pieces)
+        needed = functools.reduce(jnp.maximum, [tiles_needed(p0) for n, p0 in pieces])
+        least = 0
+        for tiles in (2, 3, most_tiles):
+            fits = needed > least if tiles == most_tiles else (needed > least) & (needed <= tiles)
+            pl.when(fits)(functools.partial(some_pieces, pieces, tiles * tile))
+            least = tiles
         return carry
 
     lax.fori_loop(0, 2 * count // together, step, 0)
@@ -338,7 +351,7 @@
     return pl.pallas_call(
         functools.partial(_attend_kernel, groups, names),
         out_shape=[jax.ShapeDtypeStruct((2 * piece, queries.shape[1]), jnp.bfloat16) for _ in groups]
-        + [_quarter(out_weight) for _ in names],
+        + [_eighth(out_weight) for _ in names],
         in_specs=[SMEM] + [VMEM] * 6 + [HBM],
         out_specs=[VMEM] * (len(groups) + len(names)),
         scratch_shapes=[
@@ -346,7 +359,7 @@
             pltpu.VMEM((4 * rows, 2 * kv[0].shape[1]), jnp.bfloat16),
             pltpu.VMEM((2 * len(groups), piece, queries.shape[1]), jnp.bfloat16),
             pltpu.VMEM((2 * len(groups), piece, queries.shape[1]), jnp.bfloat16),
-            pltpu.SemaphoreType.DMA((2 * len(names),)),
+            pltpu.SemaphoreType.DMA((len(names),)),
         ],
         compiler_params=pltpu.CompilerParams(vmem_limit_bytes=12 * 2**20),
         cost_estimate=pl.CostEstimate(flops=1, bytes_accessed=1, transcendentals=0),
@@ -358,94 +371,78 @@
     out_ref[...] = jnp.dot(weight_ref[...], tokens, preferred_element_type=jnp.float32).astype(out_ref.dtype)
 
 
-def _leaving_rows_kernel(meta_ref, a_ref, b_ref, wx_ref, wy_ref, x_ref, y_ref, joined_ref, catbuf):
+def _leaving_rows_kernel(meta_ref, a_ref, b_ref, *rest):
+    w_refs, out_refs, (joined_ref, catbuf) = rest[:4], rest[4:8], rest[8:]
     second = lax.rem(lax.div(meta_ref[0], 2), 2)
     mid = a_ref.shape[0]
     catbuf[_rows(second * mid, mid)] = a_ref[...]
     catbuf[_rows((1 - second) * mid, mid)] = b_ref[...]
     joined = catbuf[...].T
     joined_ref[...] = joined
-    _dot_to(x_ref, wx_ref, joined)
-    _dot_to(y_ref, wy_ref, joined)
-
-
-def _pass_rows_kernel(joined_ref, w_ref, out_ref):
-    _dot_to(out_ref, w_ref, joined_ref[...])
-
-
-def _keep_rows_kernel(near_ref, far_ref, w_ref, near_out, far_out):
-    tokens = near_ref.shape[1]
-    both = jnp.concatenate([near_ref[...], far_ref[...]], axis=1)
-    out = jnp.dot(w_ref[...], both, preferred_element_type=jnp.float32).astype(near_out.dtype)
-    near_out[...] = out[:, :tokens]
-    far_out[...] = out[:, tokens:]
-
-
-def _leaving_rows(meta, a, b, w_x, w_y):
-    (rows, depth), tokens = w_x.shape, a.shape[0] + b.shape[0]
+    for w_ref, out_ref in zip(w_refs, out_refs):
+        _dot_to(out_ref, w_ref, joined)
+
+
+def _pass_rows_kernel(joined_ref, w0_ref, w1_ref, out0_ref, out1_ref):
+    joined = joined_ref[...]
+    _dot_to(out0_ref, w0_ref, joined)
+    _dot_to(out1_ref, w1_ref, joined)
+
+
+def _keep_rows_kernel(first_ref, second_ref, w0_ref, w1_ref, first_out, second_out):
+    half, tokens = w0_ref.shape[0], first_ref.shape[1]
+    both = jnp.concatenate([first_ref[...], second_ref[...]], axis=1)
+    for i, w_ref in enumerate((w0_ref, w1_ref)):
+        out = jnp.dot(w_ref[...], both, preferred_element_type=jnp.float32).astype(first_out.dtype)
+        first_out[i * half:(i + 1) * half] = out[:, :tokens]
+        second_out[i * half:(i + 1) * half] = out[:, tokens:]
+
+
+def _project(kernel, name, out_shape, operands, scratch=(), scalars=()):
+    return pl.pallas_call(
+        kernel,
+        out_shape=out_shape,
+        in_specs=[SMEM] * len(scalars) + [VMEM] * len(operands),
+        out_specs=[VMEM] * len(out_shape),
+        scratch_shapes=scratch,
+        compiler_params=pltpu.CompilerParams(vmem_limit_bytes=8 * 2**20),
+        cost_estimate=pl.CostEstimate(flops=1, bytes_accessed=1, transcendentals=0),
+        name=name,
+    )(*scalars, *operands)
+
+
+def _leaving_rows(meta, a, b, weights):
+    (rows, depth), tokens = weights["xf"].shape, a.shape[0] + b.shape[0]
     part = jax.ShapeDtypeStruct((rows, tokens), jnp.bfloat16)
-    return pl.pallas_call(
-        _leaving_rows_kernel,
-        out_shape=[part, part, jax.ShapeDtypeStruct((depth, tokens), jnp.bfloat16)],
-        in_specs=[SMEM] + [VMEM] * 4,
-        out_specs=[VMEM] * 3,
-        scratch_shapes=[pltpu.VMEM((tokens, depth), jnp.bfloat16)],
-        compiler_params=pltpu.CompilerParams(vmem_limit_bytes=8 * 2**20),
-        cost_estimate=pl.CostEstimate(flops=1, bytes_accessed=1, transcendentals=0),
-        name="leaving_rows",
-    )(meta, a, b, w_x, w_y)
-
-
-def _pass_rows(joined, weight):
-    return pl.pallas_call(
-        _pass_rows_kernel,
-        out_shape=jax.ShapeDtypeStruct((weight.shape[0], joined.shape[1]), jnp.bfloat16),
-        in_specs=[VMEM] * 2,
-        out_specs=VMEM,
-        compiler_params=pltpu.CompilerParams(vmem_limit_bytes=8 * 2**20),
-        cost_estimate=pl.CostEstimate(flops=1, bytes_accessed=1, transcendentals=0),
-        name="pass_rows",
-    )(joined, weight)
-
-
-def _keep_rows(near, far, weight):
-    part = jax.ShapeDtypeStruct((weight.shape[0], near.shape[1]), jnp.bfloat16)
-    return pl.pallas_call(
-        _keep_rows_kernel,
-        out_shape=[part, part],
-        in_specs=[VMEM] * 3,
-        out_specs=[VMEM] * 2,
-        compiler_params=pltpu.CompilerParams(vmem_limit_bytes=8 * 2**20),
-        cost_estimate=pl.CostEstimate(flops=1, bytes_accessed=1, transcendentals=0),
-        name="keep_rows",
-    )(near, far, weight)
-
-
-def _add_halves_kernel(a_half, b_half, a_ref, b_ref, out_ref):
-    rows = out_ref.shape[0]
-    a = a_ref[a_half * rows:(a_half + 1) * rows].astype(jnp.float32)
-    b = b_ref[b_half * rows:(b_half + 1) * rows].astype(jnp.float32)
-    out_ref[...] = (a + b).astype(out_ref.dtype)
-
-
-def _add_halves(a, a_half, b, b_half):
-    rows, tokens = a.shape[0] // 2, a.shape[1]
-    return pl.pallas_call(
-        functools.partial(_add_halves_kernel, a_half, b_half),
-        out_shape=jax.ShapeDtypeStruct((rows, tokens), jnp.bfloat16),
-        in_specs=[VMEM] * 2,
-        out_specs=VMEM,
-        compiler_params=pltpu.CompilerParams(vmem_limit_bytes=2 * 2**20),
-        cost_estimate=pl.CostEstimate(flops=1, bytes_accessed=1, transcendentals=0),
-        name="add_halves",
-    )(a, b)
+    return _project(
+        _leaving_rows_kernel, "leaving_rows", [part] * 4 + [jax.ShapeDtypeStruct((depth, tokens), jnp.bfloat16)],
+        (a, b) + tuple(weights[name] for name in ("xf", "xp", "yf", "yp")),
+        [pltpu.VMEM((tokens, depth), jnp.bfloat16)], (meta,))
+
+
+def _pass_rows(joined, weights):
+    part = jax.ShapeDtypeStruct((weights["py"].shape[0], joined.shape[1]), jnp.bfloat16)
+    return _project(_pass_rows_kernel, "pass_rows", [part] * 2, (joined, weights["py"], weights["px"]))
+
+
+def _keep_rows(first, second, weights):
+    part = jax.ShapeDtypeStruct((2 * weights["k0"].shape[0], first.shape[1]), jnp.bfloat16)
+    return _project(_keep_rows_kernel, "keep_rows", [part] * 2, (first, second, weights["k0"], weights["k1"]))
+
+
+def _add_kernel(a_ref, b_ref, out_ref):
+    out_ref[...] = (a_ref[...].astype(jnp.float32) + b_ref[...].astype(jnp.float32)).astype(out_ref.dtype)
+
+
+def _add(a, b):
+    return _project(_add_kernel, "add", [jax.ShapeDtypeStruct(a.shape, jnp.bfloat16)], (a, b))[0]
 
 
 def _sum_parts(keep_ref, x1_ref, y1_ref, y2_ref, x2_ref):
     half = y2_ref.shape[0]
     f32 = jnp.float32
-    first = keep_ref[:half].astype(f32) + x1_ref[:half].astype(f32) + y2_ref[...].astype(f32)
-    second = keep_ref[half:].astype(f32) + y1_ref[:half].astype(f32) + x2_ref[...].astype(f32)
+    first = keep_ref[:half].astype(f32) + x1_ref[...].astype(f32) + y2_ref[...].astype(f32)
+    second = keep_ref[half:].astype(f32) + y1_ref[...].astype(f32) + x2_ref[...].astype(f32)
     return first, second
 
 
@@ -463,19 +460,51 @@
     away_ref[...] = jnp.where(own, pltpu.roll(bottom, tokens // 2, 1), top).astype(away_ref.dtype)
 
 
-def _finish_second_kernel(meta_ref, first_ref, away_ref, keep_ref, x1_ref, y1_ref, y2_ref, x2_ref, out_ref):
+def _unpack_kernel(meta_ref, away_ref, out_ref):
+    half, tokens = away_ref.shape
+    out_ref[:half] = pltpu.roll(away_ref[...].astype(jnp.float32), tokens // 2, 1).astype(out_ref.dtype)
+    out_ref[half:] = away_ref[...]
+
+
+def _sum_first_step_kernel(meta_ref, keep_ref, x1_ref, y1_ref, out_ref):
+    half = x1_ref.shape[0]
+    for i, one_ref in enumerate((x1_ref, y1_ref)):
+        at = pl.ds(i * half, half)
+        out_ref[at] = keep_ref[at].astype(jnp.float32) + one_ref[...].astype(jnp.float32)
+
+
+def _finish_second_kernel(meta_ref, first_ref, away_ref, sum_ref, y2_ref, x2_ref, out_ref, rows_ref, sems):
     half, tokens = y2_ref.shape
+    part = half // 2
     upper = lax.div(meta_ref[0], 4)
-    own = _own_half(meta_ref, half, tokens)
     mine, others = _rows(upper * tokens, tokens), _rows((1 - upper) * tokens, tokens)
-    away = away_ref[...].astype(jnp.float32)
-    sums = _sum_parts(keep_ref, x1_ref, y1_ref, y2_ref, x2_ref)
-    arrived = (pltpu.roll(away, tokens // 2, 1), away)
-    for i in range(2):
-        at = pl.ds(i * half, half)
-        first = first_ref[at].astype(jnp.float32)
-        out_ref[at, mine] = jnp.where(own, first, pltpu.roll(sums[i], tokens // 2, 1)).astype(out_ref.dtype)
-        out_ref[at, others] = jnp.where(own, arrived[i], sums[i]).astype(out_ref.dtype)
+    own = _own_half(meta_ref, part, tokens)
+    copies = []
+    for i in range(4):
+        at, inside = pl.ds(i * part, part), pl.ds(i % 2 * part, part)
+        two_ref = y2_ref if i < 2 else x2_ref
+        sums = sum_ref[at] + two_ref[inside].astype(jnp.float32)
+        first, away = first_ref[at].astype(jnp.float32), away_ref[at].astype(jnp.float32)
+        rows_ref[at, mine] = jnp.where(own, first, pltpu.roll(sums, tokens // 2, 1)).astype(rows_ref.dtype)
+        rows_ref[at, others] = jnp.where(own, away, sums).astype(rows_ref.dtype)
+        copies.append(pltpu.make_async_copy(rows_ref.at[at], out_ref.at[at], sems.at[i]))
+        copies[-1].start()
+    for copy in copies:
+        copy.wait()
+
+
+def _finish_second(meta, first, away, summed, y2, x2):
+    rows, tokens = summed.shape
+    return pl.pallas_call(
+        _finish_second_kernel,
+        out_shape=jax.ShapeDtypeStruct((rows, 2 * tokens), jnp.bfloat16),
+        in_specs=[SMEM] + [VMEM] * 5,
+        out_specs=HBM,
+        scratch_shapes=[pltpu.VMEM((rows, 2 * tokens), jnp.bfloat16), pltpu.SemaphoreType.DMA((4,))],
+        compiler_params=pltpu.CompilerParams(vmem_limit_bytes=8 * 2**20),
+        cost_estimate=pl.CostEstimate(flops=1, bytes_accessed=1, transcendentals=0),
+        name="finish_second",
+    )(meta, first, away, summed, y2, x2)
 
 
 def _finish(kernel, out_shape, operands):
@@ -505,41 +534,47 @@
     meta = jnp.concatenate([
         lax.axis_index("ctx").reshape(1), lax.axis_index("head").reshape(1), owners.reshape(-1), doc_lengths,
     ]).astype(jnp.int32)
-    leaving, queries = _queries_for_other_core(meta, queries)
+    weights = {}
+    leaving, queries, weights["xp"] = _queries_for_other_core(("xp",), meta, queries, out_weight)
     other = _flip(leaving, "ctx", 1)
-    (w_x,) = _stage_weights(("x",), meta, out_weight, 8)
-    kv2, w_x = lax.optimization_barrier((kv2, w_x))
+    weights["yp"], weights["xf"] = _stage_weights(("yp", "xf"), meta, out_weight)
+    kv2, weights["xf"] = lax.optimization_barrier((kv2, weights["xf"]))
     kv = (kv0, kv1, kv2, _flip(kv2, "ctx", 1))
-    ctx0, ctx2, ctx1, ctx3, w_y, w_pass = _attend_groups(
-        (0, 2, 1, 3), ("y", "pass"), meta, queries, other, kv, out_weight)
+    loaded = ("yf", "py", "px")
+    ctx0, ctx2, ctx1, ctx3, *loads = _attend_groups((0, 2, 1, 3), loaded, meta, queries, other, kv, out_weight)
+    weights.update(zip(loaded, loads))
     ctx1, ctx3 = _flip(ctx1, "ctx", 2), _flip(ctx3, "ctx", 6)
 
-    xmsg, ymsg, joined = _leaving_rows(meta, ctx0, ctx2, w_x, w_y)
-    x1, y1 = _flip(xmsg, "head", 1), _flip(ymsg, "head", 2)
-    pass_on = _pass_rows(joined, w_pass)
-    pass_on, keep_meta = lax.optimization_barrier((pass_on, meta))
-    (w_keep,) = _stage_weights(("keep",), keep_meta, out_weight, 8)
-    pass_on, w_keep = lax.optimization_barrier((pass_on, w_keep))
-    ymsg, xmsg = _add_halves(pass_on, 0, x1, 1), _add_halves(pass_on, 1, y1, 1)
-    meta, ymsg, xmsg = lax.optimization_barrier((meta, ymsg, xmsg))
-    y2, x2 = _flip(ymsg, "head", 2), _flip(xmsg, "head", 1)
-
-    xmsg, ymsg, joined2 = _leaving_rows(meta, ctx1, ctx3, w_x, w_y)
-    xmsg, ymsg, y2, x2 = lax.optimization_barrier((xmsg, ymsg, y2, x2))
-    next_x1, next_y1 = _flip(xmsg, "head", 1), _flip(ymsg, "head", 2)
-    keep, next_keep = _keep_rows(joined, joined2, w_keep)
+    xf, xp, yf, yp, joined = _leaving_rows(meta, ctx0, ctx2, weights)
+    x1f, x1p, y1f, y1p = _flip(xf, "head", 1), _flip(xp, "head", 1), _flip(yf, "head", 2), _flip(yp, "head", 2)
+    later_meta, joined = lax.optimization_barrier((meta, joined))
+    weights["k0"], weights["k1"] = _stage_weights(("k0", "k1"), later_meta, out_weight)
+    joined, weights["k0"], ctx1, ctx3 = lax.optimization_barrier((joined, weights["k0"], ctx1, ctx3))
+    y2, x2 = _pass_rows(joined, weights)
+    y2, x2 = _add(y2, x1p), _add(x2, y1p)
+    meta, y2, x2 = lax.optimization_barrier((meta, y2, x2))
+    y2, x2 = _flip(y2, "head", 2), _flip(x2, "head", 1)
+
+    xf, xp, yf, yp, joined2 = _leaving_rows(meta, ctx1, ctx3, weights)
+    xf, xp, yf, yp, x1f, y1f = lax.optimization_barrier((xf, xp, yf, yp, x1f, y1f))
+    next_x1f, next_x1p = _flip(xf, "head", 1), _flip(xp, "head", 1)
+    next_y1f, next_y1p = _flip(yf, "head", 2), _flip(yp, "head", 2)
+    keep, next_keep = _keep_rows(joined, joined2, weights)
     rows, tokens = keep.shape
     first, away = _finish(_finish_first_kernel, [
         jax.ShapeDtypeStruct((rows, tokens), jnp.bfloat16),
         jax.ShapeDtypeStruct((rows // 2, tokens), jnp.bfloat16),
-    ], (meta, keep, x1, y1, y2, x2))
-    joined2, away_sent = lax.optimization_barrier((joined2, away))
-    pass_on = _pass_rows(joined2, w_pass)
-    ymsg, xmsg = _add_halves(pass_on, 0, next_x1, 1), _add_halves(pass_on, 1, next_y1, 1)
-    away = _flip(away_sent, "ctx", 4)
-    y2, x2 = _flip(ymsg, "head", 2), _flip(xmsg, "head", 1)
-    return _finish(_finish_second_kernel, jax.ShapeDtypeStruct((rows, 2 * tokens), jnp.bfloat16),
-                   (meta, first, away, next_keep, next_x1, next_y1, y2, x2))
+    ], (meta, keep, x1f, y1f, y2, x2))
+    joined2, away = lax.optimization_barrier((joined2, away))
+    away = _flip(away, "ctx", 4)
+    y2, x2 = _pass_rows(joined2, weights)
+    y2, x2 = _add(y2, next_x1p), _add(x2, next_y1p)
+    y2, x2 = _flip(y2, "head", 2), _flip(x2, "head", 1)
+    away = _finish(_unpack_kernel, [jax.ShapeDtypeStruct((rows, tokens), jnp.bfloat16)], (meta, away))[0]
+    away, next_keep = lax.optimization_barrier((away, next_keep))
+    summed = _finish(_sum_first_step_kernel, [jax.ShapeDtypeStruct((rows, tokens), jnp.float32)],
+                     (meta, next_keep, next_x1f, next_y1f))[0]
+    return _finish_second(meta, first, away, summed, y2, x2)
 
 
 def solution(mesh):

time: 72.4 us -> 70.7 us (0.977)
  waiting for transfers between devices: 10.9 us -> 8.04 us
    ppermute x14 -> x18, waiting for transfers between devices: 10.9 us -> 8.04 us  [_flip(): return lax.ppermute(x, axis, [(i, i ^ bits) for i in range(n)])]
    pallas_call x12 -> x13, Pallas kernels: 28 us -> 30.3 us  [the longest x9 17.4 us: _project(): pl.pallas_call(kernel, out_shape=out_shape, in_specs=[SMEM] * len(scalars...]
    pallas_call x1, Pallas kernels: 6.54 us -> 5.36 us  [_attend_groups(): pl.pallas_call(functools.partial(_attend_kernel, groups, names), out_shap...]
    pallas_call x2 -> x3, Pallas kernels: 2.79 us -> 2.12 us  [_finish(): pl.pallas_call(kernel, out_shape=out_shape, in_specs=[SMEM] + [VMEM] * (l...]
    ppermute x14 -> x18, starting transfers between devices: 17.1 us -> 17.7 us  [_flip(): return lax.ppermute(x, axis, [(i, i ^ bits) for i in range(n)])]
  transfers between devices with their start and end apart: 15 -> 19, of which waited for: 6 -> 3; matrix products, arithmetic and copies ran while one was open for 1% -> 1% of each run, Pallas kernels for 33% -> 44%
where the time goes in v6:
time: 70.7 us; the launch traced here: 70.5 us
  Pallas kernels  38.7 us (55%)
  starting transfers between devices  22.6 us (32%)
  waiting for transfers between devices  8.04 us (11%)
  other arithmetic  0.75 us (1%)
    ppermute x18, starting transfers between devices, _flip(): return lax.ppermute(x, axis, [(i, i ^ bits) for i in range(n)])  17.7 us
    pallas_call x9, Pallas kernels, _project(): pl.pallas_call(kernel, out_shape=out_shape, in_specs=[SMEM] * len(scalars...  17.4 us
    pallas_call x2, Pallas kernels, _stage_weights(): pl.pallas_call(functools.partial(_stage_kernel, names), out_shape=[_eight...  8.05 us
    ppermute x18, waiting for transfers between devices, _flip(): return lax.ppermute(x, axis, [(i, i ^ bits) for i in range(n)])  8.04 us
    pallas_call x1, Pallas kernels, _attend_groups(): pl.pallas_call(functools.partial(_attend_kernel, groups, names), out_shap...  5.36 us
    ppermute x1, starting transfers between devices, per_device_fast(): kv2 = lax.ppermute(kv0, 'ctx', [(i, i + 2) for i in range(places - 2)])  4.94 us
    pallas_call x1, Pallas kernels, _queries_for_other_core(): pl.pallas_call(functools.partial(_queries_for_other_core_kernel, names),...  3.07 us
    pallas_call x3, Pallas kernels, _finish(): pl.pallas_call(kernel, out_shape=out_shape, in_specs=[SMEM] + [VMEM] * (l...  2.12 us
  transfers between devices with their start and end apart: 19, of which 3 were waited for; matrix products, arithmetic and copies ran while one was open for 1% of the time, Pallas kernels for 44%

profile of v6, /device:TPU:0, one launch (start us, length us, event | category | flops | bytes accessed | tf_op | source)
XLA Modules:
  0.0 70.5 jit_solution(7175850261701257050)
XLA Ops:
  0.0 1.0 %join_keys_values.1.kv0_ref = bf16[512,256]{1,0:T(8,128)(2,1)S(1)} custom-call(bf16[256,256]{1,0:T(8,128)(2,1)} %keys_ref.1, bf16[256,256]{1,0:T(8,128)(2,1)} %values_ref.1), custom_call_target="tpu_custom_call" | custom-call | flops 1 | bytes 1 | tf_op jit(solution)/shard_map/join_keys_values/pallas_call | solution.py:153
  1.0 4.9 %collective-permute-start.2 = (bf16[512,256]{1,0:T(8,128)(2,1)S(1)}, bf16[512,256]{1,0:T(8,128)(2,1)S(1)}, u32[]{:S(2)}, u32[]{:S(2)}) collective-permute-start(bf16[512,256]{1,0:T(8,128)(2,1)S(1)} %join_keys_values.1.kv0_ref), channel_id=1, source_target_pairs={{0,8},{4,12},{8,16},{12,20},{16,24},{20,28},{1,9},{5,13},{9,17},{1... | collective-permute-start | bytes 786440 | tf_op jit(solution)/shard_map/ppermute | solution.py:532
  5.9 0.8 %pad_add_fusion.meta_ref = s32[82]{0:T(128)S(1)} fusion(s32[16]{0:T(128)} %param.10, s32[64]{0:T(128)} %bitcast.3, s32[1]{0:T(128)} %bitcast.1, s32[1]{0:T(128)} %bitcast), kind=kLoop, calls=%fused_computation | loop fusion | flops 246 | bytes 656 | tf_op jit(solution)/shard_map/concatenate | solution.py:534
  6.7 3.1 %queries_for_other_core.1 = (bf16[128,2048]{1,0:T(8,128)(2,1)S(1)}, bf16[256,2048]{1,0:T(8,128)(2,1)S(1)}, bf16[1024,2048]{1,0:T(8,128)(2,1)S(1)}) custom-call(s32[82]{0:T(128)S(1)} %pad_add_fusion.meta_ref, bf16[256,2048]{1,0:T(8,128)(2,1)} %queries_ref.1, bf16[8192,2048]{1,0:T(8,128)(2,1)} %w_ref.7), custom_call_target="tpu_custom_call" | custom-call | flops 1 | bytes 1 | tf_op jit(solution)/shard_map/queries_for_other_core/pallas_call | solution.py:184
  9.8 0.1 collective-permute-start
  9.9 0.5 collective-permute-start.1
  10.4 4.0 %stage_weights.2 = (bf16[1024,2048]{1,0:T(8,128)(2,1)S(1)}, bf16[1024,2048]{1,0:T(8,128)(2,1)S(1)}) custom-call(s32[82]{0:T(128)S(1)} %pad_add_fusion.meta_ref, bf16[8192,2048]{1,0:T(8,128)(2,1)} %w_ref.7), custom_call_target="tpu_custom_call" | custom-call | flops 1 | bytes 1 | tf_op jit(solution)/shard_map/stage_weights/pallas_call | solution.py:227
  14.4 0.0 collective-permute-done.2.kv2_ref
  14.4 0.1 collective-permute-start.3
  14.5 0.0 collective-permute-done.1.kv1_ref
  14.5 0.0 collective-permute-done.other_ref
  14.6 1.5 %collective-permute-done.3.kv3_ref = bf16[512,256]{1,0:T(8,128)(2,1)S(1)} collective-permute-done((bf16[512,256]{1,0:T(8,128)(2,1)S(1)}, bf16[512,256]{1,0:T(8,128)(2,1)S(1)}, u32[]{:S(2)}, u32[]{:S(2)}) %collective-permute-start.3) | collective-permute-done | bytes 262176 | tf_op jit(solution)/shard_map/ppermute | solution.py:524
  16.0 5.4 %attend_groups.1 = (bf16[64,2048]{1,0:T(8,128)(2,1)S(1)}, bf16[64,2048]{1,0:T(8,128)(2,1)S(1)}, bf16[64,2048]{1,0:T(8,128)(2,1)S(1)}, bf16[64,2048]{1,0:T(8,128)...) custom-call(s32[82]{0:T(128)S(1)} %pad_add_fusion.meta_ref, ...), custom_call_target="tpu_custom_call" | custom-call | flops 1 | bytes 1 | tf_op jit(solution)/shard_map/attend_groups/pallas_call | solution.py:351
  21.4 1.6 %collective-permute-start.4 = (bf16[64,2048]{1,0:T(8,128)(2,1)S(1)}, bf16[64,2048]{1,0:T(8,128)(2,1)S(1)}, u32[]{:S(2)}, u32[]{:S(2)}) collective-permute-start(bf16[64,2048]{1,0:T(8,128)(2,1)S(1)} %get-tuple-element.72), channel_id=1, source_target_pairs={{0,8},{4,12},{8,0},{12,4},{16,24},{20,28},{24,16},{28,20},{1,9},{5... | collective-permute-start | bytes 786440 | tf_op jit(solution)/shard_map/ppermute | solution.py:524
  23.0 2.5 %collective-permute-start.5 = (bf16[64,2048]{1,0:T(8,128)(2,1)S(1)}, bf16[64,2048]{1,0:T(8,128)(2,1)S(1)}, u32[]{:S(2)}, u32[]{:S(2)}) collective-permute-start(bf16[64,2048]{1,0:T(8,128)(2,1)S(1)} %get-tuple-element.73), channel_id=1, source_target_pairs={{0,24},{4,28},{8,16},{12,20},{16,8},{20,12},{24,0},{28,4},{1,25},{... | collective-permute-start | bytes 786440 | tf_op jit(solution)/shard_map/ppermute | solution.py:524
  25.5 5.1 %leaving_rows.2 = (bf16[1024,128]{1,0:T(8,128)(2,1)S(1)}, bf16[1024,128]{1,0:T(8,128)(2,1)S(1)}, bf16[1024,128]{1,0:T(8,128)(2,1)S(1)}, bf16[1024,128]{1,0:T(8,128)(2,1)S(1)}, bf16[2048,128]{1,0:T(8,128)(2,1)S(1)}) custom-call(s32[82]{0:T(128)S(1)} %pad_add_fusion.meta_ref, bf16[64,2048]{1,0:T(8,128)(2,1)S(1)} %get-tuple-element.62.a_ref, ...), custom_call_target="tpu_custom_call" | custom-call | flops 1 | bytes 1 | tf_op jit(solution)/shard_map/leaving_rows/pallas_call | solution.py:402
  30.6 1.6 %collective-permute-start.6 = (bf16[1024,128]{1,0:T(8,128)(2,1)S(1)}, bf16[1024,128]{1,0:T(8,128)(2,1)S(1)}, u32[]{:S(2)}, u32[]{:S(2)}) collective-permute-start(bf16[1024,128]{1,0:T(8,128)(2,1)S(1)} %get-tuple-element.78), channel_id=1, source_target_pairs={{0,1},{1,0},{2,3},{3,2},{4,5},{5,4},{6,7},{7,6},{8,9},{9,8},{10,11... | collective-permute-start | bytes 786440 | tf_op jit(solution)/shard_map/ppermute | solution.py:524
  32.1 1.5 %collective-permute-start.7 = (bf16[1024,128]{1,0:T(8,128)(2,1)S(1)}, bf16[1024,128]{1,0:T(8,128)(2,1)S(1)}, u32[]{:S(2)}, u32[]{:S(2)}) collective-permute-start(bf16[1024,128]{1,0:T(8,128)(2,1)S(1)} %get-tuple-element.80), channel_id=1, source_target_pairs={{0,2},{1,3},{2,0},{3,1},{4,6},{5,7},{6,4},{7,5},{8,10},{9,11},{10,... | collective-permute-start | bytes 786440 | tf_op jit(solution)/shard_map/ppermute | solution.py:524
  33.7 0.5 collective-permute-start.8
  34.2 0.0 collective-permute-done.4.a_ref
  34.2 0.5 collective-permute-start.9
  34.7 4.0 %stage_weights.3 = (bf16[1024,2048]{1,0:T(8,128)(2,1)S(1)}, bf16[1024,2048]{1,0:T(8,128)(2,1)S(1)}) custom-call(s32[82]{0:T(128)S(1)} %pad_add_fusion.meta_ref, bf16[8192,2048]{1,0:T(8,128)(2,1)} %w_ref.7), custom_call_target="tpu_custom_call" | custom-call | flops 1 | bytes 1 | tf_op jit(solution)/shard_map/stage_weights/pallas_call | solution.py:227
  38.7 0.0 collective-permute-done.5.b_ref
  38.8 2.3 %pass_rows.2 = (bf16[1024,128]{1,0:T(8,128)(2,1)S(1)}, bf16[1024,128]{1,0:T(8,128)(2,1)S(1)}) custom-call(bf16[2048,128]{1,0:T(8,128)(2,1)S(1)} %get-tuple-element.74.joined_ref.first_ref, bf16[1024,2048]{1,0:T(8,128)(2,1)S(1)} %get-tuple-element.75.w0_ref, bf16[1024,2048]{1,0:T(8,128)(2,1)S(1)} %get-tuple-element.76.w1_ref), custom_call_target="tpu_custom_call" | custom-call | flops 1 | bytes 1 | tf_op jit(solution)/shard_map/pass_rows/pallas_call | solution.py:402
  41.1 0.0 collective-permute-done.6.b_ref
  41.1 0.1 add.10
  41.2 0.2 collective-permute-done.7.b_ref
  41.4 0.1 add.11
  41.5 1.6 %collective-permute-start.10 = (bf16[1024,128]{1,0:T(8,128)(2,1)S(1)}, bf16[1024,128]{1,0:T(8,128)(2,1)S(1)}, u32[]{:S(2)}, u32[]{:S(2)}) collective-permute-start(bf16[1024,128]{1,0:T(8,128)(2,1)S(1)} %add.10), channel_id=1, source_target_pairs={{0,2},{1,3},{2,0},{3,1},{4,6},{5,7},{6,4},{7,5},{8,10},{9,11},{10,... | collective-permute-start | bytes 786440 | tf_op jit(solution)/shard_map/ppermute | solution.py:524
  43.0 1.3 %collective-permute-start.11 = (bf16[1024,128]{1,0:T(8,128)(2,1)S(1)}, bf16[1024,128]{1,0:T(8,128)(2,1)S(1)}, u32[]{:S(2)}, u32[]{:S(2)}) collective-permute-start(bf16[1024,128]{1,0:T(8,128)(2,1)S(1)} %add.11), channel_id=1, source_target_pairs={{0,1},{1,0},{2,3},{3,2},{4,5},{5,4},{6,7},{7,6},{8,9},{9,8},{10,11... | collective-permute-start | bytes 786440 | tf_op jit(solution)/shard_map/ppermute | solution.py:524
  44.3 5.1 %leaving_rows.3 = (bf16[1024,128]{1,0:T(8,128)(2,1)S(1)}, bf16[1024,128]{1,0:T(8,128)(2,1)S(1)}, bf16[1024,128]{1,0:T(8,128)(2,1)S(1)}, bf16[1024,128]{1,0:T(8,128)(2,1)S(1)}, bf16[2048,128]{1,0:T(8,128)(2,1)S(1)}) custom-call(s32[82]{0:T(128)S(1)} %pad_add_fusion.meta_ref, bf16[64,2048]{1,0:T(8,128)(2,1)S(1)} %collective-permute-done.4.a_ref, ...), custom_call_target="tpu_custom_call" | custom-call | flops 1 | bytes 1 | tf_op jit(solution)/shard_map/leaving_rows/pallas_call | solution.py:402
  49.4 0.0 collective-permute-done.8.x1_ref
  49.4 0.0 collective-permute-done.9.y1_ref
  49.5 0.6 collective-permute-start.17
  50.0 0.8 %collective-permute-start.15 = (bf16[1024,128]{1,0:T(8,128)(2,1)S(1)}, bf16[1024,128]{1,0:T(8,128)(2,1)S(1)}, u32[]{:S(2)}, u32[]{:S(2)}) collective-permute-start(bf16[1024,128]{1,0:T(8,128)(2,1)S(1)} %get-tuple-element.108), channel_id=1, source_target_pairs={{0,1},{1,0},{2,3},{3,2},{4,5},{5,4},{6,7},{7,6},{8,9},{9,8},{10,11... | collective-permute-start | bytes 786440 | tf_op jit(solution)/shard_map/ppermute | solution.py:524
  50.8 1.3 %collective-permute-start.13 = (bf16[1024,128]{1,0:T(8,128)(2,1)S(1)}, bf16[1024,128]{1,0:T(8,128)(2,1)S(1)}, u32[]{:S(2)}, u32[]{:S(2)}) collective-permute-start(bf16[1024,128]{1,0:T(8,128)(2,1)S(1)} %get-tuple-element.104), channel_id=1, source_target_pairs={{0,1},{1,0},{2,3},{3,2},{4,5},{5,4},{6,7},{7,6},{8,9},{9,8},{10,11... | collective-permute-start | bytes 786440 | tf_op jit(solution)/shard_map/ppermute | solution.py:524
  52.1 2.3 %keep_rows.1 = (bf16[2048,128]{1,0:T(8,128)(2,1)S(1)}, bf16[2048,128]{1,0:T(8,128)(2,1)S(1)}) custom-call(bf16[2048,128]{1,0:T(8,128)(2,1)S(1)} %get-tuple-element.74.joined_ref.first_ref, bf16[2048,128]{1,0:T(8,128)(2,1)S(1)} %get-tuple-element.106.second_ref.joined_ref, bf16[1024,2048]{1,0:T(8,128)(2,1)S(1)} %get-tuple-element.85.w0_ref, ...), custom_call_target="tpu_custom_call" | custom-call | flops 1 | bytes 1 | tf_op jit(solution)/shard_map/keep_rows/pallas_call | solution.py:402
  54.4 0.0 collective-permute-done.10.y2_ref
  54.4 1.6 %collective-permute-start.14 = (bf16[1024,128]{1,0:T(8,128)(2,1)S(1)}, bf16[1024,128]{1,0:T(8,128)(2,1)S(1)}, u32[]{:S(2)}, u32[]{:S(2)}) collective-permute-start(bf16[1024,128]{1,0:T(8,128)(2,1)S(1)} %get-tuple-element.105), channel_id=1, source_target_pairs={{0,2},{1,3},{2,0},{3,1},{4,6},{5,7},{6,4},{7,5},{8,10},{9,11},{10,... | collective-permute-start | bytes 786440 | tf_op jit(solution)/shard_map/ppermute | solution.py:524
  56.0 0.0 collective-permute-done.11.x2_ref
  56.0 0.8 %finish.3 = (bf16[2048,128]{1,0:T(8,128)(2,1)S(1)}, bf16[1024,128]{1,0:T(8,128)(2,1)S(1)}) custom-call(s32[82]{0:T(128)S(1)} %pad_add_fusion.meta_ref, bf16[2048,128]{1,0:T(8,128)(2,1)S(1)} %get-tuple-element.87.keep_ref, bf16[1024,128]{1,0:T(8,128)(2,1)S(1)} %collective-permute-done.8.x1_ref, bf16[1024,128]{1,0:T(8,128)(2,1)S(1)} %collective-permute-done.9.y1_ref, ...), custom_call_target="tpu_custom_call" | custom-call | flops 1 | bytes 1 | tf_op jit(solution)/shard_map/finish/pallas_call | solution.py:511
  56.8 0.1 collective-permute-start.12
  56.8 2.3 %pass_rows.3 = (bf16[1024,128]{1,0:T(8,128)(2,1)S(1)}, bf16[1024,128]{1,0:T(8,128)(2,1)S(1)}) custom-call(bf16[2048,128]{1,0:T(8,128)(2,1)S(1)} %get-tuple-element.106.second_ref.joined_ref, bf16[1024,2048]{1,0:T(8,128)(2,1)S(1)} %get-tuple-element.75.w0_ref, bf16[1024,2048]{1,0:T(8,128)(2,1)S(1)} %get-tuple-element.76.w1_ref), custom_call_target="tpu_custom_call" | custom-call | flops 1 | bytes 1 | tf_op jit(solution)/shard_map/pass_rows/pallas_call | solution.py:402
  59.2 0.0 collective-permute-done.17.b_ref
  59.2 0.1 add.13
  59.3 0.8 %collective-permute-start.18 = (bf16[1024,128]{1,0:T(8,128)(2,1)S(1)}, bf16[1024,128]{1,0:T(8,128)(2,1)S(1)}, u32[]{:S(2)}, u32[]{:S(2)}) collective-permute-start(bf16[1024,128]{1,0:T(8,128)(2,1)S(1)} %add.13), channel_id=1, source_target_pairs={{0,1},{1,0},{2,3},{3,2},{4,5},{5,4},{6,7},{7,6},{8,9},{9,8},{10,11... | collective-permute-start | bytes 786440 | tf_op jit(solution)/shard_map/ppermute | solution.py:524
  60.1 0.0 collective-permute-done.15.b_ref
  60.1 0.1 add.12
  60.1 0.8 %collective-permute-start.16 = (bf16[1024,128]{1,0:T(8,128)(2,1)S(1)}, bf16[1024,128]{1,0:T(8,128)(2,1)S(1)}, u32[]{:S(2)}, u32[]{:S(2)}) collective-permute-start(bf16[1024,128]{1,0:T(8,128)(2,1)S(1)} %add.12), channel_id=1, source_target_pairs={{0,2},{1,3},{2,0},{3,1},{4,6},{5,7},{6,4},{7,5},{8,10},{9,11},{10,... | collective-permute-start | bytes 786440 | tf_op jit(solution)/shard_map/ppermute | solution.py:524
  60.9 6.3 %collective-permute-done.12.away_ref = bf16[1024,128]{1,0:T(8,128)(2,1)S(1)} collective-permute-done((bf16[1024,128]{1,0:T(8,128)(2,1)S(1)}, bf16[1024,128]{1,0:T(8,128)(2,1)S(1)}, u32[]{:S(2)}, u32[]{:S(2)}) %collective-permute-start.12) | collective-permute-done | bytes 262176 | tf_op jit(solution)/shard_map/ppermute | solution.py:524
  67.2 0.7 finish.4.away_ref
  67.9 0.0 collective-permute-done.13.x1_ref
  67.9 0.0 collective-permute-done.14.y1_ref
  67.9 0.7 finish.5.sum_ref
  68.6 0.0 collective-permute-done.18.x2_ref
  68.6 0.0 collective-permute-done.16.y2_ref
  68.6 1.7 %finish_second.1 = bf16[2048,256]{1,0:T(8,128)(2,1)} custom-call(s32[82]{0:T(128)S(1)} %pad_add_fusion.meta_ref, bf16[2048,128]{1,0:T(8,128)(2,1)S(1)} %get-tuple-element.98.first_ref, bf16[2048,128]{1,0:T(8,128)(2,1)S(1)} %finish.4.away_ref, f32[2048,128]{1,0:T(8,128)S(1)} %finish.5.sum_ref, bf16[1024,128]{1,0:T(8,128)(2,1)S(1)} %collective-permute-done.16.y2_ref, ...), custom_call_target="tpu_custom_call" | custom-call | flops 1 | bytes 1 | tf_op jit(solution)/shard_map/finish_second/pallas_call | solution.py:498
Async XLA Ops:
  1.0 13.4 %collective-permute-start.2 = (bf16[512,256]{1,0:T(8,128)(2,1)S(1)}, bf16[512,256]{1,0:T(8,128)(2,1)S(1)}, u32[]{:S(2)}, u32[]{:S(2)}) collective-permute-start(bf16[512,256]{1,0:T(8,128)(2,1)S(1)} %join_keys_values.1.kv0_ref), channel_id=1, source_target_pairs={{0,8},{4,12},{8,16},{12,20},{16,24},{20,28},{1,9},{5,13},{9,17},{1... | collective-permute-start | bytes 786440 | tf_op jit(solution)/shard_map/ppermute | solution.py:532
  9.8 4.8 %collective-permute-start = (bf16[128,2048]{1,0:T(8,128)(2,1)S(1)}, bf16[128,2048]{1,0:T(8,128)(2,1)S(1)}, u32[]{:S(2)}, u32[]{:S(2)}) collective-permute-start(bf16[128,2048]{1,0:T(8,128)(2,1)S(1)} %get-tuple-element.59), channel_id=1, source_target_pairs={{0,4},{4,0},{8,12},{12,8},{16,20},{20,16},{24,28},{28,24},{1,5},{5... | collective-permute-start | bytes 1572872 | tf_op jit(solution)/shard_map/ppermute | solution.py:524
  9.9 4.7 %collective-permute-start.1 = (bf16[512,256]{1,0:T(8,128)(2,1)S(1)}, bf16[512,256]{1,0:T(8,128)(2,1)S(1)}, u32[]{:S(2)}, u32[]{:S(2)}) collective-permute-start(bf16[512,256]{1,0:T(8,128)(2,1)S(1)} %join_keys_values.1.kv0_ref), channel_id=1, source_target_pairs={{0,4},{4,0},{8,12},{12,8},{16,20},{20,16},{24,28},{28,24},{1,5},{5... | collective-permute-start | bytes 786440 | tf_op jit(solution)/shard_map/ppermute | solution.py:524
  14.4 1.6 %collective-permute-start.3 = (bf16[512,256]{1,0:T(8,128)(2,1)S(1)}, bf16[512,256]{1,0:T(8,128)(2,1)S(1)}, u32[]{:S(2)}, u32[]{:S(2)}) collective-permute-start(bf16[512,256]{1,0:T(8,128)(2,1)S(1)} %collective-permute-done.2.kv2_ref), channel_id=1, source_target_pairs={{0,4},{4,0},{8,12},{12,8},{16,20},{20,16},{24,28},{28,24},{1,5},{5... | collective-permute-start | bytes 786440 | tf_op jit(solution)/shard_map/ppermute | solution.py:524
  21.4 12.8 %collective-permute-start.4 = (bf16[64,2048]{1,0:T(8,128)(2,1)S(1)}, bf16[64,2048]{1,0:T(8,128)(2,1)S(1)}, u32[]{:S(2)}, u32[]{:S(2)}) collective-permute-start(bf16[64,2048]{1,0:T(8,128)(2,1)S(1)} %get-tuple-element.72), channel_id=1, source_target_pairs={{0,8},{4,12},{8,0},{12,4},{16,24},{20,28},{24,16},{28,20},{1,9},{5... | collective-permute-start | bytes 786440 | tf_op jit(solution)/shard_map/ppermute | solution.py:524
  23.0 15.8 %collective-permute-start.5 = (bf16[64,2048]{1,0:T(8,128)(2,1)S(1)}, bf16[64,2048]{1,0:T(8,128)(2,1)S(1)}, u32[]{:S(2)}, u32[]{:S(2)}) collective-permute-start(bf16[64,2048]{1,0:T(8,128)(2,1)S(1)} %get-tuple-element.73), channel_id=1, source_target_pairs={{0,24},{4,28},{8,16},{12,20},{16,8},{20,12},{24,0},{28,4},{1,25},{... | collective-permute-start | bytes 786440 | tf_op jit(solution)/shard_map/ppermute | solution.py:524
  30.6 10.5 %collective-permute-start.6 = (bf16[1024,128]{1,0:T(8,128)(2,1)S(1)}, bf16[1024,128]{1,0:T(8,128)(2,1)S(1)}, u32[]{:S(2)}, u32[]{:S(2)}) collective-permute-start(bf16[1024,128]{1,0:T(8,128)(2,1)S(1)} %get-tuple-element.78), channel_id=1, source_target_pairs={{0,1},{1,0},{2,3},{3,2},{4,5},{5,4},{6,7},{7,6},{8,9},{9,8},{10,11... | collective-permute-start | bytes 786440 | tf_op jit(solution)/shard_map/ppermute | solution.py:524
  32.1 9.2 %collective-permute-start.7 = (bf16[1024,128]{1,0:T(8,128)(2,1)S(1)}, bf16[1024,128]{1,0:T(8,128)(2,1)S(1)}, u32[]{:S(2)}, u32[]{:S(2)}) collective-permute-start(bf16[1024,128]{1,0:T(8,128)(2,1)S(1)} %get-tuple-element.80), channel_id=1, source_target_pairs={{0,2},{1,3},{2,0},{3,1},{4,6},{5,7},{6,4},{7,5},{8,10},{9,11},{10,... | collective-permute-start | bytes 786440 | tf_op jit(solution)/shard_map/ppermute | solution.py:524
  33.7 15.8 %collective-permute-start.8 = (bf16[1024,128]{1,0:T(8,128)(2,1)S(1)}, bf16[1024,128]{1,0:T(8,128)(2,1)S(1)}, u32[]{:S(2)}, u32[]{:S(2)}) collective-permute-start(bf16[1024,128]{1,0:T(8,128)(2,1)S(1)} %get-tuple-element.92), channel_id=1, source_target_pairs={{0,1},{1,0},{2,3},{3,2},{4,5},{5,4},{6,7},{7,6},{8,9},{9,8},{10,11... | collective-permute-start | bytes 786440 | tf_op jit(solution)/shard_map/ppermute | solution.py:524
  34.2 15.2 %collective-permute-start.9 = (bf16[1024,128]{1,0:T(8,128)(2,1)S(1)}, bf16[1024,128]{1,0:T(8,128)(2,1)S(1)}, u32[]{:S(2)}, u32[]{:S(2)}) collective-permute-start(bf16[1024,128]{1,0:T(8,128)(2,1)S(1)} %get-tuple-element.93), channel_id=1, source_target_pairs={{0,2},{1,3},{2,0},{3,1},{4,6},{5,7},{6,4},{7,5},{8,10},{9,11},{10,... | collective-permute-start | bytes 786440 | tf_op jit(solution)/shard_map/ppermute | solution.py:524
  41.5 12.9 %collective-permute-start.10 = (bf16[1024,128]{1,0:T(8,128)(2,1)S(1)}, bf16[1024,128]{1,0:T(8,128)(2,1)S(1)}, u32[]{:S(2)}, u32[]{:S(2)}) collective-permute-start(bf16[1024,128]{1,0:T(8,128)(2,1)S(1)} %add.10), channel_id=1, source_target_pairs={{0,2},{1,3},{2,0},{3,1},{4,6},{5,7},{6,4},{7,5},{8,10},{9,11},{10,... | collective-permute-start | bytes 786440 | tf_op jit(solution)/shard_map/ppermute | solution.py:524
  43.0 12.9 %collective-permute-start.11 = (bf16[1024,128]{1,0:T(8,128)(2,1)S(1)}, bf16[1024,128]{1,0:T(8,128)(2,1)S(1)}, u32[]{:S(2)}, u32[]{:S(2)}) collective-permute-start(bf16[1024,128]{1,0:T(8,128)(2,1)S(1)} %add.11), channel_id=1, source_target_pairs={{0,1},{1,0},{2,3},{3,2},{4,5},{5,4},{6,7},{7,6},{8,9},{9,8},{10,11... | collective-permute-start | bytes 786440 | tf_op jit(solution)/shard_map/ppermute | solution.py:524
  49.5 9.7 %collective-permute-start.17 = (bf16[1024,128]{1,0:T(8,128)(2,1)S(1)}, bf16[1024,128]{1,0:T(8,128)(2,1)S(1)}, u32[]{:S(2)}, u32[]{:S(2)}) collective-permute-start(bf16[1024,128]{1,0:T(8,128)(2,1)S(1)} %get-tuple-element.110), channel_id=1, source_target_pairs={{0,2},{1,3},{2,0},{3,1},{4,6},{5,7},{6,4},{7,5},{8,10},{9,11},{10,... | collective-permute-start | bytes 786440 | tf_op jit(solution)/shard_map/ppermute | solution.py:524
  50.0 10.1 %collective-permute-start.15 = (bf16[1024,128]{1,0:T(8,128)(2,1)S(1)}, bf16[1024,128]{1,0:T(8,128)(2,1)S(1)}, u32[]{:S(2)}, u32[]{:S(2)}) collective-permute-start(bf16[1024,128]{1,0:T(8,128)(2,1)S(1)} %get-tuple-element.108), channel_id=1, source_target_pairs={{0,1},{1,0},{2,3},{3,2},{4,5},{5,4},{6,7},{7,6},{8,9},{9,8},{10,11... | collective-permute-start | bytes 786440 | tf_op jit(solution)/shard_map/ppermute | solution.py:524
  50.8 17.1 %collective-permute-start.13 = (bf16[1024,128]{1,0:T(8,128)(2,1)S(1)}, bf16[1024,128]{1,0:T(8,128)(2,1)S(1)}, u32[]{:S(2)}, u32[]{:S(2)}) collective-permute-start(bf16[1024,128]{1,0:T(8,128)(2,1)S(1)} %get-tuple-element.104), channel_id=1, source_target_pairs={{0,1},{1,0},{2,3},{3,2},{4,5},{5,4},{6,7},{7,6},{8,9},{9,8},{10,11... | collective-permute-start | bytes 786440 | tf_op jit(solution)/shard_map/ppermute | solution.py:524
  54.4 13.5 %collective-permute-start.14 = (bf16[1024,128]{1,0:T(8,128)(2,1)S(1)}, bf16[1024,128]{1,0:T(8,128)(2,1)S(1)}, u32[]{:S(2)}, u32[]{:S(2)}) collective-permute-start(bf16[1024,128]{1,0:T(8,128)(2,1)S(1)} %get-tuple-element.105), channel_id=1, source_target_pairs={{0,2},{1,3},{2,0},{3,1},{4,6},{5,7},{6,4},{7,5},{8,10},{9,11},{10,... | collective-permute-start | bytes 786440 | tf_op jit(solution)/shard_map/ppermute | solution.py:524
  56.8 10.5 %collective-permute-start.12 = (bf16[1024,128]{1,0:T(8,128)(2,1)S(1)}, bf16[1024,128]{1,0:T(8,128)(2,1)S(1)}, u32[]{:S(2)}, u32[]{:S(2)}) collective-permute-start(bf16[1024,128]{1,0:T(8,128)(2,1)S(1)} %get-tuple-element.100), channel_id=1, source_target_pairs={{0,16},{4,20},{8,24},{12,28},{16,0},{20,4},{24,8},{28,12},{1,17},{... | collective-permute-start | bytes 786440 | tf_op jit(solution)/shard_map/ppermute | solution.py:524
  59.3 9.4 %collective-permute-start.18 = (bf16[1024,128]{1,0:T(8,128)(2,1)S(1)}, bf16[1024,128]{1,0:T(8,128)(2,1)S(1)}, u32[]{:S(2)}, u32[]{:S(2)}) collective-permute-start(bf16[1024,128]{1,0:T(8,128)(2,1)S(1)} %add.13), channel_id=1, source_target_pairs={{0,1},{1,0},{2,3},{3,2},{4,5},{5,4},{6,7},{7,6},{8,9},{9,8},{10,11... | collective-permute-start | bytes 786440 | tf_op jit(solution)/shard_map/ppermute | solution.py:524
  60.1 8.5 %collective-permute-start.16 = (bf16[1024,128]{1,0:T(8,128)(2,1)S(1)}, bf16[1024,128]{1,0:T(8,128)(2,1)S(1)}, u32[]{:S(2)}, u32[]{:S(2)}) collective-permute-start(bf16[1024,128]{1,0:T(8,128)(2,1)S(1)} %add.12), channel_id=1, source_target_pairs={{0,2},{1,3},{2,0},{3,1},{4,6},{5,7},{6,4},{7,5},{8,10},{9,11},{10,... | collective-permute-start | bytes 786440 | tf_op jit(solution)/shard_map/ppermute | solution.py:524

commit v7 on v6

--- a/solution.py
+++ b/solution.py
@@ -123,13 +123,18 @@
 HBM = pl.BlockSpec(memory_space=pltpu.HBM)
 
 
-OWNERS_AT = 2
+def _own_ctx():
+    return lax.axis_index("ctx")
+
+
+def _own_z():
+    return lax.div(_own_ctx(), 2)
 
 
 def _find_piece(table_ref, source, owner):
     piece = jnp.int32(0)
     for i in range(PIECES):
-        piece = jnp.where(table_ref[OWNERS_AT + source * PIECES + i] == owner, jnp.int32(i), piece)
+        piece = jnp.where(table_ref[source * PIECES + i] == owner, jnp.int32(i), piece)
     return piece
 
 
@@ -164,13 +169,13 @@
 
 def _queries_for_other_core_kernel(names, meta_ref, queries_ref, w_ref, out_ref, kept_ref, *rest):
     *w_out, sem, w_sems = rest
-    w_copies = _weight_copies(names, meta_ref, w_ref, w_out, w_sems)
+    w_copies = _weight_copies(names, w_ref, w_out, w_sems)
     copy = pltpu.make_async_copy(queries_ref, kept_ref, sem)
     copy.start()
     for w_copy in w_copies:
         w_copy.start()
     copy.wait()
-    c = meta_ref[0]
+    c = _own_ctx()
     core = lax.rem(c, 2)
     rows = queries_ref.shape[0] // PIECES
     for j in range(PIECES // 2):
@@ -201,12 +206,12 @@
 }
 
 
-def _weight_copies(names, meta_ref, w_ref, out_refs, sems):
+def _weight_copies(names, w_ref, out_refs, sems):
     half = w_ref.shape[0] // (2 * N_FAST_HEAD)
     copies = []
     for n, name in enumerate(names):
         flip, side = EIGHTHS[name]
-        row = (meta_ref[1] ^ flip) * (2 * half) + side * half
+        row = (lax.axis_index("head") ^ flip) * (2 * half) + side * half
         copies.append(pltpu.make_async_copy(w_ref.at[_rows(row, half)], out_refs[n], sems.at[n]))
     return copies
 
@@ -215,25 +220,25 @@
     return jax.ShapeDtypeStruct((out_weight.shape[0] // (2 * N_FAST_HEAD), out_weight.shape[1]), out_weight.dtype)
 
 
-def _stage_kernel(names, meta_ref, w_ref, *rest):
-    copies = _weight_copies(names, meta_ref, w_ref, rest[:-1], rest[-1])
+def _stage_kernel(names, w_ref, after_ref, *rest):
+    copies = _weight_copies(names, w_ref, rest[:-1], rest[-1])
     for copy in copies:
         copy.start()
     for copy in copies:
         copy.wait()
 
 
-def _stage_weights(names, meta, out_weight):
+def _stage_weights(names, out_weight, after):
     return pl.pallas_call(
         functools.partial(_stage_kernel, names),
         out_shape=[_eighth(out_weight) for _ in names],
-        in_specs=[SMEM, HBM],
+        in_specs=[HBM, VMEM],
         out_specs=[VMEM] * len(names),
         scratch_shapes=[pltpu.SemaphoreType.DMA((len(names),))],
         compiler_params=pltpu.CompilerParams(vmem_limit_bytes=8 * 2**20),
         cost_estimate=pl.CostEstimate(flops=1, bytes_accessed=1, transcendentals=0),
         name="stage_weights",
-    )(meta, out_weight)
+    )(out_weight, after)
 
 
 def _attend_kernel(
@@ -244,10 +249,10 @@
     count = len(groups)
     out_refs, w_out = rest[:count], rest[count:count + len(names)]
     kbuf, vbuf, qbuf, ctxbuf, w_sems = rest[count + len(names):]
-    w_copies = _weight_copies(names, meta_ref, w_ref, w_out, w_sems)
+    w_copies = _weight_copies(names, w_ref, w_out, w_sems)
     for copy in w_copies:
         copy.start()
-    c = meta_ref[0]
+    c = _own_ctx()
     core = lax.rem(c, 2)
     z = lax.div(c, 2)
     rows = kv0_ref.shape[0] // 2
@@ -275,7 +280,7 @@
         starts.append((at0 * piece_rows, rows + at1 * piece_rows))
     doc_start = []
     running = jnp.int32(0)
-    lengths_at = OWNERS_AT + PIECES * PIECES
+    lengths_at = PIECES * PIECES
     for d in range(lengths_at, meta_ref.shape[0]):
         doc_start.append(running)
         running = running + meta_ref[d]
@@ -371,19 +376,18 @@
     out_ref[...] = jnp.dot(weight_ref[...], tokens, preferred_element_type=jnp.float32).astype(out_ref.dtype)
 
 
-def _leaving_rows_kernel(meta_ref, a_ref, b_ref, *rest):
-    w_refs, out_refs, (joined_ref, catbuf) = rest[:4], rest[4:8], rest[8:]
-    second = lax.rem(lax.div(meta_ref[0], 2), 2)
+def _join_kernel(a_ref, b_ref, wx_ref, wy_ref, x_ref, y_ref, joined_ref, catbuf):
+    second = lax.rem(_own_z(), 2)
     mid = a_ref.shape[0]
     catbuf[_rows(second * mid, mid)] = a_ref[...]
     catbuf[_rows((1 - second) * mid, mid)] = b_ref[...]
     joined = catbuf[...].T
     joined_ref[...] = joined
-    for w_ref, out_ref in zip(w_refs, out_refs):
-        _dot_to(out_ref, w_ref, joined)
-
-
-def _pass_rows_kernel(joined_ref, w0_ref, w1_ref, out0_ref, out1_ref):
+    _dot_to(x_ref, wx_ref, joined)
+    _dot_to(y_ref, wy_ref, joined)
+
+
+def _two_rows_kernel(joined_ref, w0_ref, w1_ref, out0_ref, out1_ref):
     joined = joined_ref[...]
     _dot_to(out0_ref, w0_ref, joined)
     _dot_to(out1_ref, w1_ref, joined)
@@ -398,31 +402,30 @@
         second_out[i * half:(i + 1) * half] = out[:, tokens:]
 
 
-def _project(kernel, name, out_shape, operands, scratch=(), scalars=()):
+def _project(kernel, name, out_shape, operands, scratch=()):
     return pl.pallas_call(
         kernel,
         out_shape=out_shape,
-        in_specs=[SMEM] * len(scalars) + [VMEM] * len(operands),
+        in_specs=[VMEM] * len(operands),
         out_specs=[VMEM] * len(out_shape),
         scratch_shapes=scratch,
         compiler_params=pltpu.CompilerParams(vmem_limit_bytes=8 * 2**20),
         cost_estimate=pl.CostEstimate(flops=1, bytes_accessed=1, transcendentals=0),
         name=name,
-    )(*scalars, *operands)
-
-
-def _leaving_rows(meta, a, b, weights):
-    (rows, depth), tokens = weights["xf"].shape, a.shape[0] + b.shape[0]
+    )(*operands)
+
+
+def _join(a, b, weights):
+    (rows, depth), tokens = weights["xp"].shape, a.shape[0] + b.shape[0]
     part = jax.ShapeDtypeStruct((rows, tokens), jnp.bfloat16)
     return _project(
-        _leaving_rows_kernel, "leaving_rows", [part] * 4 + [jax.ShapeDtypeStruct((depth, tokens), jnp.bfloat16)],
-        (a, b) + tuple(weights[name] for name in ("xf", "xp", "yf", "yp")),
-        [pltpu.VMEM((tokens, depth), jnp.bfloat16)], (meta,))
-
-
-def _pass_rows(joined, weights):
-    part = jax.ShapeDtypeStruct((weights["py"].shape[0], joined.shape[1]), jnp.bfloat16)
-    return _project(_pass_rows_kernel, "pass_rows", [part] * 2, (joined, weights["py"], weights["px"]))
+        _join_kernel, "join", [part] * 2 + [jax.ShapeDtypeStruct((depth, tokens), jnp.bfloat16)],
+        (a, b, weights["xp"], weights["yp"]), [pltpu.VMEM((tokens, depth), jnp.bfloat16)])
+
+
+def _two_rows(name, joined, weights, names):
+    part = jax.ShapeDtypeStruct((weights[names[0]].shape[0], joined.shape[1]), jnp.bfloat16)
+    return _project(_two_rows_kernel, name, [part] * 2, (joined, weights[names[0]], weights[names[1]]))
 
 
 def _keep_rows(first, second, weights):
@@ -446,44 +449,46 @@
     return first, second
 
 
-def _own_half(meta_ref, rows, tokens):
+def _own_half(rows, tokens):
     lane = lax.broadcasted_iota(jnp.int32, (rows, tokens), 1)
-    return lax.div(lane, tokens // 2) == lax.rem(lax.div(meta_ref[0], 2), 2)
-
-
-def _finish_first_kernel(meta_ref, keep_ref, x1_ref, y1_ref, y2_ref, x2_ref, out_ref, away_ref):
+    return lax.div(lane, tokens // 2) == lax.rem(_own_z(), 2)
+
+
+def _finish_first_kernel(keep_ref, x1_ref, y1_ref, y2_ref, x2_ref, out_ref, away_ref):
     half, tokens = y2_ref.shape
     top, bottom = _sum_parts(keep_ref, x1_ref, y1_ref, y2_ref, x2_ref)
     out_ref[:half] = top.astype(out_ref.dtype)
     out_ref[half:] = bottom.astype(out_ref.dtype)
-    own = _own_half(meta_ref, half, tokens)
+    own = _own_half(half, tokens)
     away_ref[...] = jnp.where(own, pltpu.roll(bottom, tokens // 2, 1), top).astype(away_ref.dtype)
 
 
-def _unpack_kernel(meta_ref, away_ref, out_ref):
+def _unpack_kernel(away_ref, out_ref):
     half, tokens = away_ref.shape
     out_ref[:half] = pltpu.roll(away_ref[...].astype(jnp.float32), tokens // 2, 1).astype(out_ref.dtype)
     out_ref[half:] = away_ref[...]
 
 
-def _sum_first_step_kernel(meta_ref, keep_ref, x1_ref, y1_ref, out_ref):
-    half = x1_ref.shape[0]
-    for i, one_ref in enumerate((x1_ref, y1_ref)):
-        at = pl.ds(i * half, half)
-        out_ref[at] = keep_ref[at].astype(jnp.float32) + one_ref[...].astype(jnp.float32)
-
-
-def _finish_second_kernel(meta_ref, first_ref, away_ref, sum_ref, y2_ref, x2_ref, out_ref, rows_ref, sems):
+def _half_sum_kernel(side, keep_ref, one_ref, out_ref):
+    half = one_ref.shape[0]
+    out_ref[...] = keep_ref[side * half:(side + 1) * half].astype(jnp.float32) + one_ref[...].astype(jnp.float32)
+
+
+def _half_sum(side, keep, one):
+    return _finish(functools.partial(_half_sum_kernel, side), [jax.ShapeDtypeStruct(one.shape, jnp.float32)], (keep, one))[0]
+
+
+def _finish_second_kernel(first_ref, away_ref, top_ref, bottom_ref, y2_ref, x2_ref, out_ref, rows_ref, sems):
     half, tokens = y2_ref.shape
     part = half // 2
-    upper = lax.div(meta_ref[0], 4)
+    upper = lax.div(_own_z(), 2)
     mine, others = _rows(upper * tokens, tokens), _rows((1 - upper) * tokens, tokens)
-    own = _own_half(meta_ref, part, tokens)
+    own = _own_half(part, tokens)
     copies = []
     for i in range(4):
         at, inside = pl.ds(i * part, part), pl.ds(i % 2 * part, part)
-        two_ref = y2_ref if i < 2 else x2_ref
-        sums = sum_ref[at] + two_ref[inside].astype(jnp.float32)
+        one_ref, two_ref = (top_ref, y2_ref) if i < 2 else (bottom_ref, x2_ref)
+        sums = one_ref[inside] + two_ref[inside].astype(jnp.float32)
         first, away = first_ref[at].astype(jnp.float32), away_ref[at].astype(jnp.float32)
         rows_ref[at, mine] = jnp.where(own, first, pltpu.roll(sums, tokens // 2, 1)).astype(rows_ref.dtype)
         rows_ref[at, others] = jnp.where(own, away, sums).astype(rows_ref.dtype)
@@ -493,25 +498,25 @@
         copy.wait()
 
 
-def _finish_second(meta, first, away, summed, y2, x2):
-    rows, tokens = summed.shape
+def _finish_second(first, away, top, bottom, y2, x2):
+    rows, tokens = first.shape
     return pl.pallas_call(
         _finish_second_kernel,
         out_shape=jax.ShapeDtypeStruct((rows, 2 * tokens), jnp.bfloat16),
-        in_specs=[SMEM] + [VMEM] * 5,
+        in_specs=[VMEM] * 6,
         out_specs=HBM,
         scratch_shapes=[pltpu.VMEM((rows, 2 * tokens), jnp.bfloat16), pltpu.SemaphoreType.DMA((4,))],
         compiler_params=pltpu.CompilerParams(vmem_limit_bytes=8 * 2**20),
         cost_estimate=pl.CostEstimate(flops=1, bytes_accessed=1, transcendentals=0),
         name="finish_second",
-    )(meta, first, away, summed, y2, x2)
+    )(first, away, top, bottom, y2, x2)
 
 
 def _finish(kernel, out_shape, operands):
     return pl.pallas_call(
         kernel,
         out_shape=out_shape,
-        in_specs=[SMEM] + [VMEM] * (len(operands) - 1),
+        in_specs=[VMEM] * len(operands),
         out_specs=jax.tree.map(lambda _: VMEM, out_shape),
         compiler_params=pltpu.CompilerParams(vmem_limit_bytes=8 * 2**20),
         cost_estimate=pl.CostEstimate(flops=1, bytes_accessed=1, transcendentals=0),
@@ -531,13 +536,11 @@
     kv0 = _join_keys_values(keys, values)
     kv2 = lax.ppermute(kv0, "ctx", [(i, i + 2) for i in range(places - 2)])
     kv1 = _flip(kv0, "ctx", 1)
-    meta = jnp.concatenate([
-        lax.axis_index("ctx").reshape(1), lax.axis_index("head").reshape(1), owners.reshape(-1), doc_lengths,
-    ]).astype(jnp.int32)
+    meta = jnp.concatenate([owners.reshape(-1), doc_lengths])
     weights = {}
     leaving, queries, weights["xp"] = _queries_for_other_core(("xp",), meta, queries, out_weight)
     other = _flip(leaving, "ctx", 1)
-    weights["yp"], weights["xf"] = _stage_weights(("yp", "xf"), meta, out_weight)
+    weights["yp"], weights["xf"] = _stage_weights(("yp", "xf"), out_weight, leaving)
     kv2, weights["xf"] = lax.optimization_barrier((kv2, weights["xf"]))
     kv = (kv0, kv1, kv2, _flip(kv2, "ctx", 1))
     loaded = ("yf", "py", "px")
@@ -545,36 +548,39 @@
     weights.update(zip(loaded, loads))
     ctx1, ctx3 = _flip(ctx1, "ctx", 2), _flip(ctx3, "ctx", 6)
 
-    xf, xp, yf, yp, joined = _leaving_rows(meta, ctx0, ctx2, weights)
-    x1f, x1p, y1f, y1p = _flip(xf, "head", 1), _flip(xp, "head", 1), _flip(yf, "head", 2), _flip(yp, "head", 2)
-    later_meta, joined = lax.optimization_barrier((meta, joined))
-    weights["k0"], weights["k1"] = _stage_weights(("k0", "k1"), later_meta, out_weight)
+    xp, yp, joined = _join(ctx0, ctx2, weights)
+    x1p, y1p = _flip(xp, "head", 1), _flip(yp, "head", 2)
+    xf, yf = _two_rows("last_rows", joined, weights, ("xf", "yf"))
+    x1f, y1f = _flip(xf, "head", 1), _flip(yf, "head", 2)
+    weights["k0"], weights["k1"] = _stage_weights(("k0", "k1"), out_weight, joined)
     joined, weights["k0"], ctx1, ctx3 = lax.optimization_barrier((joined, weights["k0"], ctx1, ctx3))
-    y2, x2 = _pass_rows(joined, weights)
+    y2, x2 = _two_rows("pass_rows", joined, weights, ("py", "px"))
     y2, x2 = _add(y2, x1p), _add(x2, y1p)
-    meta, y2, x2 = lax.optimization_barrier((meta, y2, x2))
+    weights["xp"], y2, x2 = lax.optimization_barrier((weights["xp"], y2, x2))
     y2, x2 = _flip(y2, "head", 2), _flip(x2, "head", 1)
 
-    xf, xp, yf, yp, joined2 = _leaving_rows(meta, ctx1, ctx3, weights)
-    xf, xp, yf, yp, x1f, y1f = lax.optimization_barrier((xf, xp, yf, yp, x1f, y1f))
-    next_x1f, next_x1p = _flip(xf, "head", 1), _flip(xp, "head", 1)
-    next_y1f, next_y1p = _flip(yf, "head", 2), _flip(yp, "head", 2)
+    xp, yp, joined2 = _join(ctx1, ctx3, weights)
+    xp, yp, x1f, y1f = lax.optimization_barrier((xp, yp, x1f, y1f))
+    next_x1p, next_y1p = _flip(xp, "head", 1), _flip(yp, "head", 2)
+    xf, yf = _two_rows("last_rows", joined2, weights, ("xf", "yf"))
+    next_x1f, next_y1f = _flip(xf, "head", 1), _flip(yf, "head", 2)
     keep, next_keep = _keep_rows(joined, joined2, weights)
     rows, tokens = keep.shape
     first, away = _finish(_finish_first_kernel, [
         jax.ShapeDtypeStruct((rows, tokens), jnp.bfloat16),
         jax.ShapeDtypeStruct((rows // 2, tokens), jnp.bfloat16),
-    ], (meta, keep, x1f, y1f, y2, x2))
+    ], (keep, x1f, y1f, y2, x2))
     joined2, away = lax.optimization_barrier((joined2, away))
     away = _flip(away, "ctx", 4)
-    y2, x2 = _pass_rows(joined2, weights)
+    y2, x2 = _two_rows("pass_rows", joined2, weights, ("py", "px"))
     y2, x2 = _add(y2, next_x1p), _add(x2, next_y1p)
     y2, x2 = _flip(y2, "head", 2), _flip(x2, "head", 1)
-    away = _finish(_unpack_kernel, [jax.ShapeDtypeStruct((rows, tokens), jnp.bfloat16)], (meta, away))[0]
+    away = _finish(_unpack_kernel, [jax.ShapeDtypeStruct((rows, tokens), jnp.bfloat16)], (away,))[0]
     away, next_keep = lax.optimization_barrier((away, next_keep))
-    summed = _finish(_sum_first_step_kernel, [jax.ShapeDtypeStruct((rows, tokens), jnp.float32)],
-                     (meta, next_keep, next_x1f, next_y1f))[0]
-    return _finish_second(meta, first, away, summed, y2, x2)
+    bottom = _half_sum(1, next_keep, next_y1f)
+    bottom, next_keep = lax.optimization_barrier((bottom, next_keep))
+    top = _half_sum(0, next_keep, next_x1f)
+    return _finish_second(first, away, top, bottom, y2, x2)
 
 
 def solution(mesh):

time: 70.7 us -> 67.2 us (0.950)
  Pallas kernels: 38.7 us -> 34.7 us
    pallas_call x12 -> x15, Pallas kernels: 19.6 us -> 17.2 us  [the longest x11 16.7 us: _project(): pl.pallas_call(kernel, out_shape=out_shape, in_specs=[VMEM] * len(operand...]
    pallas_call x2, Pallas kernels: 8.05 us -> 6.96 us  [_stage_weights(): pl.pallas_call(functools.partial(_stage_kernel, names), out_shape=[_eight...]
  transfers between devices with their start and end apart: 19 -> 19, of which waited for: 3 -> 5; matrix products, arithmetic and copies ran while one was open for 1% -> 1% of each run, Pallas kernels for 44% -> 40%
where the time goes in v7:
time: 67.2 us; the launch traced here: 67.4 us
  Pallas kernels  34.7 us (52%)
  starting transfers between devices  23 us (34%)
  waiting for transfers between devices  8.56 us (13%)
  other arithmetic  0.75 us (1%)
    ppermute x18, starting transfers between devices, _flip(): return lax.ppermute(x, axis, [(i, i ^ bits) for i in range(n)])  18.1 us
    pallas_call x11, Pallas kernels, _project(): pl.pallas_call(kernel, out_shape=out_shape, in_specs=[VMEM] * len(operand...  16.7 us
    ppermute x18, waiting for transfers between devices, _flip(): return lax.ppermute(x, axis, [(i, i ^ bits) for i in range(n)])  8.56 us
    pallas_call x2, Pallas kernels, _stage_weights(): pl.pallas_call(functools.partial(_stage_kernel, names), out_shape=[_eight...  6.96 us
    pallas_call x1, Pallas kernels, _attend_groups(): pl.pallas_call(functools.partial(_attend_kernel, groups, names), out_shap...  5.36 us
    ppermute x1, starting transfers between devices, per_device_fast(): kv2 = lax.ppermute(kv0, 'ctx', [(i, i + 2) for i in range(places - 2)])  4.94 us
    pallas_call x1, Pallas kernels, _queries_for_other_core(): pl.pallas_call(functools.partial(_queries_for_other_core_kernel, names),...  3.07 us
  transfers between devices with their start and end apart: 19, of which 5 were waited for; matrix products, arithmetic and copies ran while one was open for 1% of the time, Pallas kernels for 40%

profile of v7, /device:TPU:0, one launch (start us, length us, event | category | flops | bytes accessed | tf_op | source)
XLA Modules:
  0.0 67.4 jit_solution(9473395959185141541)
XLA Ops:
  0.0 1.0 %join_keys_values.1.kv0_ref = bf16[512,256]{1,0:T(8,128)(2,1)S(1)} custom-call(bf16[256,256]{1,0:T(8,128)(2,1)} %keys_ref.1, bf16[256,256]{1,0:T(8,128)(2,1)} %values_ref.1), custom_call_target="tpu_custom_call" | custom-call | flops 1 | bytes 1 | tf_op jit(solution)/shard_map/join_keys_values/pallas_call | solution.py:158
  1.0 4.9 %collective-permute-start.2 = (bf16[512,256]{1,0:T(8,128)(2,1)S(1)}, bf16[512,256]{1,0:T(8,128)(2,1)S(1)}, u32[]{:S(2)}, u32[]{:S(2)}) collective-permute-start(bf16[512,256]{1,0:T(8,128)(2,1)S(1)} %join_keys_values.1.kv0_ref), channel_id=1, source_target_pairs={{0,8},{4,12},{8,16},{12,20},{16,24},{20,28},{1,9},{5,13},{9,17},{1... | collective-permute-start | bytes 786440 | tf_op jit(solution)/shard_map/ppermute | solution.py:537
  5.9 0.7 %pad_add_fusion.meta_ref = s32[80]{0:T(128)S(1)} fusion(s32[16]{0:T(128)} %param.10, s32[64]{0:T(128)} %bitcast.1), kind=kLoop, calls=%fused_computation | loop fusion | flops 80 | bytes 640 | tf_op jit(solution)/shard_map/concatenate | solution.py:539
  6.7 3.1 %queries_for_other_core.1 = (bf16[128,2048]{1,0:T(8,128)(2,1)S(1)}, bf16[256,2048]{1,0:T(8,128)(2,1)S(1)}, bf16[1024,2048]{1,0:T(8,128)(2,1)S(1)}) custom-call(s32[80]{0:T(128)S(1)} %pad_add_fusion.meta_ref, bf16[256,2048]{1,0:T(8,128)(2,1)} %queries_ref.1, bf16[8192,2048]{1,0:T(8,128)(2,1)} %w_ref.7), custom_call_target="tpu_custom_call" | custom-call | flops 1 | bytes 1 | tf_op jit(solution)/shard_map/queries_for_other_core/pallas_call | solution.py:189
  9.8 0.1 collective-permute-start
  9.9 0.5 collective-permute-start.1
  10.3 3.5 %stage_weights.2 = (bf16[1024,2048]{1,0:T(8,128)(2,1)S(1)}, bf16[1024,2048]{1,0:T(8,128)(2,1)S(1)}) custom-call(bf16[8192,2048]{1,0:T(8,128)(2,1)} %w_ref.7, bf16[128,2048]{1,0:T(8,128)(2,1)S(1)} %get-tuple-element.57.after_ref), custom_call_target="tpu_custom_call" | custom-call | flops 1 | bytes 1 | tf_op jit(solution)/shard_map/stage_weights/pallas_call | solution.py:232
  13.8 0.0 collective-permute-done.2.kv2_ref
  13.8 0.1 collective-permute-start.3
  14.0 0.0 collective-permute-done.1.kv1_ref
  14.0 0.0 collective-permute-done.other_ref
  14.0 1.5 %collective-permute-done.3.kv3_ref = bf16[512,256]{1,0:T(8,128)(2,1)S(1)} collective-permute-done((bf16[512,256]{1,0:T(8,128)(2,1)S(1)}, bf16[512,256]{1,0:T(8,128)(2,1)S(1)}, u32[]{:S(2)}, u32[]{:S(2)}) %collective-permute-start.3) | collective-permute-done | bytes 262176 | tf_op jit(solution)/shard_map/ppermute | solution.py:529
  15.4 5.4 %attend_groups.1 = (bf16[64,2048]{1,0:T(8,128)(2,1)S(1)}, bf16[64,2048]{1,0:T(8,128)(2,1)S(1)}, bf16[64,2048]{1,0:T(8,128)(2,1)S(1)}, bf16[64,2048]{1,0:T(8,128)...) custom-call(s32[80]{0:T(128)S(1)} %pad_add_fusion.meta_ref, ...), custom_call_target="tpu_custom_call" | custom-call | flops 1 | bytes 1 | tf_op jit(solution)/shard_map/attend_groups/pallas_call | solution.py:356
  20.8 1.6 %collective-permute-start.4 = (bf16[64,2048]{1,0:T(8,128)(2,1)S(1)}, bf16[64,2048]{1,0:T(8,128)(2,1)S(1)}, u32[]{:S(2)}, u32[]{:S(2)}) collective-permute-start(bf16[64,2048]{1,0:T(8,128)(2,1)S(1)} %get-tuple-element.66), channel_id=1, source_target_pairs={{0,8},{4,12},{8,0},{12,4},{16,24},{20,28},{24,16},{28,20},{1,9},{5... | collective-permute-start | bytes 786440 | tf_op jit(solution)/shard_map/ppermute | solution.py:529
  22.5 2.5 %collective-permute-start.5 = (bf16[64,2048]{1,0:T(8,128)(2,1)S(1)}, bf16[64,2048]{1,0:T(8,128)(2,1)S(1)}, u32[]{:S(2)}, u32[]{:S(2)}) collective-permute-start(bf16[64,2048]{1,0:T(8,128)(2,1)S(1)} %get-tuple-element.67), channel_id=1, source_target_pairs={{0,24},{4,28},{8,16},{12,20},{16,8},{20,12},{24,0},{28,4},{1,25},{... | collective-permute-start | bytes 786440 | tf_op jit(solution)/shard_map/ppermute | solution.py:529
  24.9 2.4 %join.2 = (bf16[1024,128]{1,0:T(8,128)(2,1)S(1)}, bf16[1024,128]{1,0:T(8,128)(2,1)S(1)}, bf16[2048,128]{1,0:T(8,128)(2,1)S(1)}) custom-call(bf16[64,2048]{1,0:T(8,128)(2,1)S(1)} %get-tuple-element.60.a_ref, bf16[64,2048]{1,0:T(8,128)(2,1)S(1)} %get-tuple-element.61.b_ref, bf16[1024,2048]{1,0:T(8,128)(2,1)S(1)} %get-tuple-element.77.wx_ref, ...), custom_call_target="tpu_custom_call" | custom-call | flops 1 | bytes 1 | tf_op jit(solution)/shard_map/join/pallas_call | solution.py:406
  27.3 1.6 %collective-permute-start.6 = (bf16[1024,128]{1,0:T(8,128)(2,1)S(1)}, bf16[1024,128]{1,0:T(8,128)(2,1)S(1)}, u32[]{:S(2)}, u32[]{:S(2)}) collective-permute-start(bf16[1024,128]{1,0:T(8,128)(2,1)S(1)} %get-tuple-element.74), channel_id=1, source_target_pairs={{0,1},{1,0},{2,3},{3,2},{4,5},{5,4},{6,7},{7,6},{8,9},{9,8},{10,11... | collective-permute-start | bytes 786440 | tf_op jit(solution)/shard_map/ppermute | solution.py:529
  28.9 1.5 %collective-permute-start.7 = (bf16[1024,128]{1,0:T(8,128)(2,1)S(1)}, bf16[1024,128]{1,0:T(8,128)(2,1)S(1)}, u32[]{:S(2)}, u32[]{:S(2)}) collective-permute-start(bf16[1024,128]{1,0:T(8,128)(2,1)S(1)} %get-tuple-element.76), channel_id=1, source_target_pairs={{0,2},{1,3},{2,0},{3,1},{4,6},{5,7},{6,4},{7,5},{8,10},{9,11},{10,... | collective-permute-start | bytes 786440 | tf_op jit(solution)/shard_map/ppermute | solution.py:529
  30.4 2.3 %last_rows.2 = (bf16[1024,128]{1,0:T(8,128)(2,1)S(1)}, bf16[1024,128]{1,0:T(8,128)(2,1)S(1)}) custom-call(bf16[2048,128]{1,0:T(8,128)(2,1)S(1)} %get-tuple-element.68.after_ref.joined_ref.first_ref, bf16[1024,2048]{1,0:T(8,128)(2,1)S(1)} %get-tuple-element.84.w0_ref, bf16[1024,2048]{1,0:T(8,128)(2,1)S(1)} %get-tuple-element.85.w1_ref), custom_call_target="tpu_custom_call" | custom-call | flops 1 | bytes 1 | tf_op jit(solution)/shard_map/last_rows/pallas_call | solution.py:406
  32.8 0.6 collective-permute-start.8
  33.4 0.0 collective-permute-done.4.a_ref
  33.4 0.5 collective-permute-start.9
  33.9 3.5 %stage_weights.3 = (bf16[1024,2048]{1,0:T(8,128)(2,1)S(1)}, bf16[1024,2048]{1,0:T(8,128)(2,1)S(1)}) custom-call(bf16[8192,2048]{1,0:T(8,128)(2,1)} %w_ref.7, bf16[2048,128]{1,0:T(8,128)(2,1)S(1)} %get-tuple-element.68.after_ref.joined_ref.first_ref), custom_call_target="tpu_custom_call" | custom-call | flops 1 | bytes 1 | tf_op jit(solution)/shard_map/stage_weights/pallas_call | solution.py:232
  37.3 0.1 collective-permute-done.5.b_ref
  37.4 2.3 %pass_rows.2 = (bf16[1024,128]{1,0:T(8,128)(2,1)S(1)}, bf16[1024,128]{1,0:T(8,128)(2,1)S(1)}) custom-call(bf16[2048,128]{1,0:T(8,128)(2,1)S(1)} %get-tuple-element.68.after_ref.joined_ref.first_ref, bf16[1024,2048]{1,0:T(8,128)(2,1)S(1)} %get-tuple-element.71.w0_ref, bf16[1024,2048]{1,0:T(8,128)(2,1)S(1)} %get-tuple-element.72.w1_ref), custom_call_target="tpu_custom_call" | custom-call | flops 1 | bytes 1 | tf_op jit(solution)/shard_map/pass_rows/pallas_call | solution.py:406
  39.7 0.0 collective-permute-done.6.b_ref
  39.8 0.1 add.6
  39.8 0.0 collective-permute-done.7.b_ref
  39.8 0.1 add.7
  39.9 1.6 %collective-permute-start.10 = (bf16[1024,128]{1,0:T(8,128)(2,1)S(1)}, bf16[1024,128]{1,0:T(8,128)(2,1)S(1)}, u32[]{:S(2)}, u32[]{:S(2)}) collective-permute-start(bf16[1024,128]{1,0:T(8,128)(2,1)S(1)} %add.6), channel_id=1, source_target_pairs={{0,2},{1,3},{2,0},{3,1},{4,6},{5,7},{6,4},{7,5},{8,10},{9,11},{10,... | collective-permute-start | bytes 786440 | tf_op jit(solution)/shard_map/ppermute | solution.py:529
  41.5 1.5 %collective-permute-start.11 = (bf16[1024,128]{1,0:T(8,128)(2,1)S(1)}, bf16[1024,128]{1,0:T(8,128)(2,1)S(1)}, u32[]{:S(2)}, u32[]{:S(2)}) collective-permute-start(bf16[1024,128]{1,0:T(8,128)(2,1)S(1)} %add.7), channel_id=1, source_target_pairs={{0,1},{1,0},{2,3},{3,2},{4,5},{5,4},{6,7},{7,6},{8,9},{9,8},{10,11... | collective-permute-start | bytes 786440 | tf_op jit(solution)/shard_map/ppermute | solution.py:529
  43.0 2.4 %join.3 = (bf16[1024,128]{1,0:T(8,128)(2,1)S(1)}, bf16[1024,128]{1,0:T(8,128)(2,1)S(1)}, bf16[2048,128]{1,0:T(8,128)(2,1)S(1)}) custom-call(bf16[64,2048]{1,0:T(8,128)(2,1)S(1)} %collective-permute-done.4.a_ref, bf16[64,2048]{1,0:T(8,128)(2,1)S(1)} %collective-permute-done.5.b_ref, bf16[1024,2048]{1,0:T(8,128)(2,1)S(1)} %get-tuple-element.77.wx_ref, ...), custom_call_target="tpu_custom_call" | custom-call | flops 1 | bytes 1 | tf_op jit(solution)/shard_map/join/pallas_call | solution.py:406
  45.4 0.0 collective-permute-done.8.x1_ref
  45.4 0.0 collective-permute-done.9.y1_ref
  45.4 0.6 collective-permute-start.15
  46.0 0.5 collective-permute-start.17
  46.5 2.3 %last_rows.3 = (bf16[1024,128]{1,0:T(8,128)(2,1)S(1)}, bf16[1024,128]{1,0:T(8,128)(2,1)S(1)}) custom-call(bf16[2048,128]{1,0:T(8,128)(2,1)S(1)} %get-tuple-element.102.second_ref.joined_ref, bf16[1024,2048]{1,0:T(8,128)(2,1)S(1)} %get-tuple-element.84.w0_ref, bf16[1024,2048]{1,0:T(8,128)(2,1)S(1)} %get-tuple-element.85.w1_ref), custom_call_target="tpu_custom_call" | custom-call | flops 1 | bytes 1 | tf_op jit(solution)/shard_map/last_rows/pallas_call | solution.py:406
  48.9 2.3 %keep_rows.1 = (bf16[2048,128]{1,0:T(8,128)(2,1)S(1)}, bf16[2048,128]{1,0:T(8,128)(2,1)S(1)}) custom-call(bf16[2048,128]{1,0:T(8,128)(2,1)S(1)} %get-tuple-element.68.after_ref.joined_ref.first_ref, bf16[2048,128]{1,0:T(8,128)(2,1)S(1)} %get-tuple-element.102.second_ref.joined_ref, bf16[1024,2048]{1,0:T(8,128)(2,1)S(1)} %get-tuple-element.79.w0_ref, ...), custom_call_target="tpu_custom_call" | custom-call | flops 1 | bytes 1 | tf_op jit(solution)/shard_map/keep_rows/pallas_call | solution.py:406
  51.2 0.0 collective-permute-done.10.y2_ref
  51.2 0.0 collective-permute-done.11.x2_ref
  51.2 0.2 finish.4
  51.5 0.7 %collective-permute-start.12 = (bf16[1024,128]{1,0:T(8,128)(2,1)S(1)}, bf16[1024,128]{1,0:T(8,128)(2,1)S(1)}, u32[]{:S(2)}, u32[]{:S(2)}) collective-permute-start(bf16[1024,128]{1,0:T(8,128)(2,1)S(1)} %get-tuple-element.94), channel_id=1, source_target_pairs={{0,16},{4,20},{8,24},{12,28},{16,0},{20,4},{24,8},{28,12},{1,17},{... | collective-permute-start | bytes 786440 | tf_op jit(solution)/shard_map/ppermute | solution.py:529
  52.2 1.5 %collective-permute-start.13 = (bf16[1024,128]{1,0:T(8,128)(2,1)S(1)}, bf16[1024,128]{1,0:T(8,128)(2,1)S(1)}, u32[]{:S(2)}, u32[]{:S(2)}) collective-permute-start(bf16[1024,128]{1,0:T(8,128)(2,1)S(1)} %get-tuple-element.98), channel_id=1, source_target_pairs={{0,2},{1,3},{2,0},{3,1},{4,6},{5,7},{6,4},{7,5},{8,10},{9,11},{10,... | collective-permute-start | bytes 786440 | tf_op jit(solution)/shard_map/ppermute | solution.py:529
  53.7 1.5 %collective-permute-start.14 = (bf16[1024,128]{1,0:T(8,128)(2,1)S(1)}, bf16[1024,128]{1,0:T(8,128)(2,1)S(1)}, u32[]{:S(2)}, u32[]{:S(2)}) collective-permute-start(bf16[1024,128]{1,0:T(8,128)(2,1)S(1)} %get-tuple-element.100), channel_id=1, source_target_pairs={{0,1},{1,0},{2,3},{3,2},{4,5},{5,4},{6,7},{7,6},{8,9},{9,8},{10,11... | collective-permute-start | bytes 786440 | tf_op jit(solution)/shard_map/ppermute | solution.py:529
  55.2 2.3 %pass_rows.3 = (bf16[1024,128]{1,0:T(8,128)(2,1)S(1)}, bf16[1024,128]{1,0:T(8,128)(2,1)S(1)}) custom-call(bf16[2048,128]{1,0:T(8,128)(2,1)S(1)} %get-tuple-element.102.second_ref.joined_ref, bf16[1024,2048]{1,0:T(8,128)(2,1)S(1)} %get-tuple-element.71.w0_ref, bf16[1024,2048]{1,0:T(8,128)(2,1)S(1)} %get-tuple-element.72.w1_ref), custom_call_target="tpu_custom_call" | custom-call | flops 1 | bytes 1 | tf_op jit(solution)/shard_map/pass_rows/pallas_call | solution.py:406
  57.5 0.0 collective-permute-done.15.b_ref
  57.5 0.1 add.8
  57.6 0.6 collective-permute-start.16
  58.2 0.0 collective-permute-done.17.b_ref
  58.2 0.1 add.9
  58.2 0.6 collective-permute-start.18
  58.8 4.2 %collective-permute-done.12.away_ref = bf16[1024,128]{1,0:T(8,128)(2,1)S(1)} collective-permute-done((bf16[1024,128]{1,0:T(8,128)(2,1)S(1)}, bf16[1024,128]{1,0:T(8,128)(2,1)S(1)}, u32[]{:S(2)}, u32[]{:S(2)}) %collective-permute-start.12) | collective-permute-done | bytes 262176 | tf_op jit(solution)/shard_map/ppermute | solution.py:529
  63.0 0.1 finish.5.away_ref
  63.2 0.0 collective-permute-done.13.one_ref
  63.2 0.1 finish.6.bottom_ref
  63.2 0.0 collective-permute-done.14.one_ref
  63.2 0.1 finish.7.top_ref
  63.3 1.8 %collective-permute-done.16.y2_ref = bf16[1024,128]{1,0:T(8,128)(2,1)S(1)} collective-permute-done((bf16[1024,128]{1,0:T(8,128)(2,1)S(1)}, bf16[1024,128]{1,0:T(8,128)(2,1)S(1)}, u32[]{:S(2)}, u32[]{:S(2)}) %collective-permute-start.16) | collective-permute-done | bytes 262176 | tf_op jit(solution)/shard_map/ppermute | solution.py:529
  65.1 1.0 %collective-permute-done.18.x2_ref = bf16[1024,128]{1,0:T(8,128)(2,1)S(1)} collective-permute-done((bf16[1024,128]{1,0:T(8,128)(2,1)S(1)}, bf16[1024,128]{1,0:T(8,128)(2,1)S(1)}, u32[]{:S(2)}, u32[]{:S(2)}) %collective-permute-start.18) | collective-permute-done | bytes 262176 | tf_op jit(solution)/shard_map/ppermute | solution.py:529
  66.1 1.2 %finish_second.1 = bf16[2048,256]{1,0:T(8,128)(2,1)} custom-call(bf16[2048,128]{1,0:T(8,128)(2,1)S(1)} %get-tuple-element.92.first_ref, bf16[2048,128]{1,0:T(8,128)(2,1)S(1)} %finish.5.away_ref, f32[1024,128]{1,0:T(8,128)S(1)} %finish.7.top_ref, f32[1024,128]{1,0:T(8,128)S(1)} %finish.6.bottom_ref, bf16[1024,128]{1,0:T(8,128)(2,1)S(1)} %collective-permute-done.16.y2_ref, ...), custom_call_target="tpu_custom_call" | custom-call | flops 1 | bytes 1 | tf_op jit(solution)/shard_map/finish_second/pallas_call | solution.py:503
Async XLA Ops:
  1.0 12.8 %collective-permute-start.2 = (bf16[512,256]{1,0:T(8,128)(2,1)S(1)}, bf16[512,256]{1,0:T(8,128)(2,1)S(1)}, u32[]{:S(2)}, u32[]{:S(2)}) collective-permute-start(bf16[512,256]{1,0:T(8,128)(2,1)S(1)} %join_keys_values.1.kv0_ref), channel_id=1, source_target_pairs={{0,8},{4,12},{8,16},{12,20},{16,24},{20,28},{1,9},{5,13},{9,17},{1... | collective-permute-start | bytes 786440 | tf_op jit(solution)/shard_map/ppermute | solution.py:537
  9.8 4.2 %collective-permute-start = (bf16[128,2048]{1,0:T(8,128)(2,1)S(1)}, bf16[128,2048]{1,0:T(8,128)(2,1)S(1)}, u32[]{:S(2)}, u32[]{:S(2)}) collective-permute-start(bf16[128,2048]{1,0:T(8,128)(2,1)S(1)} %get-tuple-element.57.after_ref), channel_id=1, source_target_pairs={{0,4},{4,0},{8,12},{12,8},{16,20},{20,16},{24,28},{28,24},{1,5},{5... | collective-permute-start | bytes 1572872 | tf_op jit(solution)/shard_map/ppermute | solution.py:529
  9.9 4.1 %collective-permute-start.1 = (bf16[512,256]{1,0:T(8,128)(2,1)S(1)}, bf16[512,256]{1,0:T(8,128)(2,1)S(1)}, u32[]{:S(2)}, u32[]{:S(2)}) collective-permute-start(bf16[512,256]{1,0:T(8,128)(2,1)S(1)} %join_keys_values.1.kv0_ref), channel_id=1, source_target_pairs={{0,4},{4,0},{8,12},{12,8},{16,20},{20,16},{24,28},{28,24},{1,5},{5... | collective-permute-start | bytes 786440 | tf_op jit(solution)/shard_map/ppermute | solution.py:529
  13.8 1.6 %collective-permute-start.3 = (bf16[512,256]{1,0:T(8,128)(2,1)S(1)}, bf16[512,256]{1,0:T(8,128)(2,1)S(1)}, u32[]{:S(2)}, u32[]{:S(2)}) collective-permute-start(bf16[512,256]{1,0:T(8,128)(2,1)S(1)} %collective-permute-done.2.kv2_ref), channel_id=1, source_target_pairs={{0,4},{4,0},{8,12},{12,8},{16,20},{20,16},{24,28},{28,24},{1,5},{5... | collective-permute-start | bytes 786440 | tf_op jit(solution)/shard_map/ppermute | solution.py:529
  20.8 12.5 %collective-permute-start.4 = (bf16[64,2048]{1,0:T(8,128)(2,1)S(1)}, bf16[64,2048]{1,0:T(8,128)(2,1)S(1)}, u32[]{:S(2)}, u32[]{:S(2)}) collective-permute-start(bf16[64,2048]{1,0:T(8,128)(2,1)S(1)} %get-tuple-element.66), channel_id=1, source_target_pairs={{0,8},{4,12},{8,0},{12,4},{16,24},{20,28},{24,16},{28,20},{1,9},{5... | collective-permute-start | bytes 786440 | tf_op jit(solution)/shard_map/ppermute | solution.py:529
  22.5 15.0 %collective-permute-start.5 = (bf16[64,2048]{1,0:T(8,128)(2,1)S(1)}, bf16[64,2048]{1,0:T(8,128)(2,1)S(1)}, u32[]{:S(2)}, u32[]{:S(2)}) collective-permute-start(bf16[64,2048]{1,0:T(8,128)(2,1)S(1)} %get-tuple-element.67), channel_id=1, source_target_pairs={{0,24},{4,28},{8,16},{12,20},{16,8},{20,12},{24,0},{28,4},{1,25},{... | collective-permute-start | bytes 786440 | tf_op jit(solution)/shard_map/ppermute | solution.py:529
  27.3 12.4 %collective-permute-start.6 = (bf16[1024,128]{1,0:T(8,128)(2,1)S(1)}, bf16[1024,128]{1,0:T(8,128)(2,1)S(1)}, u32[]{:S(2)}, u32[]{:S(2)}) collective-permute-start(bf16[1024,128]{1,0:T(8,128)(2,1)S(1)} %get-tuple-element.74), channel_id=1, source_target_pairs={{0,1},{1,0},{2,3},{3,2},{4,5},{5,4},{6,7},{7,6},{8,9},{9,8},{10,11... | collective-permute-start | bytes 786440 | tf_op jit(solution)/shard_map/ppermute | solution.py:529
  28.9 10.9 %collective-permute-start.7 = (bf16[1024,128]{1,0:T(8,128)(2,1)S(1)}, bf16[1024,128]{1,0:T(8,128)(2,1)S(1)}, u32[]{:S(2)}, u32[]{:S(2)}) collective-permute-start(bf16[1024,128]{1,0:T(8,128)(2,1)S(1)} %get-tuple-element.76), channel_id=1, source_target_pairs={{0,2},{1,3},{2,0},{3,1},{4,6},{5,7},{6,4},{7,5},{8,10},{9,11},{10,... | collective-permute-start | bytes 786440 | tf_op jit(solution)/shard_map/ppermute | solution.py:529
  32.8 12.7 %collective-permute-start.8 = (bf16[1024,128]{1,0:T(8,128)(2,1)S(1)}, bf16[1024,128]{1,0:T(8,128)(2,1)S(1)}, u32[]{:S(2)}, u32[]{:S(2)}) collective-permute-start(bf16[1024,128]{1,0:T(8,128)(2,1)S(1)} %get-tuple-element.86), channel_id=1, source_target_pairs={{0,1},{1,0},{2,3},{3,2},{4,5},{5,4},{6,7},{7,6},{8,9},{9,8},{10,11... | collective-permute-start | bytes 786440 | tf_op jit(solution)/shard_map/ppermute | solution.py:529
  33.4 12.1 %collective-permute-start.9 = (bf16[1024,128]{1,0:T(8,128)(2,1)S(1)}, bf16[1024,128]{1,0:T(8,128)(2,1)S(1)}, u32[]{:S(2)}, u32[]{:S(2)}) collective-permute-start(bf16[1024,128]{1,0:T(8,128)(2,1)S(1)} %get-tuple-element.87), channel_id=1, source_target_pairs={{0,2},{1,3},{2,0},{3,1},{4,6},{5,7},{6,4},{7,5},{8,10},{9,11},{10,... | collective-permute-start | bytes 786440 | tf_op jit(solution)/shard_map/ppermute | solution.py:529
  39.9 11.3 %collective-permute-start.10 = (bf16[1024,128]{1,0:T(8,128)(2,1)S(1)}, bf16[1024,128]{1,0:T(8,128)(2,1)S(1)}, u32[]{:S(2)}, u32[]{:S(2)}) collective-permute-start(bf16[1024,128]{1,0:T(8,128)(2,1)S(1)} %add.6), channel_id=1, source_target_pairs={{0,2},{1,3},{2,0},{3,1},{4,6},{5,7},{6,4},{7,5},{8,10},{9,11},{10,... | collective-permute-start | bytes 786440 | tf_op jit(solution)/shard_map/ppermute | solution.py:529
  41.5 9.7 %collective-permute-start.11 = (bf16[1024,128]{1,0:T(8,128)(2,1)S(1)}, bf16[1024,128]{1,0:T(8,128)(2,1)S(1)}, u32[]{:S(2)}, u32[]{:S(2)}) collective-permute-start(bf16[1024,128]{1,0:T(8,128)(2,1)S(1)} %add.7), channel_id=1, source_target_pairs={{0,1},{1,0},{2,3},{3,2},{4,5},{5,4},{6,7},{7,6},{8,9},{9,8},{10,11... | collective-permute-start | bytes 786440 | tf_op jit(solution)/shard_map/ppermute | solution.py:529
  45.4 12.1 %collective-permute-start.15 = (bf16[1024,128]{1,0:T(8,128)(2,1)S(1)}, bf16[1024,128]{1,0:T(8,128)(2,1)S(1)}, u32[]{:S(2)}, u32[]{:S(2)}) collective-permute-start(bf16[1024,128]{1,0:T(8,128)(2,1)S(1)} %get-tuple-element.104), channel_id=1, source_target_pairs={{0,1},{1,0},{2,3},{3,2},{4,5},{5,4},{6,7},{7,6},{8,9},{9,8},{10,11... | collective-permute-start | bytes 786440 | tf_op jit(solution)/shard_map/ppermute | solution.py:529
  46.0 12.1 %collective-permute-start.17 = (bf16[1024,128]{1,0:T(8,128)(2,1)S(1)}, bf16[1024,128]{1,0:T(8,128)(2,1)S(1)}, u32[]{:S(2)}, u32[]{:S(2)}) collective-permute-start(bf16[1024,128]{1,0:T(8,128)(2,1)S(1)} %get-tuple-element.106), channel_id=1, source_target_pairs={{0,2},{1,3},{2,0},{3,1},{4,6},{5,7},{6,4},{7,5},{8,10},{9,11},{10,... | collective-permute-start | bytes 786440 | tf_op jit(solution)/shard_map/ppermute | solution.py:529
  51.5 11.6 %collective-permute-start.12 = (bf16[1024,128]{1,0:T(8,128)(2,1)S(1)}, bf16[1024,128]{1,0:T(8,128)(2,1)S(1)}, u32[]{:S(2)}, u32[]{:S(2)}) collective-permute-start(bf16[1024,128]{1,0:T(8,128)(2,1)S(1)} %get-tuple-element.94), channel_id=1, source_target_pairs={{0,16},{4,20},{8,24},{12,28},{16,0},{20,4},{24,8},{28,12},{1,17},{... | collective-permute-start | bytes 786440 | tf_op jit(solution)/shard_map/ppermute | solution.py:529
  52.2 11.0 %collective-permute-start.13 = (bf16[1024,128]{1,0:T(8,128)(2,1)S(1)}, bf16[1024,128]{1,0:T(8,128)(2,1)S(1)}, u32[]{:S(2)}, u32[]{:S(2)}) collective-permute-start(bf16[1024,128]{1,0:T(8,128)(2,1)S(1)} %get-tuple-element.98), channel_id=1, source_target_pairs={{0,2},{1,3},{2,0},{3,1},{4,6},{5,7},{6,4},{7,5},{8,10},{9,11},{10,... | collective-permute-start | bytes 786440 | tf_op jit(solution)/shard_map/ppermute | solution.py:529
  53.7 9.5 %collective-permute-start.14 = (bf16[1024,128]{1,0:T(8,128)(2,1)S(1)}, bf16[1024,128]{1,0:T(8,128)(2,1)S(1)}, u32[]{:S(2)}, u32[]{:S(2)}) collective-permute-start(bf16[1024,128]{1,0:T(8,128)(2,1)S(1)} %get-tuple-element.100), channel_id=1, source_target_pairs={{0,1},{1,0},{2,3},{3,2},{4,5},{5,4},{6,7},{7,6},{8,9},{9,8},{10,11... | collective-permute-start | bytes 786440 | tf_op jit(solution)/shard_map/ppermute | solution.py:529
  57.6 7.5 %collective-permute-start.16 = (bf16[1024,128]{1,0:T(8,128)(2,1)S(1)}, bf16[1024,128]{1,0:T(8,128)(2,1)S(1)}, u32[]{:S(2)}, u32[]{:S(2)}) collective-permute-start(bf16[1024,128]{1,0:T(8,128)(2,1)S(1)} %add.8), channel_id=1, source_target_pairs={{0,2},{1,3},{2,0},{3,1},{4,6},{5,7},{6,4},{7,5},{8,10},{9,11},{10,... | collective-permute-start | bytes 786440 | tf_op jit(solution)/shard_map/ppermute | solution.py:529
  58.2 7.9 %collective-permute-start.18 = (bf16[1024,128]{1,0:T(8,128)(2,1)S(1)}, bf16[1024,128]{1,0:T(8,128)(2,1)S(1)}, u32[]{:S(2)}, u32[]{:S(2)}) collective-permute-start(bf16[1024,128]{1,0:T(8,128)(2,1)S(1)} %add.9), channel_id=1, source_target_pairs={{0,1},{1,0},{2,3},{3,2},{4,5},{5,4},{6,7},{7,6},{8,9},{9,8},{10,11... | collective-permute-start | bytes 786440 | tf_op jit(solution)/shard_map/ppermute | solution.py:529

commit v8 on v7

--- a/solution.py
+++ b/solution.py
@@ -121,6 +121,7 @@
 SMEM = pl.BlockSpec(memory_space=pltpu.SMEM)
 VMEM = pl.BlockSpec(memory_space=pltpu.VMEM)
 HBM = pl.BlockSpec(memory_space=pltpu.HBM)
+ANY = pl.BlockSpec(memory_space=pl.ANY)
 
 
 def _own_ctx():
@@ -168,18 +169,21 @@
 
 
 def _queries_for_other_core_kernel(names, meta_ref, queries_ref, w_ref, out_ref, kept_ref, *rest):
-    *w_out, sem, w_sems = rest
+    *w_out, sem, w_sems, table_ref, table_sem = rest
     w_copies = _weight_copies(names, w_ref, w_out, w_sems)
+    table_copy = pltpu.make_async_copy(meta_ref, table_ref, table_sem)
+    table_copy.start()
     copy = pltpu.make_async_copy(queries_ref, kept_ref, sem)
     copy.start()
     for w_copy in w_copies:
         w_copy.start()
     copy.wait()
+    table_copy.wait()
     c = _own_ctx()
     core = lax.rem(c, 2)
     rows = queries_ref.shape[0] // PIECES
     for j in range(PIECES // 2):
-        piece = _find_piece(meta_ref, c, 2 * j + 1 - core)
+        piece = _find_piece(table_ref, c, 2 * j + 1 - core)
         out_ref[j * rows:(j + 1) * rows] = kept_ref[_rows(piece * rows, rows)]
     for w_copy in w_copies:
         w_copy.wait()
@@ -192,9 +196,11 @@
             jax.ShapeDtypeStruct((queries.shape[0] // 2, queries.shape[1]), queries.dtype),
             jax.ShapeDtypeStruct(queries.shape, queries.dtype),
         ] + [_eighth(out_weight) for _ in names],
-        in_specs=[SMEM, HBM, HBM],
+        in_specs=[ANY, HBM, HBM],
         out_specs=[VMEM] * (2 + len(names)),
-        scratch_shapes=[pltpu.SemaphoreType.DMA, pltpu.SemaphoreType.DMA((len(names),))],
+        scratch_shapes=[
+            pltpu.SemaphoreType.DMA, pltpu.SemaphoreType.DMA((len(names),)),
+            pltpu.SMEM(meta.shape, meta.dtype), pltpu.SemaphoreType.DMA],
         compiler_params=pltpu.CompilerParams(vmem_limit_bytes=2 * 2**20),
         cost_estimate=pl.CostEstimate(flops=1, bytes_accessed=1, transcendentals=0),
         name="queries_for_other_core",
@@ -242,13 +248,15 @@
 
 
 def _attend_kernel(
-    groups, names, meta_ref, queries_ref, other_ref,
+    groups, names, documents, meta_ref, queries_ref, other_ref,
     kv0_ref, kv1_ref, kv2_ref, kv3_ref, w_ref,
     *rest,
 ):
     count = len(groups)
     out_refs, w_out = rest[:count], rest[count:count + len(names)]
-    kbuf, vbuf, qbuf, ctxbuf, w_sems = rest[count + len(names):]
+    kbuf, vbuf, qbuf, ctxbuf, w_sems, table_ref, table_sem = rest[count + len(names):]
+    table_copy = pltpu.make_async_copy(meta_ref, table_ref, table_sem)
+    table_copy.start()
     w_copies = _weight_copies(names, w_ref, w_out, w_sems)
     for copy in w_copies:
         copy.start()
@@ -267,12 +275,13 @@
             vbuf[at, 2 * kv * HEAD_SIZE:(2 * kv + 1) * HEAD_SIZE] = (
                 kv_ref[rows:, kv * HEAD_SIZE:(kv + 1) * HEAD_SIZE])
             vbuf[at, (2 * kv + 1) * HEAD_SIZE:(2 * kv + 2) * HEAD_SIZE] = jnp.ones((rows, HEAD_SIZE), jnp.bfloat16)
+    table_copy.wait()
     starts = []
     for n, k in enumerate(groups):
         zdest = z ^ k
         owner = 2 * zdest + core
-        mine = _find_piece(meta_ref, c, owner)
-        theirs = _find_piece(meta_ref, c + 1 - 2 * core, owner)
+        mine = _find_piece(table_ref, c, owner)
+        theirs = _find_piece(table_ref, c + 1 - 2 * core, owner)
         qbuf[2 * n + core] = queries_ref[_rows(mine * piece_rows, piece_rows)]
         qbuf[2 * n + 1 - core] = other_ref[_rows(zdest * piece_rows, piece_rows)]
         at0 = jnp.where(core == 0, mine, theirs)
@@ -281,9 +290,9 @@
     doc_start = []
     running = jnp.int32(0)
     lengths_at = PIECES * PIECES
-    for d in range(lengths_at, meta_ref.shape[0]):
+    for d in range(lengths_at, lengths_at + documents):
         doc_start.append(running)
-        running = running + meta_ref[d]
+        running = running + table_ref[d]
     base = 2 * rows * (z - 1)
     group = queries_ref.shape[1] // kv0_ref.shape[1]
     scale = math.log2(math.e) / math.sqrt(HEAD_SIZE)
@@ -350,14 +359,14 @@
         copy.wait()
 
 
-def _attend_groups(groups, names, meta, queries, other, kv, out_weight):
+def _attend_groups(groups, names, documents, meta, queries, other, kv, out_weight):
     piece = queries.shape[0] // PIECES
     rows = kv[0].shape[0] // 2
     return pl.pallas_call(
-        functools.partial(_attend_kernel, groups, names),
+        functools.partial(_attend_kernel, groups, names, documents),
         out_shape=[jax.ShapeDtypeStruct((2 * piece, queries.shape[1]), jnp.bfloat16) for _ in groups]
         + [_eighth(out_weight) for _ in names],
-        in_specs=[SMEM] + [VMEM] * 6 + [HBM],
+        in_specs=[ANY] + [VMEM] * 6 + [HBM],
         out_specs=[VMEM] * (len(groups) + len(names)),
         scratch_shapes=[
             pltpu.VMEM((4 * rows, kv[0].shape[1]), jnp.bfloat16),
@@ -365,6 +374,8 @@
             pltpu.VMEM((2 * len(groups), piece, queries.shape[1]), jnp.bfloat16),
             pltpu.VMEM((2 * len(groups), piece, queries.shape[1]), jnp.bfloat16),
             pltpu.SemaphoreType.DMA((len(names),)),
+            pltpu.SMEM(meta.shape, meta.dtype),
+            pltpu.SemaphoreType.DMA,
         ],
         compiler_params=pltpu.CompilerParams(vmem_limit_bytes=12 * 2**20),
         cost_estimate=pl.CostEstimate(flops=1, bytes_accessed=1, transcendentals=0),
@@ -544,7 +555,8 @@
     kv2, weights["xf"] = lax.optimization_barrier((kv2, weights["xf"]))
     kv = (kv0, kv1, kv2, _flip(kv2, "ctx", 1))
     loaded = ("yf", "py", "px")
-    ctx0, ctx2, ctx1, ctx3, *loads = _attend_groups((0, 2, 1, 3), loaded, meta, queries, other, kv, out_weight)
+    ctx0, ctx2, ctx1, ctx3, *loads = _attend_groups(
+        (0, 2, 1, 3), loaded, doc_lengths.shape[0], meta, queries, other, kv, out_weight)
     weights.update(zip(loaded, loads))
     ctx1, ctx3 = _flip(ctx1, "ctx", 2), _flip(ctx3, "ctx", 6)
 

time: 67.2 us -> 65.8 us (0.979)
  waiting for transfers between devices: 8.56 us -> 7.61 us
    ppermute x18, waiting for transfers between devices: 8.56 us -> 7.61 us  [_flip(): return lax.ppermute(x, axis, [(i, i ^ bits) for i in range(n)])]
  transfers between devices with their start and end apart: 19 -> 19, of which waited for: 5 -> 4; matrix products, arithmetic and copies ran while one was open for 1% -> 1% of each run, Pallas kernels for 40% -> 41%
where the time goes in v8:
time: 65.8 us; the launch traced here: 65.6 us
  Pallas kernels  34.1 us (52%)
  starting transfers between devices  22.8 us (35%)
  waiting for transfers between devices  7.61 us (12%)
  other arithmetic  0.75 us (1%)
    ppermute x18, starting transfers between devices, _flip(): return lax.ppermute(x, axis, [(i, i ^ bits) for i in range(n)])  17.8 us
    pallas_call x11, Pallas kernels, _project(): pl.pallas_call(kernel, out_shape=out_shape, in_specs=[VMEM] * len(operand...  16.7 us
    ppermute x18, waiting for transfers between devices, _flip(): return lax.ppermute(x, axis, [(i, i ^ bits) for i in range(n)])  7.61 us
    pallas_call x2, Pallas kernels, _stage_weights(): pl.pallas_call(functools.partial(_stage_kernel, names), out_shape=[_eight...  6.96 us
    pallas_call x1, Pallas kernels, _attend_groups(): pl.pallas_call(functools.partial(_attend_kernel, groups, names, documents...  5.3 us
    ppermute x1, starting transfers between devices, per_device_fast(): kv2 = lax.ppermute(kv0, 'ctx', [(i, i + 2) for i in range(places - 2)])  4.94 us
    pallas_call x1, Pallas kernels, _queries_for_other_core(): pl.pallas_call(functools.partial(_queries_for_other_core_kernel, names),...  2.54 us
  transfers between devices with their start and end apart: 19, of which 4 were waited for; matrix products, arithmetic and copies ran while one was open for 1% of the time, Pallas kernels for 41%

profile of v8, /device:TPU:0, one launch (start us, length us, event | category | flops | bytes accessed | tf_op | source)
XLA Modules:
  0.0 65.6 jit_solution(8852602575057812816)
XLA Ops:
  0.0 1.0 %join_keys_values.1.kv0_ref = bf16[512,256]{1,0:T(8,128)(2,1)S(1)} custom-call(bf16[256,256]{1,0:T(8,128)(2,1)} %keys_ref.1, bf16[256,256]{1,0:T(8,128)(2,1)} %values_ref.1), custom_call_target="tpu_custom_call" | custom-call | flops 1 | bytes 1 | tf_op jit(solution)/shard_map/join_keys_values/pallas_call | solution.py:159
  1.0 4.9 %collective-permute-start.2 = (bf16[512,256]{1,0:T(8,128)(2,1)S(1)}, bf16[512,256]{1,0:T(8,128)(2,1)S(1)}, u32[]{:S(2)}, u32[]{:S(2)}) collective-permute-start(bf16[512,256]{1,0:T(8,128)(2,1)S(1)} %join_keys_values.1.kv0_ref), channel_id=1, source_target_pairs={{0,8},{4,12},{8,16},{12,20},{16,24},{20,28},{1,9},{5,13},{9,17},{1... | collective-permute-start | bytes 786440 | tf_op jit(solution)/shard_map/ppermute | solution.py:548
  5.9 0.7 %pad_add_fusion.meta_ref = s32[80]{0:T(128)S(1)} fusion(s32[16]{0:T(128)} %param.10, s32[64]{0:T(128)} %bitcast.1), kind=kLoop, calls=%fused_computation | loop fusion | flops 80 | bytes 640 | tf_op jit(solution)/shard_map/concatenate | solution.py:550
  6.7 2.5 %queries_for_other_core.1 = (bf16[128,2048]{1,0:T(8,128)(2,1)S(1)}, bf16[256,2048]{1,0:T(8,128)(2,1)S(1)}, bf16[1024,2048]{1,0:T(8,128)(2,1)S(1)}) custom-call(s32[80]{0:T(128)S(1)} %pad_add_fusion.meta_ref, bf16[256,2048]{1,0:T(8,128)(2,1)} %queries_ref.1, bf16[8192,2048]{1,0:T(8,128)(2,1)} %w_ref.7), custom_call_target="tpu_custom_call" | custom-call | flops 1 | bytes 1 | tf_op jit(solution)/shard_map/queries_for_other_core/pallas_call | solution.py:193
  9.2 0.1 collective-permute-start
  9.3 0.5 collective-permute-start.1
  9.8 3.5 %stage_weights.2 = (bf16[1024,2048]{1,0:T(8,128)(2,1)S(1)}, bf16[1024,2048]{1,0:T(8,128)(2,1)S(1)}) custom-call(bf16[8192,2048]{1,0:T(8,128)(2,1)} %w_ref.7, bf16[128,2048]{1,0:T(8,128)(2,1)S(1)} %get-tuple-element.57.after_ref), custom_call_target="tpu_custom_call" | custom-call | flops 1 | bytes 1 | tf_op jit(solution)/shard_map/stage_weights/pallas_call | solution.py:238
  13.3 0.0 collective-permute-done.2.kv2_ref
  13.3 0.1 collective-permute-start.3
  13.5 0.0 collective-permute-done.1.kv1_ref
  13.5 0.0 collective-permute-done.other_ref
  13.5 1.5 %collective-permute-done.3.kv3_ref = bf16[512,256]{1,0:T(8,128)(2,1)S(1)} collective-permute-done((bf16[512,256]{1,0:T(8,128)(2,1)S(1)}, bf16[512,256]{1,0:T(8,128)(2,1)S(1)}, u32[]{:S(2)}, u32[]{:S(2)}) %collective-permute-start.3) | collective-permute-done | bytes 262176 | tf_op jit(solution)/shard_map/ppermute | solution.py:540
  14.9 5.3 %attend_groups.1 = (bf16[64,2048]{1,0:T(8,128)(2,1)S(1)}, bf16[64,2048]{1,0:T(8,128)(2,1)S(1)}, bf16[64,2048]{1,0:T(8,128)(2,1)S(1)}, bf16[64,2048]{1,0:T(8,128)...) custom-call(s32[80]{0:T(128)S(1)} %pad_add_fusion.meta_ref, ...), custom_call_target="tpu_custom_call" | custom-call | flops 1 | bytes 1 | tf_op jit(solution)/shard_map/attend_groups/pallas_call | solution.py:365
  20.2 1.0 %collective-permute-start.4 = (bf16[64,2048]{1,0:T(8,128)(2,1)S(1)}, bf16[64,2048]{1,0:T(8,128)(2,1)S(1)}, u32[]{:S(2)}, u32[]{:S(2)}) collective-permute-start(bf16[64,2048]{1,0:T(8,128)(2,1)S(1)} %get-tuple-element.66), channel_id=1, source_target_pairs={{0,8},{4,12},{8,0},{12,4},{16,24},{20,28},{24,16},{28,20},{1,9},{5... | collective-permute-start | bytes 786440 | tf_op jit(solution)/shard_map/ppermute | solution.py:540
  21.3 2.6 %collective-permute-start.5 = (bf16[64,2048]{1,0:T(8,128)(2,1)S(1)}, bf16[64,2048]{1,0:T(8,128)(2,1)S(1)}, u32[]{:S(2)}, u32[]{:S(2)}) collective-permute-start(bf16[64,2048]{1,0:T(8,128)(2,1)S(1)} %get-tuple-element.67), channel_id=1, source_target_pairs={{0,24},{4,28},{8,16},{12,20},{16,8},{20,12},{24,0},{28,4},{1,25},{... | collective-permute-start | bytes 786440 | tf_op jit(solution)/shard_map/ppermute | solution.py:540
  23.8 2.4 %join.2 = (bf16[1024,128]{1,0:T(8,128)(2,1)S(1)}, bf16[1024,128]{1,0:T(8,128)(2,1)S(1)}, bf16[2048,128]{1,0:T(8,128)(2,1)S(1)}) custom-call(bf16[64,2048]{1,0:T(8,128)(2,1)S(1)} %get-tuple-element.60.a_ref, bf16[64,2048]{1,0:T(8,128)(2,1)S(1)} %get-tuple-element.61.b_ref, bf16[1024,2048]{1,0:T(8,128)(2,1)S(1)} %get-tuple-element.77.wx_ref, ...), custom_call_target="tpu_custom_call" | custom-call | flops 1 | bytes 1 | tf_op jit(solution)/shard_map/join/pallas_call | solution.py:417
  26.3 1.6 %collective-permute-start.6 = (bf16[1024,128]{1,0:T(8,128)(2,1)S(1)}, bf16[1024,128]{1,0:T(8,128)(2,1)S(1)}, u32[]{:S(2)}, u32[]{:S(2)}) collective-permute-start(bf16[1024,128]{1,0:T(8,128)(2,1)S(1)} %get-tuple-element.74), channel_id=1, source_target_pairs={{0,1},{1,0},{2,3},{3,2},{4,5},{5,4},{6,7},{7,6},{8,9},{9,8},{10,11... | collective-permute-start | bytes 786440 | tf_op jit(solution)/shard_map/ppermute | solution.py:540
  27.8 1.5 %collective-permute-start.7 = (bf16[1024,128]{1,0:T(8,128)(2,1)S(1)}, bf16[1024,128]{1,0:T(8,128)(2,1)S(1)}, u32[]{:S(2)}, u32[]{:S(2)}) collective-permute-start(bf16[1024,128]{1,0:T(8,128)(2,1)S(1)} %get-tuple-element.76), channel_id=1, source_target_pairs={{0,2},{1,3},{2,0},{3,1},{4,6},{5,7},{6,4},{7,5},{8,10},{9,11},{10,... | collective-permute-start | bytes 786440 | tf_op jit(solution)/shard_map/ppermute | solution.py:540
  29.3 2.3 %last_rows.2 = (bf16[1024,128]{1,0:T(8,128)(2,1)S(1)}, bf16[1024,128]{1,0:T(8,128)(2,1)S(1)}) custom-call(bf16[2048,128]{1,0:T(8,128)(2,1)S(1)} %get-tuple-element.68.after_ref.joined_ref.first_ref, bf16[1024,2048]{1,0:T(8,128)(2,1)S(1)} %get-tuple-element.84.w0_ref, bf16[1024,2048]{1,0:T(8,128)(2,1)S(1)} %get-tuple-element.85.w1_ref), custom_call_target="tpu_custom_call" | custom-call | flops 1 | bytes 1 | tf_op jit(solution)/shard_map/last_rows/pallas_call | solution.py:417
  31.7 0.6 collective-permute-start.8
  32.3 0.0 collective-permute-done.4.a_ref
  32.3 0.5 collective-permute-start.9
  32.8 3.5 %stage_weights.3 = (bf16[1024,2048]{1,0:T(8,128)(2,1)S(1)}, bf16[1024,2048]{1,0:T(8,128)(2,1)S(1)}) custom-call(bf16[8192,2048]{1,0:T(8,128)(2,1)} %w_ref.7, bf16[2048,128]{1,0:T(8,128)(2,1)S(1)} %get-tuple-element.68.after_ref.joined_ref.first_ref), custom_call_target="tpu_custom_call" | custom-call | flops 1 | bytes 1 | tf_op jit(solution)/shard_map/stage_weights/pallas_call | solution.py:238
  36.3 0.0 collective-permute-done.5.b_ref
  36.3 2.3 %pass_rows.2 = (bf16[1024,128]{1,0:T(8,128)(2,1)S(1)}, bf16[1024,128]{1,0:T(8,128)(2,1)S(1)}) custom-call(bf16[2048,128]{1,0:T(8,128)(2,1)S(1)} %get-tuple-element.68.after_ref.joined_ref.first_ref, bf16[1024,2048]{1,0:T(8,128)(2,1)S(1)} %get-tuple-element.71.w0_ref, bf16[1024,2048]{1,0:T(8,128)(2,1)S(1)} %get-tuple-element.72.w1_ref), custom_call_target="tpu_custom_call" | custom-call | flops 1 | bytes 1 | tf_op jit(solution)/shard_map/pass_rows/pallas_call | solution.py:417
  38.6 0.0 collective-permute-done.6.b_ref
  38.6 0.1 add.6
  38.7 0.0 collective-permute-done.7.b_ref
  38.7 0.1 add.7
  38.8 1.6 %collective-permute-start.10 = (bf16[1024,128]{1,0:T(8,128)(2,1)S(1)}, bf16[1024,128]{1,0:T(8,128)(2,1)S(1)}, u32[]{:S(2)}, u32[]{:S(2)}) collective-permute-start(bf16[1024,128]{1,0:T(8,128)(2,1)S(1)} %add.6), channel_id=1, source_target_pairs={{0,2},{1,3},{2,0},{3,1},{4,6},{5,7},{6,4},{7,5},{8,10},{9,11},{10,... | collective-permute-start | bytes 786440 | tf_op jit(solution)/shard_map/ppermute | solution.py:540
  40.3 1.5 %collective-permute-start.11 = (bf16[1024,128]{1,0:T(8,128)(2,1)S(1)}, bf16[1024,128]{1,0:T(8,128)(2,1)S(1)}, u32[]{:S(2)}, u32[]{:S(2)}) collective-permute-start(bf16[1024,128]{1,0:T(8,128)(2,1)S(1)} %add.7), channel_id=1, source_target_pairs={{0,1},{1,0},{2,3},{3,2},{4,5},{5,4},{6,7},{7,6},{8,9},{9,8},{10,11... | collective-permute-start | bytes 786440 | tf_op jit(solution)/shard_map/ppermute | solution.py:540
  41.8 2.4 %join.3 = (bf16[1024,128]{1,0:T(8,128)(2,1)S(1)}, bf16[1024,128]{1,0:T(8,128)(2,1)S(1)}, bf16[2048,128]{1,0:T(8,128)(2,1)S(1)}) custom-call(bf16[64,2048]{1,0:T(8,128)(2,1)S(1)} %collective-permute-done.4.a_ref, bf16[64,2048]{1,0:T(8,128)(2,1)S(1)} %collective-permute-done.5.b_ref, bf16[1024,2048]{1,0:T(8,128)(2,1)S(1)} %get-tuple-element.77.wx_ref, ...), custom_call_target="tpu_custom_call" | custom-call | flops 1 | bytes 1 | tf_op jit(solution)/shard_map/join/pallas_call | solution.py:417
  44.2 0.0 collective-permute-done.8.x1_ref
  44.3 0.0 collective-permute-done.9.y1_ref
  44.3 0.6 collective-permute-start.15
  44.9 0.5 collective-permute-start.17
  45.4 2.3 %last_rows.3 = (bf16[1024,128]{1,0:T(8,128)(2,1)S(1)}, bf16[1024,128]{1,0:T(8,128)(2,1)S(1)}) custom-call(bf16[2048,128]{1,0:T(8,128)(2,1)S(1)} %get-tuple-element.102.second_ref.joined_ref, bf16[1024,2048]{1,0:T(8,128)(2,1)S(1)} %get-tuple-element.84.w0_ref, bf16[1024,2048]{1,0:T(8,128)(2,1)S(1)} %get-tuple-element.85.w1_ref), custom_call_target="tpu_custom_call" | custom-call | flops 1 | bytes 1 | tf_op jit(solution)/shard_map/last_rows/pallas_call | solution.py:417
  47.7 2.3 %keep_rows.1 = (bf16[2048,128]{1,0:T(8,128)(2,1)S(1)}, bf16[2048,128]{1,0:T(8,128)(2,1)S(1)}) custom-call(bf16[2048,128]{1,0:T(8,128)(2,1)S(1)} %get-tuple-element.68.after_ref.joined_ref.first_ref, bf16[2048,128]{1,0:T(8,128)(2,1)S(1)} %get-tuple-element.102.second_ref.joined_ref, bf16[1024,2048]{1,0:T(8,128)(2,1)S(1)} %get-tuple-element.79.w0_ref, ...), custom_call_target="tpu_custom_call" | custom-call | flops 1 | bytes 1 | tf_op jit(solution)/shard_map/keep_rows/pallas_call | solution.py:417
  50.0 0.0 collective-permute-done.10.y2_ref
  50.1 0.0 collective-permute-done.11.x2_ref
  50.1 0.2 finish.4
  50.3 0.9 %collective-permute-start.12 = (bf16[1024,128]{1,0:T(8,128)(2,1)S(1)}, bf16[1024,128]{1,0:T(8,128)(2,1)S(1)}, u32[]{:S(2)}, u32[]{:S(2)}) collective-permute-start(bf16[1024,128]{1,0:T(8,128)(2,1)S(1)} %get-tuple-element.94), channel_id=1, source_target_pairs={{0,16},{4,20},{8,24},{12,28},{16,0},{20,4},{24,8},{28,12},{1,17},{... | collective-permute-start | bytes 786440 | tf_op jit(solution)/shard_map/ppermute | solution.py:540
  51.3 1.5 %collective-permute-start.13 = (bf16[1024,128]{1,0:T(8,128)(2,1)S(1)}, bf16[1024,128]{1,0:T(8,128)(2,1)S(1)}, u32[]{:S(2)}, u32[]{:S(2)}) collective-permute-start(bf16[1024,128]{1,0:T(8,128)(2,1)S(1)} %get-tuple-element.98), channel_id=1, source_target_pairs={{0,2},{1,3},{2,0},{3,1},{4,6},{5,7},{6,4},{7,5},{8,10},{9,11},{10,... | collective-permute-start | bytes 786440 | tf_op jit(solution)/shard_map/ppermute | solution.py:540
  52.8 1.5 %collective-permute-start.14 = (bf16[1024,128]{1,0:T(8,128)(2,1)S(1)}, bf16[1024,128]{1,0:T(8,128)(2,1)S(1)}, u32[]{:S(2)}, u32[]{:S(2)}) collective-permute-start(bf16[1024,128]{1,0:T(8,128)(2,1)S(1)} %get-tuple-element.100), channel_id=1, source_target_pairs={{0,1},{1,0},{2,3},{3,2},{4,5},{5,4},{6,7},{7,6},{8,9},{9,8},{10,11... | collective-permute-start | bytes 786440 | tf_op jit(solution)/shard_map/ppermute | solution.py:540
  54.3 2.3 %pass_rows.3 = (bf16[1024,128]{1,0:T(8,128)(2,1)S(1)}, bf16[1024,128]{1,0:T(8,128)(2,1)S(1)}) custom-call(bf16[2048,128]{1,0:T(8,128)(2,1)S(1)} %get-tuple-element.102.second_ref.joined_ref, bf16[1024,2048]{1,0:T(8,128)(2,1)S(1)} %get-tuple-element.71.w0_ref, bf16[1024,2048]{1,0:T(8,128)(2,1)S(1)} %get-tuple-element.72.w1_ref), custom_call_target="tpu_custom_call" | custom-call | flops 1 | bytes 1 | tf_op jit(solution)/shard_map/pass_rows/pallas_call | solution.py:417
  56.6 0.0 collective-permute-done.15.b_ref
  56.6 0.1 add.8
  56.7 0.6 collective-permute-start.16
  57.2 0.0 collective-permute-done.17.b_ref
  57.2 0.1 add.9
  57.3 0.6 collective-permute-start.18
  57.9 4.2 %collective-permute-done.12.away_ref = bf16[1024,128]{1,0:T(8,128)(2,1)S(1)} collective-permute-done((bf16[1024,128]{1,0:T(8,128)(2,1)S(1)}, bf16[1024,128]{1,0:T(8,128)(2,1)S(1)}, u32[]{:S(2)}, u32[]{:S(2)}) %collective-permute-start.12) | collective-permute-done | bytes 262176 | tf_op jit(solution)/shard_map/ppermute | solution.py:540
  62.1 0.1 finish.5.away_ref
  62.2 0.0 collective-permute-done.13.one_ref
  62.2 0.1 finish.6.bottom_ref
  62.3 0.0 collective-permute-done.14.one_ref
  62.3 0.1 finish.7.top_ref
  62.4 0.9 %collective-permute-done.16.y2_ref = bf16[1024,128]{1,0:T(8,128)(2,1)S(1)} collective-permute-done((bf16[1024,128]{1,0:T(8,128)(2,1)S(1)}, bf16[1024,128]{1,0:T(8,128)(2,1)S(1)}, u32[]{:S(2)}, u32[]{:S(2)}) %collective-permute-start.16) | collective-permute-done | bytes 262176 | tf_op jit(solution)/shard_map/ppermute | solution.py:540
  63.3 1.0 %collective-permute-done.18.x2_ref = bf16[1024,128]{1,0:T(8,128)(2,1)S(1)} collective-permute-done((bf16[1024,128]{1,0:T(8,128)(2,1)S(1)}, bf16[1024,128]{1,0:T(8,128)(2,1)S(1)}, u32[]{:S(2)}, u32[]{:S(2)}) %collective-permute-start.18) | collective-permute-done | bytes 262176 | tf_op jit(solution)/shard_map/ppermute | solution.py:540
  64.3 1.2 %finish_second.1 = bf16[2048,256]{1,0:T(8,128)(2,1)} custom-call(bf16[2048,128]{1,0:T(8,128)(2,1)S(1)} %get-tuple-element.92.first_ref, bf16[2048,128]{1,0:T(8,128)(2,1)S(1)} %finish.5.away_ref, f32[1024,128]{1,0:T(8,128)S(1)} %finish.7.top_ref, f32[1024,128]{1,0:T(8,128)S(1)} %finish.6.bottom_ref, bf16[1024,128]{1,0:T(8,128)(2,1)S(1)} %collective-permute-done.16.y2_ref, ...), custom_call_target="tpu_custom_call" | custom-call | flops 1 | bytes 1 | tf_op jit(solution)/shard_map/finish_second/pallas_call | solution.py:514
Async XLA Ops:
  1.0 12.3 %collective-permute-start.2 = (bf16[512,256]{1,0:T(8,128)(2,1)S(1)}, bf16[512,256]{1,0:T(8,128)(2,1)S(1)}, u32[]{:S(2)}, u32[]{:S(2)}) collective-permute-start(bf16[512,256]{1,0:T(8,128)(2,1)S(1)} %join_keys_values.1.kv0_ref), channel_id=1, source_target_pairs={{0,8},{4,12},{8,16},{12,20},{16,24},{20,28},{1,9},{5,13},{9,17},{1... | collective-permute-start | bytes 786440 | tf_op jit(solution)/shard_map/ppermute | solution.py:548
  9.2 4.2 %collective-permute-start = (bf16[128,2048]{1,0:T(8,128)(2,1)S(1)}, bf16[128,2048]{1,0:T(8,128)(2,1)S(1)}, u32[]{:S(2)}, u32[]{:S(2)}) collective-permute-start(bf16[128,2048]{1,0:T(8,128)(2,1)S(1)} %get-tuple-element.57.after_ref), channel_id=1, source_target_pairs={{0,4},{4,0},{8,12},{12,8},{16,20},{20,16},{24,28},{28,24},{1,5},{5... | collective-permute-start | bytes 1572872 | tf_op jit(solution)/shard_map/ppermute | solution.py:540
  9.3 4.1 %collective-permute-start.1 = (bf16[512,256]{1,0:T(8,128)(2,1)S(1)}, bf16[512,256]{1,0:T(8,128)(2,1)S(1)}, u32[]{:S(2)}, u32[]{:S(2)}) collective-permute-start(bf16[512,256]{1,0:T(8,128)(2,1)S(1)} %join_keys_values.1.kv0_ref), channel_id=1, source_target_pairs={{0,4},{4,0},{8,12},{12,8},{16,20},{20,16},{24,28},{28,24},{1,5},{5... | collective-permute-start | bytes 786440 | tf_op jit(solution)/shard_map/ppermute | solution.py:540
  13.3 1.6 %collective-permute-start.3 = (bf16[512,256]{1,0:T(8,128)(2,1)S(1)}, bf16[512,256]{1,0:T(8,128)(2,1)S(1)}, u32[]{:S(2)}, u32[]{:S(2)}) collective-permute-start(bf16[512,256]{1,0:T(8,128)(2,1)S(1)} %collective-permute-done.2.kv2_ref), channel_id=1, source_target_pairs={{0,4},{4,0},{8,12},{12,8},{16,20},{20,16},{24,28},{28,24},{1,5},{5... | collective-permute-start | bytes 786440 | tf_op jit(solution)/shard_map/ppermute | solution.py:540
  20.2 12.0 %collective-permute-start.4 = (bf16[64,2048]{1,0:T(8,128)(2,1)S(1)}, bf16[64,2048]{1,0:T(8,128)(2,1)S(1)}, u32[]{:S(2)}, u32[]{:S(2)}) collective-permute-start(bf16[64,2048]{1,0:T(8,128)(2,1)S(1)} %get-tuple-element.66), channel_id=1, source_target_pairs={{0,8},{4,12},{8,0},{12,4},{16,24},{20,28},{24,16},{28,20},{1,9},{5... | collective-permute-start | bytes 786440 | tf_op jit(solution)/shard_map/ppermute | solution.py:540
  21.3 15.0 %collective-permute-start.5 = (bf16[64,2048]{1,0:T(8,128)(2,1)S(1)}, bf16[64,2048]{1,0:T(8,128)(2,1)S(1)}, u32[]{:S(2)}, u32[]{:S(2)}) collective-permute-start(bf16[64,2048]{1,0:T(8,128)(2,1)S(1)} %get-tuple-element.67), channel_id=1, source_target_pairs={{0,24},{4,28},{8,16},{12,20},{16,8},{20,12},{24,0},{28,4},{1,25},{... | collective-permute-start | bytes 786440 | tf_op jit(solution)/shard_map/ppermute | solution.py:540
  26.3 12.3 %collective-permute-start.6 = (bf16[1024,128]{1,0:T(8,128)(2,1)S(1)}, bf16[1024,128]{1,0:T(8,128)(2,1)S(1)}, u32[]{:S(2)}, u32[]{:S(2)}) collective-permute-start(bf16[1024,128]{1,0:T(8,128)(2,1)S(1)} %get-tuple-element.74), channel_id=1, source_target_pairs={{0,1},{1,0},{2,3},{3,2},{4,5},{5,4},{6,7},{7,6},{8,9},{9,8},{10,11... | collective-permute-start | bytes 786440 | tf_op jit(solution)/shard_map/ppermute | solution.py:540
  27.8 10.9 %collective-permute-start.7 = (bf16[1024,128]{1,0:T(8,128)(2,1)S(1)}, bf16[1024,128]{1,0:T(8,128)(2,1)S(1)}, u32[]{:S(2)}, u32[]{:S(2)}) collective-permute-start(bf16[1024,128]{1,0:T(8,128)(2,1)S(1)} %get-tuple-element.76), channel_id=1, source_target_pairs={{0,2},{1,3},{2,0},{3,1},{4,6},{5,7},{6,4},{7,5},{8,10},{9,11},{10,... | collective-permute-start | bytes 786440 | tf_op jit(solution)/shard_map/ppermute | solution.py:540
  31.7 12.6 %collective-permute-start.8 = (bf16[1024,128]{1,0:T(8,128)(2,1)S(1)}, bf16[1024,128]{1,0:T(8,128)(2,1)S(1)}, u32[]{:S(2)}, u32[]{:S(2)}) collective-permute-start(bf16[1024,128]{1,0:T(8,128)(2,1)S(1)} %get-tuple-element.86), channel_id=1, source_target_pairs={{0,1},{1,0},{2,3},{3,2},{4,5},{5,4},{6,7},{7,6},{8,9},{9,8},{10,11... | collective-permute-start | bytes 786440 | tf_op jit(solution)/shard_map/ppermute | solution.py:540
  32.3 12.0 %collective-permute-start.9 = (bf16[1024,128]{1,0:T(8,128)(2,1)S(1)}, bf16[1024,128]{1,0:T(8,128)(2,1)S(1)}, u32[]{:S(2)}, u32[]{:S(2)}) collective-permute-start(bf16[1024,128]{1,0:T(8,128)(2,1)S(1)} %get-tuple-element.87), channel_id=1, source_target_pairs={{0,2},{1,3},{2,0},{3,1},{4,6},{5,7},{6,4},{7,5},{8,10},{9,11},{10,... | collective-permute-start | bytes 786440 | tf_op jit(solution)/shard_map/ppermute | solution.py:540
  38.8 11.3 %collective-permute-start.10 = (bf16[1024,128]{1,0:T(8,128)(2,1)S(1)}, bf16[1024,128]{1,0:T(8,128)(2,1)S(1)}, u32[]{:S(2)}, u32[]{:S(2)}) collective-permute-start(bf16[1024,128]{1,0:T(8,128)(2,1)S(1)} %add.6), channel_id=1, source_target_pairs={{0,2},{1,3},{2,0},{3,1},{4,6},{5,7},{6,4},{7,5},{8,10},{9,11},{10,... | collective-permute-start | bytes 786440 | tf_op jit(solution)/shard_map/ppermute | solution.py:540
  40.3 9.7 %collective-permute-start.11 = (bf16[1024,128]{1,0:T(8,128)(2,1)S(1)}, bf16[1024,128]{1,0:T(8,128)(2,1)S(1)}, u32[]{:S(2)}, u32[]{:S(2)}) collective-permute-start(bf16[1024,128]{1,0:T(8,128)(2,1)S(1)} %add.7), channel_id=1, source_target_pairs={{0,1},{1,0},{2,3},{3,2},{4,5},{5,4},{6,7},{7,6},{8,9},{9,8},{10,11... | collective-permute-start | bytes 786440 | tf_op jit(solution)/shard_map/ppermute | solution.py:540
  44.3 12.3 %collective-permute-start.15 = (bf16[1024,128]{1,0:T(8,128)(2,1)S(1)}, bf16[1024,128]{1,0:T(8,128)(2,1)S(1)}, u32[]{:S(2)}, u32[]{:S(2)}) collective-permute-start(bf16[1024,128]{1,0:T(8,128)(2,1)S(1)} %get-tuple-element.104), channel_id=1, source_target_pairs={{0,1},{1,0},{2,3},{3,2},{4,5},{5,4},{6,7},{7,6},{8,9},{9,8},{10,11... | collective-permute-start | bytes 786440 | tf_op jit(solution)/shard_map/ppermute | solution.py:540
  44.9 12.4 %collective-permute-start.17 = (bf16[1024,128]{1,0:T(8,128)(2,1)S(1)}, bf16[1024,128]{1,0:T(8,128)(2,1)S(1)}, u32[]{:S(2)}, u32[]{:S(2)}) collective-permute-start(bf16[1024,128]{1,0:T(8,128)(2,1)S(1)} %get-tuple-element.106), channel_id=1, source_target_pairs={{0,2},{1,3},{2,0},{3,1},{4,6},{5,7},{6,4},{7,5},{8,10},{9,11},{10,... | collective-permute-start | bytes 786440 | tf_op jit(solution)/shard_map/ppermute | solution.py:540
  50.3 11.8 %collective-permute-start.12 = (bf16[1024,128]{1,0:T(8,128)(2,1)S(1)}, bf16[1024,128]{1,0:T(8,128)(2,1)S(1)}, u32[]{:S(2)}, u32[]{:S(2)}) collective-permute-start(bf16[1024,128]{1,0:T(8,128)(2,1)S(1)} %get-tuple-element.94), channel_id=1, source_target_pairs={{0,16},{4,20},{8,24},{12,28},{16,0},{20,4},{24,8},{28,12},{1,17},{... | collective-permute-start | bytes 786440 | tf_op jit(solution)/shard_map/ppermute | solution.py:540
  51.3 11.0 %collective-permute-start.13 = (bf16[1024,128]{1,0:T(8,128)(2,1)S(1)}, bf16[1024,128]{1,0:T(8,128)(2,1)S(1)}, u32[]{:S(2)}, u32[]{:S(2)}) collective-permute-start(bf16[1024,128]{1,0:T(8,128)(2,1)S(1)} %get-tuple-element.98), channel_id=1, source_target_pairs={{0,2},{1,3},{2,0},{3,1},{4,6},{5,7},{6,4},{7,5},{8,10},{9,11},{10,... | collective-permute-start | bytes 786440 | tf_op jit(solution)/shard_map/ppermute | solution.py:540
  52.8 9.5 %collective-permute-start.14 = (bf16[1024,128]{1,0:T(8,128)(2,1)S(1)}, bf16[1024,128]{1,0:T(8,128)(2,1)S(1)}, u32[]{:S(2)}, u32[]{:S(2)}) collective-permute-start(bf16[1024,128]{1,0:T(8,128)(2,1)S(1)} %get-tuple-element.100), channel_id=1, source_target_pairs={{0,1},{1,0},{2,3},{3,2},{4,5},{5,4},{6,7},{7,6},{8,9},{9,8},{10,11... | collective-permute-start | bytes 786440 | tf_op jit(solution)/shard_map/ppermute | solution.py:540
  56.7 6.7 %collective-permute-start.16 = (bf16[1024,128]{1,0:T(8,128)(2,1)S(1)}, bf16[1024,128]{1,0:T(8,128)(2,1)S(1)}, u32[]{:S(2)}, u32[]{:S(2)}) collective-permute-start(bf16[1024,128]{1,0:T(8,128)(2,1)S(1)} %add.8), channel_id=1, source_target_pairs={{0,2},{1,3},{2,0},{3,1},{4,6},{5,7},{6,4},{7,5},{8,10},{9,11},{10,... | collective-permute-start | bytes 786440 | tf_op jit(solution)/shard_map/ppermute | solution.py:540
  57.3 7.0 %collective-permute-start.18 = (bf16[1024,128]{1,0:T(8,128)(2,1)S(1)}, bf16[1024,128]{1,0:T(8,128)(2,1)S(1)}, u32[]{:S(2)}, u32[]{:S(2)}) collective-permute-start(bf16[1024,128]{1,0:T(8,128)(2,1)S(1)} %add.9), channel_id=1, source_target_pairs={{0,1},{1,0},{2,3},{3,2},{4,5},{5,4},{6,7},{7,6},{8,9},{9,8},{10,11... | collective-permute-start | bytes 786440 | tf_op jit(solution)/shard_map/ppermute | solution.py:540

commit v9 on v8

--- a/solution.py
+++ b/solution.py
@@ -208,15 +208,21 @@
 
 
 EIGHTHS = {
-    "xf": (1, 0), "xp": (3, 0), "yf": (2, 1), "yp": (3, 1), "py": (2, 0), "px": (1, 1), "k0": (0, 0), "k1": (0, 1),
+    "xf": ("first", 0), "xp": ("both", 0), "yf": ("second", 1), "yp": ("both", 1),
+    "py": ("second", 0), "px": ("first", 1), "k0": ("own", 0), "k1": ("own", 1),
 }
+
+
+def _neighbour(which, core):
+    return {"own": 0, "first": 1 + core, "second": 2 - core, "both": 3}[which]
 
 
 def _weight_copies(names, w_ref, out_refs, sems):
     half = w_ref.shape[0] // (2 * N_FAST_HEAD)
     copies = []
     for n, name in enumerate(names):
-        flip, side = EIGHTHS[name]
+        which, side = EIGHTHS[name]
+        flip = _neighbour(which, lax.rem(_own_ctx(), 2))
         row = (lax.axis_index("head") ^ flip) * (2 * half) + side * half
         copies.append(pltpu.make_async_copy(w_ref.at[_rows(row, half)], out_refs[n], sems.at[n]))
     return copies
@@ -346,7 +352,7 @@
             pieces.append((n, p0))
         needed = functools.reduce(jnp.maximum, [tiles_needed(p0) for n, p0 in pieces])
         least = 0
-        for tiles in (2, 3, most_tiles):
+        for tiles in range(1, most_tiles + 1):
             fits = needed > least if tiles == most_tiles else (needed > least) & (needed <= tiles)
             pl.when(fits)(functools.partial(some_pieces, pieces, tiles * tile))
             least = tiles
@@ -540,6 +546,12 @@
     return lax.ppermute(x, axis, [(i, i ^ bits) for i in range(n)])
 
 
+def _swap(x, which):
+    places, heads = lax.axis_size("ctx"), lax.axis_size("head")
+    pairs = [(c * heads + h, c * heads + (h ^ _neighbour(which, c % 2))) for c in range(places) for h in range(heads)]
+    return lax.ppermute(x, ("ctx", "head"), pairs)
+
+
 def per_device_fast(queries, keys, values, out_weight, doc_lengths, owners):
     places = lax.axis_size("ctx")
     queries, keys, values, out_weight = (
@@ -561,21 +573,21 @@
     ctx1, ctx3 = _flip(ctx1, "ctx", 2), _flip(ctx3, "ctx", 6)
 
     xp, yp, joined = _join(ctx0, ctx2, weights)
-    x1p, y1p = _flip(xp, "head", 1), _flip(yp, "head", 2)
+    x1p, y1p = _swap(xp, "first"), _swap(yp, "second")
     xf, yf = _two_rows("last_rows", joined, weights, ("xf", "yf"))
-    x1f, y1f = _flip(xf, "head", 1), _flip(yf, "head", 2)
+    x1f, y1f = _swap(xf, "first"), _swap(yf, "second")
     weights["k0"], weights["k1"] = _stage_weights(("k0", "k1"), out_weight, joined)
     joined, weights["k0"], ctx1, ctx3 = lax.optimization_barrier((joined, weights["k0"], ctx1, ctx3))
     y2, x2 = _two_rows("pass_rows", joined, weights, ("py", "px"))
     y2, x2 = _add(y2, x1p), _add(x2, y1p)
     weights["xp"], y2, x2 = lax.optimization_barrier((weights["xp"], y2, x2))
-    y2, x2 = _flip(y2, "head", 2), _flip(x2, "head", 1)
+    y2, x2 = _swap(y2, "second"), _swap(x2, "first")
 
     xp, yp, joined2 = _join(ctx1, ctx3, weights)
     xp, yp, x1f, y1f = lax.optimization_barrier((xp, yp, x1f, y1f))
-    next_x1p, next_y1p = _flip(xp, "head", 1), _flip(yp, "head", 2)
+    next_x1p, next_y1p = _swap(xp, "first"), _swap(yp, "second")
     xf, yf = _two_rows("last_rows", joined2, weights, ("xf", "yf"))
-    next_x1f, next_y1f = _flip(xf, "head", 1), _flip(yf, "head", 2)
+    next_x1f, next_y1f = _swap(xf, "first"), _swap(yf, "second")
     keep, next_keep = _keep_rows(joined, joined2, weights)
     rows, tokens = keep.shape
     first, away = _finish(_finish_first_kernel, [
@@ -586,7 +598,7 @@
     away = _flip(away, "ctx", 4)
     y2, x2 = _two_rows("pass_rows", joined2, weights, ("py", "px"))
     y2, x2 = _add(y2, next_x1p), _add(x2, next_y1p)
-    y2, x2 = _flip(y2, "head", 2), _flip(x2, "head", 1)
+    y2, x2 = _swap(y2, "second"), _swap(x2, "first")
     away = _finish(_unpack_kernel, [jax.ShapeDtypeStruct((rows, tokens), jnp.bfloat16)], (away,))[0]
     away, next_keep = lax.optimization_barrier((away, next_keep))
     bottom = _half_sum(1, next_keep, next_y1f)

time: 65.8 us -> 65.7 us (level)
    ppermute x0 -> x12, starting transfers between devices: none -> 12.5 us  [_swap(): return lax.ppermute(x, ('ctx', 'head'), pairs)]
    ppermute x18 -> x6, starting transfers between devices: 17.8 us -> 5.84 us  [_flip(): return lax.ppermute(x, axis, [(i, i ^ bits) for i in range(n)])]
    ppermute x0 -> x12, waiting for transfers between devices: none -> 2.29 us  [_swap(): return lax.ppermute(x, ('ctx', 'head'), pairs)]
    ppermute x18 -> x6, waiting for transfers between devices: 7.61 us -> 5.35 us  [_flip(): return lax.ppermute(x, axis, [(i, i ^ bits) for i in range(n)])]
where the time goes in v9:
time: 65.7 us
  Pallas kernels  33.6 us (51%)
  starting transfers between devices  23.3 us (35%)
  waiting for transfers between devices  7.64 us (12%)
  other arithmetic  0.75 us (1%)
    pallas_call x11, Pallas kernels, _project(): pl.pallas_call(kernel, out_shape=out_shape, in_specs=[VMEM] * len(operand...  16.7 us
    ppermute x12, starting transfers between devices, _swap(): return lax.ppermute(x, ('ctx', 'head'), pairs)  12.5 us
    pallas_call x2, Pallas kernels, _stage_weights(): pl.pallas_call(functools.partial(_stage_kernel, names), out_shape=[_eight...  6.96 us
    ppermute x6, starting transfers between devices, _flip(): return lax.ppermute(x, axis, [(i, i ^ bits) for i in range(n)])  5.84 us
    ppermute x6, waiting for transfers between devices, _flip(): return lax.ppermute(x, axis, [(i, i ^ bits) for i in range(n)])  5.35 us
    ppermute x1, starting transfers between devices, per_device_fast(): kv2 = lax.ppermute(kv0, 'ctx', [(i, i + 2) for i in range(places - 2)])  4.94 us
    pallas_call x1, Pallas kernels, _attend_groups(): pl.pallas_call(functools.partial(_attend_kernel, groups, names, documents...  4.74 us
    pallas_call x1, Pallas kernels, _queries_for_other_core(): pl.pallas_call(functools.partial(_queries_for_other_core_kernel, names),...  2.54 us
  transfers between devices with their start and end apart: 19, of which 4 were waited for; matrix products, arithmetic and copies ran while one was open for 1% of the time, Pallas kernels for 41%

profile of v9, /device:TPU:0, one launch (start us, length us, event | category | flops | bytes accessed | tf_op | source)
XLA Modules:
  0.0 65.7 jit_solution(11772141661194956062)
XLA Ops:
  0.0 1.0 %join_keys_values.1.kv0_ref = bf16[512,256]{1,0:T(8,128)(2,1)S(1)} custom-call(bf16[256,256]{1,0:T(8,128)(2,1)} %keys_ref.1, bf16[256,256]{1,0:T(8,128)(2,1)} %values_ref.1), custom_call_target="tpu_custom_call" | custom-call | flops 1 | bytes 1 | tf_op jit(solution)/shard_map/join_keys_values/pallas_call | solution.py:159
  1.0 4.9 %collective-permute-start.2 = (bf16[512,256]{1,0:T(8,128)(2,1)S(1)}, bf16[512,256]{1,0:T(8,128)(2,1)S(1)}, u32[]{:S(2)}, u32[]{:S(2)}) collective-permute-start(bf16[512,256]{1,0:T(8,128)(2,1)S(1)} %join_keys_values.1.kv0_ref), channel_id=1, source_target_pairs={{0,8},{4,12},{8,16},{12,20},{16,24},{20,28},{1,9},{5,13},{9,17},{1... | collective-permute-start | bytes 786440 | tf_op jit(solution)/shard_map/ppermute | solution.py:560
  5.9 0.7 %pad_add_fusion.meta_ref = s32[80]{0:T(128)S(1)} fusion(s32[16]{0:T(128)} %param.10, s32[64]{0:T(128)} %bitcast.1), kind=kLoop, calls=%fused_computation | loop fusion | flops 80 | bytes 640 | tf_op jit(solution)/shard_map/concatenate | solution.py:562
  6.7 2.5 %queries_for_other_core.1 = (bf16[128,2048]{1,0:T(8,128)(2,1)S(1)}, bf16[256,2048]{1,0:T(8,128)(2,1)S(1)}, bf16[1024,2048]{1,0:T(8,128)(2,1)S(1)}) custom-call(s32[80]{0:T(128)S(1)} %pad_add_fusion.meta_ref, bf16[256,2048]{1,0:T(8,128)(2,1)} %queries_ref.1, bf16[8192,2048]{1,0:T(8,128)(2,1)} %w_ref.7), custom_call_target="tpu_custom_call" | custom-call | flops 1 | bytes 1 | tf_op jit(solution)/shard_map/queries_for_other_core/pallas_call | solution.py:193
  9.2 0.1 collective-permute-start
  9.3 0.5 collective-permute-start.1
  9.8 3.5 %stage_weights.2 = (bf16[1024,2048]{1,0:T(8,128)(2,1)S(1)}, bf16[1024,2048]{1,0:T(8,128)(2,1)S(1)}) custom-call(bf16[8192,2048]{1,0:T(8,128)(2,1)} %w_ref.7, bf16[128,2048]{1,0:T(8,128)(2,1)S(1)} %get-tuple-element.57.after_ref), custom_call_target="tpu_custom_call" | custom-call | flops 1 | bytes 1 | tf_op jit(solution)/shard_map/stage_weights/pallas_call | solution.py:244
  13.3 0.0 collective-permute-done.2.kv2_ref
  13.3 0.1 collective-permute-start.3
  13.5 0.0 collective-permute-done.1.kv1_ref
  13.5 0.0 collective-permute-done.other_ref
  13.5 1.5 %collective-permute-done.3.kv3_ref = bf16[512,256]{1,0:T(8,128)(2,1)S(1)} collective-permute-done((bf16[512,256]{1,0:T(8,128)(2,1)S(1)}, bf16[512,256]{1,0:T(8,128)(2,1)S(1)}, u32[]{:S(2)}, u32[]{:S(2)}) %collective-permute-start.3) | collective-permute-done | bytes 262176 | tf_op jit(solution)/shard_map/ppermute | solution.py:546
  14.9 4.7 %attend_groups.1 = (bf16[64,2048]{1,0:T(8,128)(2,1)S(1)}, bf16[64,2048]{1,0:T(8,128)(2,1)S(1)}, bf16[64,2048]{1,0:T(8,128)(2,1)S(1)}, bf16[64,2048]{1,0:T(8,128)...) custom-call(s32[80]{0:T(128)S(1)} %pad_add_fusion.meta_ref, ...), custom_call_target="tpu_custom_call" | custom-call | flops 1 | bytes 1 | tf_op jit(solution)/shard_map/attend_groups/pallas_call | solution.py:371
  19.7 1.6 %collective-permute-start.4 = (bf16[64,2048]{1,0:T(8,128)(2,1)S(1)}, bf16[64,2048]{1,0:T(8,128)(2,1)S(1)}, u32[]{:S(2)}, u32[]{:S(2)}) collective-permute-start(bf16[64,2048]{1,0:T(8,128)(2,1)S(1)} %get-tuple-element.66), channel_id=1, source_target_pairs={{0,8},{4,12},{8,0},{12,4},{16,24},{20,28},{24,16},{28,20},{1,9},{5... | collective-permute-start | bytes 786440 | tf_op jit(solution)/shard_map/ppermute | solution.py:546
  21.3 3.2 %collective-permute-start.5 = (bf16[64,2048]{1,0:T(8,128)(2,1)S(1)}, bf16[64,2048]{1,0:T(8,128)(2,1)S(1)}, u32[]{:S(2)}, u32[]{:S(2)}) collective-permute-start(bf16[64,2048]{1,0:T(8,128)(2,1)S(1)} %get-tuple-element.67), channel_id=1, source_target_pairs={{0,24},{4,28},{8,16},{12,20},{16,8},{20,12},{24,0},{28,4},{1,25},{... | collective-permute-start | bytes 786440 | tf_op jit(solution)/shard_map/ppermute | solution.py:546
  24.4 2.4 %join.2 = (bf16[1024,128]{1,0:T(8,128)(2,1)S(1)}, bf16[1024,128]{1,0:T(8,128)(2,1)S(1)}, bf16[2048,128]{1,0:T(8,128)(2,1)S(1)}) custom-call(bf16[64,2048]{1,0:T(8,128)(2,1)S(1)} %get-tuple-element.60.a_ref, bf16[64,2048]{1,0:T(8,128)(2,1)S(1)} %get-tuple-element.61.b_ref, bf16[1024,2048]{1,0:T(8,128)(2,1)S(1)} %get-tuple-element.77.wx_ref, ...), custom_call_target="tpu_custom_call" | custom-call | flops 1 | bytes 1 | tf_op jit(solution)/shard_map/join/pallas_call | solution.py:423
  26.9 1.5 %collective-permute-start.6 = (bf16[1024,128]{1,0:T(8,128)(2,1)S(1)}, bf16[1024,128]{1,0:T(8,128)(2,1)S(1)}, u32[]{:S(2)}, u32[]{:S(2)}) collective-permute-start(bf16[1024,128]{1,0:T(8,128)(2,1)S(1)} %get-tuple-element.74), channel_id=1, source_target_pairs={{0,1},{1,0},{2,3},{3,2},{4,6},{5,7},{6,4},{7,5},{8,9},{9,8},{10,11... | collective-permute-start | bytes 786440 | tf_op jit(solution)/shard_map/ppermute | solution.py:552
  28.4 1.5 %collective-permute-start.7 = (bf16[1024,128]{1,0:T(8,128)(2,1)S(1)}, bf16[1024,128]{1,0:T(8,128)(2,1)S(1)}, u32[]{:S(2)}, u32[]{:S(2)}) collective-permute-start(bf16[1024,128]{1,0:T(8,128)(2,1)S(1)} %get-tuple-element.76), channel_id=1, source_target_pairs={{0,2},{1,3},{2,0},{3,1},{4,5},{5,4},{6,7},{7,6},{8,10},{9,11},{10,... | collective-permute-start | bytes 786440 | tf_op jit(solution)/shard_map/ppermute | solution.py:552
  29.9 2.3 %last_rows.2 = (bf16[1024,128]{1,0:T(8,128)(2,1)S(1)}, bf16[1024,128]{1,0:T(8,128)(2,1)S(1)}) custom-call(bf16[2048,128]{1,0:T(8,128)(2,1)S(1)} %get-tuple-element.68.after_ref.joined_ref.first_ref, bf16[1024,2048]{1,0:T(8,128)(2,1)S(1)} %get-tuple-element.84.w0_ref, bf16[1024,2048]{1,0:T(8,128)(2,1)S(1)} %get-tuple-element.85.w1_ref), custom_call_target="tpu_custom_call" | custom-call | flops 1 | bytes 1 | tf_op jit(solution)/shard_map/last_rows/pallas_call | solution.py:423
  32.3 0.6 collective-permute-start.8
  32.9 0.0 collective-permute-done.4.a_ref
  32.9 0.5 collective-permute-start.9
  33.4 3.5 %stage_weights.3 = (bf16[1024,2048]{1,0:T(8,128)(2,1)S(1)}, bf16[1024,2048]{1,0:T(8,128)(2,1)S(1)}) custom-call(bf16[8192,2048]{1,0:T(8,128)(2,1)} %w_ref.7, bf16[2048,128]{1,0:T(8,128)(2,1)S(1)} %get-tuple-element.68.after_ref.joined_ref.first_ref), custom_call_target="tpu_custom_call" | custom-call | flops 1 | bytes 1 | tf_op jit(solution)/shard_map/stage_weights/pallas_call | solution.py:244
  36.9 0.0 collective-permute-done.5.b_ref
  36.9 2.3 %pass_rows.2 = (bf16[1024,128]{1,0:T(8,128)(2,1)S(1)}, bf16[1024,128]{1,0:T(8,128)(2,1)S(1)}) custom-call(bf16[2048,128]{1,0:T(8,128)(2,1)S(1)} %get-tuple-element.68.after_ref.joined_ref.first_ref, bf16[1024,2048]{1,0:T(8,128)(2,1)S(1)} %get-tuple-element.71.w0_ref, bf16[1024,2048]{1,0:T(8,128)(2,1)S(1)} %get-tuple-element.72.w1_ref), custom_call_target="tpu_custom_call" | custom-call | flops 1 | bytes 1 | tf_op jit(solution)/shard_map/pass_rows/pallas_call | solution.py:423
  39.2 0.0 collective-permute-done.6.b_ref
  39.2 0.1 add.6
  39.3 0.0 collective-permute-done.7.b_ref
  39.3 0.1 add.7
  39.4 1.6 %collective-permute-start.10 = (bf16[1024,128]{1,0:T(8,128)(2,1)S(1)}, bf16[1024,128]{1,0:T(8,128)(2,1)S(1)}, u32[]{:S(2)}, u32[]{:S(2)}) collective-permute-start(bf16[1024,128]{1,0:T(8,128)(2,1)S(1)} %add.6), channel_id=1, source_target_pairs={{0,2},{1,3},{2,0},{3,1},{4,5},{5,4},{6,7},{7,6},{8,10},{9,11},{10,... | collective-permute-start | bytes 786440 | tf_op jit(solution)/shard_map/ppermute | solution.py:552
  40.9 1.5 %collective-permute-start.11 = (bf16[1024,128]{1,0:T(8,128)(2,1)S(1)}, bf16[1024,128]{1,0:T(8,128)(2,1)S(1)}, u32[]{:S(2)}, u32[]{:S(2)}) collective-permute-start(bf16[1024,128]{1,0:T(8,128)(2,1)S(1)} %add.7), channel_id=1, source_target_pairs={{0,1},{1,0},{2,3},{3,2},{4,6},{5,7},{6,4},{7,5},{8,9},{9,8},{10,11... | collective-permute-start | bytes 786440 | tf_op jit(solution)/shard_map/ppermute | solution.py:552
  42.4 2.4 %join.3 = (bf16[1024,128]{1,0:T(8,128)(2,1)S(1)}, bf16[1024,128]{1,0:T(8,128)(2,1)S(1)}, bf16[2048,128]{1,0:T(8,128)(2,1)S(1)}) custom-call(bf16[64,2048]{1,0:T(8,128)(2,1)S(1)} %collective-permute-done.4.a_ref, bf16[64,2048]{1,0:T(8,128)(2,1)S(1)} %collective-permute-done.5.b_ref, bf16[1024,2048]{1,0:T(8,128)(2,1)S(1)} %get-tuple-element.77.wx_ref, ...), custom_call_target="tpu_custom_call" | custom-call | flops 1 | bytes 1 | tf_op jit(solution)/shard_map/join/pallas_call | solution.py:423
  44.8 0.0 collective-permute-done.8.x1_ref
  44.9 0.0 collective-permute-done.9.y1_ref
  44.9 0.6 collective-permute-start.15
  45.5 0.5 collective-permute-start.17
  46.0 2.3 %last_rows.3 = (bf16[1024,128]{1,0:T(8,128)(2,1)S(1)}, bf16[1024,128]{1,0:T(8,128)(2,1)S(1)}) custom-call(bf16[2048,128]{1,0:T(8,128)(2,1)S(1)} %get-tuple-element.102.second_ref.joined_ref, bf16[1024,2048]{1,0:T(8,128)(2,1)S(1)} %get-tuple-element.84.w0_ref, bf16[1024,2048]{1,0:T(8,128)(2,1)S(1)} %get-tuple-element.85.w1_ref), custom_call_target="tpu_custom_call" | custom-call | flops 1 | bytes 1 | tf_op jit(solution)/shard_map/last_rows/pallas_call | solution.py:423
  48.3 2.3 %keep_rows.1 = (bf16[2048,128]{1,0:T(8,128)(2,1)S(1)}, bf16[2048,128]{1,0:T(8,128)(2,1)S(1)}) custom-call(bf16[2048,128]{1,0:T(8,128)(2,1)S(1)} %get-tuple-element.68.after_ref.joined_ref.first_ref, bf16[2048,128]{1,0:T(8,128)(2,1)S(1)} %get-tuple-element.102.second_ref.joined_ref, bf16[1024,2048]{1,0:T(8,128)(2,1)S(1)} %get-tuple-element.79.w0_ref, ...), custom_call_target="tpu_custom_call" | custom-call | flops 1 | bytes 1 | tf_op jit(solution)/shard_map/keep_rows/pallas_call | solution.py:423
  50.7 0.0 collective-permute-done.10.y2_ref
  50.7 0.0 collective-permute-done.11.x2_ref
  50.7 0.2 finish.4
  50.9 0.3 collective-permute-start.12
  51.3 1.3 %collective-permute-start.13 = (bf16[1024,128]{1,0:T(8,128)(2,1)S(1)}, bf16[1024,128]{1,0:T(8,128)(2,1)S(1)}, u32[]{:S(2)}, u32[]{:S(2)}) collective-permute-start(bf16[1024,128]{1,0:T(8,128)(2,1)S(1)} %get-tuple-element.98), channel_id=1, source_target_pairs={{0,2},{1,3},{2,0},{3,1},{4,5},{5,4},{6,7},{7,6},{8,10},{9,11},{10,... | collective-permute-start | bytes 786440 | tf_op jit(solution)/shard_map/ppermute | solution.py:552
  52.6 1.5 %collective-permute-start.14 = (bf16[1024,128]{1,0:T(8,128)(2,1)S(1)}, bf16[1024,128]{1,0:T(8,128)(2,1)S(1)}, u32[]{:S(2)}, u32[]{:S(2)}) collective-permute-start(bf16[1024,128]{1,0:T(8,128)(2,1)S(1)} %get-tuple-element.100), channel_id=1, source_target_pairs={{0,1},{1,0},{2,3},{3,2},{4,6},{5,7},{6,4},{7,5},{8,9},{9,8},{10,11... | collective-permute-start | bytes 786440 | tf_op jit(solution)/shard_map/ppermute | solution.py:552
  54.1 2.3 %pass_rows.3 = (bf16[1024,128]{1,0:T(8,128)(2,1)S(1)}, bf16[1024,128]{1,0:T(8,128)(2,1)S(1)}) custom-call(bf16[2048,128]{1,0:T(8,128)(2,1)S(1)} %get-tuple-element.102.second_ref.joined_ref, bf16[1024,2048]{1,0:T(8,128)(2,1)S(1)} %get-tuple-element.71.w0_ref, bf16[1024,2048]{1,0:T(8,128)(2,1)S(1)} %get-tuple-element.72.w1_ref), custom_call_target="tpu_custom_call" | custom-call | flops 1 | bytes 1 | tf_op jit(solution)/shard_map/pass_rows/pallas_call | solution.py:423
  56.4 0.0 collective-permute-done.15.b_ref
  56.4 0.1 add.8
  56.5 0.8 %collective-permute-start.16 = (bf16[1024,128]{1,0:T(8,128)(2,1)S(1)}, bf16[1024,128]{1,0:T(8,128)(2,1)S(1)}, u32[]{:S(2)}, u32[]{:S(2)}) collective-permute-start(bf16[1024,128]{1,0:T(8,128)(2,1)S(1)} %add.8), channel_id=1, source_target_pairs={{0,2},{1,3},{2,0},{3,1},{4,5},{5,4},{6,7},{7,6},{8,10},{9,11},{10,... | collective-permute-start | bytes 786440 | tf_op jit(solution)/shard_map/ppermute | solution.py:552
  57.3 0.0 collective-permute-done.17.b_ref
  57.3 0.1 add.9
  57.3 0.6 collective-permute-start.18
  57.9 3.9 %collective-permute-done.12.away_ref = bf16[1024,128]{1,0:T(8,128)(2,1)S(1)} collective-permute-done((bf16[1024,128]{1,0:T(8,128)(2,1)S(1)}, bf16[1024,128]{1,0:T(8,128)(2,1)S(1)}, u32[]{:S(2)}, u32[]{:S(2)}) %collective-permute-start.12) | collective-permute-done | bytes 262176 | tf_op jit(solution)/shard_map/ppermute | solution.py:546
  61.8 0.1 finish.5.away_ref
  62.0 0.0 collective-permute-done.13.one_ref
  62.0 0.1 finish.6.bottom_ref
  62.0 0.0 collective-permute-done.14.one_ref
  62.0 0.1 finish.7.top_ref
  62.1 2.1 %collective-permute-done.16.y2_ref = bf16[1024,128]{1,0:T(8,128)(2,1)S(1)} collective-permute-done((bf16[1024,128]{1,0:T(8,128)(2,1)S(1)}, bf16[1024,128]{1,0:T(8,128)(2,1)S(1)}, u32[]{:S(2)}, u32[]{:S(2)}) %collective-permute-start.16) | collective-permute-done | bytes 262176 | tf_op jit(solution)/shard_map/ppermute | solution.py:552
  64.2 0.2 collective-permute-done.18.x2_ref
  64.4 1.2 %finish_second.1 = bf16[2048,256]{1,0:T(8,128)(2,1)} custom-call(bf16[2048,128]{1,0:T(8,128)(2,1)S(1)} %get-tuple-element.92.first_ref, bf16[2048,128]{1,0:T(8,128)(2,1)S(1)} %finish.5.away_ref, f32[1024,128]{1,0:T(8,128)S(1)} %finish.7.top_ref, f32[1024,128]{1,0:T(8,128)S(1)} %finish.6.bottom_ref, bf16[1024,128]{1,0:T(8,128)(2,1)S(1)} %collective-permute-done.16.y2_ref, ...), custom_call_target="tpu_custom_call" | custom-call | flops 1 | bytes 1 | tf_op jit(solution)/shard_map/finish_second/pallas_call | solution.py:520
Async XLA Ops:
  1.0 12.3 %collective-permute-start.2 = (bf16[512,256]{1,0:T(8,128)(2,1)S(1)}, bf16[512,256]{1,0:T(8,128)(2,1)S(1)}, u32[]{:S(2)}, u32[]{:S(2)}) collective-permute-start(bf16[512,256]{1,0:T(8,128)(2,1)S(1)} %join_keys_values.1.kv0_ref), channel_id=1, source_target_pairs={{0,8},{4,12},{8,16},{12,20},{16,24},{20,28},{1,9},{5,13},{9,17},{1... | collective-permute-start | bytes 786440 | tf_op jit(solution)/shard_map/ppermute | solution.py:560
  9.2 4.2 %collective-permute-start = (bf16[128,2048]{1,0:T(8,128)(2,1)S(1)}, bf16[128,2048]{1,0:T(8,128)(2,1)S(1)}, u32[]{:S(2)}, u32[]{:S(2)}) collective-permute-start(bf16[128,2048]{1,0:T(8,128)(2,1)S(1)} %get-tuple-element.57.after_ref), channel_id=1, source_target_pairs={{0,4},{4,0},{8,12},{12,8},{16,20},{20,16},{24,28},{28,24},{1,5},{5... | collective-permute-start | bytes 1572872 | tf_op jit(solution)/shard_map/ppermute | solution.py:546
  9.3 4.1 %collective-permute-start.1 = (bf16[512,256]{1,0:T(8,128)(2,1)S(1)}, bf16[512,256]{1,0:T(8,128)(2,1)S(1)}, u32[]{:S(2)}, u32[]{:S(2)}) collective-permute-start(bf16[512,256]{1,0:T(8,128)(2,1)S(1)} %join_keys_values.1.kv0_ref), channel_id=1, source_target_pairs={{0,4},{4,0},{8,12},{12,8},{16,20},{20,16},{24,28},{28,24},{1,5},{5... | collective-permute-start | bytes 786440 | tf_op jit(solution)/shard_map/ppermute | solution.py:546
  13.3 1.6 %collective-permute-start.3 = (bf16[512,256]{1,0:T(8,128)(2,1)S(1)}, bf16[512,256]{1,0:T(8,128)(2,1)S(1)}, u32[]{:S(2)}, u32[]{:S(2)}) collective-permute-start(bf16[512,256]{1,0:T(8,128)(2,1)S(1)} %collective-permute-done.2.kv2_ref), channel_id=1, source_target_pairs={{0,4},{4,0},{8,12},{12,8},{16,20},{20,16},{24,28},{28,24},{1,5},{5... | collective-permute-start | bytes 786440 | tf_op jit(solution)/shard_map/ppermute | solution.py:546
  19.7 13.2 %collective-permute-start.4 = (bf16[64,2048]{1,0:T(8,128)(2,1)S(1)}, bf16[64,2048]{1,0:T(8,128)(2,1)S(1)}, u32[]{:S(2)}, u32[]{:S(2)}) collective-permute-start(bf16[64,2048]{1,0:T(8,128)(2,1)S(1)} %get-tuple-element.66), channel_id=1, source_target_pairs={{0,8},{4,12},{8,0},{12,4},{16,24},{20,28},{24,16},{28,20},{1,9},{5... | collective-permute-start | bytes 786440 | tf_op jit(solution)/shard_map/ppermute | solution.py:546
  21.3 15.6 %collective-permute-start.5 = (bf16[64,2048]{1,0:T(8,128)(2,1)S(1)}, bf16[64,2048]{1,0:T(8,128)(2,1)S(1)}, u32[]{:S(2)}, u32[]{:S(2)}) collective-permute-start(bf16[64,2048]{1,0:T(8,128)(2,1)S(1)} %get-tuple-element.67), channel_id=1, source_target_pairs={{0,24},{4,28},{8,16},{12,20},{16,8},{20,12},{24,0},{28,4},{1,25},{... | collective-permute-start | bytes 786440 | tf_op jit(solution)/shard_map/ppermute | solution.py:546
  26.9 12.3 %collective-permute-start.6 = (bf16[1024,128]{1,0:T(8,128)(2,1)S(1)}, bf16[1024,128]{1,0:T(8,128)(2,1)S(1)}, u32[]{:S(2)}, u32[]{:S(2)}) collective-permute-start(bf16[1024,128]{1,0:T(8,128)(2,1)S(1)} %get-tuple-element.74), channel_id=1, source_target_pairs={{0,1},{1,0},{2,3},{3,2},{4,6},{5,7},{6,4},{7,5},{8,9},{9,8},{10,11... | collective-permute-start | bytes 786440 | tf_op jit(solution)/shard_map/ppermute | solution.py:552
  28.4 10.9 %collective-permute-start.7 = (bf16[1024,128]{1,0:T(8,128)(2,1)S(1)}, bf16[1024,128]{1,0:T(8,128)(2,1)S(1)}, u32[]{:S(2)}, u32[]{:S(2)}) collective-permute-start(bf16[1024,128]{1,0:T(8,128)(2,1)S(1)} %get-tuple-element.76), channel_id=1, source_target_pairs={{0,2},{1,3},{2,0},{3,1},{4,5},{5,4},{6,7},{7,6},{8,10},{9,11},{10,... | collective-permute-start | bytes 786440 | tf_op jit(solution)/shard_map/ppermute | solution.py:552
  32.3 12.6 %collective-permute-start.8 = (bf16[1024,128]{1,0:T(8,128)(2,1)S(1)}, bf16[1024,128]{1,0:T(8,128)(2,1)S(1)}, u32[]{:S(2)}, u32[]{:S(2)}) collective-permute-start(bf16[1024,128]{1,0:T(8,128)(2,1)S(1)} %get-tuple-element.86), channel_id=1, source_target_pairs={{0,1},{1,0},{2,3},{3,2},{4,6},{5,7},{6,4},{7,5},{8,9},{9,8},{10,11... | collective-permute-start | bytes 786440 | tf_op jit(solution)/shard_map/ppermute | solution.py:552
  32.9 12.0 %collective-permute-start.9 = (bf16[1024,128]{1,0:T(8,128)(2,1)S(1)}, bf16[1024,128]{1,0:T(8,128)(2,1)S(1)}, u32[]{:S(2)}, u32[]{:S(2)}) collective-permute-start(bf16[1024,128]{1,0:T(8,128)(2,1)S(1)} %get-tuple-element.87), channel_id=1, source_target_pairs={{0,2},{1,3},{2,0},{3,1},{4,5},{5,4},{6,7},{7,6},{8,10},{9,11},{10,... | collective-permute-start | bytes 786440 | tf_op jit(solution)/shard_map/ppermute | solution.py:552
  39.4 11.3 %collective-permute-start.10 = (bf16[1024,128]{1,0:T(8,128)(2,1)S(1)}, bf16[1024,128]{1,0:T(8,128)(2,1)S(1)}, u32[]{:S(2)}, u32[]{:S(2)}) collective-permute-start(bf16[1024,128]{1,0:T(8,128)(2,1)S(1)} %add.6), channel_id=1, source_target_pairs={{0,2},{1,3},{2,0},{3,1},{4,5},{5,4},{6,7},{7,6},{8,10},{9,11},{10,... | collective-permute-start | bytes 786440 | tf_op jit(solution)/shard_map/ppermute | solution.py:552
  40.9 9.7 %collective-permute-start.11 = (bf16[1024,128]{1,0:T(8,128)(2,1)S(1)}, bf16[1024,128]{1,0:T(8,128)(2,1)S(1)}, u32[]{:S(2)}, u32[]{:S(2)}) collective-permute-start(bf16[1024,128]{1,0:T(8,128)(2,1)S(1)} %add.7), channel_id=1, source_target_pairs={{0,1},{1,0},{2,3},{3,2},{4,6},{5,7},{6,4},{7,5},{8,9},{9,8},{10,11... | collective-permute-start | bytes 786440 | tf_op jit(solution)/shard_map/ppermute | solution.py:552
  44.9 11.5 %collective-permute-start.15 = (bf16[1024,128]{1,0:T(8,128)(2,1)S(1)}, bf16[1024,128]{1,0:T(8,128)(2,1)S(1)}, u32[]{:S(2)}, u32[]{:S(2)}) collective-permute-start(bf16[1024,128]{1,0:T(8,128)(2,1)S(1)} %get-tuple-element.104), channel_id=1, source_target_pairs={{0,1},{1,0},{2,3},{3,2},{4,6},{5,7},{6,4},{7,5},{8,9},{9,8},{10,11... | collective-permute-start | bytes 786440 | tf_op jit(solution)/shard_map/ppermute | solution.py:552
  45.5 11.8 %collective-permute-start.17 = (bf16[1024,128]{1,0:T(8,128)(2,1)S(1)}, bf16[1024,128]{1,0:T(8,128)(2,1)S(1)}, u32[]{:S(2)}, u32[]{:S(2)}) collective-permute-start(bf16[1024,128]{1,0:T(8,128)(2,1)S(1)} %get-tuple-element.106), channel_id=1, source_target_pairs={{0,2},{1,3},{2,0},{3,1},{4,5},{5,4},{6,7},{7,6},{8,10},{9,11},{10,... | collective-permute-start | bytes 786440 | tf_op jit(solution)/shard_map/ppermute | solution.py:552
  50.9 10.9 %collective-permute-start.12 = (bf16[1024,128]{1,0:T(8,128)(2,1)S(1)}, bf16[1024,128]{1,0:T(8,128)(2,1)S(1)}, u32[]{:S(2)}, u32[]{:S(2)}) collective-permute-start(bf16[1024,128]{1,0:T(8,128)(2,1)S(1)} %get-tuple-element.94), channel_id=1, source_target_pairs={{0,16},{4,20},{8,24},{12,28},{16,0},{20,4},{24,8},{28,12},{1,17},{... | collective-permute-start | bytes 786440 | tf_op jit(solution)/shard_map/ppermute | solution.py:546
  51.3 10.7 %collective-permute-start.13 = (bf16[1024,128]{1,0:T(8,128)(2,1)S(1)}, bf16[1024,128]{1,0:T(8,128)(2,1)S(1)}, u32[]{:S(2)}, u32[]{:S(2)}) collective-permute-start(bf16[1024,128]{1,0:T(8,128)(2,1)S(1)} %get-tuple-element.98), channel_id=1, source_target_pairs={{0,2},{1,3},{2,0},{3,1},{4,5},{5,4},{6,7},{7,6},{8,10},{9,11},{10,... | collective-permute-start | bytes 786440 | tf_op jit(solution)/shard_map/ppermute | solution.py:552
  52.6 9.5 %collective-permute-start.14 = (bf16[1024,128]{1,0:T(8,128)(2,1)S(1)}, bf16[1024,128]{1,0:T(8,128)(2,1)S(1)}, u32[]{:S(2)}, u32[]{:S(2)}) collective-permute-start(bf16[1024,128]{1,0:T(8,128)(2,1)S(1)} %get-tuple-element.100), channel_id=1, source_target_pairs={{0,1},{1,0},{2,3},{3,2},{4,6},{5,7},{6,4},{7,5},{8,9},{9,8},{10,11... | collective-permute-start | bytes 786440 | tf_op jit(solution)/shard_map/ppermute | solution.py:552
  56.5 7.7 %collective-permute-start.16 = (bf16[1024,128]{1,0:T(8,128)(2,1)S(1)}, bf16[1024,128]{1,0:T(8,128)(2,1)S(1)}, u32[]{:S(2)}, u32[]{:S(2)}) collective-permute-start(bf16[1024,128]{1,0:T(8,128)(2,1)S(1)} %add.8), channel_id=1, source_target_pairs={{0,2},{1,3},{2,0},{3,1},{4,5},{5,4},{6,7},{7,6},{8,10},{9,11},{10,... | collective-permute-start | bytes 786440 | tf_op jit(solution)/shard_map/ppermute | solution.py:552
  57.3 7.0 %collective-permute-start.18 = (bf16[1024,128]{1,0:T(8,128)(2,1)S(1)}, bf16[1024,128]{1,0:T(8,128)(2,1)S(1)}, u32[]{:S(2)}, u32[]{:S(2)}) collective-permute-start(bf16[1024,128]{1,0:T(8,128)(2,1)S(1)} %add.9), channel_id=1, source_target_pairs={{0,1},{1,0},{2,3},{3,2},{4,6},{5,7},{6,4},{7,5},{8,9},{9,8},{10,11... | collective-permute-start | bytes 786440 | tf_op jit(solution)/shard_map/ppermute | solution.py:552
